TPU v7x, 32 devices: a whole 2x2x4 slice. The times are simulated.
32 devices in a mesh: groups: 2 (over y), pool: 4 (over x, core), tensor: 4 (over z).
Axes of the slice: x: 2, y: 2, z: 4, core: 2. Of those that a mesh axis runs over, the one named last changes fastest.
Arguments:
- hidden: bfloat16 [1024, 28672], P(('groups', 'pool'), 'tensor'), parts along dimension 0, may hold values from -6 to 6
- down_weight: bfloat16 [28672, 8192], P('tensor', 'pool'), may hold values from -0.03125 to 0.03125
- adapter_input_maps: bfloat16 [64, 64, 28672], P('pool', None, 'tensor'), may hold values from -0.03125 to 0.03125
- adapter_output_maps: bfloat16 [4096, 8192], P(('pool', 'tensor')), may hold values from -0.75 to 0.75
- request_list_slot: int32 [1024], P('groups'), parts along dimension 0, may hold values from 0 to 15
- group_adapter_lists: int32 [8, 16], P('groups'), parts along dimension 0, may hold values from 0 to 63, as said below
Outputs:
- mixed: bfloat16 [1024, 8192], P(('groups', 'tensor'), 'pool'), parts along dimension 0
There are 2 independent parts, one for each index of `groups`. A program takes and returns all parts, laid end to end along the dimension named above; an argument that names none is the same for every part. Nothing has to cross between parts.
Inputs may be any that keep to these rules, and one draw needn't show every extreme that they name: `group_adapter_lists`: row g lists 16 distinct adapters for request group g. The owner of adapter a is a // 16; each row's adapters belong to exactly 4 owners, exactly 4 from each of them.
All inputs are finite; a program needn't handle non-finite values.
Results may differ from a plain program's by a relative error of at most 0.0065.
Values may be sent and summed in bfloat16 or wider, within the bound.
No kernel may reach another device: no remote copies, remote signals or barrier semaphores. Data moves between devices by JAX's collectives and lax.ppermute only.
A program may use at most 192 MiB of HBM per device.

v0:
```python
import jax
import jax.numpy as jnp
from jax import lax
from jax.sharding import PartitionSpec as P

CAP = 4


def pick_rank(values, wanted, rank_extent):
    columns = jnp.arange(values.shape[1], dtype=jnp.int32)
    keep = wanted[:, None] == (columns // rank_extent)[None, :]
    masked = jnp.where(keep, values, 0.0)
    fold = (
        (columns % rank_extent)[:, None] == jnp.arange(rank_extent, dtype=jnp.int32)[None, :]
    ).astype(jnp.float32)
    return jnp.dot(
        masked, fold, precision=lax.Precision.HIGHEST, preferred_element_type=jnp.float32
    )


def per_device(
    hidden,
    down_weight,
    adapter_input_maps,
    adapter_output_maps,
    request_list_slot,
    group_adapter_lists,
):
    group_rows = hidden.shape[0]
    hidden_extent = hidden.shape[1]
    pool_count = lax.axis_size("pool")
    tensor_count = lax.axis_size("tensor")
    pool_index = lax.axis_index("pool")
    tensor_index = lax.axis_index("tensor")
    holding_count = adapter_input_maps.shape[0]
    rank_extent = adapter_input_maps.shape[1]
    slot_count = group_adapter_lists.shape[1]
    total_rows = group_rows * pool_count
    contract = (((1,), (1,)), ((), ()))
    row_group = jnp.arange(total_rows, dtype=jnp.int32) // group_rows
    group_hot = row_group[:, None] == jnp.arange(pool_count, dtype=jnp.int32)[None, :]
    row_lists = jnp.sum(
        jnp.where(group_hot[:, :, None], group_adapter_lists[None, :, :], 0), axis=1
    )
    positions = jnp.arange(slot_count, dtype=jnp.int32)
    slot_hot = request_list_slot[:, None] == positions[None, :]
    adapter_ids = jnp.sum(jnp.where(slot_hot, row_lists, 0), axis=1)
    gathered = lax.all_gather(hidden, "pool", axis=0, tiled=True)
    owners = group_adapter_lists // holding_count
    places = group_adapter_lists % holding_count
    earlier = positions[None, :] < positions[:, None]
    shared = owners[:, :, None] == owners[:, None, :]
    slot_order = jnp.sum(shared & earlier[None, :, :], axis=2)
    capacity_ids = jnp.arange(CAP, dtype=jnp.int32)
    owned_ids = jnp.arange(holding_count, dtype=jnp.int32)
    wanted = (
        (owners == pool_index)[:, :, None, None]
        & (slot_order[:, :, None, None] == capacity_ids[None, None, :, None])
        & (places[:, :, None, None] == owned_ids[None, None, None, :])
    )
    selection = (
        jnp.sum(wanted, axis=1).astype(jnp.bfloat16).reshape(pool_count * CAP, holding_count)
    )
    outgoing = jnp.dot(
        selection,
        adapter_input_maps.reshape(holding_count, rank_extent * hidden_extent),
        preferred_element_type=jnp.float32,
    ).astype(jnp.bfloat16)
    received = lax.all_to_all(outgoing, "pool", split_axis=0, concat_axis=0, tiled=True)
    own_owners = lax.dynamic_index_in_dim(owners, pool_index, 0, keepdims=False)
    own_order = lax.dynamic_index_in_dim(slot_order, pool_index, 0, keepdims=False)
    entry_of_slot = own_owners * CAP + own_order
    group_slots = lax.dynamic_slice_in_dim(
        request_list_slot, pool_index * group_rows, group_rows, 0
    )
    row_entry = jnp.sum(
        jnp.where(group_slots[:, None] == positions[None, :], entry_of_slot[None, :], 0), axis=1
    )
    entries = pool_count * CAP
    scores = lax.dot_general(
        hidden,
        received.reshape(entries * rank_extent, hidden_extent),
        contract,
        preferred_element_type=jnp.float32,
    )
    partial_value = pick_rank(scores, row_entry, rank_extent)
    summed = lax.psum(partial_value, "tensor")
    lowrank = lax.all_gather(summed.astype(jnp.bfloat16), "pool", axis=0, tiled=True)
    held_rows = adapter_output_maps.shape[0]
    b_matrix = lax.all_to_all(adapter_output_maps, "pool", split_axis=1, concat_axis=0, tiled=True)
    column_ids = jnp.arange(pool_count * held_rows, dtype=jnp.int32)
    global_rows = (
        column_ids // held_rows * tensor_count + tensor_index
    ) * held_rows + column_ids % held_rows
    column_adapter = global_rows // rank_extent
    column_rank = global_rows % rank_extent
    rank_pick = (column_rank[None, :] == jnp.arange(rank_extent, dtype=jnp.int32)[:, None]).astype(
        jnp.bfloat16
    )
    placed = jnp.dot(lowrank, rank_pick, preferred_element_type=jnp.float32).astype(jnp.bfloat16)
    spread = jnp.where(
        adapter_ids[:, None] == column_adapter[None, :], placed, jnp.zeros_like(placed)
    )
    base = jnp.dot(gathered, down_weight, preferred_element_type=jnp.float32)
    mixed = lax.psum_scatter(
        base + jnp.dot(spread, b_matrix, preferred_element_type=jnp.float32),
        "tensor",
        scatter_dimension=0,
        tiled=True,
    )
    return mixed.astype(jnp.bfloat16)


def solution(mesh):
    placed = (
        P(("groups", "pool"), "tensor"),
        P("tensor", "pool"),
        P("pool", None, "tensor"),
        P(("pool", "tensor"), None),
        P("groups"),
        P("groups", None),
    )
    return jax.shard_map(
        per_device,
        mesh=mesh,
        in_specs=placed,
        out_specs=P(("groups", "tensor"), "pool"),
        check_vma=False,
    )
```

profile of v0, /device:TPU:0, one launch (start us, length us, event | category | flops | bytes accessed | tf_op | source)
XLA Modules:
  0.0 439.9 jit_solution(15171201968316244429)
XLA Ops:
  6.5 6.4 %copy.9 = bf16[256,8192]{0,1:T(8,128)(2,1)} copy(bf16[256,8192]{1,0:T(8,128)(2,1)} %param.9) | data formatting | bytes 8388608 | tf_op args[3]
  12.9 4.9 %all-to-all-start.1 = ((bf16[256,4,2048]{0,2,1:T(8,128)(2,1)}), bf16[256,4,2048]{0,2,1:T(8,128)(2,1)}, u32[]{:S(2)}, u32[]{:S(2)}) async-start(bf16[256,4,2048]{0,2,1:T(8,128)(2,1)} %bitcast.22), calls=%async_computation.1 | async-start | bytes 8388608 | tf_op jit(solution)/shard_map/all_to_all | solution.py:90
  17.8 0.0 copy-done.1
  17.9 0.2 convert_reduce_fusion.1
  18.1 0.1 iota_compare_fusion.5
  18.2 0.1 convert_reduce_fusion
  18.3 16.8 %copy.11 = bf16[2,8,64,7168]{3,1,2,0:T(8,128)(2,1)} copy(bf16[2,8,64,7168]{3,2,1,0:T(8,128)(2,1)} %bitcast.23) | data formatting | bytes 29360128
  35.1 14.3 %convolution_convert_fusion = bf16[16,458752]{1,0:T(8,128)(2,1)} fusion(bf16[16,16]{1,0:T(8,128)(2,1)S(1)} %bitcast.25, bf16[16,458752]{1,0:T(8,128)(2,1)} %bitcast.21), kind=kOutput, calls=%fused_computation | convolution fusion | flops 242221056 | bytes 29360640 | tf_op jit(solution)/shard_map/dot_general | solution.py:64
  49.4 17.4 %all_to_all.20 = bf16[4,4,458752]{2,1,0:T(4,128)(2,1)} reshape(bf16[16,458752]{1,0:T(8,128)(2,1)} %convolution_convert_fusion) | data formatting | bytes 29360128 | tf_op jit(solution)/shard_map/all_to_all | solution.py:69
  66.8 0.0 copy-start.2
  66.8 0.0 all-to-all-done.1
  66.8 6.8 %all-to-all-start = ((bf16[4,4,458752]{2,1,0:T(4,128)(2,1)}), bf16[4,4,458752]{2,1,0:T(4,128)(2,1)}, u32[]{:S(2)}, u32[]{:S(2)}) async-start(bf16[4,4,458752]{2,1,0:T(4,128)(2,1)} %all_to_all.20), calls=%async_computation | async-start | bytes 29360128 | tf_op jit(solution)/shard_map/all_to_all | solution.py:69
  73.6 0.0 all-gather.2.cloned.1.call-start
  73.6 0.7 all-gather.2.cloned.1.call-update
  74.3 0.2 reduce-scatter.2.cloned.1.call-start
  74.5 0.0 copy-done.2
  74.5 0.1 dynamic_slice.10
  74.7 0.1 select_reduce_fusion.2
  74.8 0.1 select_reduce_fusion
  74.9 6.3 %copy.10 = bf16[4,256,2048]{2,1,0:T(8,128)(2,1)} copy(bf16[4,256,2048]{1,2,0:T(8,128)(2,1)} %bitcast.4) | data formatting | bytes 8388608 | tf_op jit(solution)/shard_map/all_to_all | solution.py:90
  81.2 192.9 %all-to-all-done = bf16[4,4,458752]{2,1,0:T(4,128)(2,1)} async-done(((bf16[4,4,458752]{2,1,0:T(4,128)(2,1)}), bf16[4,4,458752]{2,1,0:T(4,128)(2,1)}, u32[]{:S(2)}, u32[]{:S(2)}) %all-to-all-start) | async-done | bytes 14680096 | tf_op jit(solution)/shard_map/all_to_all | solution.py:69
  274.0 17.5 %reshape.168 = bf16[1024,7168]{1,0:T(8,128)(2,1)} reshape(bf16[4,4,458752]{2,1,0:T(4,128)(2,1)} %all-to-all-done) | data formatting | bytes 29360128 | tf_op jit(solution)/shard_map/reshape | solution.py:82
  291.5 0.0 copy-done
  291.5 7.2 %fusion.1 = f32[128,1024]{0,1:T(8,128)S(1)} fusion(bf16[1024,7168]{1,0:T(8,128)(2,1)} %reshape.168, bf16[128,7168]{1,0:T(8,128)(2,1)S(1)} %copy-done, s32[128]{0:T(128)S(1)} %select_reduce_fusion.2, s32[1024]{0:T(1024)S(1)} %add_select_fusion.2), kind=kOutput, calls=%fused_computation.6 | convolution fusion | flops 1879310336 | bytes 17043968 | tf_op jit(solution)/shard_map/dot_general | solution.py:80
  298.8 0.7 fusion.5
  299.6 20.2 %psum.7 = bf16[128,64]{0,1:T(8,128)(2,1)S(1)} all-reduce(f32[128,64]{0,1:T(8,128)S(1)} %fusion.5), channel_id=1, replica_groups=mesh['groups'=2,'pool'=4,'tensor'=4] {'tensor'}, use_global_device_ids=true, to_apply=%region_5.6 | all-reduce | flops 8192 | bytes 49152 | tf_op jit(solution)/shard_map/psum | solution.py:87
  319.7 5.5 %all_gather.7 = bf16[512,64]{0,1:T(8,128)(2,1)S(1)} all-gather(bf16[128,64]{0,1:T(8,128)(2,1)S(1)} %psum.7), channel_id=1, replica_groups=mesh['groups'=2,'pool'=4,'tensor'=4] {'pool'}, dimensions={0}, use_global_device_ids=true | all-gather | bytes 81920 | tf_op jit(solution)/shard_map/all_gather | solution.py:88
  325.2 6.8 %fusion = f32[512,2048]{1,0:T(8,128)} fusion(bf16[1024,2048]{1,0:T(8,128)(2,1)} %bitcast.24, bf16[512,64]{0,1:T(8,128)(2,1)S(1)} %all_gather.7, s32[1024]{0:T(1024)S(1)} %get-tuple-element.8, s32[512]{0:T(512)S(1)} %select_reduce_fusion.1, s32[1024]{0:T(1024)S(1)} %get-tuple-element.7), kind=kOutput, calls=%fused_computation.4 | convolution fusion | flops 2216230912 | bytes 8464384 | tf_op jit(solution)/shard_map/dot_general | solution.py:106
  332.0 24.7 %convolution_add_fusion = f32[512,2048]{1,0:T(8,128)} fusion(f32[512,2048]{1,0:T(8,128)} %fusion, bf16[512,7168]{1,0:T(8,128)(2,1)} %all-gather.2.cloned.1.call-done, bf16[7168,2048]{1,0:T(8,128)(2,1)} %param.7), kind=kOutput, calls=%fused_computation.1 | convolution fusion | flops 15033434112 | bytes 45088768 | tf_op jit(solution)/shard_map/dot_general | solution.py:104
  356.7 0.0 reduce-scatter.2.cloned.1.call-update
  356.7 74.3 %reduce-scatter.2.cloned.1.call-done = f32[128,2048]{1,0:T(8,128)} async-done(((f32[512,2048]{1,0:T(8,128)}), f32[128,2048]{1,0:T(8,128)}) %reduce-scatter.2.cloned.1.call-update) | async-done | bytes 1048592 | tf_op jit(solution)/shard_map/reduce_scatter | solution.py:105
  431.0 2.1 convert_element_type.40
  (15 shorter events, 0.1 us)
Async XLA Ops:
  6.5 11.3 %copy-start.1 = (s32[4,16]{1,0:T(4,128)S(1)}, s32[4,16]{1,0:T(4,128)}, u32[]{:S(2)}) copy-start(s32[4,16]{1,0:T(4,128)} %param.11) | copy-start | bytes 772
  12.9 53.9 %all-to-all-start.1 = ((bf16[256,4,2048]{0,2,1:T(8,128)(2,1)}), bf16[256,4,2048]{0,2,1:T(8,128)(2,1)}, u32[]{:S(2)}, u32[]{:S(2)}) async-start(bf16[256,4,2048]{0,2,1:T(8,128)(2,1)} %bitcast.22), calls=%async_computation.1 | async-start | bytes 8388608 | tf_op jit(solution)/shard_map/all_to_all | solution.py:90
  66.8 7.8 %copy-start.2 = (s32[512]{0:T(512)S(1)}, s32[512]{0:T(512)}, u32[]{:S(2)}) copy-start(s32[512]{0:T(512)} %param.10) | copy-start | bytes 6148
  66.8 207.3 %all-to-all-start = ((bf16[4,4,458752]{2,1,0:T(4,128)(2,1)}), bf16[4,4,458752]{2,1,0:T(4,128)(2,1)}, u32[]{:S(2)}, u32[]{:S(2)}) async-start(bf16[4,4,458752]{2,1,0:T(4,128)(2,1)} %all_to_all.20), calls=%async_computation | async-start | bytes 29360128 | tf_op jit(solution)/shard_map/all_to_all | solution.py:69
  73.6 258.5 %all-gather.2.cloned.1.call-start = ((), (), s32[]{:S(2)}) async-start(), calls=%async_computation.3 | async-start | bytes 9175040 | tf_op jit(solution)/shard_map/all_gather | solution.py:48
  74.3 356.7 %reduce-scatter.2.cloned.1.call-start = ((), (), s32[]{:S(2)}) async-start(), calls=%async_computation.4 | async-start | bytes 5242880 | tf_op jit(solution)/shard_map/reduce_scatter | solution.py:105
  81.2 210.4 %copy-start = (bf16[128,7168]{1,0:T(8,128)(2,1)S(1)}, bf16[128,7168]{1,0:T(8,128)(2,1)}, u32[]{:S(2)}) copy-start(bf16[128,7168]{1,0:T(8,128)(2,1)} %param.6) | copy-start | bytes 5505028
Sparse Core Ops, SparseCore 0:
  76.0 94.9 all-gather.1
  356.8 74.0 reduce-scatter.1
where the time goes:
time: 441 us; the launch traced here: 440 us
  waiting for transfers between devices  268 us (61%)
  local copies, waits for them, and re-layouts  64.4 us (15%)
  matrix products  53.8 us (12%)
  blocking collectives  25.6 us (6%)
  between operations  13.5 us (3%)
  starting transfers between devices  11.9 us (3%)
    all_to_all x1, waiting for transfers between devices, per_device(): lax.all_to_all(outgoing, 'pool', split_axis=0, concat_axis=0, tiled=True)  193 us
    reduce_scatter x1, waiting for transfers between devices, per_device(): lax.psum_scatter(base + jnp.dot(spread, b_matrix, preferred_element_type=...  74.3 us
    dot_general x1, matrix products, per_device(): base = jnp.dot(gathered, down_weight, preferred_element_type=jnp.float32)  24.7 us
    unnamed x8, local copies, waits for them, and re-layouts  23.2 us
    psum x1, blocking collectives, per_device(): summed = lax.psum(partial_value, 'tensor')  20.2 us
    reshape x1, local copies, waits for them, and re-layouts, per_device(): received.reshape(entries * rank_extent, hidden_extent)  17.5 us
    all_to_all x1, local copies, waits for them, and re-layouts, per_device(): lax.all_to_all(outgoing, 'pool', split_axis=0, concat_axis=0, tiled=True)  17.4 us
    dot_general x1, matrix products, per_device(): jnp.dot(selection, adapter_input_maps.reshape(holding_count, rank_extent...  14.3 us
  transfers between devices with their start and end apart: 4, of which 2 were waited for; matrix products, arithmetic and copies ran while one was open for 16% of the time, Pallas kernels for 0%

commit v1 on v0

v1 whole, which is shorter than its diff:
```python
import jax
import jax.numpy as jnp
from jax import lax
from jax.experimental import pallas as pl
from jax.experimental.pallas import tpu as pltpu
from jax.sharding import PartitionSpec as P

F32 = jnp.float32
BF16 = jnp.bfloat16
VMEM_LIMIT = 56 * 1024 * 1024
CHUNKS = 2


def partners(count, step):
    return [(i, i ^ step) for i in range(count)]


def swap(values, axis, step):
    return lax.ppermute(values, axis, partners(lax.axis_size(axis), step))


def base_kernel(a_ref, b_ref, w_ref, out_ref):
    step = pl.program_id(0)
    rows = jnp.concatenate([a_ref[...], b_ref[...]], axis=0)
    width = out_ref.shape[1]
    tile = 512
    for start in range(0, width, tile):
        term = jnp.dot(rows, w_ref[:, start : start + tile], preferred_element_type=F32)

        @pl.when(step == 0)
        def _():
            out_ref[:, start : start + tile] = term

        @pl.when(step > 0)
        def _():
            out_ref[:, start : start + tile] += term


def base_product(a, b, weight):
    rows, depth = a.shape
    width = weight.shape[1]
    block = 1024
    return pl.pallas_call(
        base_kernel,
        grid=(depth // block,),
        in_specs=[
            pl.BlockSpec((rows, block), lambda k: (0, k)),
            pl.BlockSpec((rows, block), lambda k: (0, k)),
            pl.BlockSpec((block, width), lambda k: (k, 0)),
        ],
        out_specs=pl.BlockSpec((2 * rows, width), lambda k: (0, 0)),
        out_shape=jax.ShapeDtypeStruct((2 * rows, width), F32),
        compiler_params=pltpu.CompilerParams(vmem_limit_bytes=VMEM_LIMIT),
        cost_estimate=pl.CostEstimate(
            flops=4 * rows * depth * width,
            bytes_accessed=2 * depth * (width + 2 * rows) + 8 * rows * width,
            transcendentals=0,
        ),
        name="base",
    )(a, b, weight)


def add_scores(a_ref, b_ref, maps_ref, total):
    step = pl.program_id(0)
    rows = jnp.concatenate([a_ref[...], b_ref[...]], axis=0)
    columns = maps_ref.shape[0]
    tile = 256
    for start in range(0, columns, tile):
        term = lax.dot_general(
            rows,
            maps_ref[start : start + tile, :],
            (((1,), (1,)), ((), ())),
            preferred_element_type=F32,
        )

        @pl.when(step == 0)
        def _():
            total[:, start : start + tile] = term

        @pl.when(step > 0)
        def _():
            total[:, start : start + tile] += term


def picked(place_ref, ids_ref, total):
    pair, rows, lanes = ids_ref.shape
    ids = ids_ref[...].reshape(pair * rows, lanes)
    upper = (lax.broadcasted_iota(jnp.int32, ids.shape, 1) >= lanes // 2).astype(jnp.int32)
    wanted = ids - upper - 16 * place_ref[0]
    found = jnp.zeros(ids.shape, F32)
    for start in range(0, total.shape[1], lanes):
        found += jnp.where(wanted == 2 * (start // lanes), total[:, start : start + lanes], 0.0)
    return found + pltpu.roll(found, lanes // 2, 1)


def near_scores_kernel(place_ref, a_ref, b_ref, maps_ref, ids_ref, out_ref, total):
    add_scores(a_ref, b_ref, maps_ref, total)

    @pl.when(pl.program_id(0) == pl.num_programs(0) - 1)
    def _():
        out_ref[...] = picked(place_ref, ids_ref, total)


def far_scores_kernel(place_ref, a_ref, b_ref, maps_ref, ids_ref, near_ref, out_ref, total):
    add_scores(a_ref, b_ref, maps_ref, total)

    @pl.when(pl.program_id(0) == pl.num_programs(0) - 1)
    def _():
        total[:, : out_ref.shape[1]] = picked(place_ref, ids_ref, total)
        place = place_ref[0]
        chip, core = place // 2, place % 2
        rows, lanes = out_ref.shape[0] // 2, out_ref.shape[1]
        half = (lax.broadcasted_iota(jnp.int32, (rows, lanes), 1) >= lanes // 2).astype(jnp.int32)
        for group in range(2):
            source = pl.ds(pl.multiple_of((group ^ core) * rows, rows), rows)
            out_ref[group * rows : (group + 1) * rows, :] = jnp.where(
                half == chip, near_ref[source, :], total[source, :lanes]
            )


def scores(place, a, b, maps, ids, near=None):
    rows, depth = a.shape
    columns = maps.shape[0]
    block = 1024
    lanes = 128
    in_specs = [
        pl.BlockSpec((rows, block), lambda k, s: (0, k)),
        pl.BlockSpec((rows, block), lambda k, s: (0, k)),
        pl.BlockSpec((columns, block), lambda k, s: (0, k)),
        pl.BlockSpec((2, rows, lanes), lambda k, s: (0, 0, 0)),
    ]
    args = [place, a, b, maps, ids]
    if near is not None:
        in_specs.append(pl.BlockSpec((2 * rows, lanes), lambda k, s: (0, 0)))
        args.append(near)
    return pl.pallas_call(
        near_scores_kernel if near is None else far_scores_kernel,
        grid_spec=pltpu.PrefetchScalarGridSpec(
            num_scalar_prefetch=1,
            grid=(depth // block,),
            in_specs=in_specs,
            out_specs=pl.BlockSpec((2 * rows, lanes), lambda k, s: (0, 0)),
            scratch_shapes=[pltpu.VMEM((2 * rows, columns), F32)],
        ),
        out_shape=jax.ShapeDtypeStruct((2 * rows, lanes), F32),
        compiler_params=pltpu.CompilerParams(vmem_limit_bytes=VMEM_LIMIT),
        cost_estimate=pl.CostEstimate(
            flops=4 * rows * depth * columns,
            bytes_accessed=2 * depth * (columns + 2 * rows),
            transcendentals=0,
        ),
        name="near_scores" if near is None else "far_scores",
    )(*args)


def combine_kernel(
    info_ref,
    near_ref,
    far_ref,
    lowrank_ref,
    ids_ref,
    own_ref,
    core_ref,
    mine_ref,
    other_ref,
    keep_ref,
    send_ref,
    spread,
    maps,
):
    rows, lanes = ids_ref.shape[1], ids_ref.shape[2]
    parity, place = info_ref[0], info_ref[1]
    half = rows

    @pl.when(pl.program_id(0) == 0)
    def _():
        upper = (lax.broadcasted_iota(jnp.int32, (rows, lanes), 1) >= lanes // 2).astype(jnp.int32)
        for slot in range(4):
            local = ((slot // 2) ^ parity) + 2 * (slot % 2)
            group = place ^ local
            packed = lowrank_ref[group % 2]
            values = jnp.where(
                upper == group // 2, packed, pltpu.roll(packed, lanes // 2, 1)
            )
            wanted = ids_ref[local] - upper
            for piece in range(8):
                spread[slot * rows : (slot + 1) * rows, piece * lanes : (piece + 1) * lanes] = (
                    jnp.where(wanted == info_ref[2 + piece], values, 0.0).astype(BF16)
                )

    maps[0:256, :] = own_ref[...]
    maps[256:512, :] = core_ref[...]
    maps[512:640, :] = mine_ref[0]
    maps[640:768, :] = mine_ref[1]
    maps[768:896, :] = other_ref[0]
    maps[896:1024, :] = other_ref[1]
    for slot in range(4):
        delta = jnp.dot(
            spread[slot * rows : (slot + 1) * rows, :], maps[...], preferred_element_type=F32
        )
        source = near_ref if slot % 2 == 0 else far_ref
        value = source[(slot // 2) ^ parity] + delta
        start = (slot % 2) * half
        if slot < 2:
            keep_ref[start : start + half, :] = value
        else:
            send_ref[start : start + half, :] = value.astype(BF16)


def combine(info, near, far, lowrank, ids, own_maps, core_maps, mine, other, chunk):
    rows, lanes = ids.shape[1], ids.shape[2]
    width = mine.shape[2]
    tile = 512
    steps = width // tile
    first = chunk * steps
    per_place = core_maps.shape[1] // tile
    held = own_maps.shape[0]
    return pl.pallas_call(
        combine_kernel,
        grid_spec=pltpu.PrefetchScalarGridSpec(
            num_scalar_prefetch=1,
            grid=(steps,),
            in_specs=[
                pl.BlockSpec((2, rows, tile), lambda n, s: (0, 0, first + n)),
                pl.BlockSpec((2, rows, tile), lambda n, s: (0, 0, first + n)),
                pl.BlockSpec((2, rows, lanes), lambda n, s: (0, 0, 0)),
                pl.BlockSpec((4, rows, lanes), lambda n, s: (0, 0, 0)),
                pl.BlockSpec((held, tile), lambda n, s: (0, s[1] * per_place + first + n)),
                pl.BlockSpec((held, tile), lambda n, s: (0, first + n)),
                pl.BlockSpec((2, held // 2, tile), lambda n, s: (0, 0, n)),
                pl.BlockSpec((2, held // 2, tile), lambda n, s: (0, 0, n)),
            ],
            out_specs=[
                pl.BlockSpec((2 * rows, tile), lambda n, s: (0, n)),
                pl.BlockSpec((2 * rows, tile), lambda n, s: (0, n)),
            ],
            scratch_shapes=[
                pltpu.VMEM((4 * rows, 4 * held), BF16),
                pltpu.VMEM((4 * held, tile), BF16),
            ],
        ),
        out_shape=[
            jax.ShapeDtypeStruct((2 * rows, width), F32),
            jax.ShapeDtypeStruct((2 * rows, width), BF16),
        ],
        compiler_params=pltpu.CompilerParams(vmem_limit_bytes=VMEM_LIMIT),
        cost_estimate=pl.CostEstimate(
            flops=32 * rows * held * width,
            bytes_accessed=26 * rows * width + 8 * held * width,
            transcendentals=0,
        ),
        name="combine",
    )(info, near, far, lowrank, ids, own_maps, core_maps, mine, other)


def per_device_fast(hidden, weight, input_maps, output_maps, slots, lists):
    rows, depth = hidden.shape
    x_core = lax.axis_index("pool")
    t = lax.axis_index("tensor")
    y = lax.axis_index("groups")
    holding, rank = input_maps.shape[:2]
    held, features = output_maps.shape
    width = features // 4
    chip, core = x_core // 2, x_core % 2

    far_a = swap(hidden, "pool", 2)
    near_b = swap(hidden, "pool", 1)

    core_maps = swap(
        lax.dynamic_slice(output_maps, (0, (x_core ^ 1) * width), (held, width)), "pool", 1
    )
    chunk_width = width // CHUNKS
    crossing = []
    for chunk in range(CHUNKS):
        start = (1 - chip) * 2 * width + chunk * chunk_width
        block = jnp.stack(
            [
                lax.dynamic_slice(
                    output_maps, (y * (held // 2), start + c * width), (held // 2, chunk_width)
                )
                for c in range(2)
            ]
        )
        block, _ = lax.optimization_barrier((block, near_b))
        crossing.append(swap(block, "pool", 2))

    order = x_core ^ jnp.arange(4, dtype=jnp.int32)
    hot = order[:, None] == jnp.arange(4, dtype=jnp.int32)[None, :]
    slots_local = jnp.sum(jnp.where(hot[:, :, None], slots.reshape(1, 4, rows), 0), axis=1)
    lists_local = jnp.sum(jnp.where(hot[:, :, None], lists[None, :, :], 0), axis=1)
    slot_ids = jnp.arange(lists.shape[1], dtype=jnp.int32)
    ids = jnp.sum(
        jnp.where(slots_local[:, :, None] == slot_ids, lists_local[:, None, :], 0), axis=2
    )
    ids = jnp.broadcast_to(ids[:, :, None], (4, rows, 128))
    place = x_core.reshape(1).astype(jnp.int32)

    flat_maps = input_maps.reshape(holding * rank, depth)
    near_lowrank = scores(place, hidden, near_b, flat_maps, ids[:2])
    near_base = base_product(hidden, near_b, weight)

    far_b = swap(far_a, "pool", 1)
    total = scores(place, far_a, far_b, flat_maps, ids[2:], near_lowrank)
    for axis, step in (("tensor", 1), ("tensor", 2), ("pool", 1), ("pool", 2)):
        total = total + swap(total.astype(BF16), axis, step).astype(F32)
    far_base = base_product(far_a, far_b, weight)
    lowrank = total.astype(BF16).astype(F32).reshape(2, rows, 128)

    mine, other = [], []
    for block in crossing:
        kept = lax.dynamic_index_in_dim(block, core, 0, keepdims=False)
        passed = lax.dynamic_index_in_dim(block, 1 - core, 0, keepdims=False)
        mine.append(jnp.stack([kept, swap(passed, "pool", 1)]))
        other.append(swap(mine[-1], "groups", 1))

    parity = (x_core ^ t) % 2
    per_owner = held // rank
    first = holding * order + per_owner * t
    half_step = per_owner // 2
    info = jnp.stack(
        [
            parity,
            x_core,
            first[0],
            first[0] + half_step,
            first[1],
            first[1] + half_step,
            first[2] + half_step * y,
            first[3] + half_step * y,
            first[2] + half_step * (1 - y),
            first[3] + half_step * (1 - y),
        ]
    ).astype(jnp.int32)

    near_base = near_base.reshape(2, rows, width)
    far_base = far_base.reshape(2, rows, width)
    side = ((x_core ^ t) // 2) % 2
    parts = []
    for chunk in range(CHUNKS):
        keep, send = combine(
            info, near_base, far_base, lowrank, ids, output_maps, core_maps,
            mine[chunk], other[chunk], chunk,
        )
        pair = keep + swap(send, "tensor", 1).astype(F32)
        pair = pair.reshape(2, rows, chunk_width)
        sent = jnp.where(side == 0, pair[1], pair[0]).astype(BF16)
        kept = jnp.where(side == 0, pair[0], pair[1])
        parts.append(kept + swap(sent, "tensor", 2).astype(F32))
    return jnp.concatenate(parts, axis=1).astype(BF16)


def per_device_general(hidden, weight, input_maps, output_maps, slots, lists):
    rows, depth = hidden.shape
    pool_count = lax.axis_size("pool")
    tensor_count = lax.axis_size("tensor")
    place = lax.axis_index("pool")
    t = lax.axis_index("tensor")
    holding, rank = input_maps.shape[:2]
    held = output_maps.shape[0]
    total_rows = rows * pool_count
    slot_ids = jnp.arange(lists.shape[1], dtype=jnp.int32)
    slot_hot = slots.reshape(pool_count, rows)[:, :, None] == slot_ids
    ids = jnp.sum(jnp.where(slot_hot, lists[:, None, :], 0), axis=2).reshape(total_rows)
    gathered = lax.all_gather(hidden, "pool", axis=0, tiled=True)
    scored = lax.dot_general(
        gathered,
        input_maps.reshape(holding * rank, depth),
        (((1,), (1,)), ((), ())),
        preferred_element_type=F32,
    ).reshape(total_rows, holding, rank)
    owned = place * holding + jnp.arange(holding, dtype=jnp.int32)
    partial = jnp.sum(
        jnp.where((ids[:, None] == owned[None, :])[:, :, None], scored, 0.0), axis=1
    )
    lowrank = lax.psum(partial, ("tensor", "pool")).astype(BF16)
    maps = lax.all_to_all(output_maps, "pool", split_axis=1, concat_axis=0, tiled=True)
    columns = jnp.arange(pool_count * held, dtype=jnp.int32)
    source = (columns // held * tensor_count + t) * held + columns % held
    pick = (source[None, :] % rank == jnp.arange(rank, dtype=jnp.int32)[:, None]).astype(BF16)
    placed = jnp.dot(lowrank, pick, preferred_element_type=F32).astype(BF16)
    spread = jnp.where(ids[:, None] == source[None, :] // rank, placed, jnp.zeros_like(placed))
    value = jnp.dot(gathered, weight, preferred_element_type=F32)
    value = value + jnp.dot(spread, maps, preferred_element_type=F32)
    mixed = lax.psum_scatter(value, "tensor", scatter_dimension=0, tiled=True)
    return mixed.astype(BF16)


def solution(mesh):
    shape = dict(mesh.shape)
    fast = shape["groups"] == 2 and shape["pool"] == 4 and shape["tensor"] == 4
    placed = (
        P(("groups", "pool"), "tensor"),
        P("tensor", "pool"),
        P("pool", None, "tensor"),
        P(("pool", "tensor"), None),
        P("groups"),
        P("groups", None),
    )
    return jax.shard_map(
        per_device_fast if fast else per_device_general,
        mesh=mesh,
        in_specs=placed,
        out_specs=P(("groups", "tensor"), "pool"),
        check_vma=False,
    )
```

time: 441 us -> 194 us (0.44)
  waiting for transfers between devices: 268 us -> 75 us
  Pallas kernels: 0 us -> 79.8 us
  local copies, waits for them, and re-layouts: 64.4 us -> 9.78 us
  matrix products: 53.8 us -> 0 us
  blocking collectives: 25.6 us -> 0 us
  between operations: 13.5 us -> 3.93 us
  starting transfers between devices: 11.9 us -> 20.6 us
    all_to_all x2 -> x0, waiting for transfers between devices: 193 us -> none  [the longest x1 193 us: per_device(): lax.all_to_all(outgoing, 'pool', split_axis=0, concat_axis=0, tiled=True)]
    pallas_call x0 -> x6, Pallas kernels: none -> 79.8 us  [the longest x2 37.1 us: base_product(): pl.pallas_call(base_kernel, grid=(depth // block,), in_specs=[pl.BlockSpe...]
    ppermute x0 -> x18, waiting for transfers between devices: none -> 75 us  [swap(): return lax.ppermute(values, axis, partners(lax.axis_size(axis), step))]
    reduce_scatter x1 -> x0, waiting for transfers between devices: 74.3 us -> none  [per_device(): lax.psum_scatter(base + jnp.dot(spread, b_matrix, preferred_element_type=...]
    dot_general x5 -> x0, matrix products: 53.8 us -> none  [the longest x1 24.7 us: per_device(): base = jnp.dot(gathered, down_weight, preferred_element_type=jnp.float32)]
    all_to_all x2 -> x0, local copies, waits for them, and re-layouts: 23.7 us -> none  [the longest x1 17.4 us: per_device(): lax.all_to_all(outgoing, 'pool', split_axis=0, concat_axis=0, tiled=True)]
    unnamed x8 -> x22, local copies, waits for them, and re-layouts: 23.2 us -> 1.05 us
    ppermute x0 -> x18, starting transfers between devices: none -> 20.6 us  [swap(): return lax.ppermute(values, axis, partners(lax.axis_size(axis), step))]
  transfers between devices with their start and end apart: 4 -> 18, of which waited for: 2 -> 6; matrix products, arithmetic and copies ran while one was open for 16% -> 6% of each run, Pallas kernels for 0% -> 41%
where the time goes in v1:
time: 194 us
  Pallas kernels  79.8 us (41%)
  waiting for transfers between devices  75 us (39%)
  starting transfers between devices  20.6 us (11%)
  local copies, waits for them, and re-layouts  9.78 us (5%)
  other arithmetic  4.69 us (2%)
  between operations  3.93 us (2%)
    ppermute x18, waiting for transfers between devices, swap(): return lax.ppermute(values, axis, partners(lax.axis_size(axis), step))  75 us
    pallas_call x2, Pallas kernels, base_product(): pl.pallas_call(base_kernel, grid=(depth // block,), in_specs=[pl.BlockSpe...  37.1 us
    pallas_call x2, Pallas kernels, scores(): pl.pallas_call(near_scores_kernel if near is None else far_scores_kernel,...  32.5 us
    ppermute x18, starting transfers between devices, swap(): return lax.ppermute(values, axis, partners(lax.axis_size(axis), step))  20.6 us
    pallas_call x2, Pallas kernels, combine(): pl.pallas_call(combine_kernel, grid_spec=pltpu.PrefetchScalarGridSpec(num...  10.3 us
  transfers between devices with their start and end apart: 18, of which 6 were waited for; matrix products, arithmetic and copies ran while one was open for 6% of the time, Pallas kernels for 41%

profile of v1, /device:TPU:0, one launch (start us, length us, event | category | flops | bytes accessed | tf_op | source)
XLA Modules:
  0.0 193.9 jit_solution(9625769511572002782)
XLA Ops:
  0.0 2.9 %collective-permute-start.1 = (bf16[128,7168]{1,0:T(8,128)(2,1)}, bf16[128,7168]{1,0:T(8,128)(2,1)S(1)}, u32[]{:S(2)}, u32[]{:S(2)}) collective-permute-start(bf16[128,7168]{1,0:T(8,128)(2,1)} %a_ref.3), channel_id=1, source_target_pairs={{0,8},{4,12},{8,0},{12,4},{1,9},{5,13},{9,1},{13,5},{2,10},{6,14},... | collective-permute-start | bytes 5505032 | tf_op jit(solution)/shard_map/ppermute | solution.py:19
  2.9 2.3 %constant_dynamic-slice_fusion.1 = bf16[256,2048]{1,0:T(8,128)(2,1)} fusion(bf16[256,8192]{1,0:T(8,128)(2,1)} %own_ref.3, s32[]{:T(128)S(6)} %select_n.91), kind=kLoop, calls=%fused_computation.29 | loop fusion | bytes 2097156 | tf_op jit(solution)/shard_map/dynamic_slice | solution.py:270
  6.0 37.1 %collective-permute-done.1.a_ref = bf16[128,7168]{1,0:T(8,128)(2,1)S(1)} collective-permute-done((bf16[128,7168]{1,0:T(8,128)(2,1)}, bf16[128,7168]{1,0:T(8,128)(2,1)S(1)}, u32[]{:S(2)}, u32[]{:S(2)}) %collective-permute-start.1) | collective-permute-done | bytes 1835040 | tf_op jit(solution)/shard_map/ppermute | solution.py:19
  47.6 1.9 stack.61.info_ref
  49.5 1.3 dynamic-slice_bitcast_fusion.5
  50.9 1.8 collective-permute-start.8
  53.0 18.6 %base.2 = f32[256,2048]{1,0:T(8,128)} custom-call(bf16[128,7168]{1,0:T(8,128)(2,1)} %a_ref.3, bf16[128,7168]{1,0:T(8,128)(2,1)} %collective-permute-done.b_ref, bf16[7168,2048]{1,0:T(8,128)(2,1)} %w_ref.3), custom_call_target="tpu_custom_call" | custom-call | flops 7516192768 | bytes 35127296 | tf_op jit(solution)/shard_map/base/pallas_call | solution.py:43
  71.6 0.8 broadcast_in_dim.82.ids_ref
  72.3 16.2 %near_scores.1.near_ref = f32[256,128]{1,0:T(8,128)} custom-call(s32[1]{0:T(128)} %bitcast.1.place_ref, bf16[128,7168]{1,0:T(8,128)(2,1)} %a_ref.3, bf16[128,7168]{1,0:T(8,128)(2,1)} %collective-permute-done.b_ref, bf16[1024,7168]{1,0:T(8,128)(2,1)} %bitcast.28, s32[2,128,128]{2,1,0:T(8,128)} %broadcast_in_dim.82.ids_ref), custom_call_target="tpu_custom_call" | custom-call | flops 3758096384 | bytes 18350080 | tf_op jit(solution)/shard_map/near_scores/pallas_call | solution.py:136
  88.7 0.8 broadcast_in_dim.81.ids_ref
  89.4 16.3 %far_scores.1 = f32[256,128]{1,0:T(8,128)} custom-call(s32[1]{0:T(128)} %bitcast.1.place_ref, bf16[128,7168]{1,0:T(8,128)(2,1)} %copy-done, bf16[128,7168]{1,0:T(8,128)(2,1)} %collective-permute-done.2.b_ref, bf16[1024,7168]{1,0:T(8,128)(2,1)} %bitcast.29, s32[2,128,128]{2,1,0:T(8,128)} %broadcast_in_dim.81.ids_ref, f32[256,128]{1,0:T(8,128)} %near_scores.1.near_ref), custom_call_target="tpu_custom_call" | custom-call | flops 3758096384 | bytes 18350080 | tf_op jit(solution)/shard_map/far_scores/pallas_call | solution.py:136
  105.7 1.0 convert_element_type.47
  106.7 1.8 collective-permute-start.3
  108.8 2.4 %collective-permute-done.3 = bf16[256,128]{1,0:T(8,128)(2,1)S(1)} collective-permute-done((bf16[256,128]{1,0:T(8,128)(2,1)S(1)}, bf16[256,128]{1,0:T(8,128)(2,1)S(1)}, u32[]{:S(2)}, u32[]{:S(2)}) %collective-permute-start.3) | collective-permute-done | bytes 65568 | tf_op jit(solution)/shard_map/ppermute | solution.py:19
  111.3 0.9 fusion
  112.2 2.8 %collective-permute-start.4 = (bf16[256,128]{1,0:T(8,128)(2,1)S(1)}, bf16[256,128]{1,0:T(8,128)(2,1)S(1)}, u32[]{:S(2)}, u32[]{:S(2)}) collective-permute-start(bf16[256,128]{1,0:T(8,128)(2,1)S(1)} %fusion), channel_id=1, source_target_pairs={{0,2},{1,3},{2,0},{3,1},{4,6},{5,7},{6,4},{7,5},{8,10},{9,11},{10,... | collective-permute-start | bytes 196616 | tf_op jit(solution)/shard_map/ppermute | solution.py:19
  115.1 1.6 collective-permute-start.10
  116.7 2.1 %collective-permute-done.4 = bf16[256,128]{1,0:T(8,128)(2,1)S(1)} collective-permute-done((bf16[256,128]{1,0:T(8,128)(2,1)S(1)}, bf16[256,128]{1,0:T(8,128)(2,1)S(1)}, u32[]{:S(2)}, u32[]{:S(2)}) %collective-permute-start.4) | collective-permute-done | bytes 65568 | tf_op jit(solution)/shard_map/ppermute | solution.py:19
  118.9 1.6 collective-permute-start.15
  120.6 1.6 collective-permute-start.6
  122.1 18.6 %base.3 = f32[256,2048]{1,0:T(8,128)} custom-call(bf16[128,7168]{1,0:T(8,128)(2,1)} %copy-done, bf16[128,7168]{1,0:T(8,128)(2,1)} %collective-permute-done.2.b_ref, bf16[7168,2048]{1,0:T(8,128)(2,1)} %w_ref.3), custom_call_target="tpu_custom_call" | custom-call | flops 7516192768 | bytes 35127296 | tf_op jit(solution)/shard_map/base/pallas_call | solution.py:43
  141.5 1.0 broadcast_in_dim.83.ids_ref
  142.7 5.1 %combine.2 = (f32[256,1024]{1,0:T(8,128)}, bf16[256,1024]{1,0:T(8,128)(2,1)}) custom-call(s32[10]{0:T(128)} %stack.61.info_ref, f32[2,128,2048]{2,1,0:T(8,128)} %bitcast.30, f32[2,128,2048]{2,1,0:T(8,128)} %bitcast.32, f32[2,128,128]{2,1,0:T(8,128)} %convert.9.lowrank_ref, s32[4,128,128]{2,1,0:T(8,128)} %broadcast_in_dim.83.ids_ref, ...), custom_call_target="tpu_custom_call" | custom-call | flops 1073741824 | bytes 5505024 | tf_op jit(solution)/shard_map/combine/pallas_call | solution.py:218
  148.3 0.8 copy-done.7
  149.1 5.1 %combine.3 = (f32[256,1024]{1,0:T(8,128)}, bf16[256,1024]{1,0:T(8,128)(2,1)}) custom-call(s32[10]{0:T(128)} %stack.61.info_ref, f32[2,128,2048]{2,1,0:T(8,128)} %bitcast.31, f32[2,128,2048]{2,1,0:T(8,128)} %bitcast.33, f32[2,128,128]{2,1,0:T(8,128)} %convert.9.lowrank_ref, s32[4,128,128]{2,1,0:T(8,128)} %broadcast_in_dim.83.ids_ref, ...), custom_call_target="tpu_custom_call" | custom-call | flops 1073741824 | bytes 5505024 | tf_op jit(solution)/shard_map/combine/pallas_call | solution.py:218
  154.3 1.6 collective-permute-start.16
  155.8 7.0 %collective-permute-done.11 = bf16[256,1024]{1,0:T(8,128)(2,1)S(1)} collective-permute-done((bf16[256,1024]{1,0:T(8,128)(2,1)}, bf16[256,1024]{1,0:T(8,128)(2,1)S(1)}, u32[]{:S(2)}, u32[]{:S(2)}) %collective-permute-start.11) | collective-permute-done | bytes 524320 | tf_op jit(solution)/shard_map/ppermute | solution.py:19
  163.0 1.7 collective-permute-start.12
  164.8 13.9 %collective-permute-done.16 = bf16[256,1024]{1,0:T(8,128)(2,1)S(1)} collective-permute-done((bf16[256,1024]{1,0:T(8,128)(2,1)}, bf16[256,1024]{1,0:T(8,128)(2,1)S(1)}, u32[]{:S(2)}, u32[]{:S(2)}) %collective-permute-start.16) | collective-permute-done | bytes 524320 | tf_op jit(solution)/shard_map/ppermute | solution.py:19
  179.0 1.4 collective-permute-start.17
  180.5 12.4 %collective-permute-done.17 = bf16[128,1024]{1,0:T(8,128)(2,1)S(1)} collective-permute-done((bf16[128,1024]{1,0:T(8,128)(2,1)S(1)}, bf16[128,1024]{1,0:T(8,128)(2,1)S(1)}, u32[]{:S(2)}, u32[]{:S(2)}) %collective-permute-start.17) | collective-permute-done | bytes 262176 | tf_op jit(solution)/shard_map/ppermute | solution.py:19
  193.0 0.8 pad_maximum_fusion.4
  (63 shorter events, 4.8 us)
Async XLA Ops:
  0.0 5.9 %copy-start.9 = (s32[4,16]{1,0:T(4,128)S(1)}, s32[4,16]{1,0:T(4,128)}, u32[]{:S(2)}) copy-start(s32[4,16]{1,0:T(4,128)} %param.11) | copy-start | bytes 772
  0.0 6.0 %copy-start.10 = (s32[512]{0:T(512)S(1)}, s32[512]{0:T(512)}, u32[]{:S(2)}) copy-start(s32[512]{0:T(512)} %param.10) | copy-start | bytes 6148
  0.0 43.2 %collective-permute-start.1 = (bf16[128,7168]{1,0:T(8,128)(2,1)}, bf16[128,7168]{1,0:T(8,128)(2,1)S(1)}, u32[]{:S(2)}, u32[]{:S(2)}) collective-permute-start(bf16[128,7168]{1,0:T(8,128)(2,1)} %a_ref.3), channel_id=1, source_target_pairs={{0,8},{4,12},{8,0},{12,4},{1,9},{5,13},{9,1},{13,5},{2,10},{6,14},... | collective-permute-start | bytes 5505032 | tf_op jit(solution)/shard_map/ppermute | solution.py:19
  2.9 48.0 %collective-permute-start = (bf16[128,7168]{1,0:T(8,128)(2,1)}, bf16[128,7168]{1,0:T(8,128)(2,1)}, u32[]{:S(2)}, u32[]{:S(2)}) collective-permute-start(bf16[128,7168]{1,0:T(8,128)(2,1)} %a_ref.3), channel_id=1, source_target_pairs={{0,4},{4,0},{8,12},{12,8},{1,5},{5,1},{9,13},{13,9},{2,6},{6,2},{1... | collective-permute-start | bytes 5505032 | tf_op jit(solution)/shard_map/ppermute | solution.py:19
  5.3 136.2 %collective-permute-start.7 = (bf16[256,2048]{1,0:T(8,128)(2,1)}, bf16[256,2048]{1,0:T(8,128)(2,1)S(1)}, u32[]{:S(2)}, u32[]{:S(2)}) collective-permute-start(bf16[256,2048]{1,0:T(8,128)(2,1)} %constant_dynamic-slice_fusion.1), channel_id=1, source_target_pairs={{0,4},{4,0},{8,12},{12,8},{1,5},{5,1},{9,13},{13,9},{2,6},{6,2},{1... | collective-permute-start | bytes 3145736 | tf_op jit(solution)/shard_map/ppermute | solution.py:19
  43.2 7.7 %copy-start = (bf16[128,7168]{1,0:T(8,128)(2,1)}, bf16[128,7168]{1,0:T(8,128)(2,1)S(1)}, u32[]{:S(2)}) copy-start(bf16[128,7168]{1,0:T(8,128)(2,1)S(1)} %collective-permute-done.1.a_ref) | copy-start | bytes 5505028
  43.2 45.5 %collective-permute-start.2 = (bf16[128,7168]{1,0:T(8,128)(2,1)S(1)}, bf16[128,7168]{1,0:T(8,128)(2,1)}, u32[]{:S(2)}, u32[]{:S(2)}) collective-permute-start(bf16[128,7168]{1,0:T(8,128)(2,1)S(1)} %collective-permute-done.1.a_ref), channel_id=1, source_target_pairs={{0,4},{4,0},{8,12},{12,8},{1,5},{5,1},{9,13},{13,9},{2,6},{6,2},{1... | collective-permute-start | bytes 5505032 | tf_op jit(solution)/shard_map/ppermute | solution.py:19
  50.9 37.6 %collective-permute-start.8 = (bf16[2,128,1024]{2,1,0:T(8,128)(2,1)S(1)}, bf16[2,128,1024]{2,1,0:T(8,128)(2,1)S(1)}, u32[]{:S(2)}, u32[]{:S(2)}) collective-permute-start(bf16[2,128,1024]{2,1,0:T(8,128)(2,1)S(1)} %get-tuple-element.11), channel_id=1, source_target_pairs={{0,8},{4,12},{8,0},{12,4},{1,9},{5,13},{9,1},{13,5},{2,10},{6,14},... | collective-permute-start | bytes 1572872 | tf_op jit(solution)/shard_map/ppermute | solution.py:19
  52.8 55.8 %collective-permute-start.13 = (bf16[2,128,1024]{2,1,0:T(8,128)(2,1)S(1)}, bf16[2,128,1024]{2,1,0:T(8,128)(2,1)S(1)}, u32[]{:S(2)}, u32[]{:S(2)}) collective-permute-start(bf16[2,128,1024]{2,1,0:T(8,128)(2,1)S(1)} %get-tuple-element.14), channel_id=1, source_target_pairs={{0,8},{4,12},{8,0},{12,4},{1,9},{5,13},{9,1},{13,5},{2,10},{6,14},... | collective-permute-start | bytes 1572872 | tf_op jit(solution)/shard_map/ppermute | solution.py:19
  88.6 26.4 %collective-permute-start.9 = (bf16[128,1024]{1,0:T(8,128)(2,1)S(1)}, bf16[128,1024]{1,0:T(8,128)(2,1)S(1)}, u32[]{:S(2)}, u32[]{:S(2)}) collective-permute-start(bf16[128,1024]{1,0:T(8,128)(2,1)S(1)} %get-tuple-element.22), channel_id=1, source_target_pairs={{0,4},{4,0},{8,12},{12,8},{1,5},{5,1},{9,13},{13,9},{2,6},{6,2},{1... | collective-permute-start | bytes 786440 | tf_op jit(solution)/shard_map/ppermute | solution.py:19
  105.7 13.1 %copy-start.1 = (f32[256,128]{1,0:T(8,128)S(1)}, f32[256,128]{1,0:T(8,128)}, u32[]{:S(2)}) copy-start(f32[256,128]{1,0:T(8,128)} %far_scores.1) | copy-start | bytes 393220
  106.7 4.6 %collective-permute-start.3 = (bf16[256,128]{1,0:T(8,128)(2,1)S(1)}, bf16[256,128]{1,0:T(8,128)(2,1)S(1)}, u32[]{:S(2)}, u32[]{:S(2)}) collective-permute-start(bf16[256,128]{1,0:T(8,128)(2,1)S(1)} %convert_element_type.47), channel_id=1, source_target_pairs={{0,1},{1,0},{2,3},{3,2},{4,5},{5,4},{6,7},{7,6},{8,9},{9,8},{10,11... | collective-permute-start | bytes 196616 | tf_op jit(solution)/shard_map/ppermute | solution.py:19
  108.5 10.3 %collective-permute-start.14 = (bf16[128,1024]{1,0:T(8,128)(2,1)S(1)}, bf16[128,1024]{1,0:T(8,128)(2,1)S(1)}, u32[]{:S(2)}, u32[]{:S(2)}) collective-permute-start(bf16[128,1024]{1,0:T(8,128)(2,1)S(1)} %get-tuple-element.24), channel_id=1, source_target_pairs={{0,4},{4,0},{8,12},{12,8},{1,5},{5,1},{9,13},{13,9},{2,6},{6,2},{1... | collective-permute-start | bytes 786440 | tf_op jit(solution)/shard_map/ppermute | solution.py:19
  112.2 6.6 %collective-permute-start.4 = (bf16[256,128]{1,0:T(8,128)(2,1)S(1)}, bf16[256,128]{1,0:T(8,128)(2,1)S(1)}, u32[]{:S(2)}, u32[]{:S(2)}) collective-permute-start(bf16[256,128]{1,0:T(8,128)(2,1)S(1)} %fusion), channel_id=1, source_target_pairs={{0,2},{1,3},{2,0},{3,1},{4,6},{5,7},{6,4},{7,5},{8,10},{9,11},{10,... | collective-permute-start | bytes 196616 | tf_op jit(solution)/shard_map/ppermute | solution.py:19
  115.1 25.7 %copy-start.4 = (bf16[2,128,1024]{2,1,0:T(8,128)(2,1)}, bf16[2,128,1024]{2,1,0:T(8,128)(2,1)S(1)}, u32[]{:S(2)}) copy-start(bf16[2,128,1024]{2,1,0:T(8,128)(2,1)S(1)} %pad_maximum_fusion.1.mine_ref) | copy-start | bytes 1572868
  115.1 26.4 %collective-permute-start.10 = (bf16[2,128,1024]{2,1,0:T(8,128)(2,1)S(1)}, bf16[2,128,1024]{2,1,0:T(8,128)(2,1)S(1)}, u32[]{:S(2)}, u32[]{:S(2)}) collective-permute-start(bf16[2,128,1024]{2,1,0:T(8,128)(2,1)S(1)} %pad_maximum_fusion.1.mine_ref), channel_id=1, source_target_pairs={{0,16},{16,0},{1,17},{17,1},{2,18},{18,2},{3,19},{19,3},{4,20},{20... | collective-permute-start | bytes 1572872 | tf_op jit(solution)/shard_map/ppermute | solution.py:19
  118.8 1.7 collective-permute-start.5
  118.9 21.8 %copy-start.3 = (bf16[2,128,1024]{2,1,0:T(8,128)(2,1)}, bf16[2,128,1024]{2,1,0:T(8,128)(2,1)S(1)}, u32[]{:S(2)}) copy-start(bf16[2,128,1024]{2,1,0:T(8,128)(2,1)S(1)} %pad_maximum_fusion.3.mine_ref) | copy-start | bytes 1572868
  118.9 29.4 %collective-permute-start.15 = (bf16[2,128,1024]{2,1,0:T(8,128)(2,1)S(1)}, bf16[2,128,1024]{2,1,0:T(8,128)(2,1)S(1)}, u32[]{:S(2)}, u32[]{:S(2)}) collective-permute-start(bf16[2,128,1024]{2,1,0:T(8,128)(2,1)S(1)} %pad_maximum_fusion.3.mine_ref), channel_id=1, source_target_pairs={{0,16},{16,0},{1,17},{17,1},{2,18},{18,2},{3,19},{19,3},{4,20},{20... | collective-permute-start | bytes 1572872 | tf_op jit(solution)/shard_map/ppermute | solution.py:19
  120.6 20.2 %collective-permute-start.6 = (bf16[256,128]{1,0:T(8,128)(2,1)S(1)}, bf16[256,128]{1,0:T(8,128)(2,1)S(1)}, u32[]{:S(2)}, u32[]{:S(2)}) collective-permute-start(bf16[256,128]{1,0:T(8,128)(2,1)S(1)} %fusion.1), channel_id=1, source_target_pairs={{0,8},{4,12},{8,0},{12,4},{1,9},{5,13},{9,1},{13,5},{2,10},{6,14},... | collective-permute-start | bytes 196616 | tf_op jit(solution)/shard_map/ppermute | solution.py:19
  141.4 1.1 copy-start.2
  141.5 1.2 copy-start.8
  147.8 15.0 %collective-permute-start.11 = (bf16[256,1024]{1,0:T(8,128)(2,1)}, bf16[256,1024]{1,0:T(8,128)(2,1)S(1)}, u32[]{:S(2)}, u32[]{:S(2)}) collective-permute-start(bf16[256,1024]{1,0:T(8,128)(2,1)} %get-tuple-element.13), channel_id=1, source_target_pairs={{0,1},{1,0},{2,3},{3,2},{4,5},{5,4},{6,7},{7,6},{8,9},{9,8},{10,11... | collective-permute-start | bytes 1572872 | tf_op jit(solution)/shard_map/ppermute | solution.py:19
  148.3 14.5 %copy-start.5 = (f32[256,1024]{1,0:T(8,128)S(1)}, f32[256,1024]{1,0:T(8,128)}, u32[]{:S(2)}) copy-start(f32[256,1024]{1,0:T(8,128)} %get-tuple-element.12) | copy-start | bytes 3145732
  148.3 0.8 copy-start.7
  154.2 24.5 %copy-start.6 = (f32[256,1024]{1,0:T(8,128)S(1)}, f32[256,1024]{1,0:T(8,128)}, u32[]{:S(2)}) copy-start(f32[256,1024]{1,0:T(8,128)} %get-tuple-element.15) | copy-start | bytes 3145732
  154.3 24.5 %collective-permute-start.16 = (bf16[256,1024]{1,0:T(8,128)(2,1)}, bf16[256,1024]{1,0:T(8,128)(2,1)S(1)}, u32[]{:S(2)}, u32[]{:S(2)}) collective-permute-start(bf16[256,1024]{1,0:T(8,128)(2,1)} %get-tuple-element.16), channel_id=1, source_target_pairs={{0,1},{1,0},{2,3},{3,2},{4,5},{5,4},{6,7},{7,6},{8,9},{9,8},{10,11... | collective-permute-start | bytes 1572872 | tf_op jit(solution)/shard_map/ppermute | solution.py:19
  163.0 17.3 %collective-permute-start.12 = (bf16[128,1024]{1,0:T(8,128)(2,1)S(1)}, bf16[128,1024]{1,0:T(8,128)(2,1)S(1)}, u32[]{:S(2)}, u32[]{:S(2)}) collective-permute-start(bf16[128,1024]{1,0:T(8,128)(2,1)S(1)} %select_convert_fusion.1), channel_id=1, source_target_pairs={{0,2},{1,3},{2,0},{3,1},{4,6},{5,7},{6,4},{7,5},{8,10},{9,11},{10,... | collective-permute-start | bytes 786440 | tf_op jit(solution)/shard_map/ppermute | solution.py:19
  179.0 14.0 %collective-permute-start.17 = (bf16[128,1024]{1,0:T(8,128)(2,1)S(1)}, bf16[128,1024]{1,0:T(8,128)(2,1)S(1)}, u32[]{:S(2)}, u32[]{:S(2)}) collective-permute-start(bf16[128,1024]{1,0:T(8,128)(2,1)S(1)} %select_convert_fusion), channel_id=1, source_target_pairs={{0,2},{1,3},{2,0},{3,1},{4,6},{5,7},{6,4},{7,5},{8,10},{9,11},{10,... | collective-permute-start | bytes 786440 | tf_op jit(solution)/shard_map/ppermute | solution.py:19

commit v2 on v1

v2 whole, which is shorter than its diff:
```python
import jax
import jax.numpy as jnp
from jax import lax
from jax.experimental import pallas as pl
from jax.experimental.pallas import tpu as pltpu
from jax.sharding import PartitionSpec as P

F32 = jnp.float32
BF16 = jnp.bfloat16
VMEM_LIMIT = 56 * 1024 * 1024
CHUNKS = 4
CAP = 4
HALVES = 2


def partners(count, step):
    return [(i, i ^ step) for i in range(count)]


def swap(values, axis, step):
    return lax.ppermute(values, axis, partners(lax.axis_size(axis), step))


def tie(values, *after):
    return lax.optimization_barrier((values, *after))[0]


def params():
    return pltpu.CompilerParams(vmem_limit_bytes=VMEM_LIMIT)


def base_kernel(has_prior, *refs):
    if has_prior:
        prior_ref, refs = refs[0], refs[1:]
    a_ref, b_ref, w_ref, out_ref, rows = refs

    @pl.when(pl.program_id(0) == 0)
    def _():
        half = a_ref.shape[0]
        rows[:half, :] = a_ref[...]
        rows[half:, :] = b_ref[...]

    value = jnp.dot(rows[...], w_ref[...], preferred_element_type=F32)
    if has_prior:
        value += prior_ref[...]
    out_ref[...] = value


def base_product(a, b, weight, depth_block=0, prior=None, first=0, width=None):
    rows, depth = a.shape
    width = weight.shape[1] if width is None else width
    tile = 512
    in_specs = [
        pl.BlockSpec((rows, depth), lambda n: (0, 0)),
        pl.BlockSpec((rows, depth), lambda n: (0, 0)),
        pl.BlockSpec((depth, tile), lambda n: (depth_block, first // tile + n)),
    ]
    args = [a, b, weight]
    if prior is not None:
        in_specs.insert(0, pl.BlockSpec((2 * rows, tile), lambda n: (0, first // tile + n)))
        args.insert(0, prior)
    return pl.pallas_call(
        lambda *refs: base_kernel(prior is not None, *refs),
        grid=(width // tile,),
        in_specs=in_specs,
        out_specs=pl.BlockSpec((2 * rows, tile), lambda n: (0, n)),
        out_shape=jax.ShapeDtypeStruct((2 * rows, width), F32),
        scratch_shapes=[pltpu.VMEM((2 * rows, depth), BF16)],
        compiler_params=params(),
        cost_estimate=pl.CostEstimate(
            flops=4 * rows * depth * width,
            bytes_accessed=2 * depth * (width + 2 * rows) + 8 * rows * width,
            transcendentals=0,
        ),
        name="base",
    )(*args)


def scores_kernel(first, has_prior, last, chosen_ref, *refs):
    a_ref, b_ref = refs[:2]
    maps = refs[2 : 2 + 2 * CAP]
    refs = refs[2 + 2 * CAP :]
    if has_prior:
        prior_ref, refs = refs[0], refs[1:]
    if last:
        ids_ref, out_ref, total = refs
    else:
        (total,) = refs
    for pair, rows_ref in enumerate((a_ref, b_ref)):
        picked = jnp.concatenate([m[0] for m in maps[pair * CAP : (pair + 1) * CAP]], axis=0)
        term = lax.dot_general(
            rows_ref[...], picked, (((1,), (1,)), ((), ())), preferred_element_type=F32
        )

        @pl.when(pl.program_id(0) == 0)
        def _():
            total[pair] = term + prior_ref[pair] if has_prior else term

        @pl.when(pl.program_id(0) > 0)
        def _():
            total[pair] += term

    if last:

        @pl.when(pl.program_id(0) == pl.num_programs(0) - 1)
        def _():
            for pair in range(2):
                wanted = ids_ref[pair]
                lanes = wanted.shape[1]
                upper = lax.broadcasted_iota(jnp.int32, wanted.shape, 1) >= lanes // 2
                found = jnp.zeros(wanted.shape, F32)
                for k in range(0, CAP, 2):
                    spot = (first + pair) * CAP + k
                    mine = jnp.where(upper, chosen_ref[spot + 1], chosen_ref[spot])
                    column = (k // 2) * lanes
                    found += jnp.where(
                        wanted == mine, total[pair, :, column : column + lanes], 0.0
                    )
                out_ref[pair] = found + pltpu.roll(found, lanes // 2, 1)


def scores(chosen, first, a, b, maps, depth_block, prior=None, ids=None):
    rows, depth = a.shape
    rank = maps.shape[1]
    block = 1792
    steps = depth // block
    lanes = 128

    def maps_spec(spot):
        return pl.BlockSpec(
            (1, rank, block), lambda k, s: (s[spot], 0, depth_block * steps + k)
        )

    in_specs = [pl.BlockSpec((rows, block), lambda k, s: (0, k))] * 2
    in_specs += [maps_spec(first * CAP + spot) for spot in range(2 * CAP)]
    args = [a, b] + [maps] * (2 * CAP)
    if prior is not None:
        in_specs.append(pl.BlockSpec((2, rows, CAP * rank), lambda k, s: (0, 0, 0)))
        args.append(prior)
    last = ids is not None
    scratch = []
    out_columns = CAP * rank
    if last:
        in_specs.append(pl.BlockSpec((2, rows, lanes), lambda k, s: (first // 2, 0, 0)))
        args.append(ids)
        scratch = [pltpu.VMEM((2, rows, CAP * rank), F32)]
        out_columns = lanes
    has_prior = prior is not None
    return pl.pallas_call(
        lambda *refs: scores_kernel(first, has_prior, last, *refs),
        grid_spec=pltpu.PrefetchScalarGridSpec(
            num_scalar_prefetch=1,
            grid=(steps,),
            in_specs=in_specs,
            out_specs=pl.BlockSpec((2, rows, out_columns), lambda k, s: (0, 0, 0)),
            scratch_shapes=scratch,
        ),
        out_shape=jax.ShapeDtypeStruct((2, rows, out_columns), F32),
        compiler_params=params(),
        cost_estimate=pl.CostEstimate(
            flops=4 * rows * depth * CAP * rank,
            bytes_accessed=4 * depth * (CAP * rank + rows),
            transcendentals=0,
        ),
        name="scores",
    )(chosen, *args)


def spread_kernel(info_ref, lowrank_ref, ids_ref, spread_ref):
    rows, lanes = ids_ref.shape[1], ids_ref.shape[2]
    parity, place = info_ref[0], info_ref[1]
    upper = (lax.broadcasted_iota(jnp.int32, (rows, lanes), 1) >= lanes // 2).astype(jnp.int32)
    for slot in range(4):
        local = ((slot // 2) ^ parity) + 2 * (slot % 2)
        group = place ^ local
        packed = lowrank_ref[group % 2]
        values = jnp.where(upper == group // 2, packed, pltpu.roll(packed, lanes // 2, 1))
        wanted = ids_ref[local] - upper
        for piece in range(8):
            spread_ref[slot * rows : (slot + 1) * rows, piece * lanes : (piece + 1) * lanes] = (
                jnp.where(wanted == info_ref[2 + piece], values, 0.0).astype(BF16)
            )


def spread_rows(info, lowrank, ids):
    rows, lanes = ids.shape[1], ids.shape[2]
    return pl.pallas_call(
        spread_kernel,
        grid_spec=pltpu.PrefetchScalarGridSpec(
            num_scalar_prefetch=1,
            grid=(1,),
            in_specs=[
                pl.BlockSpec((2, rows, lanes), lambda n, s: (0, 0, 0)),
                pl.BlockSpec((4, rows, lanes), lambda n, s: (0, 0, 0)),
            ],
            out_specs=pl.BlockSpec((4 * rows, 8 * lanes), lambda n, s: (0, 0)),
        ),
        out_shape=jax.ShapeDtypeStruct((4 * rows, 8 * lanes), BF16),
        compiler_params=params(),
        cost_estimate=pl.CostEstimate(
            flops=16 * rows * lanes * 8, bytes_accessed=96 * rows * lanes, transcendentals=0
        ),
        name="spread",
    )(info, lowrank, ids)


def combine_kernel(
    info_ref, near_ref, far_ref, spread_ref, own_ref, core_ref, mine_ref, other_ref,
    keep_ref, send_ref, maps,
):
    parity = info_ref[0]
    rows = near_ref.shape[1]
    held = own_ref.shape[0]
    maps[0:held, :] = own_ref[...]
    maps[held : 2 * held, :] = core_ref[...]
    start = 2 * held
    for ref in (mine_ref, other_ref):
        for index in range(2):
            maps[start : start + held // 2, :] = ref[index]
            start += held // 2
    delta = jnp.dot(spread_ref[...], maps[...], preferred_element_type=F32)
    for slot in range(4):
        source = near_ref if slot % 2 == 0 else far_ref
        value = source[(slot // 2) ^ parity] + delta[slot * rows : (slot + 1) * rows]
        if slot < 2:
            keep_ref[slot % 2] = value
        else:
            send_ref[slot % 2] = value.astype(BF16)


def combine(info, near, far, spread, own_maps, core_maps, mine, other, chunk):
    width = mine.shape[2]
    rows = near.shape[1]
    tile = 256
    steps = width // tile
    first = chunk * steps
    per_place = core_maps.shape[1] // tile
    held = own_maps.shape[0]
    return pl.pallas_call(
        combine_kernel,
        grid_spec=pltpu.PrefetchScalarGridSpec(
            num_scalar_prefetch=1,
            grid=(steps,),
            in_specs=[
                pl.BlockSpec((2, rows, tile), lambda n, s: (0, 0, first + n)),
                pl.BlockSpec((2, rows, tile), lambda n, s: (0, 0, n)),
                pl.BlockSpec((4 * rows, 4 * held), lambda n, s: (0, 0)),
                pl.BlockSpec((held, tile), lambda n, s: (0, s[1] * per_place + first + n)),
                pl.BlockSpec((held, tile), lambda n, s: (0, first + n)),
                pl.BlockSpec((2, held // 2, tile), lambda n, s: (0, 0, n)),
                pl.BlockSpec((2, held // 2, tile), lambda n, s: (0, 0, n)),
            ],
            out_specs=[
                pl.BlockSpec((2, rows, tile), lambda n, s: (0, 0, n)),
                pl.BlockSpec((2, rows, tile), lambda n, s: (0, 0, n)),
            ],
            scratch_shapes=[pltpu.VMEM((4 * held, tile), BF16)],
        ),
        out_shape=[
            jax.ShapeDtypeStruct((2, rows, width), F32),
            jax.ShapeDtypeStruct((2, rows, width), BF16),
        ],
        compiler_params=params(),
        cost_estimate=pl.CostEstimate(
            flops=32 * rows * held * width,
            bytes_accessed=26 * rows * width + 8 * held * width,
            transcendentals=0,
        ),
        name="combine",
    )(info, near, far, spread, own_maps, core_maps, mine, other)


def per_device_fast(hidden, weight, input_maps, output_maps, slots, lists):
    rows, depth = hidden.shape
    place = lax.axis_index("pool")
    t = lax.axis_index("tensor")
    y = lax.axis_index("groups")
    holding, rank = input_maps.shape[:2]
    held, features = output_maps.shape
    width = features // 4
    chip, core = place >> 1, place & 1

    part = depth // HALVES
    crossed = []
    for half in range(HALVES):
        block = hidden[:, half * part : (half + 1) * part]
        if crossed:
            block = tie(block, previous)
        previous = block
        crossed.append(swap(block, "pool", 2))
    near_b = swap(tie(hidden, previous), "pool", 1)

    core_maps = swap(
        lax.dynamic_slice(output_maps, (0, (place ^ 1) * width), (held, width)), "pool", 1
    )
    chunk_width = width // CHUNKS
    blocks = []
    for chunk in range(CHUNKS):
        start = (1 - chip) * 2 * width + chunk * chunk_width
        blocks.append(
            jnp.stack(
                [
                    lax.dynamic_slice(
                        output_maps,
                        (y * (held // 2), start + c * width),
                        (held // 2, chunk_width),
                    )
                    for c in range(2)
                ]
            )
        )

    order = place ^ jnp.arange(4, dtype=jnp.int32)
    hot = order[:, None] == jnp.arange(4, dtype=jnp.int32)[None, :]
    slots_local = jnp.sum(jnp.where(hot[:, :, None], slots.reshape(1, 4, rows), 0), axis=1)
    lists_local = jnp.sum(jnp.where(hot[:, :, None], lists[None, :, :], 0), axis=1)
    positions = jnp.arange(lists.shape[1], dtype=jnp.int32)
    ids = jnp.sum(
        jnp.where(slots_local[:, :, None] == positions, lists_local[:, None, :], 0), axis=2
    )
    wide_ids = jnp.broadcast_to(ids[:, :, None], (4, rows, 128))
    owned_ids = wide_ids - place * holding
    owned = lists_local // holding == place
    earlier = positions[None, :] < positions[:, None]
    rank_in_list = jnp.sum(owned[:, None, :] & earlier[None], axis=2)
    caps = jnp.arange(CAP, dtype=jnp.int32)
    chosen = jnp.sum(
        jnp.where(
            owned[:, None, :] & (rank_in_list[:, None, :] == caps[None, :, None]),
            (lists_local % holding)[:, None, :],
            0,
        ),
        axis=2,
    ).reshape(4 * CAP)

    near_lowrank = scores(chosen, 0, hidden, near_b, input_maps, 0, ids=owned_ids)
    near_base = base_product(tie(hidden, near_lowrank), near_b, weight)
    blocks[0] = tie(blocks[0], near_b)
    crossing = [swap(block, "pool", 2) for block in blocks[: CHUNKS - 1]]

    a0 = tie(crossed[0], near_base)
    b0 = swap(a0, "pool", 1)
    raw = scores(chosen, 2, a0, b0, input_maps, 0)
    far_base = base_product(tie(a0, raw), b0, weight, 0)
    a1 = tie(crossed[1], far_base)
    b1 = swap(a1, "pool", 1)
    far_lowrank = scores(chosen, 2, a1, b1, input_maps, 1, prior=raw, ids=owned_ids)

    def by_core(values):
        return jnp.where(core == 0, values, values[::-1])

    near_lanes = (jnp.arange(128) // rank)[None, None, :] == chip
    total = jnp.where(near_lanes, by_core(near_lowrank), by_core(far_lowrank))
    total = total.reshape(2 * rows, 128)
    pieces = []
    for index, (axis, step) in enumerate(
        (("tensor", 1), ("tensor", 2), ("pool", 1), ("pool", 2))
    ):
        sent = total.astype(BF16)
        got = swap(sent, axis, step)
        if index > 0:
            crossing[index - 1] = tie(crossing[index - 1], sent)
        pieces.append(
            base_product(
                tie(a1, sent), b1, weight, 1, far_base, index * chunk_width, chunk_width
            )
        )
        if index == 3:
            crossing.append(swap(tie(blocks[-1], sent), "pool", 2))
        got = tie(got, pieces[-1])
        total = total + got.astype(F32)
    lowrank = total.reshape(2, rows, 128)

    mine, other = [], []
    for block in crossing:
        kept = jnp.where(core == 0, block[0], block[1])
        passed = jnp.where(core == 0, block[1], block[0])
        mine.append(jnp.stack([kept, swap(passed, "pool", 1)]))
        other.append(swap(mine[-1], "groups", 1))

    parity = (place ^ t) & 1
    per_owner = held // rank
    first = holding * order + per_owner * t
    half_step = per_owner // 2
    info = jnp.stack(
        [
            parity,
            place,
            first[0],
            first[0] + half_step,
            first[1],
            first[1] + half_step,
            first[2] + half_step * y,
            first[3] + half_step * y,
            first[2] + half_step * (1 - y),
            first[3] + half_step * (1 - y),
        ]
    ).astype(jnp.int32)

    spread = spread_rows(info, lowrank, wide_ids)
    near_base = near_base.reshape(2, rows, width)
    side = ((place ^ t) >> 1) & 1
    parts = []
    for chunk in range(CHUNKS):
        keep, send = combine(
            info, near_base, pieces[chunk].reshape(2, rows, chunk_width), spread,
            output_maps, core_maps, mine[chunk], other[chunk], chunk,
        )
        pair = keep + swap(send, "tensor", 1).astype(F32)
        sent = jnp.where(side == 0, pair[1], pair[0]).astype(BF16)
        kept = jnp.where(side == 0, pair[0], pair[1])
        parts.append(kept + swap(sent, "tensor", 2).astype(F32))
    return jnp.concatenate(parts, axis=1).astype(BF16)


def per_device_general(hidden, weight, input_maps, output_maps, slots, lists):
    rows, depth = hidden.shape
    pool_count = lax.axis_size("pool")
    tensor_count = lax.axis_size("tensor")
    place = lax.axis_index("pool")
    t = lax.axis_index("tensor")
    holding, rank = input_maps.shape[:2]
    held = output_maps.shape[0]
    total_rows = rows * pool_count
    slot_ids = jnp.arange(lists.shape[1], dtype=jnp.int32)
    slot_hot = slots.reshape(pool_count, rows)[:, :, None] == slot_ids
    ids = jnp.sum(jnp.where(slot_hot, lists[:, None, :], 0), axis=2).reshape(total_rows)
    gathered = lax.all_gather(hidden, "pool", axis=0, tiled=True)
    scored = lax.dot_general(
        gathered,
        input_maps.reshape(holding * rank, depth),
        (((1,), (1,)), ((), ())),
        preferred_element_type=F32,
    ).reshape(total_rows, holding, rank)
    owned = place * holding + jnp.arange(holding, dtype=jnp.int32)
    partial = jnp.sum(
        jnp.where((ids[:, None] == owned[None, :])[:, :, None], scored, 0.0), axis=1
    )
    lowrank = lax.psum(partial, ("tensor", "pool")).astype(BF16)
    maps = lax.all_to_all(output_maps, "pool", split_axis=1, concat_axis=0, tiled=True)
    columns = jnp.arange(pool_count * held, dtype=jnp.int32)
    source = (columns // held * tensor_count + t) * held + columns % held
    pick = (source[None, :] % rank == jnp.arange(rank, dtype=jnp.int32)[:, None]).astype(BF16)
    placed = jnp.dot(lowrank, pick, preferred_element_type=F32).astype(BF16)
    spread = jnp.where(ids[:, None] == source[None, :] // rank, placed, jnp.zeros_like(placed))
    value = jnp.dot(gathered, weight, preferred_element_type=F32)
    value = value + jnp.dot(spread, maps, preferred_element_type=F32)
    mixed = lax.psum_scatter(value, "tensor", scatter_dimension=0, tiled=True)
    return mixed.astype(BF16)


def solution(mesh):
    shape = dict(mesh.shape)
    fast = shape["groups"] == 2 and shape["pool"] == 4 and shape["tensor"] == 4
    placed = (
        P(("groups", "pool"), "tensor"),
        P("tensor", "pool"),
        P("pool", None, "tensor"),
        P(("pool", "tensor"), None),
        P("groups"),
        P("groups", None),
    )
    return jax.shard_map(
        per_device_fast if fast else per_device_general,
        mesh=mesh,
        in_specs=placed,
        out_specs=P(("groups", "tensor"), "pool"),
        check_vma=False,
    )
```

time: 194 us -> 173 us (0.89)
  waiting for transfers between devices: 75 us -> 28.3 us
  local copies, waits for them, and re-layouts: 9.78 us -> 17.8 us
  starting transfers between devices: 20.6 us -> 27.5 us
  other arithmetic: 4.69 us -> 9.98 us
  Pallas kernels: 79.8 us -> 84.2 us
    ppermute x18 -> x30, waiting for transfers between devices: 75 us -> 28.3 us  [swap(): return lax.ppermute(values, axis, partners(lax.axis_size(axis), step))]
    ppermute x18 -> x30, starting transfers between devices: 20.6 us -> 27.5 us  [swap(): return lax.ppermute(values, axis, partners(lax.axis_size(axis), step))]
    pallas_call x2 -> x4, Pallas kernels: 10.3 us -> 16.7 us  [combine(): pl.pallas_call(combine_kernel, grid_spec=pltpu.PrefetchScalarGridSpec(num...]
    unnamed x22 -> x40, local copies, waits for them, and re-layouts: 1.05 us -> 5.97 us
    select_n x0 -> x6, other arithmetic: none -> 3.04 us  [the longest x4 2.02 us: per_device_fast(): kept = jnp.where(core == 0, block[0], block[1])]
    slice x1, local copies, waits for them, and re-layouts: 0.01 us -> 2.84 us  [per_device_fast(): block = hidden[:, half * part:(half + 1) * part]]
    pallas_call x4 -> x10, Pallas kernels: 69.6 us -> 67.5 us  [the longest x6 43.5 us: base_product(): pl.pallas_call(lambda *refs: base_kernel(prior is not None, *refs), grid=...]
  transfers between devices with their start and end apart: 18 -> 30, of which waited for: 6 -> 6; matrix products, arithmetic and copies ran while one was open for 6% -> 10% of each run, Pallas kernels for 41% -> 49%
where the time goes in v2:
time: 173 us; the launch traced here: 172 us
  Pallas kernels  84.2 us (49%)
  waiting for transfers between devices  28.3 us (16%)
  starting transfers between devices  27.5 us (16%)
  local copies, waits for them, and re-layouts  17.8 us (10%)
  other arithmetic  9.98 us (6%)
  between operations  4.1 us (2%)
    pallas_call x6, Pallas kernels, base_product(): pl.pallas_call(lambda *refs: base_kernel(prior is not None, *refs), grid=...  43.5 us
    ppermute x30, waiting for transfers between devices, swap(): return lax.ppermute(values, axis, partners(lax.axis_size(axis), step))  28.3 us
    ppermute x30, starting transfers between devices, swap(): return lax.ppermute(values, axis, partners(lax.axis_size(axis), step))  27.5 us
    pallas_call x3, Pallas kernels, scores(): pl.pallas_call(lambda *refs: scores_kernel(first, has_prior, last, *refs)...  21 us
    pallas_call x4, Pallas kernels, combine(): pl.pallas_call(combine_kernel, grid_spec=pltpu.PrefetchScalarGridSpec(num...  16.7 us
    unnamed x40, local copies, waits for them, and re-layouts  5.97 us
  transfers between devices with their start and end apart: 30, of which 6 were waited for; matrix products, arithmetic and copies ran while one was open for 10% of the time, Pallas kernels for 49%

profile of v2, /device:TPU:0, one launch (start us, length us, event | category | flops | bytes accessed | tf_op | source)
XLA Modules:
  0.0 171.9 jit_solution(11346499677651208205)
XLA Ops:
  0.0 2.8 %fusion.16 = (bf16[128,3584]{1,0:T(8,128)(2,1)}, bf16[128,3584]{1,0:T(8,128)(2,1)}) fusion(bf16[128,7168]{1,0:T(8,128)(2,1)} %refs_0_), kind=kLoop, calls=%fused_computation.84 | loop fusion | bytes 3670016 | tf_op jit(solution)/shard_map/slice | solution.py:286
  3.3 2.5 %collective-permute-start.1 = (bf16[128,3584]{1,0:T(8,128)(2,1)}, bf16[128,3584]{1,0:T(8,128)(2,1)S(1)}, u32[]{:S(2)}, u32[]{:S(2)}) collective-permute-start(bf16[128,3584]{1,0:T(8,128)(2,1)} %get-tuple-element.67), channel_id=1, source_target_pairs={{0,8},{4,12},{8,0},{12,4},{1,9},{5,13},{9,1},{13,5},{2,10},{6,14},... | collective-permute-start | bytes 2752520 | tf_op jit(solution)/shard_map/ppermute | solution.py:21
  10.3 9.1 %scores.3 = f32[2,128,128]{2,1,0:T(8,128)} custom-call(s32[16]{0:T(128)} %reshape.147.refs_0_, bf16[128,7168]{1,0:T(8,128)(2,1)} %refs_0_, bf16[128,7168]{1,0:T(8,128)(2,1)} %copy-done.3, bf16[16,64,7168]{2,1,0:T(8,128)(2,1)} %refs_10_.5, bf16[16,64,7168]{2,1,0:T(8,128)(2,1)} %refs_10_.5, bf16[16,64,7168]{2,1,0:T(8,128)(2,1)} %refs_10_.5, ...), custom_call_target="tpu_custom_call" | custom-call | flops 939524096 | bytes 11010048 | tf_op jit(solution)/shard_map/scores/pallas_call | solution.py:149
  19.4 15.1 %base.6 = f32[256,2048]{1,0:T(8,128)} custom-call(bf16[128,7168]{1,0:T(8,128)(2,1)} %refs_0_, bf16[128,7168]{1,0:T(8,128)(2,1)} %copy-done.3, bf16[7168,2048]{1,0:T(8,128)(2,1)} %refs_3_.13), custom_call_target="tpu_custom_call" | custom-call | flops 7516192768 | bytes 35127296 | tf_op jit(solution)/shard_map/base/pallas_call | solution.py:62
  35.5 1.6 collective-permute-done.2.refs_2_.refs_1_
  38.0 5.8 %scores.4.refs_11_ = f32[2,128,256]{2,1,0:T(8,128)} custom-call(s32[16]{0:T(128)} %reshape.147.refs_0_, bf16[128,3584]{1,0:T(8,128)(2,1)} %copy-done.4, bf16[128,3584]{1,0:T(8,128)(2,1)} %copy-done.5, bf16[16,64,7168]{2,1,0:T(8,128)(2,1)} %refs_10_.5, bf16[16,64,7168]{2,1,0:T(8,128)(2,1)} %refs_10_.5, bf16[16,64,7168]{2,1,0:T(8,128)(2,1)} %refs_10_.5, ...), custom_call_target="tpu_custom_call" | custom-call | flops 469762048 | bytes 5505024 | tf_op jit(solution)/shard_map/scores/pallas_call | solution.py:149
  43.9 9.5 %base.7.refs_0_ = f32[256,2048]{1,0:T(8,128)} custom-call(bf16[128,3584]{1,0:T(8,128)(2,1)} %copy-done.4, bf16[128,3584]{1,0:T(8,128)(2,1)} %copy-done.5, bf16[7168,2048]{1,0:T(8,128)(2,1)} %refs_3_.13), custom_call_target="tpu_custom_call" | custom-call | flops 3758096384 | bytes 18612224 | tf_op jit(solution)/shard_map/base/pallas_call | solution.py:62
  53.4 4.2 %collective-permute-done.3.refs_1_ = bf16[128,3584]{1,0:T(8,128)(2,1)S(1)} collective-permute-done((bf16[128,3584]{1,0:T(8,128)(2,1)}, bf16[128,3584]{1,0:T(8,128)(2,1)S(1)}, u32[]{:S(2)}, u32[]{:S(2)}) %collective-permute-start.3) | collective-permute-done | bytes 917536 | tf_op jit(solution)/shard_map/ppermute | solution.py:21
  57.6 2.7 %constant_dynamic-slice_fusion = bf16[256,2048]{1,0:T(8,128)(2,1)} fusion(bf16[256,8192]{1,0:T(8,128)(2,1)} %own_ref.7, s32[]{:T(128)S(6)} %select_n.214), kind=kLoop, calls=%fused_computation.83 | loop fusion | bytes 2097156 | tf_op jit(solution)/shard_map/dynamic_slice | solution.py:294
  60.5 1.4 dynamic-slice_bitcast_fusion.7
  69.7 1.9 %stack.93.info_ref = s32[10]{0:T(128)} concatenate(s32[1]{0:T(128)} %bitcast, s32[1]{0:T(128)} %bitcast.1, s32[1]{0:T(128)} %get-tuple-element.80, s32[1]{0:T(128)S(6)} %add.162, s32[1]{0:T(128)} %get-tuple-element.79, s32[1]{0:T(128)S(6)} %add.163, s32[1]{0:T(128)} %bitcast.3, s32[1]{0:T(128)} %bitcast.5, s32[1]{0:T(128)} %bitcast.6, s32[1]{0:T(128)} %bitcast.7), dimensions={0} | concatenate | bytes 80 | tf_op jit(solution)/shard_map/stack | solution.py:385
  73.4 6.0 %scores.5 = f32[2,128,128]{2,1,0:T(8,128)} custom-call(s32[16]{0:T(128)} %reshape.147.refs_0_, bf16[128,3584]{1,0:T(8,128)(2,1)} %copy-done, bf16[128,3584]{1,0:T(8,128)(2,1)} %copy-done.1, bf16[16,64,7168]{2,1,0:T(8,128)(2,1)} %refs_10_.5, bf16[16,64,7168]{2,1,0:T(8,128)(2,1)} %refs_10_.5, bf16[16,64,7168]{2,1,0:T(8,128)(2,1)} %refs_10_.5, ...), custom_call_target="tpu_custom_call" | custom-call | flops 469762048 | bytes 5505024 | tf_op jit(solution)/shard_map/scores/pallas_call | solution.py:149
  80.5 1.6 collective-permute-start.5
  82.1 4.7 %base.8 = f32[256,512]{1,0:T(8,128)} custom-call(f32[256,2048]{1,0:T(8,128)} %base.7.refs_0_, bf16[128,3584]{1,0:T(8,128)(2,1)} %copy-done, bf16[128,3584]{1,0:T(8,128)(2,1)} %copy-done.1, bf16[7168,2048]{1,0:T(8,128)(2,1)} %refs_3_.13), custom_call_target="tpu_custom_call" | custom-call | flops 939524096 | bytes 6029312 | tf_op jit(solution)/shard_map/base/pallas_call | solution.py:62
  86.9 2.7 %collective-permute-start.6 = (bf16[256,128]{1,0:T(8,128)(2,1)S(1)}, bf16[256,128]{1,0:T(8,128)(2,1)S(1)}, u32[]{:S(2)}, u32[]{:S(2)}) collective-permute-start(bf16[256,128]{1,0:T(8,128)(2,1)S(1)} %fusion.11), channel_id=1, source_target_pairs={{0,2},{1,3},{2,0},{3,1},{4,6},{5,7},{6,4},{7,5},{8,10},{9,11},{10,... | collective-permute-start | bytes 196616 | tf_op jit(solution)/shard_map/ppermute | solution.py:21
  89.7 4.7 %base.9 = f32[256,512]{1,0:T(8,128)} custom-call(f32[256,2048]{1,0:T(8,128)} %base.7.refs_0_, bf16[128,3584]{1,0:T(8,128)(2,1)} %copy-done, bf16[128,3584]{1,0:T(8,128)(2,1)} %copy-done.1, bf16[7168,2048]{1,0:T(8,128)(2,1)} %refs_3_.13), custom_call_target="tpu_custom_call" | custom-call | flops 939524096 | bytes 6029312 | tf_op jit(solution)/shard_map/base/pallas_call | solution.py:62
  96.0 4.8 %base.10 = f32[256,512]{1,0:T(8,128)} custom-call(f32[256,2048]{1,0:T(8,128)} %base.7.refs_0_, bf16[128,3584]{1,0:T(8,128)(2,1)} %copy-done, bf16[128,3584]{1,0:T(8,128)(2,1)} %copy-done.1, bf16[7168,2048]{1,0:T(8,128)(2,1)} %refs_3_.13), custom_call_target="tpu_custom_call" | custom-call | flops 939524096 | bytes 6029312 | tf_op jit(solution)/shard_map/base/pallas_call | solution.py:62
  100.9 1.3 collective-permute-start.8
  102.3 1.6 collective-permute-start.12
  104.9 4.7 %base.11 = f32[256,512]{1,0:T(8,128)} custom-call(f32[256,2048]{1,0:T(8,128)} %base.7.refs_0_, bf16[128,3584]{1,0:T(8,128)(2,1)} %copy-done, bf16[128,3584]{1,0:T(8,128)(2,1)} %copy-done.1, bf16[7168,2048]{1,0:T(8,128)(2,1)} %refs_3_.13), custom_call_target="tpu_custom_call" | custom-call | flops 939524096 | bytes 6029312 | tf_op jit(solution)/shard_map/base/pallas_call | solution.py:62
  112.5 2.9 %spread.1.spread_ref = bf16[512,1024]{1,0:T(8,128)(2,1)} custom-call(s32[10]{0:T(128)} %stack.93.info_ref, f32[2,128,128]{2,1,0:T(8,128)} %bitcast.86, s32[4,128,128]{2,1,0:T(8,128)} %broadcast_in_dim.109.ids_ref), custom_call_target="tpu_custom_call" | custom-call | flops 2097152 | bytes 1572864 | tf_op jit(solution)/shard_map/spread/pallas_call | solution.py:187
  115.5 1.6 collective-permute-start.22
  118.1 4.1 %combine.4 = (f32[2,128,512]{2,1,0:T(8,128)}, bf16[2,128,512]{2,1,0:T(8,128)(2,1)}) custom-call(s32[10]{0:T(128)} %stack.93.info_ref, f32[2,128,2048]{2,1,0:T(8,128)} %bitcast.78, f32[2,128,512]{2,1,0:T(8,128)} %bitcast.85, bf16[512,1024]{1,0:T(8,128)(2,1)} %spread.1.spread_ref, bf16[256,8192]{1,0:T(8,128)(2,1)} %own_ref.7, bf16[256,2048]{1,0:T(8,128)(2,1)} %copy-done.2, ...), custom_call_target="tpu_custom_call" | custom-call | flops 536870912 | bytes 2752512 | tf_op jit(solution)/shard_map/combine/pallas_call | solution.py:239
  123.6 4.1 %combine.5 = (f32[2,128,512]{2,1,0:T(8,128)}, bf16[2,128,512]{2,1,0:T(8,128)(2,1)}) custom-call(s32[10]{0:T(128)} %stack.93.info_ref, f32[2,128,2048]{2,1,0:T(8,128)} %bitcast.79, f32[2,128,512]{2,1,0:T(8,128)} %bitcast.83, bf16[512,1024]{1,0:T(8,128)(2,1)} %spread.1.spread_ref, bf16[256,8192]{1,0:T(8,128)(2,1)} %own_ref.7, bf16[256,2048]{1,0:T(8,128)(2,1)} %copy-done.2, ...), custom_call_target="tpu_custom_call" | custom-call | flops 536870912 | bytes 2752512 | tf_op jit(solution)/shard_map/combine/pallas_call | solution.py:239
  127.8 1.6 collective-permute-start.18
  130.1 4.3 %combine.6 = (f32[2,128,512]{2,1,0:T(8,128)}, bf16[2,128,512]{2,1,0:T(8,128)(2,1)}) custom-call(s32[10]{0:T(128)} %stack.93.info_ref, f32[2,128,2048]{2,1,0:T(8,128)} %bitcast.80, f32[2,128,512]{2,1,0:T(8,128)} %bitcast.84, bf16[512,1024]{1,0:T(8,128)(2,1)} %spread.1.spread_ref, bf16[256,8192]{1,0:T(8,128)(2,1)} %own_ref.7, bf16[256,2048]{1,0:T(8,128)(2,1)} %copy-done.2, ...), custom_call_target="tpu_custom_call" | custom-call | flops 536870912 | bytes 2752512 | tf_op jit(solution)/shard_map/combine/pallas_call | solution.py:239
  136.8 2.0 %collective-permute-start.19 = (bf16[128,512]{1,0:T(8,128)(2,1)S(1)}, bf16[128,512]{1,0:T(8,128)(2,1)S(1)}, u32[]{:S(2)}, u32[]{:S(2)}) collective-permute-start(bf16[128,512]{1,0:T(8,128)(2,1)S(1)} %fusion.6), channel_id=1, source_target_pairs={{0,2},{1,3},{2,0},{3,1},{4,6},{5,7},{6,4},{7,5},{8,10},{9,11},{10,... | collective-permute-start | bytes 393224 | tf_op jit(solution)/shard_map/ppermute | solution.py:21
  138.8 8.3 %collective-permute-done.23 = bf16[2,128,512]{2,1,0:T(8,128)(2,1)S(1)} collective-permute-done((bf16[2,128,512]{2,1,0:T(8,128)(2,1)}, bf16[2,128,512]{2,1,0:T(8,128)(2,1)S(1)}, u32[]{:S(2)}, u32[]{:S(2)}) %collective-permute-start.23) | collective-permute-done | bytes 262176 | tf_op jit(solution)/shard_map/ppermute | solution.py:21
  148.3 4.1 %combine.7 = (f32[2,128,512]{2,1,0:T(8,128)}, bf16[2,128,512]{2,1,0:T(8,128)(2,1)}) custom-call(s32[10]{0:T(128)} %stack.93.info_ref, f32[2,128,2048]{2,1,0:T(8,128)} %bitcast.81, f32[2,128,512]{2,1,0:T(8,128)} %bitcast.82, bf16[512,1024]{1,0:T(8,128)(2,1)} %spread.1.spread_ref, bf16[256,8192]{1,0:T(8,128)(2,1)} %own_ref.7, bf16[256,2048]{1,0:T(8,128)(2,1)} %copy-done.2, ...), custom_call_target="tpu_custom_call" | custom-call | flops 536870912 | bytes 2752512 | tf_op jit(solution)/shard_map/combine/pallas_call | solution.py:239
  152.4 2.4 %collective-permute-start.28 = (bf16[2,128,512]{2,1,0:T(8,128)(2,1)}, bf16[2,128,512]{2,1,0:T(8,128)(2,1)S(1)}, u32[]{:S(2)}, u32[]{:S(2)}) collective-permute-start(bf16[2,128,512]{2,1,0:T(8,128)(2,1)} %get-tuple-element.58), channel_id=1, source_target_pairs={{0,1},{1,0},{2,3},{3,2},{4,5},{5,4},{6,7},{7,6},{8,9},{9,8},{10,11... | collective-permute-start | bytes 786440 | tf_op jit(solution)/shard_map/ppermute | solution.py:21
  154.9 6.4 %collective-permute-done.28 = bf16[2,128,512]{2,1,0:T(8,128)(2,1)S(1)} collective-permute-done((bf16[2,128,512]{2,1,0:T(8,128)(2,1)}, bf16[2,128,512]{2,1,0:T(8,128)(2,1)S(1)}, u32[]{:S(2)}, u32[]{:S(2)}) %collective-permute-start.28) | collective-permute-done | bytes 262176 | tf_op jit(solution)/shard_map/ppermute | solution.py:21
  163.9 7.0 %collective-permute-done.29 = bf16[128,512]{1,0:T(8,128)(2,1)S(1)} collective-permute-done((bf16[128,512]{1,0:T(8,128)(2,1)S(1)}, bf16[128,512]{1,0:T(8,128)(2,1)S(1)}, u32[]{:S(2)}, u32[]{:S(2)}) %collective-permute-start.29) | collective-permute-done | bytes 131104 | tf_op jit(solution)/shard_map/ppermute | solution.py:21
  (133 shorter events, 30.0 us)
Async XLA Ops:
  2.8 5.6 %collective-permute-start = (bf16[128,7168]{1,0:T(8,128)(2,1)}, bf16[128,7168]{1,0:T(8,128)(2,1)S(1)}, u32[]{:S(2)}, u32[]{:S(2)}) collective-permute-start(bf16[128,7168]{1,0:T(8,128)(2,1)} %refs_0_), channel_id=1, source_target_pairs={{0,4},{4,0},{8,12},{12,8},{1,5},{5,1},{9,13},{13,9},{2,6},{6,2},{1... | collective-permute-start | bytes 5505032 | tf_op jit(solution)/shard_map/ppermute | solution.py:21
  3.3 31.3 %collective-permute-start.1 = (bf16[128,3584]{1,0:T(8,128)(2,1)}, bf16[128,3584]{1,0:T(8,128)(2,1)S(1)}, u32[]{:S(2)}, u32[]{:S(2)}) collective-permute-start(bf16[128,3584]{1,0:T(8,128)(2,1)} %get-tuple-element.67), channel_id=1, source_target_pairs={{0,8},{4,12},{8,0},{12,4},{1,9},{5,13},{9,1},{13,5},{2,10},{6,14},... | collective-permute-start | bytes 2752520 | tf_op jit(solution)/shard_map/ppermute | solution.py:21
  34.6 2.5 %collective-permute-start.2 = (bf16[128,3584]{1,0:T(8,128)(2,1)S(1)}, bf16[128,3584]{1,0:T(8,128)(2,1)S(1)}, u32[]{:S(2)}, u32[]{:S(2)}) collective-permute-start(bf16[128,3584]{1,0:T(8,128)(2,1)S(1)} %collective-permute-done.1.refs_1_.refs_0_), channel_id=1, source_target_pairs={{0,4},{4,0},{8,12},{12,8},{1,5},{5,1},{9,13},{13,9},{2,6},{6,2},{1... | collective-permute-start | bytes 2752520 | tf_op jit(solution)/shard_map/ppermute | solution.py:21
  34.9 22.8 %collective-permute-start.3 = (bf16[128,3584]{1,0:T(8,128)(2,1)}, bf16[128,3584]{1,0:T(8,128)(2,1)S(1)}, u32[]{:S(2)}, u32[]{:S(2)}) collective-permute-start(bf16[128,3584]{1,0:T(8,128)(2,1)} %get-tuple-element.32), channel_id=1, source_target_pairs={{0,8},{4,12},{8,0},{12,4},{1,9},{5,13},{9,1},{13,5},{2,10},{6,14},... | collective-permute-start | bytes 2752520 | tf_op jit(solution)/shard_map/ppermute | solution.py:21
  57.6 14.9 %copy-start = (bf16[128,3584]{1,0:T(8,128)(2,1)}, bf16[128,3584]{1,0:T(8,128)(2,1)S(1)}, u32[]{:S(2)}) copy-start(bf16[128,3584]{1,0:T(8,128)(2,1)S(1)} %collective-permute-done.3.refs_1_) | copy-start | bytes 2752516
  57.6 14.9 %collective-permute-start.4 = (bf16[128,3584]{1,0:T(8,128)(2,1)S(1)}, bf16[128,3584]{1,0:T(8,128)(2,1)S(1)}, u32[]{:S(2)}, u32[]{:S(2)}) collective-permute-start(bf16[128,3584]{1,0:T(8,128)(2,1)S(1)} %collective-permute-done.3.refs_1_), channel_id=1, source_target_pairs={{0,4},{4,0},{8,12},{12,8},{1,5},{5,1},{9,13},{13,9},{2,6},{6,2},{1... | collective-permute-start | bytes 2752520 | tf_op jit(solution)/shard_map/ppermute | solution.py:21
  60.3 56.8 %collective-permute-start.9 = (bf16[256,2048]{1,0:T(8,128)(2,1)}, bf16[256,2048]{1,0:T(8,128)(2,1)S(1)}, u32[]{:S(2)}, u32[]{:S(2)}) collective-permute-start(bf16[256,2048]{1,0:T(8,128)(2,1)} %constant_dynamic-slice_fusion), channel_id=1, source_target_pairs={{0,4},{4,0},{8,12},{12,8},{1,5},{5,1},{9,13},{13,9},{2,6},{6,2},{1... | collective-permute-start | bytes 3145736 | tf_op jit(solution)/shard_map/ppermute | solution.py:21
  62.6 32.4 %collective-permute-start.15 = (bf16[2,128,512]{2,1,0:T(8,128)(2,1)}, bf16[2,128,512]{2,1,0:T(8,128)(2,1)}, u32[]{:S(2)}, u32[]{:S(2)}) collective-permute-start(bf16[2,128,512]{2,1,0:T(8,128)(2,1)} %pad_maximum_fusion.3), channel_id=1, source_target_pairs={{0,8},{4,12},{8,0},{12,4},{1,9},{5,13},{9,1},{13,5},{2,10},{6,14},... | collective-permute-start | bytes 786440 | tf_op jit(solution)/shard_map/ppermute | solution.py:21
  64.1 39.8 %collective-permute-start.20 = (bf16[2,128,512]{2,1,0:T(8,128)(2,1)}, bf16[2,128,512]{2,1,0:T(8,128)(2,1)}, u32[]{:S(2)}, u32[]{:S(2)}) collective-permute-start(bf16[2,128,512]{2,1,0:T(8,128)(2,1)} %pad_maximum_fusion.5), channel_id=1, source_target_pairs={{0,8},{4,12},{8,0},{12,4},{1,9},{5,13},{9,1},{13,5},{2,10},{6,14},... | collective-permute-start | bytes 786440 | tf_op jit(solution)/shard_map/ppermute | solution.py:21
  71.7 17.9 %collective-permute-start.10 = (bf16[2,128,512]{2,1,0:T(8,128)(2,1)S(1)}, bf16[2,128,512]{2,1,0:T(8,128)(2,1)S(1)}, u32[]{:S(2)}, u32[]{:S(2)}) collective-permute-start(bf16[2,128,512]{2,1,0:T(8,128)(2,1)S(1)} %pad_maximum_fusion.1), channel_id=1, source_target_pairs={{0,8},{4,12},{8,0},{12,4},{1,9},{5,13},{9,1},{13,5},{2,10},{6,14},... | collective-permute-start | bytes 786440 | tf_op jit(solution)/shard_map/ppermute | solution.py:21
  80.5 6.4 %collective-permute-start.5 = (bf16[256,128]{1,0:T(8,128)(2,1)S(1)}, bf16[256,128]{1,0:T(8,128)(2,1)S(1)}, u32[]{:S(2)}, u32[]{:S(2)}) collective-permute-start(bf16[256,128]{1,0:T(8,128)(2,1)S(1)} %bitcast_convert_fusion), channel_id=1, source_target_pairs={{0,1},{1,0},{2,3},{3,2},{4,5},{5,4},{6,7},{7,6},{8,9},{9,8},{10,11... | collective-permute-start | bytes 196616 | tf_op jit(solution)/shard_map/ppermute | solution.py:21
  86.9 7.5 %collective-permute-start.6 = (bf16[256,128]{1,0:T(8,128)(2,1)S(1)}, bf16[256,128]{1,0:T(8,128)(2,1)S(1)}, u32[]{:S(2)}, u32[]{:S(2)}) collective-permute-start(bf16[256,128]{1,0:T(8,128)(2,1)S(1)} %fusion.11), channel_id=1, source_target_pairs={{0,2},{1,3},{2,0},{3,1},{4,6},{5,7},{6,4},{7,5},{8,10},{9,11},{10,... | collective-permute-start | bytes 196616 | tf_op jit(solution)/shard_map/ppermute | solution.py:21
  89.6 12.7 %collective-permute-start.11 = (bf16[128,512]{1,0:T(8,128)(2,1)S(1)}, bf16[128,512]{1,0:T(8,128)(2,1)S(1)}, u32[]{:S(2)}, u32[]{:S(2)}) collective-permute-start(bf16[128,512]{1,0:T(8,128)(2,1)S(1)} %get-tuple-element.70), channel_id=1, source_target_pairs={{0,4},{4,0},{8,12},{12,8},{1,5},{5,1},{9,13},{13,9},{2,6},{6,2},{1... | collective-permute-start | bytes 393224 | tf_op jit(solution)/shard_map/ppermute | solution.py:21
  94.4 6.4 %collective-permute-start.7 = (bf16[256,128]{1,0:T(8,128)(2,1)S(1)}, bf16[256,128]{1,0:T(8,128)(2,1)S(1)}, u32[]{:S(2)}, u32[]{:S(2)}) collective-permute-start(bf16[256,128]{1,0:T(8,128)(2,1)S(1)} %fusion.9), channel_id=1, source_target_pairs={{0,4},{4,0},{8,12},{12,8},{1,5},{5,1},{9,13},{13,9},{2,6},{6,2},{1... | collective-permute-start | bytes 196616 | tf_op jit(solution)/shard_map/ppermute | solution.py:21
  96.0 15.1 %collective-permute-start.16 = (bf16[128,512]{1,0:T(8,128)(2,1)S(1)}, bf16[128,512]{1,0:T(8,128)(2,1)S(1)}, u32[]{:S(2)}, u32[]{:S(2)}) collective-permute-start(bf16[128,512]{1,0:T(8,128)(2,1)S(1)} %get-tuple-element.72), channel_id=1, source_target_pairs={{0,4},{4,0},{8,12},{12,8},{1,5},{5,1},{9,13},{13,9},{2,6},{6,2},{1... | collective-permute-start | bytes 393224 | tf_op jit(solution)/shard_map/ppermute | solution.py:21
  100.9 8.7 %collective-permute-start.8 = (bf16[256,128]{1,0:T(8,128)(2,1)S(1)}, bf16[256,128]{1,0:T(8,128)(2,1)S(1)}, u32[]{:S(2)}, u32[]{:S(2)}) collective-permute-start(bf16[256,128]{1,0:T(8,128)(2,1)S(1)} %fusion.10), channel_id=1, source_target_pairs={{0,8},{4,12},{8,0},{12,4},{1,9},{5,13},{9,1},{13,5},{2,10},{6,14},... | collective-permute-start | bytes 196616 | tf_op jit(solution)/shard_map/ppermute | solution.py:21
  102.3 14.8 %collective-permute-start.12 = (bf16[2,128,512]{2,1,0:T(8,128)(2,1)S(1)}, bf16[2,128,512]{2,1,0:T(8,128)(2,1)S(1)}, u32[]{:S(2)}, u32[]{:S(2)}) collective-permute-start(bf16[2,128,512]{2,1,0:T(8,128)(2,1)S(1)} %pad_maximum_fusion.2.mine_ref), channel_id=1, source_target_pairs={{0,16},{16,0},{1,17},{17,1},{2,18},{18,2},{3,19},{19,3},{4,20},{20... | collective-permute-start | bytes 786440 | tf_op jit(solution)/shard_map/ppermute | solution.py:21
  104.8 10.6 %collective-permute-start.21 = (bf16[128,512]{1,0:T(8,128)(2,1)S(1)}, bf16[128,512]{1,0:T(8,128)(2,1)S(1)}, u32[]{:S(2)}, u32[]{:S(2)}) collective-permute-start(bf16[128,512]{1,0:T(8,128)(2,1)S(1)} %get-tuple-element.74), channel_id=1, source_target_pairs={{0,4},{4,0},{8,12},{12,8},{1,5},{5,1},{9,13},{13,9},{2,6},{6,2},{1... | collective-permute-start | bytes 393224 | tf_op jit(solution)/shard_map/ppermute | solution.py:21
  109.6 13.2 %collective-permute-start.25 = (bf16[2,128,512]{2,1,0:T(8,128)(2,1)S(1)}, bf16[2,128,512]{2,1,0:T(8,128)(2,1)S(1)}, u32[]{:S(2)}, u32[]{:S(2)}) collective-permute-start(bf16[2,128,512]{2,1,0:T(8,128)(2,1)S(1)} %pad_maximum_fusion.7), channel_id=1, source_target_pairs={{0,8},{4,12},{8,0},{12,4},{1,9},{5,13},{9,1},{13,5},{2,10},{6,14},... | collective-permute-start | bytes 786440 | tf_op jit(solution)/shard_map/ppermute | solution.py:21
  111.1 11.8 %collective-permute-start.17 = (bf16[2,128,512]{2,1,0:T(8,128)(2,1)S(1)}, bf16[2,128,512]{2,1,0:T(8,128)(2,1)S(1)}, u32[]{:S(2)}, u32[]{:S(2)}) collective-permute-start(bf16[2,128,512]{2,1,0:T(8,128)(2,1)S(1)} %pad_maximum_fusion.4.mine_ref), channel_id=1, source_target_pairs={{0,16},{16,0},{1,17},{17,1},{2,18},{18,2},{3,19},{19,3},{4,20},{20... | collective-permute-start | bytes 786440 | tf_op jit(solution)/shard_map/ppermute | solution.py:21
  115.5 13.9 %copy-start.8 = (bf16[2,128,512]{2,1,0:T(8,128)(2,1)}, bf16[2,128,512]{2,1,0:T(8,128)(2,1)S(1)}, u32[]{:S(2)}) copy-start(bf16[2,128,512]{2,1,0:T(8,128)(2,1)S(1)} %pad_maximum_fusion.6.mine_ref) | copy-start | bytes 786436
  115.5 13.9 %collective-permute-start.22 = (bf16[2,128,512]{2,1,0:T(8,128)(2,1)S(1)}, bf16[2,128,512]{2,1,0:T(8,128)(2,1)S(1)}, u32[]{:S(2)}, u32[]{:S(2)}) collective-permute-start(bf16[2,128,512]{2,1,0:T(8,128)(2,1)S(1)} %pad_maximum_fusion.6.mine_ref), channel_id=1, source_target_pairs={{0,16},{16,0},{1,17},{17,1},{2,18},{18,2},{3,19},{19,3},{4,20},{20... | collective-permute-start | bytes 786440 | tf_op jit(solution)/shard_map/ppermute | solution.py:21
  122.3 13.2 %collective-permute-start.13 = (bf16[2,128,512]{2,1,0:T(8,128)(2,1)}, bf16[2,128,512]{2,1,0:T(8,128)(2,1)S(1)}, u32[]{:S(2)}, u32[]{:S(2)}) collective-permute-start(bf16[2,128,512]{2,1,0:T(8,128)(2,1)} %get-tuple-element.49), channel_id=1, source_target_pairs={{0,1},{1,0},{2,3},{3,2},{4,5},{5,4},{6,7},{7,6},{8,9},{9,8},{10,11... | collective-permute-start | bytes 786440 | tf_op jit(solution)/shard_map/ppermute | solution.py:21
  122.8 12.1 %collective-permute-start.26 = (bf16[128,512]{1,0:T(8,128)(2,1)S(1)}, bf16[128,512]{1,0:T(8,128)(2,1)S(1)}, u32[]{:S(2)}, u32[]{:S(2)}) collective-permute-start(bf16[128,512]{1,0:T(8,128)(2,1)S(1)} %get-tuple-element.76), channel_id=1, source_target_pairs={{0,4},{4,0},{8,12},{12,8},{1,5},{5,1},{9,13},{13,9},{2,6},{6,2},{1... | collective-permute-start | bytes 393224 | tf_op jit(solution)/shard_map/ppermute | solution.py:21
  127.8 8.9 %collective-permute-start.18 = (bf16[2,128,512]{2,1,0:T(8,128)(2,1)}, bf16[2,128,512]{2,1,0:T(8,128)(2,1)S(1)}, u32[]{:S(2)}, u32[]{:S(2)}) collective-permute-start(bf16[2,128,512]{2,1,0:T(8,128)(2,1)} %get-tuple-element.52), channel_id=1, source_target_pairs={{0,1},{1,0},{2,3},{3,2},{4,5},{5,4},{6,7},{7,6},{8,9},{9,8},{10,11... | collective-permute-start | bytes 786440 | tf_op jit(solution)/shard_map/ppermute | solution.py:21
  134.4 12.8 %collective-permute-start.23 = (bf16[2,128,512]{2,1,0:T(8,128)(2,1)}, bf16[2,128,512]{2,1,0:T(8,128)(2,1)S(1)}, u32[]{:S(2)}, u32[]{:S(2)}) collective-permute-start(bf16[2,128,512]{2,1,0:T(8,128)(2,1)} %get-tuple-element.55), channel_id=1, source_target_pairs={{0,1},{1,0},{2,3},{3,2},{4,5},{5,4},{6,7},{7,6},{8,9},{9,8},{10,11... | collective-permute-start | bytes 786440 | tf_op jit(solution)/shard_map/ppermute | solution.py:21
  134.9 12.6 %collective-permute-start.27 = (bf16[2,128,512]{2,1,0:T(8,128)(2,1)S(1)}, bf16[2,128,512]{2,1,0:T(8,128)(2,1)S(1)}, u32[]{:S(2)}, u32[]{:S(2)}) collective-permute-start(bf16[2,128,512]{2,1,0:T(8,128)(2,1)S(1)} %pad_maximum_fusion.8.mine_ref), channel_id=1, source_target_pairs={{0,16},{16,0},{1,17},{17,1},{2,18},{18,2},{3,19},{19,3},{4,20},{20... | collective-permute-start | bytes 786440 | tf_op jit(solution)/shard_map/ppermute | solution.py:21
  135.6 19.2 %collective-permute-start.14 = (bf16[128,512]{1,0:T(8,128)(2,1)S(1)}, bf16[128,512]{1,0:T(8,128)(2,1)S(1)}, u32[]{:S(2)}, u32[]{:S(2)}) collective-permute-start(bf16[128,512]{1,0:T(8,128)(2,1)S(1)} %fusion.5), channel_id=1, source_target_pairs={{0,2},{1,3},{2,0},{3,1},{4,6},{5,7},{6,4},{7,5},{8,10},{9,11},{10,... | collective-permute-start | bytes 393224 | tf_op jit(solution)/shard_map/ppermute | solution.py:21
  136.8 18.1 %collective-permute-start.19 = (bf16[128,512]{1,0:T(8,128)(2,1)S(1)}, bf16[128,512]{1,0:T(8,128)(2,1)S(1)}, u32[]{:S(2)}, u32[]{:S(2)}) collective-permute-start(bf16[128,512]{1,0:T(8,128)(2,1)S(1)} %fusion.6), channel_id=1, source_target_pairs={{0,2},{1,3},{2,0},{3,1},{4,6},{5,7},{6,4},{7,5},{8,10},{9,11},{10,... | collective-permute-start | bytes 393224 | tf_op jit(solution)/shard_map/ppermute | solution.py:21
  147.3 16.6 %collective-permute-start.24 = (bf16[128,512]{1,0:T(8,128)(2,1)S(1)}, bf16[128,512]{1,0:T(8,128)(2,1)S(1)}, u32[]{:S(2)}, u32[]{:S(2)}) collective-permute-start(bf16[128,512]{1,0:T(8,128)(2,1)S(1)} %fusion.7), channel_id=1, source_target_pairs={{0,2},{1,3},{2,0},{3,1},{4,6},{5,7},{6,4},{7,5},{8,10},{9,11},{10,... | collective-permute-start | bytes 393224 | tf_op jit(solution)/shard_map/ppermute | solution.py:21
  152.4 8.9 %collective-permute-start.28 = (bf16[2,128,512]{2,1,0:T(8,128)(2,1)}, bf16[2,128,512]{2,1,0:T(8,128)(2,1)S(1)}, u32[]{:S(2)}, u32[]{:S(2)}) collective-permute-start(bf16[2,128,512]{2,1,0:T(8,128)(2,1)} %get-tuple-element.58), channel_id=1, source_target_pairs={{0,1},{1,0},{2,3},{3,2},{4,5},{5,4},{6,7},{7,6},{8,9},{9,8},{10,11... | collective-permute-start | bytes 786440 | tf_op jit(solution)/shard_map/ppermute | solution.py:21
  162.5 8.4 %collective-permute-start.29 = (bf16[128,512]{1,0:T(8,128)(2,1)S(1)}, bf16[128,512]{1,0:T(8,128)(2,1)S(1)}, u32[]{:S(2)}, u32[]{:S(2)}) collective-permute-start(bf16[128,512]{1,0:T(8,128)(2,1)S(1)} %fusion.8), channel_id=1, source_target_pairs={{0,2},{1,3},{2,0},{3,1},{4,6},{5,7},{6,4},{7,5},{8,10},{9,11},{10,... | collective-permute-start | bytes 393224 | tf_op jit(solution)/shard_map/ppermute | solution.py:21
  (18 other events, 81.1 us)

commit v3 on v2

v3 whole, which is shorter than its diff:
```python
import jax
import jax.numpy as jnp
from jax import lax
from jax.experimental import pallas as pl
from jax.experimental.pallas import tpu as pltpu
from jax.sharding import PartitionSpec as P

F32 = jnp.float32
BF16 = jnp.bfloat16
VMEM_LIMIT = 40 * 1024 * 1024
WIDTHS = (512, 512, 512, 512)
CAP = 4
HALVES = 2
HINT = 1000


def partners(count, step):
    return [(i, i ^ step) for i in range(count)]


def swap(values, axis, step):
    return lax.ppermute(values, axis, partners(lax.axis_size(axis), step))


def tie(values, *after):
    return lax.optimization_barrier((values, *after))[0]


def cost(flops, moved):
    return pl.CostEstimate(flops=flops // HINT, bytes_accessed=moved // HINT, transcendentals=0)


def params():
    return pltpu.CompilerParams(vmem_limit_bytes=VMEM_LIMIT)


def base_kernel(count, has_prior, *refs):
    a_ref, pieces, refs = refs[0], refs[1 : 1 + count], refs[1 + count :]
    if has_prior:
        prior_ref, refs = refs[0], refs[1:]
    w_ref, out_ref, rows = refs

    @pl.when(pl.program_id(0) == 0)
    def _():
        half = a_ref.shape[0]
        rows[:half, :] = a_ref[...]
        start = 0
        for piece in pieces:
            rows[half:, start : start + piece.shape[1]] = piece[...]
            start += piece.shape[1]

    value = jnp.dot(rows[...], w_ref[...], preferred_element_type=F32)
    if has_prior:
        value += prior_ref[...]
    out_ref[...] = value


def base_product(a, pieces, weight, depth_block=0, prior=None, first=0, width=None, tile=512):
    rows, depth = a.shape
    width = weight.shape[1] if width is None else width
    in_specs = [pl.BlockSpec(x.shape, lambda n: (0, 0)) for x in (a, *pieces)]
    args = [a, *pieces]
    if prior is not None:
        in_specs.append(pl.BlockSpec((2 * rows, tile), lambda n: (0, first // tile + n)))
        args.append(prior)
    in_specs.append(pl.BlockSpec((depth, tile), lambda n: (depth_block, first // tile + n)))
    args.append(weight)
    return pl.pallas_call(
        lambda *refs: base_kernel(len(pieces), prior is not None, *refs),
        grid=(width // tile,),
        in_specs=in_specs,
        out_specs=pl.BlockSpec((2 * rows, tile), lambda n: (0, n)),
        out_shape=jax.ShapeDtypeStruct((2 * rows, width), F32),
        scratch_shapes=[pltpu.VMEM((2 * rows, depth), BF16)],
        compiler_params=params(),
        cost_estimate=cost(
            4 * rows * depth * width, 2 * depth * (width + 2 * rows) + 8 * rows * width
        ),
        name="base",
    )(*args)


def scores_kernel(first, offset, count, has_prior, last, info_ref, *refs):
    a_ref, pieces, maps_ref = refs[0], refs[1 : 1 + count], refs[1 + count]
    refs = refs[2 + count :]
    if has_prior:
        prior_ref, refs = refs[0], refs[1:]
    if first == 2 and last:
        near_ref, refs = refs[0], refs[1:]
    if last:
        ids_ref, refs = refs[0], refs[1:]
    outs, (rows, maps, row_sems, map_sems) = refs[:-4], refs[-4:]
    depth = rows.shape[2]
    cut = depth // 2

    def map_copy(pair, k, part):
        chosen = info_ref[1 + (first + pair) * CAP + k]
        return pltpu.make_async_copy(
            maps_ref.at[chosen, :, pl.ds(offset + part * cut, cut)],
            maps.at[pair * CAP + k, :, pl.ds(part * cut, cut)],
            map_sems.at[pair, k, part],
        )

    row_copies = [pltpu.make_async_copy(a_ref, rows.at[0], row_sems.at[0])]
    start = 0
    for index, piece in enumerate(pieces):
        row_copies.append(
            pltpu.make_async_copy(
                piece, rows.at[1, :, pl.ds(start, piece.shape[1])], row_sems.at[1 + index]
            )
        )
        start += piece.shape[1]
    for pair in range(2):
        for copy in row_copies[:1] if pair == 0 else row_copies[1:]:
            copy.start()
        for part in range(2):
            for k in range(CAP):
                map_copy(pair, k, part).start()
    for pair in range(2):
        for copy in row_copies[:1] if pair == 0 else row_copies[1:]:
            copy.wait()
        total = prior_ref[pair] if has_prior else None
        for part in range(2):
            for k in range(CAP):
                map_copy(pair, k, part).wait()
            columns = slice(part * cut, (part + 1) * cut)
            chosen = maps[pair * CAP : (pair + 1) * CAP, :, columns]
            term = lax.dot_general(
                chosen.reshape(-1, cut),
                rows[pair, :, columns],
                (((1,), (1,)), ((), ())),
                preferred_element_type=F32,
            )
            total = term if total is None else total + term
        if not last:
            outs[0][pair] = total
            continue
        wanted = ids_ref[pair]
        rank = total.shape[0] // CAP
        found = jnp.zeros((rank, total.shape[1]), F32)
        for k in range(CAP):
            mine = info_ref[1 + (first + pair) * CAP + k]
            found += jnp.where(wanted == mine, total[k * rank : (k + 1) * rank], 0.0)
        if first == 0:
            outs[0][pair] = found
        else:
            near_group = info_ref[0] ^ pair
            far_group = near_group ^ 2
            outs[0][far_group] = found
            outs[1][far_group] = found.astype(BF16)
            outs[0][near_group] = near_ref[pair]
            outs[1][near_group] = near_ref[pair].astype(BF16)


def scores(info, first, a, pieces, maps, half, prior=None, near=None, ids=None):
    rows, depth = a.shape
    rank = maps.shape[1]
    has_prior, last = prior is not None, ids is not None
    whole = lambda x: pl.BlockSpec(x.shape, lambda k, s: (0,) * x.ndim)
    args = [a, *pieces, maps]
    in_specs = [pl.BlockSpec(memory_space=pl.ANY)] * len(args)
    if has_prior:
        in_specs.append(whole(prior))
        args.append(prior)
    if near is not None:
        in_specs.append(whole(near))
        args.append(near)
    if last:
        in_specs.append(
            pl.BlockSpec((2,) + ids.shape[1:], lambda k, s: (first // 2, 0, 0))
        )
        args.append(ids)
    if not last:
        out_shape = [jax.ShapeDtypeStruct((2, CAP * rank, rows), F32)]
    elif first == 0:
        out_shape = [jax.ShapeDtypeStruct((2, rank, rows), F32)]
    else:
        out_shape = [jax.ShapeDtypeStruct((4, rank, rows), kind) for kind in (F32, BF16)]
    return pl.pallas_call(
        lambda *refs: scores_kernel(first, half * depth, len(pieces), has_prior, last, *refs),
        grid_spec=pltpu.PrefetchScalarGridSpec(
            num_scalar_prefetch=1,
            grid=(1,),
            in_specs=in_specs,
            out_specs=[whole(x) for x in out_shape],
            scratch_shapes=[
                pltpu.VMEM((2, rows, depth), BF16),
                pltpu.VMEM((2 * CAP, rank, depth), BF16),
                pltpu.SemaphoreType.DMA((1 + len(pieces),)),
                pltpu.SemaphoreType.DMA((2, CAP, 2)),
            ],
        ),
        out_shape=out_shape,
        compiler_params=params(),
        cost_estimate=cost(4 * rows * depth * CAP * rank, 4 * depth * (CAP * rank + rows)),
        name="scores",
    )(info, *args)


def build_spread(info_ref, lowrank_ref, got_ref, ids_ref, spread):
    rows, lanes = ids_ref.shape[1], ids_ref.shape[2]
    parity, place = info_ref[0], info_ref[1]
    upper = (lax.broadcasted_iota(jnp.int32, (rows, lanes), 1) >= lanes // 2).astype(jnp.int32)
    for slot in range(4):
        local = ((slot // 2) ^ parity) + 2 * (slot % 2)
        group = place ^ local
        values = lowrank_ref[group] + got_ref[group].astype(F32)
        values = jnp.concatenate([values, values], axis=0).T
        wanted = ids_ref[local] - upper
        for piece in range(8):
            spread[slot * rows : (slot + 1) * rows, piece * lanes : (piece + 1) * lanes] = (
                jnp.where(wanted == info_ref[2 + piece], values, 0.0).astype(BF16)
            )


def combine_kernel(build, info_ref, *refs):
    if build:
        lowrank_ref, got_ref, ids_ref, refs = refs[0], refs[1], refs[2], refs[3:]
        near_ref, far_ref, own_ref, core_ref, *blocks, keep_ref, send_ref, spread_ref, maps = refs

        @pl.when(pl.program_id(0) == 0)
        def _():
            build_spread(info_ref, lowrank_ref, got_ref, ids_ref, spread_ref)

    else:
        spread_ref, near_ref, far_ref, own_ref, core_ref, *blocks, keep_ref, send_ref, maps = refs
    parity = info_ref[0]
    rows = near_ref.shape[1]
    held = own_ref.shape[0]
    maps[0:held, :] = own_ref[...]
    maps[held : 2 * held, :] = core_ref[...]
    start = 2 * held
    for ref in blocks:
        maps[start : start + held // 2, :] = ref[0]
        start += held // 2
    delta = jnp.dot(spread_ref[...], maps[...], preferred_element_type=F32)
    for slot in range(4):
        source = near_ref if slot % 2 == 0 else far_ref
        value = source[(slot // 2) ^ parity] + delta[slot * rows : (slot + 1) * rows]
        if slot < 2:
            keep_ref[slot % 2] = value
        else:
            send_ref[slot % 2] = value.astype(BF16)


def combine(info, near, far, own_maps, core_maps, blocks, start, spread=None, build=()):
    rows = near.shape[1]
    width = far.shape[2]
    tile = 512
    first = start // tile
    per_place = core_maps.shape[1] // tile
    held = own_maps.shape[0]
    whole = lambda shape: pl.BlockSpec(shape, lambda n, s: (0,) * len(shape))
    ahead = list(build) if build else [spread]
    spread_shape = (4 * rows, 4 * held)
    in_specs = [whole(x.shape) for x in ahead]
    in_specs += [
        pl.BlockSpec((2, rows, tile), lambda n, s: (0, 0, first + n)),
        pl.BlockSpec((2, rows, tile), lambda n, s: (0, 0, n)),
        pl.BlockSpec((held, tile), lambda n, s: (0, s[1] * per_place + first + n)),
        pl.BlockSpec((held, tile), lambda n, s: (0, first + n)),
    ]
    in_specs += [
        pl.BlockSpec((1, held // 2, tile), lambda n, s, index=index: (index, 0, n))
        for _, index in blocks
    ]
    out_specs = [pl.BlockSpec((2, rows, tile), lambda n, s: (0, 0, n))] * 2
    out_shape = [jax.ShapeDtypeStruct((2, rows, width), kind) for kind in (F32, BF16)]
    if build:
        out_specs.append(whole(spread_shape))
        out_shape.append(jax.ShapeDtypeStruct(spread_shape, BF16))
    return pl.pallas_call(
        lambda *refs: combine_kernel(bool(build), *refs),
        grid_spec=pltpu.PrefetchScalarGridSpec(
            num_scalar_prefetch=1,
            grid=(width // tile,),
            in_specs=in_specs,
            out_specs=out_specs,
            scratch_shapes=[pltpu.VMEM((4 * held, tile), BF16)],
        ),
        out_shape=out_shape,
        compiler_params=params(),
        cost_estimate=cost(
            32 * rows * held * width, 26 * rows * width + 8 * held * width
        ),
        name="combine",
    )(info, *ahead, near, far, own_maps, core_maps, *[block for block, _ in blocks])


def per_device_fast(hidden, weight, input_maps, output_maps, slots, lists):
    rows, depth = hidden.shape
    place = lax.axis_index("pool")
    t = lax.axis_index("tensor")
    y = lax.axis_index("groups")
    holding, rank = input_maps.shape[:2]
    held, features = output_maps.shape
    width = features // 4
    chip, core = place >> 1, place & 1
    starts = [sum(WIDTHS[:i]) for i in range(len(WIDTHS))]
    count = len(WIDTHS)

    part = depth // HALVES
    crossed = [swap(hidden[:, h * part : (h + 1) * part], "pool", 2) for h in range(HALVES)]
    near_b = swap(hidden, "pool", 1)

    core_block = lax.dynamic_slice(output_maps, (0, (place ^ 1) * width), (held, width))
    blocks = [
        jnp.stack(
            [
                lax.dynamic_slice(
                    output_maps,
                    (y * (held // 2), (place ^ other) * width + start),
                    (held // 2, wide),
                )
                for other in (2, 3)
            ]
        )
        for start, wide in zip(starts, WIDTHS)
    ]

    order = place ^ jnp.arange(4, dtype=jnp.int32)
    hot = order[:, None] == jnp.arange(4, dtype=jnp.int32)[None, :]
    slots_local = jnp.sum(jnp.where(hot[:, :, None], slots.reshape(1, 4, rows), 0), axis=1)
    lists_local = jnp.sum(jnp.where(hot[:, :, None], lists[None, :, :], 0), axis=1)
    positions = jnp.arange(lists.shape[1], dtype=jnp.int32)
    ids = jnp.sum(
        jnp.where(slots_local[:, :, None] == positions, lists_local[:, None, :], 0), axis=2
    )
    wide_ids = jnp.broadcast_to(ids[:, :, None], (4, rows, 128))
    owned_ids = (ids - place * holding).reshape(4, 1, rows)
    owned = (lists_local >= place * holding) & (lists_local < (place + 1) * holding)
    earlier = positions[None, :] < positions[:, None]
    rank_in_list = jnp.sum(owned[:, None, :] & earlier[None], axis=2)
    caps = jnp.arange(CAP, dtype=jnp.int32)
    chosen = jnp.sum(
        jnp.where(
            owned[:, None, :] & (rank_in_list[:, None, :] == caps[None, :, None]),
            (lists_local - place * holding)[:, None, :],
            0,
        ),
        axis=2,
    ).reshape(4 * CAP)
    picks = jnp.concatenate([place.reshape(1), chosen]).astype(jnp.int32)

    parity = (place ^ t) & 1
    per_owner = held // rank
    half_step = per_owner // 2
    owner_first = [holding * (place ^ j) + per_owner * t for j in range(4)]
    info = jnp.stack(
        [parity, place]
        + [owner_first[j] + half_step * h for j in (0, 1) for h in (0, 1)]
        + [owner_first[2] + half_step * y, owner_first[3] + half_step * y]
        + [owner_first[2] + half_step * (1 - y), owner_first[3] + half_step * (1 - y)]
    ).astype(jnp.int32)

    ready = lax.optimization_barrier(
        (hidden, near_b, picks, info, wide_ids, owned_ids, core_block, *blocks)
    )
    own_rows, near_b, picks, info, wide_ids, owned_ids, core_block, *blocks = ready
    core_maps = swap(core_block, "pool", 1)

    (near_lowrank,) = scores(picks, 0, own_rows, [near_b], input_maps, 0, ids=owned_ids)
    near_base = base_product(tie(own_rows, near_lowrank), [near_b], weight)
    crossing = [swap(block, "pool", 2) for block in blocks[: count - 1]]

    a0 = tie(crossed[0], near_base)
    b0 = [swap(a0[:, k * (part // 2) : (k + 1) * (part // 2)], "pool", 1) for k in range(2)]
    (raw,) = scores(picks, 2, a0, b0, input_maps, 0)
    far_base = base_product(tie(a0, raw), b0, weight, 0)
    a1 = tie(crossed[1], far_base)
    b1 = [swap(a1, "pool", 1)]
    total, sent = scores(
        picks, 2, a1, b1, input_maps, 1, prior=raw, near=near_lowrank, ids=owned_ids
    )

    def far_piece(index, after):
        return base_product(
            tie(a1, after), b1, weight, 1, far_base, starts[index], WIDTHS[index], 256
        ).reshape(2, rows, WIDTHS[index])

    hops = (("tensor", 1), ("tensor", 2), ("pool", 1), ("pool", 2))
    pieces = []
    for index, (axis, step) in enumerate(hops):
        if index > 0:
            sent = total.astype(BF16)
        got = swap(sent, axis, step)
        if index < count - 1:
            crossing[index] = tie(crossing[index], sent)
            got = tie(got, crossing[index])
        if index == 1:
            pieces.append(far_piece(0, sent))
            got = tie(got, pieces[-1])
        if index == 3:
            crossing.append(swap(tie(blocks[-1], sent), "pool", 2))
            break
        total = total + got.astype(F32)

    def over_y(index, after):
        block = crossing[index] if after is None else tie(crossing[index], after)
        return block, swap(block, "pool", 1), swap(block, "groups", 1)

    def blocks_of(index, after):
        block, beside, across = moved[index]
        across = across if after is None else tie(across, after)
        return [(block, 0), (beside, 1), (across, 0), (swap(across, "pool", 1), 1)]

    moved = [over_y(index, None) for index in range(count - 1)]

    near_base = near_base.reshape(2, rows, width)
    side = ((place ^ t) >> 1) & 1
    parts = []
    spread = send = None
    for chunk in range(count):
        common = (
            info, near_base, pieces[chunk], output_maps, core_maps,
            blocks_of(chunk, send if chunk else None), starts[chunk],
        )
        if chunk == 0:
            keep, send, spread = combine(*common, build=(total, got, wide_ids))
            moved.append(over_y(count - 1, send))
        else:
            keep, send = combine(*common, spread=spread)
        if chunk + 1 < count:
            pieces.append(far_piece(chunk + 1, send))
        pair = keep + swap(send, "tensor", 1).astype(F32)
        sent = jnp.where(side == 0, pair[1], pair[0]).astype(BF16)
        kept = jnp.where(side == 0, pair[0], pair[1])
        parts.append(kept + swap(sent, "tensor", 2).astype(F32))
    return jnp.concatenate(parts, axis=1).astype(BF16)


def per_device_general(hidden, weight, input_maps, output_maps, slots, lists):
    rows, depth = hidden.shape
    pool_count = lax.axis_size("pool")
    tensor_count = lax.axis_size("tensor")
    place = lax.axis_index("pool")
    t = lax.axis_index("tensor")
    holding, rank = input_maps.shape[:2]
    held = output_maps.shape[0]
    total_rows = rows * pool_count
    slot_ids = jnp.arange(lists.shape[1], dtype=jnp.int32)
    slot_hot = slots.reshape(pool_count, rows)[:, :, None] == slot_ids
    ids = jnp.sum(jnp.where(slot_hot, lists[:, None, :], 0), axis=2).reshape(total_rows)
    gathered = lax.all_gather(hidden, "pool", axis=0, tiled=True)
    scored = lax.dot_general(
        gathered,
        input_maps.reshape(holding * rank, depth),
        (((1,), (1,)), ((), ())),
        preferred_element_type=F32,
    ).reshape(total_rows, holding, rank)
    owned = place * holding + jnp.arange(holding, dtype=jnp.int32)
    partial = jnp.sum(
        jnp.where((ids[:, None] == owned[None, :])[:, :, None], scored, 0.0), axis=1
    )
    lowrank = lax.psum(partial, ("tensor", "pool")).astype(BF16)
    maps = lax.all_to_all(output_maps, "pool", split_axis=1, concat_axis=0, tiled=True)
    columns = jnp.arange(pool_count * held, dtype=jnp.int32)
    source = (columns // held * tensor_count + t) * held + columns % held
    pick = (source[None, :] % rank == jnp.arange(rank, dtype=jnp.int32)[:, None]).astype(BF16)
    placed = jnp.dot(lowrank, pick, preferred_element_type=F32).astype(BF16)
    spread = jnp.where(ids[:, None] == source[None, :] // rank, placed, jnp.zeros_like(placed))
    value = jnp.dot(gathered, weight, preferred_element_type=F32)
    value = value + jnp.dot(spread, maps, preferred_element_type=F32)
    mixed = lax.psum_scatter(value, "tensor", scatter_dimension=0, tiled=True)
    return mixed.astype(BF16)


def solution(mesh):
    shape = dict(mesh.shape)
    fast = shape["groups"] == 2 and shape["pool"] == 4 and shape["tensor"] == 4
    placed = (
        P(("groups", "pool"), "tensor"),
        P("tensor", "pool"),
        P("pool", None, "tensor"),
        P(("pool", "tensor"), None),
        P("groups"),
        P("groups", None),
    )
    return jax.shard_map(
        per_device_fast if fast else per_device_general,
        mesh=mesh,
        in_specs=placed,
        out_specs=P(("groups", "tensor"), "pool"),
        check_vma=False,
    )
```

time: 173 us -> 137 us (0.79)
  Pallas kernels: 84.2 us -> 58.4 us
  local copies, waits for them, and re-layouts: 17.8 us -> 9.33 us
  waiting for transfers between devices: 28.3 us -> 35.2 us
  other arithmetic: 9.98 us -> 5.43 us
  between operations: 4.1 us -> 0.45 us
    pallas_call x14 -> x13, Pallas kernels: 84.2 us -> 58.4 us  [the longest x6 33.9 us: base_product(): pl.pallas_call(lambda *refs: base_kernel(len(pieces), prior is not None,...]
    ppermute x30 -> x35, waiting for transfers between devices: 28.3 us -> 35.2 us  [swap(): return lax.ppermute(values, axis, partners(lax.axis_size(axis), step))]
    unnamed x40 -> x26, local copies, waits for them, and re-layouts: 5.97 us -> 2.55 us
    select_n x6 -> x0, other arithmetic: 3.04 us -> none  [the longest x4 2.02 us: per_device_fast(): kept = jnp.where(core == 0, block[0], block[1])]
    dynamic_slice x1, local copies, waits for them, and re-layouts: 2.66 us -> 0.1 us  [per_device_fast(): lax.dynamic_slice(output_maps, (0, (place ^ 1) * width), (held, width))]
    ppermute x30 -> x35, starting transfers between devices: 27.5 us -> 28.2 us  [swap(): return lax.ppermute(values, axis, partners(lax.axis_size(axis), step))]
  transfers between devices with their start and end apart: 30 -> 35, of which waited for: 6 -> 14; matrix products, arithmetic and copies ran while one was open for 10% -> 8% of each run, Pallas kernels for 49% -> 43%
where the time goes in v3:
time: 137 us
  Pallas kernels  58.4 us (43%)
  waiting for transfers between devices  35.2 us (26%)
  starting transfers between devices  28.2 us (21%)
  local copies, waits for them, and re-layouts  9.33 us (7%)
  other arithmetic  5.43 us (4%)
    ppermute x35, waiting for transfers between devices, swap(): return lax.ppermute(values, axis, partners(lax.axis_size(axis), step))  35.2 us
    pallas_call x6, Pallas kernels, base_product(): pl.pallas_call(lambda *refs: base_kernel(len(pieces), prior is not None,...  33.9 us
    ppermute x35, starting transfers between devices, swap(): return lax.ppermute(values, axis, partners(lax.axis_size(axis), step))  28.2 us
    pallas_call x3, Pallas kernels, scores(): pl.pallas_call(lambda *refs: scores_kernel(first, half * depth, len(piece...  16.5 us
    pallas_call x4, Pallas kernels, combine(): pl.pallas_call(lambda *refs: combine_kernel(bool(build), *refs), grid_spe...  8 us
    slice x1, local copies, waits for them, and re-layouts, per_device_fast(): hidden[:, h * part:(h + 1) * part]  2.94 us
  transfers between devices with their start and end apart: 35, of which 14 were waited for; matrix products, arithmetic and copies ran while one was open for 8% of the time, Pallas kernels for 43%

profile of v3, /device:TPU:0, one launch (start us, length us, event | category | flops | bytes accessed | tf_op | source)
XLA Modules:
  0.0 137.0 jit_solution(1961267610081700547)
XLA Ops:
  0.5 2.9 %fusion.12 = (bf16[128,3584]{1,0:T(8,128)(2,1)}, bf16[128,3584]{1,0:T(8,128)(2,1)}) fusion(bf16[128,7168]{1,0:T(8,128)(2,1)} %refs_0_), kind=kLoop, calls=%fused_computation.55 | loop fusion | bytes 3670016 | tf_op jit(solution)/shard_map/slice | solution.py:303
  3.4 2.5 %collective-permute-start.2 = (bf16[128,3584]{1,0:T(8,128)(2,1)}, bf16[128,3584]{1,0:T(8,128)(2,1)}, u32[]{:S(2)}, u32[]{:S(2)}) collective-permute-start(bf16[128,3584]{1,0:T(8,128)(2,1)} %get-tuple-element.99), channel_id=1, source_target_pairs={{0,8},{4,12},{8,0},{12,4},{1,9},{5,13},{9,1},{13,5},{2,10},{6,14},... | collective-permute-start | bytes 2752520 | tf_op jit(solution)/shard_map/ppermute | solution.py:22
  8.2 1.5 %dynamic-slice_bitcast_fusion.1 = (bf16[1,128,512]{2,1,0:T(8,128)(2,1)S(1)}, bf16[1,128,512]{2,1,0:T(8,128)(2,1)S(1)}, bf16[1,128,512]{2,1,0:T(8,128)(2,1)S(1)},...) fusion(bf16[256,8192]{1,0:T(8,128)(2,1)} %refs_4_.7, ...), kind=kLoop, calls=%fused_computation.29 | loop fusion | bytes 2097188 | tf_op jit(solution)/shard_map/stack | solution.py:308
  11.2 7.1 %scores.3.refs_5_ = f32[2,64,128]{2,1,0:T(8,128)S(1)} custom-call(s32[17]{0:T(128)S(1)} %pad_add_fusion.refs_0_, bf16[128,7168]{1,0:T(8,128)(2,1)S(1)} %copy-done.8, bf16[128,7168]{1,0:T(8,128)(2,1)} %collective-permute-done.refs_2_.refs_1_, bf16[16,64,7168]{2,1,0:T(8,128)(2,1)} %refs_3_.9, s32[4,1,128]{2,1,0:T(1,128)S(1)} %bitcast.65), custom_call_target="tpu_custom_call" | custom-call | flops 939524 | bytes 11010 | tf_op jit(solution)/shard_map/scores/pallas_call | solution.py:179
  18.3 13.5 %base.6 = f32[256,2048]{1,0:T(8,128)S(1)} custom-call(bf16[128,7168]{1,0:T(8,128)(2,1)S(1)} %copy-done.8, bf16[128,7168]{1,0:T(8,128)(2,1)} %collective-permute-done.refs_2_.refs_1_, bf16[7168,2048]{1,0:T(8,128)(2,1)} %refs_3_.13), custom_call_target="tpu_custom_call" | custom-call | flops 7516192 | bytes 35127 | tf_op jit(solution)/shard_map/base/pallas_call | solution.py:68
  31.8 1.9 %fusion.13 = (bf16[128,1792]{1,0:T(8,128)(2,1)S(1)}, bf16[128,1792]{1,0:T(8,128)(2,1)S(1)}) fusion(bf16[128,3584]{1,0:T(8,128)(2,1)} %collective-permute-done.2.refs_1_.refs_0_), kind=kLoop, calls=%fused_computation.56 | loop fusion | bytes 1835008 | tf_op jit(solution)/shard_map/slice | solution.py:367
  36.3 4.9 %scores.4.refs_4_ = f32[2,256,128]{2,1,0:T(8,128)S(1)} custom-call(s32[17]{0:T(128)S(1)} %pad_add_fusion.refs_0_, bf16[128,3584]{1,0:T(8,128)(2,1)} %collective-permute-done.2.refs_1_.refs_0_, bf16[128,1792]{1,0:T(8,128)(2,1)S(1)} %collective-permute-done.3.refs_2_.refs_1_, bf16[128,1792]{1,0:T(8,128)(2,1)S(1)} %collective-permute-done.4.refs_3_.refs_2_, ...), custom_call_target="tpu_custom_call" | custom-call | flops 469762 | bytes 5505 | tf_op jit(solution)/shard_map/scores/pallas_call | solution.py:179
  41.2 8.2 %base.7.refs_2_ = f32[256,2048]{1,0:T(8,128)S(1)} custom-call(bf16[128,3584]{1,0:T(8,128)(2,1)} %collective-permute-done.2.refs_1_.refs_0_, bf16[128,1792]{1,0:T(8,128)(2,1)S(1)} %collective-permute-done.3.refs_2_.refs_1_, bf16[128,1792]{1,0:T(8,128)(2,1)S(1)} %collective-permute-done.4.refs_3_.refs_2_, bf16[7168,2048]{1,0:T(8,128)(2,1)} %refs_3_.13), custom_call_target="tpu_custom_call" | custom-call | flops 3758096 | bytes 18612 | tf_op jit(solution)/shard_map/base/pallas_call | solution.py:68
  49.7 1.9 %collective-permute-start.7 = (bf16[2,128,512]{2,1,0:T(8,128)(2,1)S(1)}, bf16[2,128,512]{2,1,0:T(8,128)(2,1)S(1)}, u32[]{:S(2)}, u32[]{:S(2)}) collective-permute-start(bf16[2,128,512]{2,1,0:T(8,128)(2,1)S(1)} %get-tuple-element.58), channel_id=1, source_target_pairs={{0,8},{4,12},{8,0},{12,4},{1,9},{5,13},{9,1},{13,5},{2,10},{6,14},... | collective-permute-start | bytes 786440 | tf_op jit(solution)/shard_map/ppermute | solution.py:22
  51.9 4.5 %scores.5 = (f32[4,64,128]{2,1,0:T(8,128)S(1)}, bf16[4,64,128]{2,1,0:T(8,128)(2,1)S(1)}) custom-call(s32[17]{0:T(128)S(1)} %pad_add_fusion.refs_0_, bf16[128,3584]{1,0:T(8,128)(2,1)S(1)} %collective-permute-done.1.refs_1_.refs_0_, bf16[128,3584]{1,0:T(8,128)(2,1)S(1)} %collective-permute-done.5.refs_2_.refs_1_, bf16[16,64,7168]{2,1,0:T(8,128)(2,1)} %refs_3_.9, ...), custom_call_target="tpu_custom_call" | custom-call | flops 469762 | bytes 5505 | tf_op jit(solution)/shard_map/scores/pallas_call | solution.py:179
  56.4 2.1 %collective-permute-start.6 = (bf16[4,64,128]{2,1,0:T(8,128)(2,1)S(1)}, bf16[4,64,128]{2,1,0:T(8,128)(2,1)S(1)}, u32[]{:S(2)}, u32[]{:S(2)}) collective-permute-start(bf16[4,64,128]{2,1,0:T(8,128)(2,1)S(1)} %get-tuple-element.57), channel_id=1, source_target_pairs={{0,1},{1,0},{2,3},{3,2},{4,5},{5,4},{6,7},{7,6},{8,9},{9,8},{10,11... | collective-permute-start | bytes 196616 | tf_op jit(solution)/shard_map/ppermute | solution.py:22
  61.0 2.9 %collective-permute-start.8 = (bf16[4,64,128]{2,1,0:T(8,128)(2,1)S(1)}, bf16[4,64,128]{2,1,0:T(8,128)(2,1)S(1)}, u32[]{:S(2)}, u32[]{:S(2)}) collective-permute-start(bf16[4,64,128]{2,1,0:T(8,128)(2,1)S(1)} %fusion.8), channel_id=1, source_target_pairs={{0,2},{1,3},{2,0},{3,1},{4,6},{5,7},{6,4},{7,5},{8,10},{9,11},{10,... | collective-permute-start | bytes 196616 | tf_op jit(solution)/shard_map/ppermute | solution.py:22
  63.9 1.5 %collective-permute-start.11 = (bf16[2,128,512]{2,1,0:T(8,128)(2,1)S(1)}, bf16[2,128,512]{2,1,0:T(8,128)(2,1)S(1)}, u32[]{:S(2)}, u32[]{:S(2)}) collective-permute-start(bf16[2,128,512]{2,1,0:T(8,128)(2,1)S(1)} %get-tuple-element.66), channel_id=1, source_target_pairs={{0,8},{4,12},{8,0},{12,4},{1,9},{5,13},{9,1},{13,5},{2,10},{6,14},... | collective-permute-start | bytes 786440 | tf_op jit(solution)/shard_map/ppermute | solution.py:22
  65.4 1.5 %collective-permute-start.15 = (bf16[2,128,512]{2,1,0:T(8,128)(2,1)S(1)}, bf16[2,128,512]{2,1,0:T(8,128)(2,1)S(1)}, u32[]{:S(2)}, u32[]{:S(2)}) collective-permute-start(bf16[2,128,512]{2,1,0:T(8,128)(2,1)S(1)} %collective-permute-done.7.refs_8_), channel_id=1, source_target_pairs={{0,16},{16,0},{1,17},{17,1},{2,18},{18,2},{3,19},{19,3},{4,20},{20... | collective-permute-start | bytes 786440 | tf_op jit(solution)/shard_map/ppermute | solution.py:22
  67.8 3.0 %base.8 = f32[256,512]{1,0:T(8,128)S(1)} custom-call(bf16[128,3584]{1,0:T(8,128)(2,1)S(1)} %collective-permute-done.1.refs_1_.refs_0_, bf16[128,3584]{1,0:T(8,128)(2,1)S(1)} %collective-permute-done.5.refs_2_.refs_1_, f32[256,2048]{1,0:T(8,128)S(1)} %base.7.refs_2_, bf16[7168,2048]{1,0:T(8,128)(2,1)} %refs_3_.13), custom_call_target="tpu_custom_call" | custom-call | flops 939524 | bytes 6029 | tf_op jit(solution)/shard_map/base/pallas_call | solution.py:68
  72.2 1.5 %collective-permute-start.20 = (bf16[2,128,512]{2,1,0:T(8,128)(2,1)}, bf16[2,128,512]{2,1,0:T(8,128)(2,1)}, u32[]{:S(2)}, u32[]{:S(2)}) collective-permute-start(bf16[2,128,512]{2,1,0:T(8,128)(2,1)} %collective-permute-done.9.refs_6_), channel_id=1, source_target_pairs={{0,16},{16,0},{1,17},{17,1},{2,18},{18,2},{3,19},{19,3},{4,20},{20... | collective-permute-start | bytes 786440 | tf_op jit(solution)/shard_map/ppermute | solution.py:22
  73.8 1.6 %collective-permute-start.12 = (bf16[4,64,128]{2,1,0:T(8,128)(2,1)S(1)}, bf16[4,64,128]{2,1,0:T(8,128)(2,1)S(1)}, u32[]{:S(2)}, u32[]{:S(2)}) collective-permute-start(bf16[4,64,128]{2,1,0:T(8,128)(2,1)S(1)} %get-tuple-element.89), channel_id=1, source_target_pairs={{0,8},{4,12},{8,0},{12,4},{1,9},{5,13},{9,1},{13,5},{2,10},{6,14},... | collective-permute-start | bytes 196616 | tf_op jit(solution)/shard_map/ppermute | solution.py:22
  75.6 2.8 %collective-permute-done.12.refs_2_ = bf16[4,64,128]{2,1,0:T(8,128)(2,1)S(1)} collective-permute-done((bf16[4,64,128]{2,1,0:T(8,128)(2,1)S(1)}, bf16[4,64,128]{2,1,0:T(8,128)(2,1)S(1)}, u32[]{:S(2)}, u32[]{:S(2)}) %collective-permute-start.12) | collective-permute-done | bytes 65568 | tf_op jit(solution)/shard_map/ppermute | solution.py:22
  78.4 1.5 %collective-permute-start.29 = (bf16[2,128,512]{2,1,0:T(8,128)(2,1)}, bf16[2,128,512]{2,1,0:T(8,128)(2,1)}, u32[]{:S(2)}, u32[]{:S(2)}) collective-permute-start(bf16[2,128,512]{2,1,0:T(8,128)(2,1)} %get-tuple-element.84), channel_id=1, source_target_pairs={{0,8},{4,12},{8,0},{12,4},{1,9},{5,13},{9,1},{13,5},{2,10},{6,14},... | collective-permute-start | bytes 786440 | tf_op jit(solution)/shard_map/ppermute | solution.py:22
  79.9 2.2 %combine.4 = (f32[2,128,512]{2,1,0:T(8,128)S(1)}, bf16[2,128,512]{2,1,0:T(8,128)(2,1)}, bf16[512,1024]{1,0:T(8,128)(2,1)S(1)}) custom-call(s32[10]{0:T(128)S(1)} %stack.76.refs_0_, f32[4,64,128]{2,1,0:T(8,128)S(1)} %get-tuple-element.90.refs_1_, bf16[4,64,128]{2,1,0:T(8,128)(2,1)S(1)} %collective-permute-done.12.refs_2_, ...), custom_call_target="tpu_custom_call" | custom-call | flops 536870 | bytes 2752 | tf_op jit(solution)/shard_map/combine/pallas_call | solution.py:272
  84.0 2.7 %collective-permute-done.29.refs_6_ = bf16[2,128,512]{2,1,0:T(8,128)(2,1)} collective-permute-done((bf16[2,128,512]{2,1,0:T(8,128)(2,1)}, bf16[2,128,512]{2,1,0:T(8,128)(2,1)}, u32[]{:S(2)}, u32[]{:S(2)}) %collective-permute-start.29) | collective-permute-done | bytes 262176 | tf_op jit(solution)/shard_map/ppermute | solution.py:22
  87.9 3.1 %base.9 = f32[256,512]{1,0:T(8,128)S(1)} custom-call(bf16[128,3584]{1,0:T(8,128)(2,1)S(1)} %collective-permute-done.1.refs_1_.refs_0_, bf16[128,3584]{1,0:T(8,128)(2,1)S(1)} %copy-done.5, f32[256,2048]{1,0:T(8,128)S(1)} %base.7.refs_2_, bf16[7168,2048]{1,0:T(8,128)(2,1)} %refs_3_.13), custom_call_target="tpu_custom_call" | custom-call | flops 939524 | bytes 6029 | tf_op jit(solution)/shard_map/base/pallas_call | solution.py:68
  91.9 2.4 %combine.5 = (f32[2,128,512]{2,1,0:T(8,128)S(1)}, bf16[2,128,512]{2,1,0:T(8,128)(2,1)S(1)}) custom-call(s32[10]{0:T(128)S(1)} %stack.76.refs_0_, bf16[512,1024]{1,0:T(8,128)(2,1)S(1)} %copy-done.10, f32[2,128,2048]{2,1,0:T(8,128)S(1)} %bitcast.58, f32[2,128,512]{2,1,0:T(8,128)S(1)} %bitcast.64, bf16[256,8192]{1,0:T(8,128)(2,1)S(1)} %copy-done.1, ...), custom_call_target="tpu_custom_call" | custom-call | flops 536870 | bytes 2752 | tf_op jit(solution)/shard_map/combine/pallas_call | solution.py:272
  96.3 2.2 %collective-permute-start.18 = (bf16[128,512]{1,0:T(8,128)(2,1)S(1)}, bf16[128,512]{1,0:T(8,128)(2,1)S(1)}, u32[]{:S(2)}, u32[]{:S(2)}) collective-permute-start(bf16[128,512]{1,0:T(8,128)(2,1)S(1)} %fusion.4), channel_id=1, source_target_pairs={{0,2},{1,3},{2,0},{3,1},{4,6},{5,7},{6,4},{7,5},{8,10},{9,11},{10,... | collective-permute-start | bytes 393224 | tf_op jit(solution)/shard_map/ppermute | solution.py:22
  98.5 3.2 %base.10 = f32[256,512]{1,0:T(8,128)S(1)} custom-call(bf16[128,3584]{1,0:T(8,128)(2,1)S(1)} %collective-permute-done.1.refs_1_.refs_0_, bf16[128,3584]{1,0:T(8,128)(2,1)S(1)} %copy-done.5, f32[256,2048]{1,0:T(8,128)S(1)} %base.7.refs_2_, bf16[7168,2048]{1,0:T(8,128)(2,1)} %refs_3_.13), custom_call_target="tpu_custom_call" | custom-call | flops 939524 | bytes 6029 | tf_op jit(solution)/shard_map/base/pallas_call | solution.py:68
  101.7 4.0 %collective-permute-done.22 = bf16[2,128,512]{2,1,0:T(8,128)(2,1)S(1)} collective-permute-done((bf16[2,128,512]{2,1,0:T(8,128)(2,1)S(1)}, bf16[2,128,512]{2,1,0:T(8,128)(2,1)S(1)}, u32[]{:S(2)}, u32[]{:S(2)}) %collective-permute-start.22) | collective-permute-done | bytes 262176 | tf_op jit(solution)/shard_map/ppermute | solution.py:22
  110.0 3.0 %base.11 = f32[256,512]{1,0:T(8,128)S(1)} custom-call(bf16[128,3584]{1,0:T(8,128)(2,1)S(1)} %collective-permute-done.1.refs_1_.refs_0_, bf16[128,3584]{1,0:T(8,128)(2,1)S(1)} %copy-done.5, f32[256,2048]{1,0:T(8,128)S(1)} %base.7.refs_2_, bf16[7168,2048]{1,0:T(8,128)(2,1)} %refs_3_.13), custom_call_target="tpu_custom_call" | custom-call | flops 939524 | bytes 6029 | tf_op jit(solution)/shard_map/base/pallas_call | solution.py:68
  113.0 2.1 %collective-permute-done.23 = bf16[128,512]{1,0:T(8,128)(2,1)S(1)} collective-permute-done((bf16[128,512]{1,0:T(8,128)(2,1)S(1)}, bf16[128,512]{1,0:T(8,128)(2,1)S(1)}, u32[]{:S(2)}, u32[]{:S(2)}) %collective-permute-start.23) | collective-permute-done | bytes 131104 | tf_op jit(solution)/shard_map/ppermute | solution.py:22
  115.2 2.2 %combine.7 = (f32[2,128,512]{2,1,0:T(8,128)S(1)}, bf16[2,128,512]{2,1,0:T(8,128)(2,1)S(1)}) custom-call(s32[10]{0:T(128)S(1)} %stack.76.refs_0_, bf16[512,1024]{1,0:T(8,128)(2,1)S(1)} %copy-done.10, f32[2,128,2048]{2,1,0:T(8,128)S(1)} %bitcast.60, f32[2,128,512]{2,1,0:T(8,128)S(1)} %bitcast.63, bf16[256,8192]{1,0:T(8,128)(2,1)S(1)} %copy-done.1, ...), custom_call_target="tpu_custom_call" | custom-call | flops 536870 | bytes 2752 | tf_op jit(solution)/shard_map/combine/pallas_call | solution.py:272
  117.5 2.1 %collective-permute-done.27 = bf16[2,128,512]{2,1,0:T(8,128)(2,1)S(1)} collective-permute-done((bf16[2,128,512]{2,1,0:T(8,128)(2,1)S(1)}, bf16[2,128,512]{2,1,0:T(8,128)(2,1)S(1)}, u32[]{:S(2)}, u32[]{:S(2)}) %collective-permute-start.27) | collective-permute-done | bytes 262176 | tf_op jit(solution)/shard_map/ppermute | solution.py:22
  120.0 8.5 %collective-permute-done.33 = bf16[2,128,512]{2,1,0:T(8,128)(2,1)S(1)} collective-permute-done((bf16[2,128,512]{2,1,0:T(8,128)(2,1)S(1)}, bf16[2,128,512]{2,1,0:T(8,128)(2,1)S(1)}, u32[]{:S(2)}, u32[]{:S(2)}) %collective-permute-start.33) | collective-permute-done | bytes 262176 | tf_op jit(solution)/shard_map/ppermute | solution.py:22
  128.8 7.3 %collective-permute-done.34 = bf16[128,512]{1,0:T(8,128)(2,1)S(1)} collective-permute-done((bf16[128,512]{1,0:T(8,128)(2,1)S(1)}, bf16[128,512]{1,0:T(8,128)(2,1)S(1)}, u32[]{:S(2)}, u32[]{:S(2)}) %collective-permute-start.34) | collective-permute-done | bytes 131104 | tf_op jit(solution)/shard_map/ppermute | solution.py:22
  (114 shorter events, 24.3 us)
Async XLA Ops:
  0.0 11.0 %collective-permute-start = (bf16[128,7168]{1,0:T(8,128)(2,1)}, bf16[128,7168]{1,0:T(8,128)(2,1)}, u32[]{:S(2)}, u32[]{:S(2)}) collective-permute-start(bf16[128,7168]{1,0:T(8,128)(2,1)} %refs_0_), channel_id=1, source_target_pairs={{0,4},{4,0},{8,12},{12,8},{1,5},{5,1},{9,13},{13,9},{2,6},{6,2},{1... | collective-permute-start | bytes 5505032 | tf_op jit(solution)/shard_map/ppermute | solution.py:22
  3.4 28.4 %collective-permute-start.2 = (bf16[128,3584]{1,0:T(8,128)(2,1)}, bf16[128,3584]{1,0:T(8,128)(2,1)}, u32[]{:S(2)}, u32[]{:S(2)}) collective-permute-start(bf16[128,3584]{1,0:T(8,128)(2,1)} %get-tuple-element.99), channel_id=1, source_target_pairs={{0,8},{4,12},{8,0},{12,4},{1,9},{5,13},{9,1},{13,5},{2,10},{6,14},... | collective-permute-start | bytes 2752520 | tf_op jit(solution)/shard_map/ppermute | solution.py:22
  5.9 43.5 %collective-permute-start.1 = (bf16[128,3584]{1,0:T(8,128)(2,1)}, bf16[128,3584]{1,0:T(8,128)(2,1)S(1)}, u32[]{:S(2)}, u32[]{:S(2)}) collective-permute-start(bf16[128,3584]{1,0:T(8,128)(2,1)} %get-tuple-element.100), channel_id=1, source_target_pairs={{0,8},{4,12},{8,0},{12,4},{1,9},{5,13},{9,1},{13,5},{2,10},{6,14},... | collective-permute-start | bytes 2752520 | tf_op jit(solution)/shard_map/ppermute | solution.py:22
  49.4 2.5 %collective-permute-start.5 = (bf16[128,3584]{1,0:T(8,128)(2,1)S(1)}, bf16[128,3584]{1,0:T(8,128)(2,1)S(1)}, u32[]{:S(2)}, u32[]{:S(2)}) collective-permute-start(bf16[128,3584]{1,0:T(8,128)(2,1)S(1)} %collective-permute-done.1.refs_1_.refs_0_), channel_id=1, source_target_pairs={{0,4},{4,0},{8,12},{12,8},{1,5},{5,1},{9,13},{13,9},{2,6},{6,2},{1... | collective-permute-start | bytes 2752520 | tf_op jit(solution)/shard_map/ppermute | solution.py:22
  49.7 10.4 %collective-permute-start.7 = (bf16[2,128,512]{2,1,0:T(8,128)(2,1)S(1)}, bf16[2,128,512]{2,1,0:T(8,128)(2,1)S(1)}, u32[]{:S(2)}, u32[]{:S(2)}) collective-permute-start(bf16[2,128,512]{2,1,0:T(8,128)(2,1)S(1)} %get-tuple-element.58), channel_id=1, source_target_pairs={{0,8},{4,12},{8,0},{12,4},{1,9},{5,13},{9,1},{13,5},{2,10},{6,14},... | collective-permute-start | bytes 786440 | tf_op jit(solution)/shard_map/ppermute | solution.py:22
  51.6 23.8 %collective-permute-start.13 = (bf16[256,2048]{1,0:T(8,128)(2,1)S(1)}, bf16[256,2048]{1,0:T(8,128)(2,1)S(1)}, u32[]{:S(2)}, u32[]{:S(2)}) collective-permute-start(bf16[256,2048]{1,0:T(8,128)(2,1)S(1)} %constant_dynamic-slice_fusion), channel_id=1, source_target_pairs={{0,4},{4,0},{8,12},{12,8},{1,5},{5,1},{9,13},{13,9},{2,6},{6,2},{1... | collective-permute-start | bytes 3145736 | tf_op jit(solution)/shard_map/ppermute | solution.py:22
  56.4 4.5 %collective-permute-start.6 = (bf16[4,64,128]{2,1,0:T(8,128)(2,1)S(1)}, bf16[4,64,128]{2,1,0:T(8,128)(2,1)S(1)}, u32[]{:S(2)}, u32[]{:S(2)}) collective-permute-start(bf16[4,64,128]{2,1,0:T(8,128)(2,1)S(1)} %get-tuple-element.57), channel_id=1, source_target_pairs={{0,1},{1,0},{2,3},{3,2},{4,5},{5,4},{6,7},{7,6},{8,9},{9,8},{10,11... | collective-permute-start | bytes 196616 | tf_op jit(solution)/shard_map/ppermute | solution.py:22
  58.5 9.3 %collective-permute-start.9 = (bf16[2,128,512]{2,1,0:T(8,128)(2,1)S(1)}, bf16[2,128,512]{2,1,0:T(8,128)(2,1)}, u32[]{:S(2)}, u32[]{:S(2)}) collective-permute-start(bf16[2,128,512]{2,1,0:T(8,128)(2,1)S(1)} %get-tuple-element.61), channel_id=1, source_target_pairs={{0,8},{4,12},{8,0},{12,4},{1,9},{5,13},{9,1},{13,5},{2,10},{6,14},... | collective-permute-start | bytes 786440 | tf_op jit(solution)/shard_map/ppermute | solution.py:22
  61.0 9.9 %collective-permute-start.8 = (bf16[4,64,128]{2,1,0:T(8,128)(2,1)S(1)}, bf16[4,64,128]{2,1,0:T(8,128)(2,1)S(1)}, u32[]{:S(2)}, u32[]{:S(2)}) collective-permute-start(bf16[4,64,128]{2,1,0:T(8,128)(2,1)S(1)} %fusion.8), channel_id=1, source_target_pairs={{0,2},{1,3},{2,0},{3,1},{4,6},{5,7},{6,4},{7,5},{8,10},{9,11},{10,... | collective-permute-start | bytes 196616 | tf_op jit(solution)/shard_map/ppermute | solution.py:22
  63.9 8.3 %collective-permute-start.11 = (bf16[2,128,512]{2,1,0:T(8,128)(2,1)S(1)}, bf16[2,128,512]{2,1,0:T(8,128)(2,1)S(1)}, u32[]{:S(2)}, u32[]{:S(2)}) collective-permute-start(bf16[2,128,512]{2,1,0:T(8,128)(2,1)S(1)} %get-tuple-element.66), channel_id=1, source_target_pairs={{0,8},{4,12},{8,0},{12,4},{1,9},{5,13},{9,1},{13,5},{2,10},{6,14},... | collective-permute-start | bytes 786440 | tf_op jit(solution)/shard_map/ppermute | solution.py:22
  65.4 8.4 %collective-permute-start.15 = (bf16[2,128,512]{2,1,0:T(8,128)(2,1)S(1)}, bf16[2,128,512]{2,1,0:T(8,128)(2,1)S(1)}, u32[]{:S(2)}, u32[]{:S(2)}) collective-permute-start(bf16[2,128,512]{2,1,0:T(8,128)(2,1)S(1)} %collective-permute-done.7.refs_8_), channel_id=1, source_target_pairs={{0,16},{16,0},{1,17},{17,1},{2,18},{18,2},{3,19},{19,3},{4,20},{20... | collective-permute-start | bytes 786440 | tf_op jit(solution)/shard_map/ppermute | solution.py:22
  70.9 2.9 %collective-permute-start.10 = (bf16[4,64,128]{2,1,0:T(8,128)(2,1)S(1)}, bf16[4,64,128]{2,1,0:T(8,128)(2,1)S(1)}, u32[]{:S(2)}, u32[]{:S(2)}) collective-permute-start(bf16[4,64,128]{2,1,0:T(8,128)(2,1)S(1)} %fusion.9), channel_id=1, source_target_pairs={{0,4},{4,0},{8,12},{12,8},{1,5},{5,1},{9,13},{13,9},{2,6},{6,2},{1... | collective-permute-start | bytes 196616 | tf_op jit(solution)/shard_map/ppermute | solution.py:22
  71.0 8.9 %collective-permute-start.14 = (bf16[2,128,512]{2,1,0:T(8,128)(2,1)S(1)}, bf16[2,128,512]{2,1,0:T(8,128)(2,1)S(1)}, u32[]{:S(2)}, u32[]{:S(2)}) collective-permute-start(bf16[2,128,512]{2,1,0:T(8,128)(2,1)S(1)} %collective-permute-done.7.refs_8_), channel_id=1, source_target_pairs={{0,4},{4,0},{8,12},{12,8},{1,5},{5,1},{9,13},{13,9},{2,6},{6,2},{1... | collective-permute-start | bytes 786440 | tf_op jit(solution)/shard_map/ppermute | solution.py:22
  72.2 10.8 %collective-permute-start.20 = (bf16[2,128,512]{2,1,0:T(8,128)(2,1)}, bf16[2,128,512]{2,1,0:T(8,128)(2,1)}, u32[]{:S(2)}, u32[]{:S(2)}) collective-permute-start(bf16[2,128,512]{2,1,0:T(8,128)(2,1)} %collective-permute-done.9.refs_6_), channel_id=1, source_target_pairs={{0,16},{16,0},{1,17},{17,1},{2,18},{18,2},{3,19},{19,3},{4,20},{20... | collective-permute-start | bytes 786440 | tf_op jit(solution)/shard_map/ppermute | solution.py:22
  73.8 6.1 %collective-permute-start.16 = (bf16[2,128,512]{2,1,0:T(8,128)(2,1)S(1)}, bf16[2,128,512]{2,1,0:T(8,128)(2,1)S(1)}, u32[]{:S(2)}, u32[]{:S(2)}) collective-permute-start(bf16[2,128,512]{2,1,0:T(8,128)(2,1)S(1)} %collective-permute-done.15.refs_10_), channel_id=1, source_target_pairs={{0,4},{4,0},{8,12},{12,8},{1,5},{5,1},{9,13},{13,9},{2,6},{6,2},{1... | collective-permute-start | bytes 786440 | tf_op jit(solution)/shard_map/ppermute | solution.py:22
  73.8 4.6 %collective-permute-start.12 = (bf16[4,64,128]{2,1,0:T(8,128)(2,1)S(1)}, bf16[4,64,128]{2,1,0:T(8,128)(2,1)S(1)}, u32[]{:S(2)}, u32[]{:S(2)}) collective-permute-start(bf16[4,64,128]{2,1,0:T(8,128)(2,1)S(1)} %get-tuple-element.89), channel_id=1, source_target_pairs={{0,8},{4,12},{8,0},{12,4},{1,9},{5,13},{9,1},{13,5},{2,10},{6,14},... | collective-permute-start | bytes 196616 | tf_op jit(solution)/shard_map/ppermute | solution.py:22
  75.4 15.7 %collective-permute-start.19 = (bf16[2,128,512]{2,1,0:T(8,128)(2,1)}, bf16[2,128,512]{2,1,0:T(8,128)(2,1)}, u32[]{:S(2)}, u32[]{:S(2)}) collective-permute-start(bf16[2,128,512]{2,1,0:T(8,128)(2,1)} %collective-permute-done.9.refs_6_), channel_id=1, source_target_pairs={{0,4},{4,0},{8,12},{12,8},{1,5},{5,1},{9,13},{13,9},{2,6},{6,2},{1... | collective-permute-start | bytes 786440 | tf_op jit(solution)/shard_map/ppermute | solution.py:22
  78.4 8.3 %collective-permute-start.29 = (bf16[2,128,512]{2,1,0:T(8,128)(2,1)}, bf16[2,128,512]{2,1,0:T(8,128)(2,1)}, u32[]{:S(2)}, u32[]{:S(2)}) collective-permute-start(bf16[2,128,512]{2,1,0:T(8,128)(2,1)} %get-tuple-element.84), channel_id=1, source_target_pairs={{0,8},{4,12},{8,0},{12,4},{1,9},{5,13},{9,1},{13,5},{2,10},{6,14},... | collective-permute-start | bytes 786440 | tf_op jit(solution)/shard_map/ppermute | solution.py:22
  83.0 8.6 %collective-permute-start.21 = (bf16[2,128,512]{2,1,0:T(8,128)(2,1)}, bf16[2,128,512]{2,1,0:T(8,128)(2,1)}, u32[]{:S(2)}, u32[]{:S(2)}) collective-permute-start(bf16[2,128,512]{2,1,0:T(8,128)(2,1)} %collective-permute-done.20.refs_8_), channel_id=1, source_target_pairs={{0,4},{4,0},{8,12},{12,8},{1,5},{5,1},{9,13},{13,9},{2,6},{6,2},{1... | collective-permute-start | bytes 786440 | tf_op jit(solution)/shard_map/ppermute | solution.py:22
  83.0 11.2 %collective-permute-start.17 = (bf16[2,128,512]{2,1,0:T(8,128)(2,1)}, bf16[2,128,512]{2,1,0:T(8,128)(2,1)}, u32[]{:S(2)}, u32[]{:S(2)}) collective-permute-start(bf16[2,128,512]{2,1,0:T(8,128)(2,1)} %get-tuple-element.72), channel_id=1, source_target_pairs={{0,1},{1,0},{2,3},{3,2},{4,5},{5,4},{6,7},{7,6},{8,9},{9,8},{10,11... | collective-permute-start | bytes 786440 | tf_op jit(solution)/shard_map/ppermute | solution.py:22
  83.5 12.8 %collective-permute-start.25 = (bf16[2,128,512]{2,1,0:T(8,128)(2,1)}, bf16[2,128,512]{2,1,0:T(8,128)(2,1)S(1)}, u32[]{:S(2)}, u32[]{:S(2)}) collective-permute-start(bf16[2,128,512]{2,1,0:T(8,128)(2,1)} %copy-done.11), channel_id=1, source_target_pairs={{0,16},{16,0},{1,17},{17,1},{2,18},{18,2},{3,19},{19,3},{4,20},{20... | collective-permute-start | bytes 786440 | tf_op jit(solution)/shard_map/ppermute | solution.py:22
  86.7 19.0 %collective-permute-start.24 = (bf16[2,128,512]{2,1,0:T(8,128)(2,1)}, bf16[2,128,512]{2,1,0:T(8,128)(2,1)S(1)}, u32[]{:S(2)}, u32[]{:S(2)}) collective-permute-start(bf16[2,128,512]{2,1,0:T(8,128)(2,1)} %copy-done.11), channel_id=1, source_target_pairs={{0,4},{4,0},{8,12},{12,8},{1,5},{5,1},{9,13},{13,9},{2,6},{6,2},{1... | collective-permute-start | bytes 786440 | tf_op jit(solution)/shard_map/ppermute | solution.py:22
  91.0 18.9 %collective-permute-start.31 = (bf16[2,128,512]{2,1,0:T(8,128)(2,1)}, bf16[2,128,512]{2,1,0:T(8,128)(2,1)S(1)}, u32[]{:S(2)}, u32[]{:S(2)}) collective-permute-start(bf16[2,128,512]{2,1,0:T(8,128)(2,1)} %collective-permute-done.29.refs_6_), channel_id=1, source_target_pairs={{0,16},{16,0},{1,17},{17,1},{2,18},{18,2},{3,19},{19,3},{4,20},{20... | collective-permute-start | bytes 786440 | tf_op jit(solution)/shard_map/ppermute | solution.py:22
  91.6 23.5 %collective-permute-start.30 = (bf16[2,128,512]{2,1,0:T(8,128)(2,1)}, bf16[2,128,512]{2,1,0:T(8,128)(2,1)S(1)}, u32[]{:S(2)}, u32[]{:S(2)}) collective-permute-start(bf16[2,128,512]{2,1,0:T(8,128)(2,1)} %collective-permute-done.29.refs_6_), channel_id=1, source_target_pairs={{0,4},{4,0},{8,12},{12,8},{1,5},{5,1},{9,13},{13,9},{2,6},{6,2},{1... | collective-permute-start | bytes 786440 | tf_op jit(solution)/shard_map/ppermute | solution.py:22
  94.2 11.4 %collective-permute-start.22 = (bf16[2,128,512]{2,1,0:T(8,128)(2,1)S(1)}, bf16[2,128,512]{2,1,0:T(8,128)(2,1)S(1)}, u32[]{:S(2)}, u32[]{:S(2)}) collective-permute-start(bf16[2,128,512]{2,1,0:T(8,128)(2,1)S(1)} %get-tuple-element.77), channel_id=1, source_target_pairs={{0,1},{1,0},{2,3},{3,2},{4,5},{5,4},{6,7},{7,6},{8,9},{9,8},{10,11... | collective-permute-start | bytes 786440 | tf_op jit(solution)/shard_map/ppermute | solution.py:22
  96.3 13.6 %collective-permute-start.18 = (bf16[128,512]{1,0:T(8,128)(2,1)S(1)}, bf16[128,512]{1,0:T(8,128)(2,1)S(1)}, u32[]{:S(2)}, u32[]{:S(2)}) collective-permute-start(bf16[128,512]{1,0:T(8,128)(2,1)S(1)} %fusion.4), channel_id=1, source_target_pairs={{0,2},{1,3},{2,0},{3,1},{4,6},{5,7},{6,4},{7,5},{8,10},{9,11},{10,... | collective-permute-start | bytes 393224 | tf_op jit(solution)/shard_map/ppermute | solution.py:22
  105.7 9.3 %collective-permute-start.23 = (bf16[128,512]{1,0:T(8,128)(2,1)S(1)}, bf16[128,512]{1,0:T(8,128)(2,1)S(1)}, u32[]{:S(2)}, u32[]{:S(2)}) collective-permute-start(bf16[128,512]{1,0:T(8,128)(2,1)S(1)} %fusion.5), channel_id=1, source_target_pairs={{0,2},{1,3},{2,0},{3,1},{4,6},{5,7},{6,4},{7,5},{8,10},{9,11},{10,... | collective-permute-start | bytes 393224 | tf_op jit(solution)/shard_map/ppermute | solution.py:22
  108.4 11.1 %collective-permute-start.27 = (bf16[2,128,512]{2,1,0:T(8,128)(2,1)S(1)}, bf16[2,128,512]{2,1,0:T(8,128)(2,1)S(1)}, u32[]{:S(2)}, u32[]{:S(2)}) collective-permute-start(bf16[2,128,512]{2,1,0:T(8,128)(2,1)S(1)} %get-tuple-element.81), channel_id=1, source_target_pairs={{0,1},{1,0},{2,3},{3,2},{4,5},{5,4},{6,7},{7,6},{8,9},{9,8},{10,11... | collective-permute-start | bytes 786440 | tf_op jit(solution)/shard_map/ppermute | solution.py:22
  109.9 5.3 %collective-permute-start.32 = (bf16[2,128,512]{2,1,0:T(8,128)(2,1)S(1)}, bf16[2,128,512]{2,1,0:T(8,128)(2,1)S(1)}, u32[]{:S(2)}, u32[]{:S(2)}) collective-permute-start(bf16[2,128,512]{2,1,0:T(8,128)(2,1)S(1)} %collective-permute-done.31.refs_8_), channel_id=1, source_target_pairs={{0,4},{4,0},{8,12},{12,8},{1,5},{5,1},{9,13},{13,9},{2,6},{6,2},{1... | collective-permute-start | bytes 786440 | tf_op jit(solution)/shard_map/ppermute | solution.py:22
  117.4 11.1 %collective-permute-start.33 = (bf16[2,128,512]{2,1,0:T(8,128)(2,1)S(1)}, bf16[2,128,512]{2,1,0:T(8,128)(2,1)S(1)}, u32[]{:S(2)}, u32[]{:S(2)}) collective-permute-start(bf16[2,128,512]{2,1,0:T(8,128)(2,1)S(1)} %get-tuple-element.88), channel_id=1, source_target_pairs={{0,1},{1,0},{2,3},{3,2},{4,5},{5,4},{6,7},{7,6},{8,9},{9,8},{10,11... | collective-permute-start | bytes 786440 | tf_op jit(solution)/shard_map/ppermute | solution.py:22
  119.7 9.0 %collective-permute-start.28 = (bf16[128,512]{1,0:T(8,128)(2,1)S(1)}, bf16[128,512]{1,0:T(8,128)(2,1)S(1)}, u32[]{:S(2)}, u32[]{:S(2)}) collective-permute-start(bf16[128,512]{1,0:T(8,128)(2,1)S(1)} %fusion.6), channel_id=1, source_target_pairs={{0,2},{1,3},{2,0},{3,1},{4,6},{5,7},{6,4},{7,5},{8,10},{9,11},{10,... | collective-permute-start | bytes 393224 | tf_op jit(solution)/shard_map/ppermute | solution.py:22
  128.6 7.5 %collective-permute-start.34 = (bf16[128,512]{1,0:T(8,128)(2,1)S(1)}, bf16[128,512]{1,0:T(8,128)(2,1)S(1)}, u32[]{:S(2)}, u32[]{:S(2)}) collective-permute-start(bf16[128,512]{1,0:T(8,128)(2,1)S(1)} %fusion.7), channel_id=1, source_target_pairs={{0,2},{1,3},{2,0},{3,1},{4,6},{5,7},{6,4},{7,5},{8,10},{9,11},{10,... | collective-permute-start | bytes 393224 | tf_op jit(solution)/shard_map/ppermute | solution.py:22
  (16 other events, 135.2 us)

commit v4 on v3

--- a/solution.py
+++ b/solution.py
@@ -8,7 +8,8 @@
 F32 = jnp.float32
 BF16 = jnp.bfloat16
 VMEM_LIMIT = 40 * 1024 * 1024
-WIDTHS = (512, 512, 512, 512)
+WIDTHS = (512, 1024, 512)
+EARLY = 2
 CAP = 4
 HALVES = 2
 HINT = 1000
@@ -34,20 +35,20 @@
     return pltpu.CompilerParams(vmem_limit_bytes=VMEM_LIMIT)
 
 
-def base_kernel(count, has_prior, *refs):
-    a_ref, pieces, refs = refs[0], refs[1 : 1 + count], refs[1 + count :]
+def base_kernel(lower, upper, has_prior, *refs):
+    pieces, refs = refs[: lower + upper], refs[lower + upper :]
     if has_prior:
         prior_ref, refs = refs[0], refs[1:]
     w_ref, out_ref, rows = refs
 
     @pl.when(pl.program_id(0) == 0)
     def _():
-        half = a_ref.shape[0]
-        rows[:half, :] = a_ref[...]
-        start = 0
-        for piece in pieces:
-            rows[half:, start : start + piece.shape[1]] = piece[...]
-            start += piece.shape[1]
+        half = rows.shape[0] // 2
+        for top, group in ((0, pieces[:lower]), (half, pieces[lower:])):
+            start = 0
+            for piece in group:
+                rows[top : top + half, start : start + piece.shape[1]] = piece[...]
+                start += piece.shape[1]
 
     value = jnp.dot(rows[...], w_ref[...], preferred_element_type=F32)
     if has_prior:
@@ -55,18 +56,18 @@
     out_ref[...] = value
 
 
-def base_product(a, pieces, weight, depth_block=0, prior=None, first=0, width=None, tile=512):
-    rows, depth = a.shape
-    width = weight.shape[1] if width is None else width
-    in_specs = [pl.BlockSpec(x.shape, lambda n: (0, 0)) for x in (a, *pieces)]
-    args = [a, *pieces]
+def product(lower, upper, weight, depth_block, prior, first, width, tile, prior_first=0):
+    rows = lower[0].shape[0]
+    depth = sum(x.shape[1] for x in lower)
+    args = [*lower, *upper]
+    in_specs = [pl.BlockSpec(x.shape, lambda n: (0, 0)) for x in args]
     if prior is not None:
-        in_specs.append(pl.BlockSpec((2 * rows, tile), lambda n: (0, first // tile + n)))
+        in_specs.append(pl.BlockSpec((2 * rows, tile), lambda n: (0, prior_first // tile + n)))
         args.append(prior)
     in_specs.append(pl.BlockSpec((depth, tile), lambda n: (depth_block, first // tile + n)))
     args.append(weight)
     return pl.pallas_call(
-        lambda *refs: base_kernel(len(pieces), prior is not None, *refs),
+        lambda *refs: base_kernel(len(lower), len(upper), prior is not None, *refs),
         grid=(width // tile,),
         in_specs=in_specs,
         out_specs=pl.BlockSpec((2 * rows, tile), lambda n: (0, n)),
@@ -78,6 +79,16 @@
         ),
         name="base",
     )(*args)
+
+
+def base_product(a, pieces, weight, depth_block=0, prior=None, first=0, width=None, tile=512):
+    width = weight.shape[1] if width is None else width
+    return product([a], pieces, weight, depth_block, prior, first, width, tile)
+
+
+def whole_product(a_pieces, b_pieces, weight, first, width, tile):
+    flat = [x for pieces in b_pieces for x in pieces]
+    return product(a_pieces, flat, weight, 0, None, first, width, tile)
 
 
 def scores_kernel(first, offset, count, has_prior, last, info_ref, *refs):
@@ -300,8 +311,12 @@
     count = len(WIDTHS)
 
     part = depth // HALVES
-    crossed = [swap(hidden[:, h * part : (h + 1) * part], "pool", 2) for h in range(HALVES)]
     near_b = swap(hidden, "pool", 1)
+    crossed, block = [], None
+    for h in range(HALVES):
+        source = hidden if block is None else tie(hidden, block)
+        block = source[:, h * part : (h + 1) * part]
+        crossed.append(swap(block, "pool", 2))
 
     core_block = lax.dynamic_slice(output_maps, (0, (place ^ 1) * width), (held, width))
     blocks = [
@@ -366,32 +381,47 @@
     a0 = tie(crossed[0], near_base)
     b0 = [swap(a0[:, k * (part // 2) : (k + 1) * (part // 2)], "pool", 1) for k in range(2)]
     (raw,) = scores(picks, 2, a0, b0, input_maps, 0)
-    far_base = base_product(tie(a0, raw), b0, weight, 0)
-    a1 = tie(crossed[1], far_base)
+    begun = []
+    a0 = tie(a0, raw)
+    for index in range(EARLY):
+        begun.append(
+            base_product(a0, b0, weight, 0, None, starts[index], WIDTHS[index])
+        )
+        a0 = tie(a0, begun[-1])
+    a1 = tie(crossed[1], begun[-1])
     b1 = [swap(a1, "pool", 1)]
     total, sent = scores(
         picks, 2, a1, b1, input_maps, 1, prior=raw, near=near_lowrank, ids=owned_ids
     )
 
     def far_piece(index, after):
-        return base_product(
-            tie(a1, after), b1, weight, 1, far_base, starts[index], WIDTHS[index], 256
-        ).reshape(2, rows, WIDTHS[index])
+        shape = (2, rows, WIDTHS[index])
+        left = tie(a1, after)
+        if index < EARLY:
+            piece = base_product(
+                left, b1, weight, 1, begun[index], starts[index], WIDTHS[index], 256
+            )
+        else:
+            piece = whole_product(
+                [crossed[0], left], [b0, b1], weight, starts[index], WIDTHS[index], 256
+            )
+        return piece.reshape(shape)
 
     hops = (("tensor", 1), ("tensor", 2), ("pool", 1), ("pool", 2))
+    arrivals = {0: 0, 2: 1}
     pieces = []
     for index, (axis, step) in enumerate(hops):
         if index > 0:
             sent = total.astype(BF16)
         got = swap(sent, axis, step)
-        if index < count - 1:
-            crossing[index] = tie(crossing[index], sent)
-            got = tie(got, crossing[index])
-        if index == 1:
+        if index in arrivals:
+            chunk = arrivals[index]
+            crossing[chunk] = tie(crossing[chunk], sent)
+            got = tie(got, crossing[chunk])
+        if index == 3:
+            crossing.append(swap(tie(blocks[-1], sent), "pool", 2))
             pieces.append(far_piece(0, sent))
             got = tie(got, pieces[-1])
-        if index == 3:
-            crossing.append(swap(tie(blocks[-1], sent), "pool", 2))
             break
         total = total + got.astype(F32)
 
@@ -410,6 +440,16 @@
     side = ((place ^ t) >> 1) & 1
     parts = []
     spread = send = None
+    halves = []
+
+    def finish(index, after):
+        keep, got = halves[index]
+        got = got if after is None else tie(got, after)
+        pair = keep + got.astype(F32)
+        sent = jnp.where(side == 0, pair[1], pair[0]).astype(BF16)
+        kept = jnp.where(side == 0, pair[0], pair[1])
+        return kept + swap(sent, "tensor", 2).astype(F32)
+
     for chunk in range(count):
         common = (
             info, near_base, pieces[chunk], output_maps, core_maps,
@@ -422,10 +462,10 @@
             keep, send = combine(*common, spread=spread)
         if chunk + 1 < count:
             pieces.append(far_piece(chunk + 1, send))
-        pair = keep + swap(send, "tensor", 1).astype(F32)
-        sent = jnp.where(side == 0, pair[1], pair[0]).astype(BF16)
-        kept = jnp.where(side == 0, pair[0], pair[1])
-        parts.append(kept + swap(sent, "tensor", 2).astype(F32))
+        halves.append((keep, swap(send, "tensor", 1)))
+        if chunk > 0:
+            parts.append(finish(chunk - 1, send))
+    parts.append(finish(count - 1, None))
     return jnp.concatenate(parts, axis=1).astype(BF16)
 
 

time: 137 us -> 144 us (1.051)
  waiting for transfers between devices: 35.2 us -> 38.4 us
  local copies, waits for them, and re-layouts: 9.33 us -> 11.3 us
    ppermute x35 -> x29, waiting for transfers between devices: 35.2 us -> 38.4 us  [swap(): return lax.ppermute(values, axis, partners(lax.axis_size(axis), step))]
    slice x1, local copies, waits for them, and re-layouts: 1.93 us -> 0.06 us  [per_device_fast(): a0[:, k * (part // 2):(k + 1) * (part // 2)]]
    unnamed x26 -> x30, local copies, waits for them, and re-layouts: 2.55 us -> 4.03 us
    slice x1 -> x2, local copies, waits for them, and re-layouts: 2.94 us -> 4.35 us  [per_device_fast(): block = source[:, h * part:(h + 1) * part]]
    ppermute x35 -> x29, starting transfers between devices: 28.2 us -> 27.7 us  [swap(): return lax.ppermute(values, axis, partners(lax.axis_size(axis), step))]
    pallas_call x4 -> x3, Pallas kernels: 8 us -> 7.55 us  [combine(): pl.pallas_call(lambda *refs: combine_kernel(bool(build), *refs), grid_spe...]
  transfers between devices with their start and end apart: 35 -> 29, of which waited for: 14 -> 12; matrix products, arithmetic and copies ran while one was open for 8% -> 9% of each run, Pallas kernels for 43% -> 41%
where the time goes in v4:
time: 144 us; the launch traced here: 143 us
  Pallas kernels  59.1 us (41%)
  waiting for transfers between devices  38.4 us (27%)
  starting transfers between devices  27.7 us (19%)
  local copies, waits for them, and re-layouts  11.3 us (8%)
  other arithmetic  6.05 us (4%)
    ppermute x29, waiting for transfers between devices, swap(): return lax.ppermute(values, axis, partners(lax.axis_size(axis), step))  38.4 us
    pallas_call x6, Pallas kernels, product(): pl.pallas_call(lambda *refs: base_kernel(len(lower), len(upper), prior is...  34.9 us
    ppermute x29, starting transfers between devices, swap(): return lax.ppermute(values, axis, partners(lax.axis_size(axis), step))  27.7 us
    pallas_call x3, Pallas kernels, scores(): pl.pallas_call(lambda *refs: scores_kernel(first, half * depth, len(piece...  16.7 us
    pallas_call x3, Pallas kernels, combine(): pl.pallas_call(lambda *refs: combine_kernel(bool(build), *refs), grid_spe...  7.55 us
    slice x2, local copies, waits for them, and re-layouts, per_device_fast(): block = source[:, h * part:(h + 1) * part]  4.35 us
    unnamed x30, local copies, waits for them, and re-layouts  4.03 us
  transfers between devices with their start and end apart: 29, of which 12 were waited for; matrix products, arithmetic and copies ran while one was open for 9% of the time, Pallas kernels for 41%

profile of v4, /device:TPU:0, one launch (start us, length us, event | category | flops | bytes accessed | tf_op | source)
XLA Modules:
  0.0 143.0 jit_solution(3232768182991119870)
XLA Ops:
  0.5 2.2 %slice.36 = bf16[128,3584]{1,0:T(8,128)(2,1)} slice(bf16[128,7168]{1,0:T(8,128)(2,1)} %refs_0_), slice={[0:128], [0:3584]} | slice | bytes 1835008 | tf_op jit(solution)/shard_map/slice | solution.py:318
  2.6 2.5 %collective-permute-start.2 = (bf16[128,3584]{1,0:T(8,128)(2,1)}, bf16[128,3584]{1,0:T(8,128)(2,1)S(1)}, u32[]{:S(2)}, u32[]{:S(2)}) collective-permute-start(bf16[128,3584]{1,0:T(8,128)(2,1)} %slice.36), channel_id=1, source_target_pairs={{0,8},{4,12},{8,0},{12,4},{1,9},{5,13},{9,1},{13,5},{2,10},{6,14},... | collective-permute-start | bytes 2752520 | tf_op jit(solution)/shard_map/ppermute | solution.py:23
  5.1 2.2 %slice.37 = bf16[128,3584]{1,0:T(8,128)(2,1)} slice(bf16[128,7168]{1,0:T(8,128)(2,1)} %refs_0_), slice={[0:128], [3584:7168]} | slice | bytes 1835008 | tf_op jit(solution)/shard_map/slice | solution.py:318
  9.8 1.3 dynamic-slice_bitcast_fusion.1
  12.8 7.1 %scores.3.refs_5_ = f32[2,64,128]{2,1,0:T(8,128)S(1)} custom-call(s32[17]{0:T(128)S(1)} %pad_add_fusion.refs_0_, bf16[128,7168]{1,0:T(8,128)(2,1)S(1)} %copy-done.2, bf16[128,7168]{1,0:T(8,128)(2,1)} %collective-permute-done.refs_2_.refs_1_, bf16[16,64,7168]{2,1,0:T(8,128)(2,1)} %refs_3_.9, s32[4,1,128]{2,1,0:T(1,128)S(1)} %bitcast.52), custom_call_target="tpu_custom_call" | custom-call | flops 939524 | bytes 11010 | tf_op jit(solution)/shard_map/scores/pallas_call | solution.py:190
  19.9 13.5 %base.6 = f32[256,2048]{1,0:T(8,128)S(1)} custom-call(bf16[128,7168]{1,0:T(8,128)(2,1)S(1)} %copy-done.3, bf16[128,7168]{1,0:T(8,128)(2,1)} %collective-permute-done.refs_2_.refs_1_, bf16[7168,2048]{1,0:T(8,128)(2,1)} %refs_5_.1), custom_call_target="tpu_custom_call" | custom-call | flops 7516192 | bytes 35127 | tf_op jit(solution)/shard_map/base/pallas_call | solution.py:69
  36.0 4.8 %scores.4.refs_4_ = f32[2,256,128]{2,1,0:T(8,128)S(1)} custom-call(s32[17]{0:T(128)S(1)} %pad_add_fusion.refs_0_, bf16[128,3584]{1,0:T(8,128)(2,1)S(1)} %collective-permute-done.2.refs_1_.refs_0_, bf16[128,1792]{1,0:T(8,128)(2,1)S(1)} %collective-permute-done.3.refs_2_.refs_1_, bf16[128,1792]{1,0:T(8,128)(2,1)S(1)} %collective-permute-done.4.refs_3_.refs_2_, ...), custom_call_target="tpu_custom_call" | custom-call | flops 469762 | bytes 5505 | tf_op jit(solution)/shard_map/scores/pallas_call | solution.py:190
  40.8 3.1 %base.7.refs_2_ = f32[256,512]{1,0:T(8,128)S(1)} custom-call(bf16[128,3584]{1,0:T(8,128)(2,1)S(1)} %collective-permute-done.2.refs_1_.refs_0_, bf16[128,1792]{1,0:T(8,128)(2,1)S(1)} %collective-permute-done.3.refs_2_.refs_1_, bf16[128,1792]{1,0:T(8,128)(2,1)S(1)} %collective-permute-done.4.refs_3_.refs_2_, bf16[7168,2048]{1,0:T(8,128)(2,1)} %refs_5_.1), custom_call_target="tpu_custom_call" | custom-call | flops 939524 | bytes 6029 | tf_op jit(solution)/shard_map/base/pallas_call | solution.py:69
  44.0 4.5 %base.8.refs_2_ = f32[256,1024]{1,0:T(8,128)S(1)} custom-call(bf16[128,3584]{1,0:T(8,128)(2,1)S(1)} %collective-permute-done.2.refs_1_.refs_0_, bf16[128,1792]{1,0:T(8,128)(2,1)S(1)} %collective-permute-done.3.refs_2_.refs_1_, bf16[128,1792]{1,0:T(8,128)(2,1)S(1)} %collective-permute-done.4.refs_3_.refs_2_, bf16[7168,2048]{1,0:T(8,128)(2,1)} %refs_5_.1), custom_call_target="tpu_custom_call" | custom-call | flops 1879048 | bytes 10223 | tf_op jit(solution)/shard_map/base/pallas_call | solution.py:69
  48.8 1.8 %collective-permute-start.7 = (bf16[2,128,512]{2,1,0:T(8,128)(2,1)S(1)}, bf16[2,128,512]{2,1,0:T(8,128)(2,1)S(1)}, u32[]{:S(2)}, u32[]{:S(2)}) collective-permute-start(bf16[2,128,512]{2,1,0:T(8,128)(2,1)S(1)} %get-tuple-element.57), channel_id=1, source_target_pairs={{0,8},{4,12},{8,0},{12,4},{1,9},{5,13},{9,1},{13,5},{2,10},{6,14},... | collective-permute-start | bytes 786440 | tf_op jit(solution)/shard_map/ppermute | solution.py:23
  51.2 4.8 %scores.5 = (f32[4,64,128]{2,1,0:T(8,128)S(1)}, bf16[4,64,128]{2,1,0:T(8,128)(2,1)S(1)}) custom-call(s32[17]{0:T(128)S(1)} %pad_add_fusion.refs_0_, bf16[128,3584]{1,0:T(8,128)(2,1)} %collective-permute-done.1.refs_1_.refs_0_, bf16[128,3584]{1,0:T(8,128)(2,1)S(1)} %collective-permute-done.5.refs_2_.refs_1_.refs_4_, bf16[16,64,7168]{2,1,0:T(8,128)(2,1)} %refs_3_.9, ...), custom_call_target="tpu_custom_call" | custom-call | flops 469762 | bytes 5505 | tf_op jit(solution)/shard_map/scores/pallas_call | solution.py:190
  56.0 2.1 %collective-permute-start.6 = (bf16[4,64,128]{2,1,0:T(8,128)(2,1)S(1)}, bf16[4,64,128]{2,1,0:T(8,128)(2,1)S(1)}, u32[]{:S(2)}, u32[]{:S(2)}) collective-permute-start(bf16[4,64,128]{2,1,0:T(8,128)(2,1)S(1)} %get-tuple-element.56), channel_id=1, source_target_pairs={{0,1},{1,0},{2,3},{3,2},{4,5},{5,4},{6,7},{7,6},{8,9},{9,8},{10,11... | collective-permute-start | bytes 196616 | tf_op jit(solution)/shard_map/ppermute | solution.py:23
  58.1 1.5 %collective-permute-start.10 = (bf16[2,128,1024]{2,1,0:T(8,128)(2,1)S(1)}, bf16[2,128,1024]{2,1,0:T(8,128)(2,1)S(1)}, u32[]{:S(2)}, u32[]{:S(2)}) collective-permute-start(bf16[2,128,1024]{2,1,0:T(8,128)(2,1)S(1)} %pad_maximum_fusion), channel_id=1, source_target_pairs={{0,8},{4,12},{8,0},{12,4},{1,9},{5,13},{9,1},{13,5},{2,10},{6,14},... | collective-permute-start | bytes 1572872 | tf_op jit(solution)/shard_map/ppermute | solution.py:23
  60.5 2.9 %collective-permute-start.8 = (bf16[4,64,128]{2,1,0:T(8,128)(2,1)S(1)}, bf16[4,64,128]{2,1,0:T(8,128)(2,1)S(1)}, u32[]{:S(2)}, u32[]{:S(2)}) collective-permute-start(bf16[4,64,128]{2,1,0:T(8,128)(2,1)S(1)} %fusion.6), channel_id=1, source_target_pairs={{0,2},{1,3},{2,0},{3,1},{4,6},{5,7},{6,4},{7,5},{8,10},{9,11},{10,... | collective-permute-start | bytes 196616 | tf_op jit(solution)/shard_map/ppermute | solution.py:23
  63.5 1.5 %collective-permute-start.14 = (bf16[2,128,512]{2,1,0:T(8,128)(2,1)S(1)}, bf16[2,128,512]{2,1,0:T(8,128)(2,1)S(1)}, u32[]{:S(2)}, u32[]{:S(2)}) collective-permute-start(bf16[2,128,512]{2,1,0:T(8,128)(2,1)S(1)} %collective-permute-done.7.refs_8_), channel_id=1, source_target_pairs={{0,16},{16,0},{1,17},{17,1},{2,18},{18,2},{3,19},{19,3},{4,20},{20... | collective-permute-start | bytes 786440 | tf_op jit(solution)/shard_map/ppermute | solution.py:23
  65.8 6.0 %collective-permute-done.10.refs_6_ = bf16[2,128,1024]{2,1,0:T(8,128)(2,1)S(1)} collective-permute-done((bf16[2,128,1024]{2,1,0:T(8,128)(2,1)S(1)}, bf16[2,128,1024]{2,1,0:T(8,128)(2,1)S(1)}, u32[]{:S(2)}, u32[]{:S(2)}) %collective-permute-start.10) | collective-permute-done | bytes 524320 | tf_op jit(solution)/shard_map/ppermute | solution.py:23
  71.8 1.5 %collective-permute-start.18 = (bf16[2,128,1024]{2,1,0:T(8,128)(2,1)S(1)}, bf16[2,128,1024]{2,1,0:T(8,128)(2,1)S(1)}, u32[]{:S(2)}, u32[]{:S(2)}) collective-permute-start(bf16[2,128,1024]{2,1,0:T(8,128)(2,1)S(1)} %collective-permute-done.10.refs_6_), channel_id=1, source_target_pairs={{0,16},{16,0},{1,17},{17,1},{2,18},{18,2},{3,19},{19,3},{4,20},{20... | collective-permute-start | bytes 1572872 | tf_op jit(solution)/shard_map/ppermute | solution.py:23
  74.8 1.5 %collective-permute-start.11 = (bf16[4,64,128]{2,1,0:T(8,128)(2,1)S(1)}, bf16[4,64,128]{2,1,0:T(8,128)(2,1)S(1)}, u32[]{:S(2)}, u32[]{:S(2)}) collective-permute-start(bf16[4,64,128]{2,1,0:T(8,128)(2,1)S(1)} %get-tuple-element.83), channel_id=1, source_target_pairs={{0,8},{4,12},{8,0},{12,4},{1,9},{5,13},{9,1},{13,5},{2,10},{6,14},... | collective-permute-start | bytes 196616 | tf_op jit(solution)/shard_map/ppermute | solution.py:23
  76.3 3.2 %base.9 = f32[256,512]{1,0:T(8,128)S(1)} custom-call(bf16[128,3584]{1,0:T(8,128)(2,1)} %collective-permute-done.1.refs_1_.refs_0_, bf16[128,3584]{1,0:T(8,128)(2,1)S(1)} %collective-permute-done.5.refs_2_.refs_1_.refs_4_, f32[256,512]{1,0:T(8,128)S(1)} %base.7.refs_2_, bf16[7168,2048]{1,0:T(8,128)(2,1)} %refs_5_.1), custom_call_target="tpu_custom_call" | custom-call | flops 939524 | bytes 6029 | tf_op jit(solution)/shard_map/base/pallas_call | solution.py:69
  79.7 2.1 %combine.3 = (f32[2,128,512]{2,1,0:T(8,128)S(1)}, bf16[2,128,512]{2,1,0:T(8,128)(2,1)}, bf16[512,1024]{1,0:T(8,128)(2,1)S(1)}) custom-call(s32[10]{0:T(128)S(1)} %stack.67.refs_0_, f32[4,64,128]{2,1,0:T(8,128)S(1)} %get-tuple-element.84.refs_1_, bf16[4,64,128]{2,1,0:T(8,128)(2,1)S(1)} %collective-permute-done.11.refs_2_, ...), custom_call_target="tpu_custom_call" | custom-call | flops 536870 | bytes 2752 | tf_op jit(solution)/shard_map/combine/pallas_call | solution.py:283
  82.7 2.0 %collective-permute-done.18.refs_8_ = bf16[2,128,1024]{2,1,0:T(8,128)(2,1)S(1)} collective-permute-done((bf16[2,128,1024]{2,1,0:T(8,128)(2,1)S(1)}, bf16[2,128,1024]{2,1,0:T(8,128)(2,1)S(1)}, u32[]{:S(2)}, u32[]{:S(2)}) %collective-permute-start.18) | collective-permute-done | bytes 524320 | tf_op jit(solution)/shard_map/ppermute | solution.py:23
  84.6 1.4 %collective-permute-start.22 = (bf16[2,128,512]{2,1,0:T(8,128)(2,1)S(1)}, bf16[2,128,512]{2,1,0:T(8,128)(2,1)}, u32[]{:S(2)}, u32[]{:S(2)}) collective-permute-start(bf16[2,128,512]{2,1,0:T(8,128)(2,1)S(1)} %get-tuple-element.77), channel_id=1, source_target_pairs={{0,8},{4,12},{8,0},{12,4},{1,9},{5,13},{9,1},{13,5},{2,10},{6,14},... | collective-permute-start | bytes 786440 | tf_op jit(solution)/shard_map/ppermute | solution.py:23
  86.5 6.9 %collective-permute-done.22.refs_6_ = bf16[2,128,512]{2,1,0:T(8,128)(2,1)} collective-permute-done((bf16[2,128,512]{2,1,0:T(8,128)(2,1)S(1)}, bf16[2,128,512]{2,1,0:T(8,128)(2,1)}, u32[]{:S(2)}, u32[]{:S(2)}) %collective-permute-start.22) | collective-permute-done | bytes 262176 | tf_op jit(solution)/shard_map/ppermute | solution.py:23
  93.4 1.5 %collective-permute-start.24 = (bf16[2,128,512]{2,1,0:T(8,128)(2,1)}, bf16[2,128,512]{2,1,0:T(8,128)(2,1)}, u32[]{:S(2)}, u32[]{:S(2)}) collective-permute-start(bf16[2,128,512]{2,1,0:T(8,128)(2,1)} %collective-permute-done.22.refs_6_), channel_id=1, source_target_pairs={{0,16},{16,0},{1,17},{17,1},{2,18},{18,2},{3,19},{19,3},{4,20},{20... | collective-permute-start | bytes 786440 | tf_op jit(solution)/shard_map/ppermute | solution.py:23
  95.0 5.6 %base.10 = f32[256,1024]{1,0:T(8,128)S(1)} custom-call(bf16[128,3584]{1,0:T(8,128)(2,1)} %collective-permute-done.1.refs_1_.refs_0_, bf16[128,3584]{1,0:T(8,128)(2,1)S(1)} %collective-permute-done.5.refs_2_.refs_1_.refs_4_, f32[256,1024]{1,0:T(8,128)S(1)} %base.8.refs_2_, bf16[7168,2048]{1,0:T(8,128)(2,1)} %refs_5_.1), custom_call_target="tpu_custom_call" | custom-call | flops 1879048 | bytes 10223 | tf_op jit(solution)/shard_map/base/pallas_call | solution.py:69
  100.6 3.1 %combine.4 = (f32[2,128,1024]{2,1,0:T(8,128)S(1)}, bf16[2,128,1024]{2,1,0:T(8,128)(2,1)}) custom-call(s32[10]{0:T(128)S(1)} %stack.67.refs_0_, bf16[512,1024]{1,0:T(8,128)(2,1)S(1)} %get-tuple-element.69.refs_1_, f32[2,128,2048]{2,1,0:T(8,128)S(1)} %bitcast.47, f32[2,128,1024]{2,1,0:T(8,128)S(1)} %bitcast.49, bf16[256,8192]{1,0:T(8,128)(2,1)S(1)} %copy-done, ...), custom_call_target="tpu_custom_call" | custom-call | flops 1073741 | bytes 5505 | tf_op jit(solution)/shard_map/combine/pallas_call | solution.py:283
  106.9 2.7 %collective-permute-start.20 = (bf16[128,512]{1,0:T(8,128)(2,1)S(1)}, bf16[128,512]{1,0:T(8,128)(2,1)S(1)}, u32[]{:S(2)}, u32[]{:S(2)}) collective-permute-start(bf16[128,512]{1,0:T(8,128)(2,1)S(1)} %fusion.4), channel_id=1, source_target_pairs={{0,2},{1,3},{2,0},{3,1},{4,6},{5,7},{6,4},{7,5},{8,10},{9,11},{10,... | collective-permute-start | bytes 393224 | tf_op jit(solution)/shard_map/ppermute | solution.py:23
  111.8 5.0 %base.11 = f32[256,512]{1,0:T(8,128)S(1)} custom-call(bf16[128,3584]{1,0:T(8,128)(2,1)S(1)} %collective-permute-done.2.refs_1_.refs_0_, bf16[128,3584]{1,0:T(8,128)(2,1)} %collective-permute-done.1.refs_1_.refs_0_, bf16[128,1792]{1,0:T(8,128)(2,1)S(1)} %collective-permute-done.3.refs_2_.refs_1_, bf16[128,1792]{1,0:T(8,128)(2,1)S(1)} %copy-done.9, ...), custom_call_target="tpu_custom_call" | custom-call | flops 1879048 | bytes 11534 | tf_op jit(solution)/shard_map/base/pallas_call | solution.py:69
  116.8 2.3 %combine.5 = (f32[2,128,512]{2,1,0:T(8,128)S(1)}, bf16[2,128,512]{2,1,0:T(8,128)(2,1)S(1)}) custom-call(s32[10]{0:T(128)S(1)} %stack.67.refs_0_, bf16[512,1024]{1,0:T(8,128)(2,1)S(1)} %copy-done.11, f32[2,128,2048]{2,1,0:T(8,128)S(1)} %bitcast.48, f32[2,128,512]{2,1,0:T(8,128)S(1)} %bitcast.51, bf16[256,8192]{1,0:T(8,128)(2,1)S(1)} %copy-done.1, ...), custom_call_target="tpu_custom_call" | custom-call | flops 536870 | bytes 2752 | tf_op jit(solution)/shard_map/combine/pallas_call | solution.py:283
  119.1 1.6 %collective-permute-start.27 = (bf16[2,128,512]{2,1,0:T(8,128)(2,1)S(1)}, bf16[2,128,512]{2,1,0:T(8,128)(2,1)S(1)}, u32[]{:S(2)}, u32[]{:S(2)}) collective-permute-start(bf16[2,128,512]{2,1,0:T(8,128)(2,1)S(1)} %get-tuple-element.80), channel_id=1, source_target_pairs={{0,1},{1,0},{2,3},{3,2},{4,5},{5,4},{6,7},{7,6},{8,9},{9,8},{10,11... | collective-permute-start | bytes 786440 | tf_op jit(solution)/shard_map/ppermute | solution.py:23
  123.6 7.1 %collective-permute-done.27 = bf16[2,128,512]{2,1,0:T(8,128)(2,1)S(1)} collective-permute-done((bf16[2,128,512]{2,1,0:T(8,128)(2,1)S(1)}, bf16[2,128,512]{2,1,0:T(8,128)(2,1)S(1)}, u32[]{:S(2)}, u32[]{:S(2)}) %collective-permute-start.27) | collective-permute-done | bytes 262176 | tf_op jit(solution)/shard_map/ppermute | solution.py:23
  131.1 10.9 %collective-permute-done.28 = bf16[128,512]{1,0:T(8,128)(2,1)S(1)} collective-permute-done((bf16[128,512]{1,0:T(8,128)(2,1)S(1)}, bf16[128,512]{1,0:T(8,128)(2,1)S(1)}, u32[]{:S(2)}, u32[]{:S(2)}) %collective-permute-start.28) | collective-permute-done | bytes 131104 | tf_op jit(solution)/shard_map/ppermute | solution.py:23
  (104 shorter events, 22.2 us)
Async XLA Ops:
  0.0 12.6 %collective-permute-start = (bf16[128,7168]{1,0:T(8,128)(2,1)}, bf16[128,7168]{1,0:T(8,128)(2,1)}, u32[]{:S(2)}, u32[]{:S(2)}) collective-permute-start(bf16[128,7168]{1,0:T(8,128)(2,1)} %refs_0_), channel_id=1, source_target_pairs={{0,4},{4,0},{8,12},{12,8},{1,5},{5,1},{9,13},{13,9},{2,6},{6,2},{1... | collective-permute-start | bytes 5505032 | tf_op jit(solution)/shard_map/ppermute | solution.py:23
  2.6 30.8 %collective-permute-start.2 = (bf16[128,3584]{1,0:T(8,128)(2,1)}, bf16[128,3584]{1,0:T(8,128)(2,1)S(1)}, u32[]{:S(2)}, u32[]{:S(2)}) collective-permute-start(bf16[128,3584]{1,0:T(8,128)(2,1)} %slice.36), channel_id=1, source_target_pairs={{0,8},{4,12},{8,0},{12,4},{1,9},{5,13},{9,1},{13,5},{2,10},{6,14},... | collective-permute-start | bytes 2752520 | tf_op jit(solution)/shard_map/ppermute | solution.py:23
  7.3 41.2 %collective-permute-start.1 = (bf16[128,3584]{1,0:T(8,128)(2,1)}, bf16[128,3584]{1,0:T(8,128)(2,1)}, u32[]{:S(2)}, u32[]{:S(2)}) collective-permute-start(bf16[128,3584]{1,0:T(8,128)(2,1)} %slice.37), channel_id=1, source_target_pairs={{0,8},{4,12},{8,0},{12,4},{1,9},{5,13},{9,1},{13,5},{2,10},{6,14},... | collective-permute-start | bytes 2752520 | tf_op jit(solution)/shard_map/ppermute | solution.py:23
  33.5 1.9 %collective-permute-start.3 = (bf16[128,1792]{1,0:T(8,128)(2,1)S(1)}, bf16[128,1792]{1,0:T(8,128)(2,1)S(1)}, u32[]{:S(2)}, u32[]{:S(2)}) collective-permute-start(bf16[128,1792]{1,0:T(8,128)(2,1)S(1)} %get-tuple-element.92), channel_id=1, source_target_pairs={{0,4},{4,0},{8,12},{12,8},{1,5},{5,1},{9,13},{13,9},{2,6},{6,2},{1... | collective-permute-start | bytes 1376264 | tf_op jit(solution)/shard_map/ppermute | solution.py:23
  33.8 2.2 %collective-permute-start.4 = (bf16[128,1792]{1,0:T(8,128)(2,1)S(1)}, bf16[128,1792]{1,0:T(8,128)(2,1)S(1)}, u32[]{:S(2)}, u32[]{:S(2)}) collective-permute-start(bf16[128,1792]{1,0:T(8,128)(2,1)S(1)} %get-tuple-element.91), channel_id=1, source_target_pairs={{0,4},{4,0},{8,12},{12,8},{1,5},{5,1},{9,13},{13,9},{2,6},{6,2},{1... | collective-permute-start | bytes 1376264 | tf_op jit(solution)/shard_map/ppermute | solution.py:23
  48.5 2.7 %collective-permute-start.5 = (bf16[128,3584]{1,0:T(8,128)(2,1)}, bf16[128,3584]{1,0:T(8,128)(2,1)S(1)}, u32[]{:S(2)}, u32[]{:S(2)}) collective-permute-start(bf16[128,3584]{1,0:T(8,128)(2,1)} %collective-permute-done.1.refs_1_.refs_0_), channel_id=1, source_target_pairs={{0,4},{4,0},{8,12},{12,8},{1,5},{5,1},{9,13},{13,9},{2,6},{6,2},{1... | collective-permute-start | bytes 2752520 | tf_op jit(solution)/shard_map/ppermute | solution.py:23
  48.8 10.8 %collective-permute-start.7 = (bf16[2,128,512]{2,1,0:T(8,128)(2,1)S(1)}, bf16[2,128,512]{2,1,0:T(8,128)(2,1)S(1)}, u32[]{:S(2)}, u32[]{:S(2)}) collective-permute-start(bf16[2,128,512]{2,1,0:T(8,128)(2,1)S(1)} %get-tuple-element.57), channel_id=1, source_target_pairs={{0,8},{4,12},{8,0},{12,4},{1,9},{5,13},{9,1},{13,5},{2,10},{6,14},... | collective-permute-start | bytes 786440 | tf_op jit(solution)/shard_map/ppermute | solution.py:23
  51.2 43.7 %copy-start.4 = (bf16[128,3584]{1,0:T(8,128)(2,1)}, bf16[128,3584]{1,0:T(8,128)(2,1)S(1)}, u32[]{:S(2)}) copy-start(bf16[128,3584]{1,0:T(8,128)(2,1)S(1)} %collective-permute-done.5.refs_2_.refs_1_.refs_4_) | copy-start | bytes 2752516
  56.0 4.5 %collective-permute-start.6 = (bf16[4,64,128]{2,1,0:T(8,128)(2,1)S(1)}, bf16[4,64,128]{2,1,0:T(8,128)(2,1)S(1)}, u32[]{:S(2)}, u32[]{:S(2)}) collective-permute-start(bf16[4,64,128]{2,1,0:T(8,128)(2,1)S(1)} %get-tuple-element.56), channel_id=1, source_target_pairs={{0,1},{1,0},{2,3},{3,2},{4,5},{5,4},{6,7},{7,6},{8,9},{9,8},{10,11... | collective-permute-start | bytes 196616 | tf_op jit(solution)/shard_map/ppermute | solution.py:23
  58.1 13.7 %collective-permute-start.10 = (bf16[2,128,1024]{2,1,0:T(8,128)(2,1)S(1)}, bf16[2,128,1024]{2,1,0:T(8,128)(2,1)S(1)}, u32[]{:S(2)}, u32[]{:S(2)}) collective-permute-start(bf16[2,128,1024]{2,1,0:T(8,128)(2,1)S(1)} %pad_maximum_fusion), channel_id=1, source_target_pairs={{0,8},{4,12},{8,0},{12,4},{1,9},{5,13},{9,1},{13,5},{2,10},{6,14},... | collective-permute-start | bytes 1572872 | tf_op jit(solution)/shard_map/ppermute | solution.py:23
  59.6 20.1 %collective-permute-start.12 = (bf16[256,2048]{1,0:T(8,128)(2,1)S(1)}, bf16[256,2048]{1,0:T(8,128)(2,1)S(1)}, u32[]{:S(2)}, u32[]{:S(2)}) collective-permute-start(bf16[256,2048]{1,0:T(8,128)(2,1)S(1)} %constant_dynamic-slice_fusion), channel_id=1, source_target_pairs={{0,4},{4,0},{8,12},{12,8},{1,5},{5,1},{9,13},{13,9},{2,6},{6,2},{1... | collective-permute-start | bytes 3145736 | tf_op jit(solution)/shard_map/ppermute | solution.py:23
  60.5 5.3 %collective-permute-start.8 = (bf16[4,64,128]{2,1,0:T(8,128)(2,1)S(1)}, bf16[4,64,128]{2,1,0:T(8,128)(2,1)S(1)}, u32[]{:S(2)}, u32[]{:S(2)}) collective-permute-start(bf16[4,64,128]{2,1,0:T(8,128)(2,1)S(1)} %fusion.6), channel_id=1, source_target_pairs={{0,2},{1,3},{2,0},{3,1},{4,6},{5,7},{6,4},{7,5},{8,10},{9,11},{10,... | collective-permute-start | bytes 196616 | tf_op jit(solution)/shard_map/ppermute | solution.py:23
  63.5 11.1 %collective-permute-start.14 = (bf16[2,128,512]{2,1,0:T(8,128)(2,1)S(1)}, bf16[2,128,512]{2,1,0:T(8,128)(2,1)S(1)}, u32[]{:S(2)}, u32[]{:S(2)}) collective-permute-start(bf16[2,128,512]{2,1,0:T(8,128)(2,1)S(1)} %collective-permute-done.7.refs_8_), channel_id=1, source_target_pairs={{0,16},{16,0},{1,17},{17,1},{2,18},{18,2},{3,19},{19,3},{4,20},{20... | collective-permute-start | bytes 786440 | tf_op jit(solution)/shard_map/ppermute | solution.py:23
  71.8 12.8 %collective-permute-start.18 = (bf16[2,128,1024]{2,1,0:T(8,128)(2,1)S(1)}, bf16[2,128,1024]{2,1,0:T(8,128)(2,1)S(1)}, u32[]{:S(2)}, u32[]{:S(2)}) collective-permute-start(bf16[2,128,1024]{2,1,0:T(8,128)(2,1)S(1)} %collective-permute-done.10.refs_6_), channel_id=1, source_target_pairs={{0,16},{16,0},{1,17},{17,1},{2,18},{18,2},{3,19},{19,3},{4,20},{20... | collective-permute-start | bytes 1572872 | tf_op jit(solution)/shard_map/ppermute | solution.py:23
  73.3 1.3 collective-permute-start.9
  73.3 6.4 %collective-permute-start.13 = (bf16[2,128,512]{2,1,0:T(8,128)(2,1)S(1)}, bf16[2,128,512]{2,1,0:T(8,128)(2,1)S(1)}, u32[]{:S(2)}, u32[]{:S(2)}) collective-permute-start(bf16[2,128,512]{2,1,0:T(8,128)(2,1)S(1)} %collective-permute-done.7.refs_8_), channel_id=1, source_target_pairs={{0,4},{4,0},{8,12},{12,8},{1,5},{5,1},{9,13},{13,9},{2,6},{6,2},{1... | collective-permute-start | bytes 786440 | tf_op jit(solution)/shard_map/ppermute | solution.py:23
  74.6 5.1 %collective-permute-start.15 = (bf16[2,128,512]{2,1,0:T(8,128)(2,1)S(1)}, bf16[2,128,512]{2,1,0:T(8,128)(2,1)S(1)}, u32[]{:S(2)}, u32[]{:S(2)}) collective-permute-start(bf16[2,128,512]{2,1,0:T(8,128)(2,1)S(1)} %collective-permute-done.14.refs_10_), channel_id=1, source_target_pairs={{0,4},{4,0},{8,12},{12,8},{1,5},{5,1},{9,13},{13,9},{2,6},{6,2},{1... | collective-permute-start | bytes 786440 | tf_op jit(solution)/shard_map/ppermute | solution.py:23
  74.8 4.8 %collective-permute-start.11 = (bf16[4,64,128]{2,1,0:T(8,128)(2,1)S(1)}, bf16[4,64,128]{2,1,0:T(8,128)(2,1)S(1)}, u32[]{:S(2)}, u32[]{:S(2)}) collective-permute-start(bf16[4,64,128]{2,1,0:T(8,128)(2,1)S(1)} %get-tuple-element.83), channel_id=1, source_target_pairs={{0,8},{4,12},{8,0},{12,4},{1,9},{5,13},{9,1},{13,5},{2,10},{6,14},... | collective-permute-start | bytes 196616 | tf_op jit(solution)/shard_map/ppermute | solution.py:23
  79.5 21.0 %collective-permute-start.17 = (bf16[2,128,1024]{2,1,0:T(8,128)(2,1)S(1)}, bf16[2,128,1024]{2,1,0:T(8,128)(2,1)S(1)}, u32[]{:S(2)}, u32[]{:S(2)}) collective-permute-start(bf16[2,128,1024]{2,1,0:T(8,128)(2,1)S(1)} %collective-permute-done.10.refs_6_), channel_id=1, source_target_pairs={{0,4},{4,0},{8,12},{12,8},{1,5},{5,1},{9,13},{13,9},{2,6},{6,2},{1... | collective-permute-start | bytes 1572872 | tf_op jit(solution)/shard_map/ppermute | solution.py:23
  79.7 20.9 %copy-start.6 = (bf16[256,2048]{1,0:T(8,128)(2,1)}, bf16[256,2048]{1,0:T(8,128)(2,1)S(1)}, u32[]{:S(2)}) copy-start(bf16[256,2048]{1,0:T(8,128)(2,1)S(1)} %collective-permute-done.12.refs_7_.refs_5_) | copy-start | bytes 3145732
  82.7 17.9 %copy-start.10 = (bf16[512,1024]{1,0:T(8,128)(2,1)}, bf16[512,1024]{1,0:T(8,128)(2,1)S(1)}, u32[]{:S(2)}) copy-start(bf16[512,1024]{1,0:T(8,128)(2,1)S(1)} %get-tuple-element.69.refs_1_) | copy-start | bytes 3145732
  84.6 15.9 %collective-permute-start.19 = (bf16[2,128,1024]{2,1,0:T(8,128)(2,1)S(1)}, bf16[2,128,1024]{2,1,0:T(8,128)(2,1)S(1)}, u32[]{:S(2)}, u32[]{:S(2)}) collective-permute-start(bf16[2,128,1024]{2,1,0:T(8,128)(2,1)S(1)} %collective-permute-done.18.refs_8_), channel_id=1, source_target_pairs={{0,4},{4,0},{8,12},{12,8},{1,5},{5,1},{9,13},{13,9},{2,6},{6,2},{1... | collective-permute-start | bytes 1572872 | tf_op jit(solution)/shard_map/ppermute | solution.py:23
  84.6 8.8 %collective-permute-start.22 = (bf16[2,128,512]{2,1,0:T(8,128)(2,1)S(1)}, bf16[2,128,512]{2,1,0:T(8,128)(2,1)}, u32[]{:S(2)}, u32[]{:S(2)}) collective-permute-start(bf16[2,128,512]{2,1,0:T(8,128)(2,1)S(1)} %get-tuple-element.77), channel_id=1, source_target_pairs={{0,8},{4,12},{8,0},{12,4},{1,9},{5,13},{9,1},{13,5},{2,10},{6,14},... | collective-permute-start | bytes 786440 | tf_op jit(solution)/shard_map/ppermute | solution.py:23
  86.1 19.1 %collective-permute-start.16 = (bf16[2,128,512]{2,1,0:T(8,128)(2,1)}, bf16[2,128,512]{2,1,0:T(8,128)(2,1)}, u32[]{:S(2)}, u32[]{:S(2)}) collective-permute-start(bf16[2,128,512]{2,1,0:T(8,128)(2,1)} %get-tuple-element.68), channel_id=1, source_target_pairs={{0,1},{1,0},{2,3},{3,2},{4,5},{5,4},{6,7},{7,6},{8,9},{9,8},{10,11... | collective-permute-start | bytes 786440 | tf_op jit(solution)/shard_map/ppermute | solution.py:23
  93.4 11.7 %collective-permute-start.24 = (bf16[2,128,512]{2,1,0:T(8,128)(2,1)}, bf16[2,128,512]{2,1,0:T(8,128)(2,1)}, u32[]{:S(2)}, u32[]{:S(2)}) collective-permute-start(bf16[2,128,512]{2,1,0:T(8,128)(2,1)} %collective-permute-done.22.refs_6_), channel_id=1, source_target_pairs={{0,16},{16,0},{1,17},{17,1},{2,18},{18,2},{3,19},{19,3},{4,20},{20... | collective-permute-start | bytes 786440 | tf_op jit(solution)/shard_map/ppermute | solution.py:23
  104.7 16.4 %collective-permute-start.21 = (bf16[2,128,1024]{2,1,0:T(8,128)(2,1)}, bf16[2,128,1024]{2,1,0:T(8,128)(2,1)}, u32[]{:S(2)}, u32[]{:S(2)}) collective-permute-start(bf16[2,128,1024]{2,1,0:T(8,128)(2,1)} %get-tuple-element.72), channel_id=1, source_target_pairs={{0,1},{1,0},{2,3},{3,2},{4,5},{5,4},{6,7},{7,6},{8,9},{9,8},{10,11... | collective-permute-start | bytes 1572872 | tf_op jit(solution)/shard_map/ppermute | solution.py:23
  105.1 11.6 %collective-permute-start.23 = (bf16[2,128,512]{2,1,0:T(8,128)(2,1)}, bf16[2,128,512]{2,1,0:T(8,128)(2,1)S(1)}, u32[]{:S(2)}, u32[]{:S(2)}) collective-permute-start(bf16[2,128,512]{2,1,0:T(8,128)(2,1)} %collective-permute-done.22.refs_6_), channel_id=1, source_target_pairs={{0,4},{4,0},{8,12},{12,8},{1,5},{5,1},{9,13},{13,9},{2,6},{6,2},{1... | collective-permute-start | bytes 786440 | tf_op jit(solution)/shard_map/ppermute | solution.py:23
  105.1 11.6 %collective-permute-start.25 = (bf16[2,128,512]{2,1,0:T(8,128)(2,1)}, bf16[2,128,512]{2,1,0:T(8,128)(2,1)S(1)}, u32[]{:S(2)}, u32[]{:S(2)}) collective-permute-start(bf16[2,128,512]{2,1,0:T(8,128)(2,1)} %collective-permute-done.24.refs_8_), channel_id=1, source_target_pairs={{0,4},{4,0},{8,12},{12,8},{1,5},{5,1},{9,13},{13,9},{2,6},{6,2},{1... | collective-permute-start | bytes 786440 | tf_op jit(solution)/shard_map/ppermute | solution.py:23
  106.9 24.1 %collective-permute-start.20 = (bf16[128,512]{1,0:T(8,128)(2,1)S(1)}, bf16[128,512]{1,0:T(8,128)(2,1)S(1)}, u32[]{:S(2)}, u32[]{:S(2)}) collective-permute-start(bf16[128,512]{1,0:T(8,128)(2,1)S(1)} %fusion.4), channel_id=1, source_target_pairs={{0,2},{1,3},{2,0},{3,1},{4,6},{5,7},{6,4},{7,5},{8,10},{9,11},{10,... | collective-permute-start | bytes 393224 | tf_op jit(solution)/shard_map/ppermute | solution.py:23
  119.1 11.7 %collective-permute-start.27 = (bf16[2,128,512]{2,1,0:T(8,128)(2,1)S(1)}, bf16[2,128,512]{2,1,0:T(8,128)(2,1)S(1)}, u32[]{:S(2)}, u32[]{:S(2)}) collective-permute-start(bf16[2,128,512]{2,1,0:T(8,128)(2,1)S(1)} %get-tuple-element.80), channel_id=1, source_target_pairs={{0,1},{1,0},{2,3},{3,2},{4,5},{5,4},{6,7},{7,6},{8,9},{9,8},{10,11... | collective-permute-start | bytes 786440 | tf_op jit(solution)/shard_map/ppermute | solution.py:23
  122.4 19.7 %collective-permute-start.26 = (bf16[128,1024]{1,0:T(8,128)(2,1)S(1)}, bf16[128,1024]{1,0:T(8,128)(2,1)S(1)}, u32[]{:S(2)}, u32[]{:S(2)}) collective-permute-start(bf16[128,1024]{1,0:T(8,128)(2,1)S(1)} %fusion.1), channel_id=1, source_target_pairs={{0,2},{1,3},{2,0},{3,1},{4,6},{5,7},{6,4},{7,5},{8,10},{9,11},{10,... | collective-permute-start | bytes 786440 | tf_op jit(solution)/shard_map/ppermute | solution.py:23
  130.9 11.1 %collective-permute-start.28 = (bf16[128,512]{1,0:T(8,128)(2,1)S(1)}, bf16[128,512]{1,0:T(8,128)(2,1)S(1)}, u32[]{:S(2)}, u32[]{:S(2)}) collective-permute-start(bf16[128,512]{1,0:T(8,128)(2,1)S(1)} %fusion.5), channel_id=1, source_target_pairs={{0,2},{1,3},{2,0},{3,1},{4,6},{5,7},{6,4},{7,5},{8,10},{9,11},{10,... | collective-permute-start | bytes 393224 | tf_op jit(solution)/shard_map/ppermute | solution.py:23
  (12 other events, 57.1 us)

commit v5 on v4

--- a/solution.py
+++ b/solution.py
@@ -8,8 +8,8 @@
 F32 = jnp.float32
 BF16 = jnp.bfloat16
 VMEM_LIMIT = 40 * 1024 * 1024
-WIDTHS = (512, 1024, 512)
-EARLY = 2
+WIDTHS = (512, 512, 512, 512)
+EARLY = 3
 CAP = 4
 HALVES = 2
 HINT = 1000
@@ -35,7 +35,35 @@
     return pltpu.CompilerParams(vmem_limit_bytes=VMEM_LIMIT)
 
 
-def base_kernel(lower, upper, has_prior, *refs):
+def cut_kernel(ref, *refs):
+    outs, sems = refs[:-1], refs[-1]
+    copies, start = [], 0
+    for index, out in enumerate(outs):
+        wide = out.shape[1]
+        copies.append(
+            pltpu.make_async_copy(ref.at[:, pl.ds(start, wide)], out, sems.at[index])
+        )
+        start += wide
+    for copy in copies:
+        copy.start()
+    for copy in copies:
+        copy.wait()
+
+
+def cut_columns(array, widths):
+    return pl.pallas_call(
+        cut_kernel,
+        in_specs=[pl.BlockSpec(memory_space=pl.ANY)],
+        out_specs=[pl.BlockSpec(memory_space=pl.ANY)] * len(widths),
+        out_shape=[jax.ShapeDtypeStruct((array.shape[0], w), array.dtype) for w in widths],
+        scratch_shapes=[pltpu.SemaphoreType.DMA((len(widths),))],
+        compiler_params=params(),
+        cost_estimate=cost(0, 4 * array.size),
+        name="cut",
+    )(array)
+
+
+def product_kernel(lower, upper, has_prior, *refs):
     pieces, refs = refs[: lower + upper], refs[lower + upper :]
     if has_prior:
         prior_ref, refs = refs[0], refs[1:]
@@ -56,18 +84,18 @@
     out_ref[...] = value
 
 
-def product(lower, upper, weight, depth_block, prior, first, width, tile, prior_first=0):
+def product(lower, upper, weight, depth_block, prior, first, width, tile):
     rows = lower[0].shape[0]
     depth = sum(x.shape[1] for x in lower)
     args = [*lower, *upper]
     in_specs = [pl.BlockSpec(x.shape, lambda n: (0, 0)) for x in args]
     if prior is not None:
-        in_specs.append(pl.BlockSpec((2 * rows, tile), lambda n: (0, prior_first // tile + n)))
+        in_specs.append(pl.BlockSpec((2 * rows, tile), lambda n: (0, n)))
         args.append(prior)
     in_specs.append(pl.BlockSpec((depth, tile), lambda n: (depth_block, first // tile + n)))
     args.append(weight)
     return pl.pallas_call(
-        lambda *refs: base_kernel(len(lower), len(upper), prior is not None, *refs),
+        lambda *refs: product_kernel(len(lower), len(upper), prior is not None, *refs),
         grid=(width // tile,),
         in_specs=in_specs,
         out_specs=pl.BlockSpec((2 * rows, tile), lambda n: (0, n)),
@@ -81,19 +109,8 @@
     )(*args)
 
 
-def base_product(a, pieces, weight, depth_block=0, prior=None, first=0, width=None, tile=512):
-    width = weight.shape[1] if width is None else width
-    return product([a], pieces, weight, depth_block, prior, first, width, tile)
-
-
-def whole_product(a_pieces, b_pieces, weight, first, width, tile):
-    flat = [x for pieces in b_pieces for x in pieces]
-    return product(a_pieces, flat, weight, 0, None, first, width, tile)
-
-
 def scores_kernel(first, offset, count, has_prior, last, info_ref, *refs):
-    a_ref, pieces, maps_ref = refs[0], refs[1 : 1 + count], refs[1 + count]
-    refs = refs[2 + count :]
+    groups, maps_ref, refs = (refs[:count], refs[count : 2 * count]), refs[2 * count], refs[2 * count + 1 :]
     if has_prior:
         prior_ref, refs = refs[0], refs[1:]
     if first == 2 and last:
@@ -112,23 +129,26 @@
             map_sems.at[pair, k, part],
         )
 
-    row_copies = [pltpu.make_async_copy(a_ref, rows.at[0], row_sems.at[0])]
-    start = 0
-    for index, piece in enumerate(pieces):
-        row_copies.append(
-            pltpu.make_async_copy(
-                piece, rows.at[1, :, pl.ds(start, piece.shape[1])], row_sems.at[1 + index]
+    row_copies = []
+    for pair, pieces in enumerate(groups):
+        start = 0
+        for index, piece in enumerate(pieces):
+            row_copies.append(
+                pltpu.make_async_copy(
+                    piece,
+                    rows.at[pair, :, pl.ds(start, piece.shape[1])],
+                    row_sems.at[pair * count + index],
+                )
             )
-        )
-        start += piece.shape[1]
+            start += piece.shape[1]
     for pair in range(2):
-        for copy in row_copies[:1] if pair == 0 else row_copies[1:]:
+        for copy in row_copies[pair * count : (pair + 1) * count]:
             copy.start()
         for part in range(2):
             for k in range(CAP):
                 map_copy(pair, k, part).start()
     for pair in range(2):
-        for copy in row_copies[:1] if pair == 0 else row_copies[1:]:
+        for copy in row_copies[pair * count : (pair + 1) * count]:
             copy.wait()
         total = prior_ref[pair] if has_prior else None
         for part in range(2):
@@ -163,12 +183,13 @@
             outs[1][near_group] = near_ref[pair].astype(BF16)
 
 
-def scores(info, first, a, pieces, maps, half, prior=None, near=None, ids=None):
-    rows, depth = a.shape
+def scores(info, first, lower, upper, maps, half, prior=None, near=None, ids=None):
+    rows, depth = lower[0].shape[0], sum(x.shape[1] for x in lower)
     rank = maps.shape[1]
     has_prior, last = prior is not None, ids is not None
+    args_rows = [*lower, *upper]
     whole = lambda x: pl.BlockSpec(x.shape, lambda k, s: (0,) * x.ndim)
-    args = [a, *pieces, maps]
+    args = [*lower, *upper, maps]
     in_specs = [pl.BlockSpec(memory_space=pl.ANY)] * len(args)
     if has_prior:
         in_specs.append(whole(prior))
@@ -188,7 +209,7 @@
     else:
         out_shape = [jax.ShapeDtypeStruct((4, rank, rows), kind) for kind in (F32, BF16)]
     return pl.pallas_call(
-        lambda *refs: scores_kernel(first, half * depth, len(pieces), has_prior, last, *refs),
+        lambda *refs: scores_kernel(first, half * depth, len(lower), has_prior, last, *refs),
         grid_spec=pltpu.PrefetchScalarGridSpec(
             num_scalar_prefetch=1,
             grid=(1,),
@@ -197,7 +218,7 @@
             scratch_shapes=[
                 pltpu.VMEM((2, rows, depth), BF16),
                 pltpu.VMEM((2 * CAP, rank, depth), BF16),
-                pltpu.SemaphoreType.DMA((1 + len(pieces),)),
+                pltpu.SemaphoreType.DMA((len(args_rows),)),
                 pltpu.SemaphoreType.DMA((2, CAP, 2)),
             ],
         ),
@@ -312,11 +333,9 @@
 
     part = depth // HALVES
     near_b = swap(hidden, "pool", 1)
-    crossed, block = [], None
-    for h in range(HALVES):
-        source = hidden if block is None else tie(hidden, block)
-        block = source[:, h * part : (h + 1) * part]
-        crossed.append(swap(block, "pool", 2))
+    first_a, first_b, second = (
+        swap(block, "pool", 2) for block in cut_columns(hidden, (part // 2, part // 2, part))
+    )
 
     core_block = lax.dynamic_slice(output_maps, (0, (place ^ 1) * width), (held, width))
     blocks = [
@@ -374,56 +393,60 @@
     own_rows, near_b, picks, info, wide_ids, owned_ids, core_block, *blocks = ready
     core_maps = swap(core_block, "pool", 1)
 
-    (near_lowrank,) = scores(picks, 0, own_rows, [near_b], input_maps, 0, ids=owned_ids)
-    near_base = base_product(tie(own_rows, near_lowrank), [near_b], weight)
-    crossing = [swap(block, "pool", 2) for block in blocks[: count - 1]]
-
-    a0 = tie(crossed[0], near_base)
-    b0 = [swap(a0[:, k * (part // 2) : (k + 1) * (part // 2)], "pool", 1) for k in range(2)]
+    (near_lowrank,) = scores(picks, 0, [own_rows], [near_b], input_maps, 0, ids=owned_ids)
+    near_base = product(
+        [tie(own_rows, near_lowrank)], [near_b], weight, 0, None, 0, width, 512
+    )
+    crossing = [swap(blocks[0], "pool", 2)]
+
+    first_a, first_b = lax.optimization_barrier((first_a, first_b, near_base))[:2]
+    a0 = [first_a, first_b]
+    b0 = [swap(x, "pool", 1) for x in a0]
     (raw,) = scores(picks, 2, a0, b0, input_maps, 0)
     begun = []
-    a0 = tie(a0, raw)
+    after = raw
     for index in range(EARLY):
         begun.append(
-            base_product(a0, b0, weight, 0, None, starts[index], WIDTHS[index])
+            product(
+                [tie(first_a, after), first_b], b0, weight, 0, None, starts[index], WIDTHS[index], 512
+            )
         )
-        a0 = tie(a0, begun[-1])
-    a1 = tie(crossed[1], begun[-1])
-    b1 = [swap(a1, "pool", 1)]
+        after = begun[-1]
+    a1 = [tie(second, after)]
+    b1 = [swap(a1[0], "pool", 1)]
     total, sent = scores(
         picks, 2, a1, b1, input_maps, 1, prior=raw, near=near_lowrank, ids=owned_ids
     )
 
     def far_piece(index, after):
-        shape = (2, rows, WIDTHS[index])
-        left = tie(a1, after)
+        left = [tie(a1[0], after)]
         if index < EARLY:
-            piece = base_product(
+            piece = product(
                 left, b1, weight, 1, begun[index], starts[index], WIDTHS[index], 256
             )
         else:
-            piece = whole_product(
-                [crossed[0], left], [b0, b1], weight, starts[index], WIDTHS[index], 256
+            piece = product(
+                a0 + left, b0 + b1, weight, 0, None, starts[index], WIDTHS[index], 256
             )
-        return piece.reshape(shape)
-
-    hops = (("tensor", 1), ("tensor", 2), ("pool", 1), ("pool", 2))
-    arrivals = {0: 0, 2: 1}
-    pieces = []
-    for index, (axis, step) in enumerate(hops):
-        if index > 0:
-            sent = total.astype(BF16)
-        got = swap(sent, axis, step)
-        if index in arrivals:
-            chunk = arrivals[index]
-            crossing[chunk] = tie(crossing[chunk], sent)
-            got = tie(got, crossing[chunk])
-        if index == 3:
-            crossing.append(swap(tie(blocks[-1], sent), "pool", 2))
-            pieces.append(far_piece(0, sent))
-            got = tie(got, pieces[-1])
-            break
-        total = total + got.astype(F32)
+        return piece.reshape(2, rows, WIDTHS[index])
+
+    got = [swap(sent, "pool", step) for step in (2, 3, 1)]
+    crossing.append(swap(tie(blocks[1], sent), "pool", 2))
+    crossing[0] = tie(crossing[0], sent)
+    got[0] = tie(got[0], crossing[0])
+    total = total + sum(x.astype(F32) for x in got)
+    sent = total.astype(BF16)
+    got = swap(sent, "tensor", 1)
+    crossing.append(swap(tie(blocks[2], sent), "pool", 2))
+    crossing[1] = tie(crossing[1], sent)
+    got = tie(got, crossing[1])
+    total = total + got.astype(F32)
+    sent = total.astype(BF16)
+    got = swap(sent, "tensor", 2)
+    crossing.append(swap(tie(blocks[3], sent), "pool", 2))
+    crossing[2] = tie(crossing[2], sent)
+    pieces = [far_piece(0, sent)]
+    got = lax.optimization_barrier((got, crossing[2], pieces[0]))[0]
 
     def over_y(index, after):
         block = crossing[index] if after is None else tie(crossing[index], after)

time: 144 us -> 144 us (level)
  waiting for transfers between devices: 38.4 us -> 32.3 us
  Pallas kernels: 59.1 us -> 64 us
  starting transfers between devices: 27.7 us -> 32.3 us
  local copies, waits for them, and re-layouts: 11.3 us -> 9.36 us
    ppermute x29 -> x37, waiting for transfers between devices: 38.4 us -> 32.3 us  [swap(): return lax.ppermute(values, axis, partners(lax.axis_size(axis), step))]
    ppermute x29 -> x37, starting transfers between devices: 27.7 us -> 32.3 us  [swap(): return lax.ppermute(values, axis, partners(lax.axis_size(axis), step))]
    slice x3 -> x0, local copies, waits for them, and re-layouts: 4.41 us -> none  [the longest x2 4.35 us: per_device_fast(): block = source[:, h * part:(h + 1) * part]]
    pallas_call x9 -> x12, Pallas kernels: 51.6 us -> 54.9 us  [the longest x8 37.3 us: product(): pl.pallas_call(lambda *refs: product_kernel(len(lower), len(upper), prior...]
    unnamed x30 -> x42, local copies, waits for them, and re-layouts: 4.03 us -> 7.39 us
    pallas_call x3 -> x4, Pallas kernels: 7.55 us -> 9.03 us  [combine(): pl.pallas_call(lambda *refs: combine_kernel(bool(build), *refs), grid_spe...]
  transfers between devices with their start and end apart: 29 -> 37, of which waited for: 12 -> 10; matrix products, arithmetic and copies ran while one was open for 9% -> 5% of each run, Pallas kernels for 41% -> 44%
where the time goes in v5:
time: 144 us
  Pallas kernels  64 us (44%)
  starting transfers between devices  32.3 us (22%)
  waiting for transfers between devices  32.3 us (22%)
  local copies, waits for them, and re-layouts  9.36 us (6%)
  other arithmetic  5.59 us (4%)
    pallas_call x8, Pallas kernels, product(): pl.pallas_call(lambda *refs: product_kernel(len(lower), len(upper), prior...  37.3 us
    ppermute x37, starting transfers between devices, swap(): return lax.ppermute(values, axis, partners(lax.axis_size(axis), step))  32.3 us
    ppermute x37, waiting for transfers between devices, swap(): return lax.ppermute(values, axis, partners(lax.axis_size(axis), step))  32.3 us
    pallas_call x3, Pallas kernels, scores(): pl.pallas_call(lambda *refs: scores_kernel(first, half * depth, len(lower...  16.4 us
    pallas_call x4, Pallas kernels, combine(): pl.pallas_call(lambda *refs: combine_kernel(bool(build), *refs), grid_spe...  9.03 us
    unnamed x42, local copies, waits for them, and re-layouts  7.39 us
  transfers between devices with their start and end apart: 37, of which 10 were waited for; matrix products, arithmetic and copies ran while one was open for 5% of the time, Pallas kernels for 44%

profile of v5, /device:TPU:0, one launch (start us, length us, event | category | flops | bytes accessed | tf_op | source)
XLA Modules:
  0.0 144.0 jit_solution(930669922985605749)
XLA Ops:
  3.2 2.6 %collective-permute-start.2 = (bf16[128,1792]{1,0:T(8,128)(2,1)}, bf16[128,1792]{1,0:T(8,128)(2,1)S(1)}, u32[]{:S(2)}, u32[]{:S(2)}) collective-permute-start(bf16[128,1792]{1,0:T(8,128)(2,1)} %get-tuple-element.60), channel_id=1, source_target_pairs={{0,8},{4,12},{8,0},{12,4},{1,9},{5,13},{9,1},{13,5},{2,10},{6,14},... | collective-permute-start | bytes 1376264 | tf_op jit(solution)/shard_map/ppermute | solution.py:23
  5.9 1.9 %collective-permute-start.1 = (bf16[128,3584]{1,0:T(8,128)(2,1)}, bf16[128,3584]{1,0:T(8,128)(2,1)S(1)}, u32[]{:S(2)}, u32[]{:S(2)}) collective-permute-start(bf16[128,3584]{1,0:T(8,128)(2,1)} %get-tuple-element.59), channel_id=1, source_target_pairs={{0,8},{4,12},{8,0},{12,4},{1,9},{5,13},{9,1},{13,5},{2,10},{6,14},... | collective-permute-start | bytes 2752520 | tf_op jit(solution)/shard_map/ppermute | solution.py:23
  13.0 7.1 %scores.3.refs_5_ = f32[2,64,128]{2,1,0:T(8,128)S(1)} custom-call(s32[17]{0:T(128)S(1)} %pad_add_fusion.refs_0_, bf16[128,7168]{1,0:T(8,128)(2,1)S(1)} %copy-done.7, bf16[128,7168]{1,0:T(8,128)(2,1)} %collective-permute-done.refs_2_.refs_1_, bf16[16,64,7168]{2,1,0:T(8,128)(2,1)} %refs_3_.6, s32[4,1,128]{2,1,0:T(1,128)S(1)} %bitcast.65), custom_call_target="tpu_custom_call" | custom-call | flops 939524 | bytes 11010 | tf_op jit(solution)/shard_map/scores/pallas_call | solution.py:211
  20.1 13.5 %base.8 = f32[256,2048]{1,0:T(8,128)S(1)} custom-call(bf16[128,7168]{1,0:T(8,128)(2,1)S(1)} %copy-done.8, bf16[128,7168]{1,0:T(8,128)(2,1)} %collective-permute-done.refs_2_.refs_1_, bf16[7168,2048]{1,0:T(8,128)(2,1)} %refs_6_.3), custom_call_target="tpu_custom_call" | custom-call | flops 7516192 | bytes 35127 | tf_op jit(solution)/shard_map/base/pallas_call | solution.py:97
  36.4 4.8 %scores.4.refs_4_ = f32[2,256,128]{2,1,0:T(8,128)S(1)} custom-call(s32[17]{0:T(128)S(1)} %pad_add_fusion.refs_0_, bf16[128,1792]{1,0:T(8,128)(2,1)S(1)} %collective-permute-done.2.refs_1_.refs_0_, bf16[128,1792]{1,0:T(8,128)(2,1)} %collective-permute-done.3.refs_2_.refs_1_, bf16[128,1792]{1,0:T(8,128)(2,1)S(1)} %collective-permute-done.4.refs_3_.refs_2_, ...), custom_call_target="tpu_custom_call" | custom-call | flops 469762 | bytes 5505 | tf_op jit(solution)/shard_map/scores/pallas_call | solution.py:211
  41.2 3.3 %base.9.refs_2_ = f32[256,512]{1,0:T(8,128)S(1)} custom-call(bf16[128,1792]{1,0:T(8,128)(2,1)S(1)} %collective-permute-done.2.refs_1_.refs_0_, bf16[128,1792]{1,0:T(8,128)(2,1)} %collective-permute-done.3.refs_2_.refs_1_, bf16[128,1792]{1,0:T(8,128)(2,1)S(1)} %collective-permute-done.4.refs_3_.refs_2_, ...), custom_call_target="tpu_custom_call" | custom-call | flops 939524 | bytes 6029 | tf_op jit(solution)/shard_map/base/pallas_call | solution.py:97
  44.5 3.3 %base.10.refs_2_ = f32[256,512]{1,0:T(8,128)S(1)} custom-call(bf16[128,1792]{1,0:T(8,128)(2,1)S(1)} %collective-permute-done.2.refs_1_.refs_0_, bf16[128,1792]{1,0:T(8,128)(2,1)} %collective-permute-done.3.refs_2_.refs_1_, bf16[128,1792]{1,0:T(8,128)(2,1)S(1)} %collective-permute-done.4.refs_3_.refs_2_, ...), custom_call_target="tpu_custom_call" | custom-call | flops 939524 | bytes 6029 | tf_op jit(solution)/shard_map/base/pallas_call | solution.py:97
  48.6 3.3 %base.11.refs_2_ = f32[256,512]{1,0:T(8,128)S(1)} custom-call(bf16[128,1792]{1,0:T(8,128)(2,1)S(1)} %collective-permute-done.2.refs_1_.refs_0_, bf16[128,1792]{1,0:T(8,128)(2,1)} %collective-permute-done.3.refs_2_.refs_1_, bf16[128,1792]{1,0:T(8,128)(2,1)S(1)} %collective-permute-done.4.refs_3_.refs_2_, ...), custom_call_target="tpu_custom_call" | custom-call | flops 939524 | bytes 6029 | tf_op jit(solution)/shard_map/base/pallas_call | solution.py:97
  53.3 1.9 %collective-permute-done.6.refs_2_.refs_1_.refs_5_ = bf16[128,3584]{1,0:T(8,128)(2,1)S(1)} collective-permute-done((bf16[128,3584]{1,0:T(8,128)(2,1)S(1)}, bf16[128,3584]{1,0:T(8,128)(2,1)S(1)}, u32[]{:S(2)}, u32[]{:S(2)}) %collective-permute-start.6) | collective-permute-done | bytes 917536 | tf_op jit(solution)/shard_map/ppermute | solution.py:23
  55.1 4.5 %scores.5 = (f32[4,64,128]{2,1,0:T(8,128)S(1)}, bf16[4,64,128]{2,1,0:T(8,128)(2,1)S(1)}) custom-call(s32[17]{0:T(128)S(1)} %pad_add_fusion.refs_0_, bf16[128,3584]{1,0:T(8,128)(2,1)S(1)} %collective-permute-done.1.refs_1_.refs_0_.refs_2_, bf16[128,3584]{1,0:T(8,128)(2,1)S(1)} %collective-permute-done.6.refs_2_.refs_1_.refs_5_, ...), custom_call_target="tpu_custom_call" | custom-call | flops 469762 | bytes 5505 | tf_op jit(solution)/shard_map/scores/pallas_call | solution.py:211
  59.9 1.9 %collective-permute-start.9 = (bf16[4,64,128]{2,1,0:T(8,128)(2,1)S(1)}, bf16[4,64,128]{2,1,0:T(8,128)(2,1)S(1)}, u32[]{:S(2)}, u32[]{:S(2)}) collective-permute-start(bf16[4,64,128]{2,1,0:T(8,128)(2,1)S(1)} %get-tuple-element.73), channel_id=1, source_target_pairs={{0,12},{4,8},{8,4},{12,0},{1,13},{5,9},{9,5},{13,1},{2,14},{6,10},... | collective-permute-start | bytes 196616 | tf_op jit(solution)/shard_map/ppermute | solution.py:23
  61.9 2.7 %collective-permute-done.7 = bf16[4,64,128]{2,1,0:T(8,128)(2,1)S(1)} collective-permute-done((bf16[4,64,128]{2,1,0:T(8,128)(2,1)S(1)}, bf16[4,64,128]{2,1,0:T(8,128)(2,1)S(1)}, u32[]{:S(2)}, u32[]{:S(2)}) %collective-permute-start.7) | collective-permute-done | bytes 65568 | tf_op jit(solution)/shard_map/ppermute | solution.py:23
  66.2 1.6 %collective-permute-start.11 = (bf16[4,64,128]{2,1,0:T(8,128)(2,1)S(1)}, bf16[4,64,128]{2,1,0:T(8,128)(2,1)S(1)}, u32[]{:S(2)}, u32[]{:S(2)}) collective-permute-start(bf16[4,64,128]{2,1,0:T(8,128)(2,1)S(1)} %fusion.8), channel_id=1, source_target_pairs={{0,1},{1,0},{2,3},{3,2},{4,5},{5,4},{6,7},{7,6},{8,9},{9,8},{10,11... | collective-permute-start | bytes 196616 | tf_op jit(solution)/shard_map/ppermute | solution.py:23
  67.9 3.8 %collective-permute-done.12.refs_6_ = bf16[2,128,512]{2,1,0:T(8,128)(2,1)} collective-permute-done((bf16[2,128,512]{2,1,0:T(8,128)(2,1)S(1)}, bf16[2,128,512]{2,1,0:T(8,128)(2,1)}, u32[]{:S(2)}, u32[]{:S(2)}) %collective-permute-start.12) | collective-permute-done | bytes 262176 | tf_op jit(solution)/shard_map/ppermute | solution.py:23
  73.6 3.0 %collective-permute-done.14.refs_6_ = bf16[2,128,512]{2,1,0:T(8,128)(2,1)} collective-permute-done((bf16[2,128,512]{2,1,0:T(8,128)(2,1)S(1)}, bf16[2,128,512]{2,1,0:T(8,128)(2,1)}, u32[]{:S(2)}, u32[]{:S(2)}) %collective-permute-start.14) | collective-permute-done | bytes 262176 | tf_op jit(solution)/shard_map/ppermute | solution.py:23
  76.6 2.7 %collective-permute-start.13 = (bf16[4,64,128]{2,1,0:T(8,128)(2,1)S(1)}, bf16[4,64,128]{2,1,0:T(8,128)(2,1)S(1)}, u32[]{:S(2)}, u32[]{:S(2)}) collective-permute-start(bf16[4,64,128]{2,1,0:T(8,128)(2,1)S(1)} %get-tuple-element.109), channel_id=1, source_target_pairs={{0,2},{1,3},{2,0},{3,1},{4,6},{5,7},{6,4},{7,5},{8,10},{9,11},{10,... | collective-permute-start | bytes 196616 | tf_op jit(solution)/shard_map/ppermute | solution.py:23
  79.3 3.0 %base.12 = f32[256,512]{1,0:T(8,128)S(1)} custom-call(bf16[128,3584]{1,0:T(8,128)(2,1)S(1)} %collective-permute-done.1.refs_1_.refs_0_.refs_2_, bf16[128,3584]{1,0:T(8,128)(2,1)S(1)} %collective-permute-done.6.refs_2_.refs_1_.refs_5_, f32[256,512]{1,0:T(8,128)S(1)} %base.9.refs_2_, bf16[7168,2048]{1,0:T(8,128)(2,1)} %refs_6_.3), custom_call_target="tpu_custom_call" | custom-call | flops 939524 | bytes 6029 | tf_op jit(solution)/shard_map/base/pallas_call | solution.py:97
  83.2 2.2 %combine.4 = (f32[2,128,512]{2,1,0:T(8,128)S(1)}, bf16[2,128,512]{2,1,0:T(8,128)(2,1)}, bf16[512,1024]{1,0:T(8,128)(2,1)S(1)}) custom-call(s32[10]{0:T(128)S(1)} %stack.76.refs_0_, f32[4,64,128]{2,1,0:T(8,128)S(1)} %get-tuple-element.110.refs_1_, bf16[4,64,128]{2,1,0:T(8,128)(2,1)S(1)} %collective-permute-done.13.refs_2_, ...), custom_call_target="tpu_custom_call" | custom-call | flops 536870 | bytes 2752 | tf_op jit(solution)/shard_map/combine/pallas_call | solution.py:304
  87.3 1.6 %collective-permute-start.19 = (bf16[2,128,512]{2,1,0:T(8,128)(2,1)}, bf16[2,128,512]{2,1,0:T(8,128)(2,1)}, u32[]{:S(2)}, u32[]{:S(2)}) collective-permute-start(bf16[2,128,512]{2,1,0:T(8,128)(2,1)} %get-tuple-element.89), channel_id=1, source_target_pairs={{0,1},{1,0},{2,3},{3,2},{4,5},{5,4},{6,7},{7,6},{8,9},{9,8},{10,11... | collective-permute-start | bytes 786440 | tf_op jit(solution)/shard_map/ppermute | solution.py:23
  93.9 3.1 %base.13 = f32[256,512]{1,0:T(8,128)S(1)} custom-call(bf16[128,3584]{1,0:T(8,128)(2,1)S(1)} %collective-permute-done.1.refs_1_.refs_0_.refs_2_, bf16[128,3584]{1,0:T(8,128)(2,1)S(1)} %copy-done.3, f32[256,512]{1,0:T(8,128)S(1)} %copy-done.18, bf16[7168,2048]{1,0:T(8,128)(2,1)} %refs_6_.3), custom_call_target="tpu_custom_call" | custom-call | flops 939524 | bytes 6029 | tf_op jit(solution)/shard_map/base/pallas_call | solution.py:97
  98.6 2.4 %combine.5 = (f32[2,128,512]{2,1,0:T(8,128)S(1)}, bf16[2,128,512]{2,1,0:T(8,128)(2,1)S(1)}) custom-call(s32[10]{0:T(128)S(1)} %stack.76.refs_0_, bf16[512,1024]{1,0:T(8,128)(2,1)S(1)} %copy-done.14, f32[2,128,2048]{2,1,0:T(8,128)S(1)} %bitcast.58, f32[2,128,512]{2,1,0:T(8,128)S(1)} %bitcast.63, bf16[256,8192]{1,0:T(8,128)(2,1)S(1)} %copy-done.1, ...), custom_call_target="tpu_custom_call" | custom-call | flops 536870 | bytes 2752 | tf_op jit(solution)/shard_map/combine/pallas_call | solution.py:304
  101.0 1.6 %collective-permute-start.24 = (bf16[2,128,512]{2,1,0:T(8,128)(2,1)S(1)}, bf16[2,128,512]{2,1,0:T(8,128)(2,1)S(1)}, u32[]{:S(2)}, u32[]{:S(2)}) collective-permute-start(bf16[2,128,512]{2,1,0:T(8,128)(2,1)S(1)} %get-tuple-element.93), channel_id=1, source_target_pairs={{0,1},{1,0},{2,3},{3,2},{4,5},{5,4},{6,7},{7,6},{8,9},{9,8},{10,11... | collective-permute-start | bytes 786440 | tf_op jit(solution)/shard_map/ppermute | solution.py:23
  103.7 3.2 %base.14 = f32[256,512]{1,0:T(8,128)S(1)} custom-call(bf16[128,3584]{1,0:T(8,128)(2,1)S(1)} %collective-permute-done.1.refs_1_.refs_0_.refs_2_, bf16[128,3584]{1,0:T(8,128)(2,1)S(1)} %copy-done.3, f32[256,512]{1,0:T(8,128)S(1)} %copy-done.16, bf16[7168,2048]{1,0:T(8,128)(2,1)} %refs_6_.3), custom_call_target="tpu_custom_call" | custom-call | flops 939524 | bytes 6029 | tf_op jit(solution)/shard_map/base/pallas_call | solution.py:97
  106.9 2.7 %collective-permute-start.23 = (bf16[128,512]{1,0:T(8,128)(2,1)S(1)}, bf16[128,512]{1,0:T(8,128)(2,1)S(1)}, u32[]{:S(2)}, u32[]{:S(2)}) collective-permute-start(bf16[128,512]{1,0:T(8,128)(2,1)S(1)} %fusion.4), channel_id=1, source_target_pairs={{0,2},{1,3},{2,0},{3,1},{4,6},{5,7},{6,4},{7,5},{8,10},{9,11},{10,... | collective-permute-start | bytes 393224 | tf_op jit(solution)/shard_map/ppermute | solution.py:23
  109.7 2.3 %combine.6 = (f32[2,128,512]{2,1,0:T(8,128)S(1)}, bf16[2,128,512]{2,1,0:T(8,128)(2,1)S(1)}) custom-call(s32[10]{0:T(128)S(1)} %stack.76.refs_0_, bf16[512,1024]{1,0:T(8,128)(2,1)S(1)} %copy-done.14, f32[2,128,2048]{2,1,0:T(8,128)S(1)} %bitcast.59, f32[2,128,512]{2,1,0:T(8,128)S(1)} %bitcast.64, bf16[256,8192]{1,0:T(8,128)(2,1)S(1)} %copy-done.1, ...), custom_call_target="tpu_custom_call" | custom-call | flops 536870 | bytes 2752 | tf_op jit(solution)/shard_map/combine/pallas_call | solution.py:304
  112.9 4.1 %collective-permute-done.23 = bf16[128,512]{1,0:T(8,128)(2,1)S(1)} collective-permute-done((bf16[128,512]{1,0:T(8,128)(2,1)S(1)}, bf16[128,512]{1,0:T(8,128)(2,1)S(1)}, u32[]{:S(2)}, u32[]{:S(2)}) %collective-permute-start.23) | collective-permute-done | bytes 131104 | tf_op jit(solution)/shard_map/ppermute | solution.py:23
  117.1 4.7 %base.15 = f32[256,512]{1,0:T(8,128)S(1)} custom-call(bf16[128,1792]{1,0:T(8,128)(2,1)S(1)} %collective-permute-done.2.refs_1_.refs_0_, bf16[128,1792]{1,0:T(8,128)(2,1)} %collective-permute-done.3.refs_2_.refs_1_, bf16[128,3584]{1,0:T(8,128)(2,1)S(1)} %collective-permute-done.1.refs_1_.refs_0_.refs_2_, bf16[128,1792]{1,0:T(8,128)(2,1)S(1)} %copy-done.10, ...), custom_call_target="tpu_custom_call" | custom-call | flops 1879048 | bytes 11534 | tf_op jit(solution)/shard_map/base/pallas_call | solution.py:97
  121.9 2.2 %combine.7 = (f32[2,128,512]{2,1,0:T(8,128)S(1)}, bf16[2,128,512]{2,1,0:T(8,128)(2,1)S(1)}) custom-call(s32[10]{0:T(128)S(1)} %stack.76.refs_0_, bf16[512,1024]{1,0:T(8,128)(2,1)S(1)} %copy-done.14, f32[2,128,2048]{2,1,0:T(8,128)S(1)} %bitcast.60, f32[2,128,512]{2,1,0:T(8,128)S(1)} %bitcast.62, bf16[256,8192]{1,0:T(8,128)(2,1)S(1)} %copy-done.1, ...), custom_call_target="tpu_custom_call" | custom-call | flops 536870 | bytes 2752 | tf_op jit(solution)/shard_map/combine/pallas_call | solution.py:304
  124.1 1.8 %collective-permute-start.35 = (bf16[2,128,512]{2,1,0:T(8,128)(2,1)S(1)}, bf16[2,128,512]{2,1,0:T(8,128)(2,1)S(1)}, u32[]{:S(2)}, u32[]{:S(2)}) collective-permute-start(bf16[2,128,512]{2,1,0:T(8,128)(2,1)S(1)} %get-tuple-element.106), channel_id=1, source_target_pairs={{0,1},{1,0},{2,3},{3,2},{4,5},{5,4},{6,7},{7,6},{8,9},{9,8},{10,11... | collective-permute-start | bytes 786440 | tf_op jit(solution)/shard_map/ppermute | solution.py:23
  127.5 7.2 %collective-permute-done.35 = bf16[2,128,512]{2,1,0:T(8,128)(2,1)S(1)} collective-permute-done((bf16[2,128,512]{2,1,0:T(8,128)(2,1)S(1)}, bf16[2,128,512]{2,1,0:T(8,128)(2,1)S(1)}, u32[]{:S(2)}, u32[]{:S(2)}) %collective-permute-start.35) | collective-permute-done | bytes 262176 | tf_op jit(solution)/shard_map/ppermute | solution.py:23
  134.8 1.9 %collective-permute-start.36 = (bf16[128,512]{1,0:T(8,128)(2,1)S(1)}, bf16[128,512]{1,0:T(8,128)(2,1)S(1)}, u32[]{:S(2)}, u32[]{:S(2)}) collective-permute-start(bf16[128,512]{1,0:T(8,128)(2,1)S(1)} %fusion.7), channel_id=1, source_target_pairs={{0,2},{1,3},{2,0},{3,1},{4,6},{5,7},{6,4},{7,5},{8,10},{9,11},{10,... | collective-permute-start | bytes 393224 | tf_op jit(solution)/shard_map/ppermute | solution.py:23
  136.7 6.3 %collective-permute-done.36 = bf16[128,512]{1,0:T(8,128)(2,1)S(1)} collective-permute-done((bf16[128,512]{1,0:T(8,128)(2,1)S(1)}, bf16[128,512]{1,0:T(8,128)(2,1)S(1)}, u32[]{:S(2)}, u32[]{:S(2)}) %collective-permute-start.36) | collective-permute-done | bytes 131104 | tf_op jit(solution)/shard_map/ppermute | solution.py:23
  (134 shorter events, 31.3 us)
Async XLA Ops:
  0.0 12.8 %collective-permute-start = (bf16[128,7168]{1,0:T(8,128)(2,1)}, bf16[128,7168]{1,0:T(8,128)(2,1)}, u32[]{:S(2)}, u32[]{:S(2)}) collective-permute-start(bf16[128,7168]{1,0:T(8,128)(2,1)} %refs_0_), channel_id=1, source_target_pairs={{0,4},{4,0},{8,12},{12,8},{1,5},{5,1},{9,13},{13,9},{2,6},{6,2},{1... | collective-permute-start | bytes 5505032 | tf_op jit(solution)/shard_map/ppermute | solution.py:23
  3.2 30.4 %collective-permute-start.2 = (bf16[128,1792]{1,0:T(8,128)(2,1)}, bf16[128,1792]{1,0:T(8,128)(2,1)S(1)}, u32[]{:S(2)}, u32[]{:S(2)}) collective-permute-start(bf16[128,1792]{1,0:T(8,128)(2,1)} %get-tuple-element.60), channel_id=1, source_target_pairs={{0,8},{4,12},{8,0},{12,4},{1,9},{5,13},{9,1},{13,5},{2,10},{6,14},... | collective-permute-start | bytes 1376264 | tf_op jit(solution)/shard_map/ppermute | solution.py:23
  5.8 27.8 %collective-permute-start.3 = (bf16[128,1792]{1,0:T(8,128)(2,1)}, bf16[128,1792]{1,0:T(8,128)(2,1)}, u32[]{:S(2)}, u32[]{:S(2)}) collective-permute-start(bf16[128,1792]{1,0:T(8,128)(2,1)} %get-tuple-element.61), channel_id=1, source_target_pairs={{0,8},{4,12},{8,0},{12,4},{1,9},{5,13},{9,1},{13,5},{2,10},{6,14},... | collective-permute-start | bytes 1376264 | tf_op jit(solution)/shard_map/ppermute | solution.py:23
  5.9 46.8 %collective-permute-start.1 = (bf16[128,3584]{1,0:T(8,128)(2,1)}, bf16[128,3584]{1,0:T(8,128)(2,1)S(1)}, u32[]{:S(2)}, u32[]{:S(2)}) collective-permute-start(bf16[128,3584]{1,0:T(8,128)(2,1)} %get-tuple-element.59), channel_id=1, source_target_pairs={{0,8},{4,12},{8,0},{12,4},{1,9},{5,13},{9,1},{13,5},{2,10},{6,14},... | collective-permute-start | bytes 2752520 | tf_op jit(solution)/shard_map/ppermute | solution.py:23
  52.8 29.5 %collective-permute-start.15 = (bf16[256,2048]{1,0:T(8,128)(2,1)S(1)}, bf16[256,2048]{1,0:T(8,128)(2,1)S(1)}, u32[]{:S(2)}, u32[]{:S(2)}) collective-permute-start(bf16[256,2048]{1,0:T(8,128)(2,1)S(1)} %constant_dynamic-slice_fusion), channel_id=1, source_target_pairs={{0,4},{4,0},{8,12},{12,8},{1,5},{5,1},{9,13},{13,9},{2,6},{6,2},{1... | collective-permute-start | bytes 3145736 | tf_op jit(solution)/shard_map/ppermute | solution.py:23
  53.2 8.7 %collective-permute-start.8 = (bf16[2,128,512]{2,1,0:T(8,128)(2,1)S(1)}, bf16[2,128,512]{2,1,0:T(8,128)(2,1)S(1)}, u32[]{:S(2)}, u32[]{:S(2)}) collective-permute-start(bf16[2,128,512]{2,1,0:T(8,128)(2,1)S(1)} %get-tuple-element.74), channel_id=1, source_target_pairs={{0,8},{4,12},{8,0},{12,4},{1,9},{5,13},{9,1},{13,5},{2,10},{6,14},... | collective-permute-start | bytes 786440 | tf_op jit(solution)/shard_map/ppermute | solution.py:23
  59.8 6.4 %collective-permute-start.10 = (bf16[4,64,128]{2,1,0:T(8,128)(2,1)S(1)}, bf16[4,64,128]{2,1,0:T(8,128)(2,1)S(1)}, u32[]{:S(2)}, u32[]{:S(2)}) collective-permute-start(bf16[4,64,128]{2,1,0:T(8,128)(2,1)S(1)} %get-tuple-element.73), channel_id=1, source_target_pairs={{0,4},{4,0},{8,12},{12,8},{1,5},{5,1},{9,13},{13,9},{2,6},{6,2},{1... | collective-permute-start | bytes 196616 | tf_op jit(solution)/shard_map/ppermute | solution.py:23
  59.9 6.3 %collective-permute-start.9 = (bf16[4,64,128]{2,1,0:T(8,128)(2,1)S(1)}, bf16[4,64,128]{2,1,0:T(8,128)(2,1)S(1)}, u32[]{:S(2)}, u32[]{:S(2)}) collective-permute-start(bf16[4,64,128]{2,1,0:T(8,128)(2,1)S(1)} %get-tuple-element.73), channel_id=1, source_target_pairs={{0,12},{4,8},{8,4},{12,0},{1,13},{5,9},{9,5},{13,1},{2,14},{6,10},... | collective-permute-start | bytes 196616 | tf_op jit(solution)/shard_map/ppermute | solution.py:23
  61.8 9.9 %collective-permute-start.12 = (bf16[2,128,512]{2,1,0:T(8,128)(2,1)S(1)}, bf16[2,128,512]{2,1,0:T(8,128)(2,1)}, u32[]{:S(2)}, u32[]{:S(2)}) collective-permute-start(bf16[2,128,512]{2,1,0:T(8,128)(2,1)S(1)} %get-tuple-element.78), channel_id=1, source_target_pairs={{0,8},{4,12},{8,0},{12,4},{1,9},{5,13},{9,1},{13,5},{2,10},{6,14},... | collective-permute-start | bytes 786440 | tf_op jit(solution)/shard_map/ppermute | solution.py:23
  64.6 8.7 %collective-permute-start.17 = (bf16[2,128,512]{2,1,0:T(8,128)(2,1)S(1)}, bf16[2,128,512]{2,1,0:T(8,128)(2,1)S(1)}, u32[]{:S(2)}, u32[]{:S(2)}) collective-permute-start(bf16[2,128,512]{2,1,0:T(8,128)(2,1)S(1)} %collective-permute-done.8.refs_8_), channel_id=1, source_target_pairs={{0,16},{16,0},{1,17},{17,1},{2,18},{18,2},{3,19},{19,3},{4,20},{20... | collective-permute-start | bytes 786440 | tf_op jit(solution)/shard_map/ppermute | solution.py:23
  67.9 8.7 %collective-permute-start.14 = (bf16[2,128,512]{2,1,0:T(8,128)(2,1)S(1)}, bf16[2,128,512]{2,1,0:T(8,128)(2,1)}, u32[]{:S(2)}, u32[]{:S(2)}) collective-permute-start(bf16[2,128,512]{2,1,0:T(8,128)(2,1)S(1)} %get-tuple-element.82), channel_id=1, source_target_pairs={{0,8},{4,12},{8,0},{12,4},{1,9},{5,13},{9,1},{13,5},{2,10},{6,14},... | collective-permute-start | bytes 786440 | tf_op jit(solution)/shard_map/ppermute | solution.py:23
  71.7 11.5 %collective-permute-start.16 = (bf16[2,128,512]{2,1,0:T(8,128)(2,1)S(1)}, bf16[2,128,512]{2,1,0:T(8,128)(2,1)S(1)}, u32[]{:S(2)}, u32[]{:S(2)}) collective-permute-start(bf16[2,128,512]{2,1,0:T(8,128)(2,1)S(1)} %collective-permute-done.8.refs_8_), channel_id=1, source_target_pairs={{0,4},{4,0},{8,12},{12,8},{1,5},{5,1},{9,13},{13,9},{2,6},{6,2},{1... | collective-permute-start | bytes 786440 | tf_op jit(solution)/shard_map/ppermute | solution.py:23
  71.7 15.4 %collective-permute-start.21 = (bf16[2,128,512]{2,1,0:T(8,128)(2,1)}, bf16[2,128,512]{2,1,0:T(8,128)(2,1)}, u32[]{:S(2)}, u32[]{:S(2)}) collective-permute-start(bf16[2,128,512]{2,1,0:T(8,128)(2,1)} %collective-permute-done.12.refs_6_), channel_id=1, source_target_pairs={{0,16},{16,0},{1,17},{17,1},{2,18},{18,2},{3,19},{19,3},{4,20},{20... | collective-permute-start | bytes 786440 | tf_op jit(solution)/shard_map/ppermute | solution.py:23
  73.3 9.9 %collective-permute-start.18 = (bf16[2,128,512]{2,1,0:T(8,128)(2,1)S(1)}, bf16[2,128,512]{2,1,0:T(8,128)(2,1)S(1)}, u32[]{:S(2)}, u32[]{:S(2)}) collective-permute-start(bf16[2,128,512]{2,1,0:T(8,128)(2,1)S(1)} %collective-permute-done.17.refs_10_), channel_id=1, source_target_pairs={{0,4},{4,0},{8,12},{12,8},{1,5},{5,1},{9,13},{13,9},{2,6},{6,2},{1... | collective-permute-start | bytes 786440 | tf_op jit(solution)/shard_map/ppermute | solution.py:23
  76.6 5.7 %collective-permute-start.13 = (bf16[4,64,128]{2,1,0:T(8,128)(2,1)S(1)}, bf16[4,64,128]{2,1,0:T(8,128)(2,1)S(1)}, u32[]{:S(2)}, u32[]{:S(2)}) collective-permute-start(bf16[4,64,128]{2,1,0:T(8,128)(2,1)S(1)} %get-tuple-element.109), channel_id=1, source_target_pairs={{0,2},{1,3},{2,0},{3,1},{4,6},{5,7},{6,4},{7,5},{8,10},{9,11},{10,... | collective-permute-start | bytes 196616 | tf_op jit(solution)/shard_map/ppermute | solution.py:23
  82.3 14.8 %collective-permute-start.20 = (bf16[2,128,512]{2,1,0:T(8,128)(2,1)}, bf16[2,128,512]{2,1,0:T(8,128)(2,1)}, u32[]{:S(2)}, u32[]{:S(2)}) collective-permute-start(bf16[2,128,512]{2,1,0:T(8,128)(2,1)} %collective-permute-done.12.refs_6_), channel_id=1, source_target_pairs={{0,4},{4,0},{8,12},{12,8},{1,5},{5,1},{9,13},{13,9},{2,6},{6,2},{1... | collective-permute-start | bytes 786440 | tf_op jit(solution)/shard_map/ppermute | solution.py:23
  82.4 9.0 %collective-permute-start.30 = (bf16[2,128,512]{2,1,0:T(8,128)(2,1)}, bf16[2,128,512]{2,1,0:T(8,128)(2,1)}, u32[]{:S(2)}, u32[]{:S(2)}) collective-permute-start(bf16[2,128,512]{2,1,0:T(8,128)(2,1)} %get-tuple-element.103), channel_id=1, source_target_pairs={{0,8},{4,12},{8,0},{12,4},{1,9},{5,13},{9,1},{13,5},{2,10},{6,14},... | collective-permute-start | bytes 786440 | tf_op jit(solution)/shard_map/ppermute | solution.py:23
  87.1 11.2 %collective-permute-start.22 = (bf16[2,128,512]{2,1,0:T(8,128)(2,1)}, bf16[2,128,512]{2,1,0:T(8,128)(2,1)}, u32[]{:S(2)}, u32[]{:S(2)}) collective-permute-start(bf16[2,128,512]{2,1,0:T(8,128)(2,1)} %collective-permute-done.21.refs_8_), channel_id=1, source_target_pairs={{0,4},{4,0},{8,12},{12,8},{1,5},{5,1},{9,13},{13,9},{2,6},{6,2},{1... | collective-permute-start | bytes 786440 | tf_op jit(solution)/shard_map/ppermute | solution.py:23
  87.3 13.7 %collective-permute-start.19 = (bf16[2,128,512]{2,1,0:T(8,128)(2,1)}, bf16[2,128,512]{2,1,0:T(8,128)(2,1)}, u32[]{:S(2)}, u32[]{:S(2)}) collective-permute-start(bf16[2,128,512]{2,1,0:T(8,128)(2,1)} %get-tuple-element.89), channel_id=1, source_target_pairs={{0,1},{1,0},{2,3},{3,2},{4,5},{5,4},{6,7},{7,6},{8,9},{9,8},{10,11... | collective-permute-start | bytes 786440 | tf_op jit(solution)/shard_map/ppermute | solution.py:23
  88.9 13.7 %collective-permute-start.26 = (bf16[2,128,512]{2,1,0:T(8,128)(2,1)}, bf16[2,128,512]{2,1,0:T(8,128)(2,1)}, u32[]{:S(2)}, u32[]{:S(2)}) collective-permute-start(bf16[2,128,512]{2,1,0:T(8,128)(2,1)} %collective-permute-done.14.refs_6_), channel_id=1, source_target_pairs={{0,16},{16,0},{1,17},{17,1},{2,18},{18,2},{3,19},{19,3},{4,20},{20... | collective-permute-start | bytes 786440 | tf_op jit(solution)/shard_map/ppermute | solution.py:23
  91.4 15.5 %collective-permute-start.25 = (bf16[2,128,512]{2,1,0:T(8,128)(2,1)}, bf16[2,128,512]{2,1,0:T(8,128)(2,1)S(1)}, u32[]{:S(2)}, u32[]{:S(2)}) collective-permute-start(bf16[2,128,512]{2,1,0:T(8,128)(2,1)} %collective-permute-done.14.refs_6_), channel_id=1, source_target_pairs={{0,4},{4,0},{8,12},{12,8},{1,5},{5,1},{9,13},{13,9},{2,6},{6,2},{1... | collective-permute-start | bytes 786440 | tf_op jit(solution)/shard_map/ppermute | solution.py:23
  97.0 15.9 %collective-permute-start.32 = (bf16[2,128,512]{2,1,0:T(8,128)(2,1)}, bf16[2,128,512]{2,1,0:T(8,128)(2,1)S(1)}, u32[]{:S(2)}, u32[]{:S(2)}) collective-permute-start(bf16[2,128,512]{2,1,0:T(8,128)(2,1)} %collective-permute-done.30.refs_6_), channel_id=1, source_target_pairs={{0,16},{16,0},{1,17},{17,1},{2,18},{18,2},{3,19},{19,3},{4,20},{20... | collective-permute-start | bytes 786440 | tf_op jit(solution)/shard_map/ppermute | solution.py:23
  98.3 23.5 %collective-permute-start.31 = (bf16[2,128,512]{2,1,0:T(8,128)(2,1)}, bf16[2,128,512]{2,1,0:T(8,128)(2,1)S(1)}, u32[]{:S(2)}, u32[]{:S(2)}) collective-permute-start(bf16[2,128,512]{2,1,0:T(8,128)(2,1)} %collective-permute-done.30.refs_6_), channel_id=1, source_target_pairs={{0,4},{4,0},{8,12},{12,8},{1,5},{5,1},{9,13},{13,9},{2,6},{6,2},{1... | collective-permute-start | bytes 786440 | tf_op jit(solution)/shard_map/ppermute | solution.py:23
  101.0 11.4 %collective-permute-start.24 = (bf16[2,128,512]{2,1,0:T(8,128)(2,1)S(1)}, bf16[2,128,512]{2,1,0:T(8,128)(2,1)S(1)}, u32[]{:S(2)}, u32[]{:S(2)}) collective-permute-start(bf16[2,128,512]{2,1,0:T(8,128)(2,1)S(1)} %get-tuple-element.93), channel_id=1, source_target_pairs={{0,1},{1,0},{2,3},{3,2},{4,5},{5,4},{6,7},{7,6},{8,9},{9,8},{10,11... | collective-permute-start | bytes 786440 | tf_op jit(solution)/shard_map/ppermute | solution.py:23
  102.6 7.0 %collective-permute-start.27 = (bf16[2,128,512]{2,1,0:T(8,128)(2,1)}, bf16[2,128,512]{2,1,0:T(8,128)(2,1)S(1)}, u32[]{:S(2)}, u32[]{:S(2)}) collective-permute-start(bf16[2,128,512]{2,1,0:T(8,128)(2,1)} %collective-permute-done.26.refs_8_), channel_id=1, source_target_pairs={{0,4},{4,0},{8,12},{12,8},{1,5},{5,1},{9,13},{13,9},{2,6},{6,2},{1... | collective-permute-start | bytes 786440 | tf_op jit(solution)/shard_map/ppermute | solution.py:23
  106.9 10.1 %collective-permute-start.23 = (bf16[128,512]{1,0:T(8,128)(2,1)S(1)}, bf16[128,512]{1,0:T(8,128)(2,1)S(1)}, u32[]{:S(2)}, u32[]{:S(2)}) collective-permute-start(bf16[128,512]{1,0:T(8,128)(2,1)S(1)} %fusion.4), channel_id=1, source_target_pairs={{0,2},{1,3},{2,0},{3,1},{4,6},{5,7},{6,4},{7,5},{8,10},{9,11},{10,... | collective-permute-start | bytes 393224 | tf_op jit(solution)/shard_map/ppermute | solution.py:23
  111.9 14.0 %collective-permute-start.29 = (bf16[2,128,512]{2,1,0:T(8,128)(2,1)S(1)}, bf16[2,128,512]{2,1,0:T(8,128)(2,1)S(1)}, u32[]{:S(2)}, u32[]{:S(2)}) collective-permute-start(bf16[2,128,512]{2,1,0:T(8,128)(2,1)S(1)} %get-tuple-element.98), channel_id=1, source_target_pairs={{0,1},{1,0},{2,3},{3,2},{4,5},{5,4},{6,7},{7,6},{8,9},{9,8},{10,11... | collective-permute-start | bytes 786440 | tf_op jit(solution)/shard_map/ppermute | solution.py:23
  112.5 9.3 %collective-permute-start.28 = (bf16[128,512]{1,0:T(8,128)(2,1)S(1)}, bf16[128,512]{1,0:T(8,128)(2,1)S(1)}, u32[]{:S(2)}, u32[]{:S(2)}) collective-permute-start(bf16[128,512]{1,0:T(8,128)(2,1)S(1)} %fusion.5), channel_id=1, source_target_pairs={{0,2},{1,3},{2,0},{3,1},{4,6},{5,7},{6,4},{7,5},{8,10},{9,11},{10,... | collective-permute-start | bytes 393224 | tf_op jit(solution)/shard_map/ppermute | solution.py:23
  112.9 9.0 %collective-permute-start.33 = (bf16[2,128,512]{2,1,0:T(8,128)(2,1)S(1)}, bf16[2,128,512]{2,1,0:T(8,128)(2,1)S(1)}, u32[]{:S(2)}, u32[]{:S(2)}) collective-permute-start(bf16[2,128,512]{2,1,0:T(8,128)(2,1)S(1)} %collective-permute-done.32.refs_8_), channel_id=1, source_target_pairs={{0,4},{4,0},{8,12},{12,8},{1,5},{5,1},{9,13},{13,9},{2,6},{6,2},{1... | collective-permute-start | bytes 786440 | tf_op jit(solution)/shard_map/ppermute | solution.py:23
  124.1 10.6 %collective-permute-start.35 = (bf16[2,128,512]{2,1,0:T(8,128)(2,1)S(1)}, bf16[2,128,512]{2,1,0:T(8,128)(2,1)S(1)}, u32[]{:S(2)}, u32[]{:S(2)}) collective-permute-start(bf16[2,128,512]{2,1,0:T(8,128)(2,1)S(1)} %get-tuple-element.106), channel_id=1, source_target_pairs={{0,1},{1,0},{2,3},{3,2},{4,5},{5,4},{6,7},{7,6},{8,9},{9,8},{10,11... | collective-permute-start | bytes 786440 | tf_op jit(solution)/shard_map/ppermute | solution.py:23
  126.1 10.6 %collective-permute-start.34 = (bf16[128,512]{1,0:T(8,128)(2,1)S(1)}, bf16[128,512]{1,0:T(8,128)(2,1)S(1)}, u32[]{:S(2)}, u32[]{:S(2)}) collective-permute-start(bf16[128,512]{1,0:T(8,128)(2,1)S(1)} %fusion.6), channel_id=1, source_target_pairs={{0,2},{1,3},{2,0},{3,1},{4,6},{5,7},{6,4},{7,5},{8,10},{9,11},{10,... | collective-permute-start | bytes 393224 | tf_op jit(solution)/shard_map/ppermute | solution.py:23
  134.8 8.3 %collective-permute-start.36 = (bf16[128,512]{1,0:T(8,128)(2,1)S(1)}, bf16[128,512]{1,0:T(8,128)(2,1)S(1)}, u32[]{:S(2)}, u32[]{:S(2)}) collective-permute-start(bf16[128,512]{1,0:T(8,128)(2,1)S(1)} %fusion.7), channel_id=1, source_target_pairs={{0,2},{1,3},{2,0},{3,1},{4,6},{5,7},{6,4},{7,5},{8,10},{9,11},{10,... | collective-permute-start | bytes 393224 | tf_op jit(solution)/shard_map/ppermute | solution.py:23
  (26 other events, 138.8 us)

commit v6 on v5

--- a/solution.py
+++ b/solution.py
@@ -9,7 +9,7 @@
 BF16 = jnp.bfloat16
 VMEM_LIMIT = 40 * 1024 * 1024
 WIDTHS = (512, 512, 512, 512)
-EARLY = 3
+EARLY = 2
 CAP = 4
 HALVES = 2
 HINT = 1000
@@ -27,8 +27,8 @@
     return lax.optimization_barrier((values, *after))[0]
 
 
-def cost(flops, moved):
-    return pl.CostEstimate(flops=flops // HINT, bytes_accessed=moved // HINT, transcendentals=0)
+def cost(flops, moved, hint=HINT):
+    return pl.CostEstimate(flops=flops // hint, bytes_accessed=moved // hint, transcendentals=0)
 
 
 def params():
@@ -84,7 +84,7 @@
     out_ref[...] = value
 
 
-def product(lower, upper, weight, depth_block, prior, first, width, tile):
+def product(lower, upper, weight, depth_block, prior, first, width, tile, hint=HINT):
     rows = lower[0].shape[0]
     depth = sum(x.shape[1] for x in lower)
     args = [*lower, *upper]
@@ -103,7 +103,7 @@
         scratch_shapes=[pltpu.VMEM((2 * rows, depth), BF16)],
         compiler_params=params(),
         cost_estimate=cost(
-            4 * rows * depth * width, 2 * depth * (width + 2 * rows) + 8 * rows * width
+            4 * rows * depth * width, 2 * depth * (width + 2 * rows) + 8 * rows * width, hint
         ),
         name="base",
     )(*args)
@@ -259,12 +259,8 @@
     parity = info_ref[0]
     rows = near_ref.shape[1]
     held = own_ref.shape[0]
-    maps[0:held, :] = own_ref[...]
-    maps[held : 2 * held, :] = core_ref[...]
-    start = 2 * held
-    for ref in blocks:
-        maps[start : start + held // 2, :] = ref[0]
-        start += held // 2
+    for index, ref in enumerate((own_ref, core_ref, *blocks)):
+        maps[index * held : (index + 1) * held, :] = ref[...]
     delta = jnp.dot(spread_ref[...], maps[...], preferred_element_type=F32)
     for slot in range(4):
         source = near_ref if slot % 2 == 0 else far_ref
@@ -293,8 +289,7 @@
         pl.BlockSpec((held, tile), lambda n, s: (0, first + n)),
     ]
     in_specs += [
-        pl.BlockSpec((1, held // 2, tile), lambda n, s, index=index: (index, 0, n))
-        for _, index in blocks
+        pl.BlockSpec((held, tile), lambda n, s: (0, n)) for _ in blocks
     ]
     out_specs = [pl.BlockSpec((2, rows, tile), lambda n, s: (0, 0, n))] * 2
     out_shape = [jax.ShapeDtypeStruct((2, rows, width), kind) for kind in (F32, BF16)]
@@ -316,18 +311,16 @@
             32 * rows * held * width, 26 * rows * width + 8 * held * width
         ),
         name="combine",
-    )(info, *ahead, near, far, own_maps, core_maps, *[block for block, _ in blocks])
+    )(info, *ahead, near, far, own_maps, core_maps, *blocks)
 
 
 def per_device_fast(hidden, weight, input_maps, output_maps, slots, lists):
     rows, depth = hidden.shape
     place = lax.axis_index("pool")
     t = lax.axis_index("tensor")
-    y = lax.axis_index("groups")
     holding, rank = input_maps.shape[:2]
     held, features = output_maps.shape
     width = features // 4
-    chip, core = place >> 1, place & 1
     starts = [sum(WIDTHS[:i]) for i in range(len(WIDTHS))]
     count = len(WIDTHS)
 
@@ -339,17 +332,9 @@
 
     core_block = lax.dynamic_slice(output_maps, (0, (place ^ 1) * width), (held, width))
     blocks = [
-        jnp.stack(
-            [
-                lax.dynamic_slice(
-                    output_maps,
-                    (y * (held // 2), (place ^ other) * width + start),
-                    (held // 2, wide),
-                )
-                for other in (2, 3)
-            ]
-        )
+        lax.dynamic_slice(output_maps, (0, (place ^ other) * width + start), (held, wide))
         for start, wide in zip(starts, WIDTHS)
+        for other in (2, 3)
     ]
 
     order = place ^ jnp.arange(4, dtype=jnp.int32)
@@ -382,9 +367,7 @@
     owner_first = [holding * (place ^ j) + per_owner * t for j in range(4)]
     info = jnp.stack(
         [parity, place]
-        + [owner_first[j] + half_step * h for j in (0, 1) for h in (0, 1)]
-        + [owner_first[2] + half_step * y, owner_first[3] + half_step * y]
-        + [owner_first[2] + half_step * (1 - y), owner_first[3] + half_step * (1 - y)]
+        + [owner_first[j] + half_step * h for j in range(4) for h in range(2)]
     ).astype(jnp.int32)
 
     ready = lax.optimization_barrier(
@@ -397,7 +380,6 @@
     near_base = product(
         [tie(own_rows, near_lowrank)], [near_b], weight, 0, None, 0, width, 512
     )
-    crossing = [swap(blocks[0], "pool", 2)]
 
     first_a, first_b = lax.optimization_barrier((first_a, first_b, near_base))[:2]
     a0 = [first_a, first_b]
@@ -418,51 +400,52 @@
         picks, 2, a1, b1, input_maps, 1, prior=raw, near=near_lowrank, ids=owned_ids
     )
 
-    def far_piece(index, after):
+    def far_piece(index, after, hint=HINT):
         left = [tie(a1[0], after)]
         if index < EARLY:
             piece = product(
-                left, b1, weight, 1, begun[index], starts[index], WIDTHS[index], 256
+                left, b1, weight, 1, begun[index], starts[index], WIDTHS[index], 256, hint
             )
         else:
             piece = product(
-                a0 + left, b0 + b1, weight, 0, None, starts[index], WIDTHS[index], 256
+                a0 + left, b0 + b1, weight, 0, None, starts[index], WIDTHS[index], 256, hint
             )
         return piece.reshape(2, rows, WIDTHS[index])
 
     got = [swap(sent, "pool", step) for step in (2, 3, 1)]
-    crossing.append(swap(tie(blocks[1], sent), "pool", 2))
-    crossing[0] = tie(crossing[0], sent)
-    got[0] = tie(got[0], crossing[0])
     total = total + sum(x.astype(F32) for x in got)
+
+    def start_maps(index, after):
+        pair = [tie(x, after) for x in blocks[2 * index : 2 * index + 2]]
+        return [swap(x, "pool", 2 + k) for k, x in enumerate(pair)]
+
+    moved = [start_maps(0, sent)]
     sent = total.astype(BF16)
     got = swap(sent, "tensor", 1)
-    crossing.append(swap(tie(blocks[2], sent), "pool", 2))
-    crossing[1] = tie(crossing[1], sent)
-    got = tie(got, crossing[1])
+    moved.append(start_maps(1, sent))
+    pieces = [far_piece(0, sent, 1)]
+    moved[0] = [tie(x, pieces[0]) for x in moved[0]]
+    got = lax.optimization_barrier((got, pieces[0]))[0]
     total = total + got.astype(F32)
     sent = total.astype(BF16)
     got = swap(sent, "tensor", 2)
-    crossing.append(swap(tie(blocks[3], sent), "pool", 2))
-    crossing[2] = tie(crossing[2], sent)
-    pieces = [far_piece(0, sent)]
-    got = lax.optimization_barrier((got, crossing[2], pieces[0]))[0]
-
-    def over_y(index, after):
-        block = crossing[index] if after is None else tie(crossing[index], after)
-        return block, swap(block, "pool", 1), swap(block, "groups", 1)
-
-    def blocks_of(index, after):
-        block, beside, across = moved[index]
-        across = across if after is None else tie(across, after)
-        return [(block, 0), (beside, 1), (across, 0), (swap(across, "pool", 1), 1)]
-
-    moved = [over_y(index, None) for index in range(count - 1)]
+    moved.append(start_maps(2, sent))
+    moved[0] = [tie(x, sent) for x in moved[0]]
+    got = lax.optimization_barrier((got, *moved[0]))[0]
 
     near_base = near_base.reshape(2, rows, width)
     side = ((place ^ t) >> 1) & 1
     parts = []
     spread = send = None
+
+    def maps_of(index, after):
+        return moved[index] if after is None else [tie(x, after) for x in moved[index]]
+
+    def pace(index):
+        return near_base if index < 2 else tie(near_base, started[index - 2])
+
+    started = []
+
     halves = []
 
     def finish(index, after):
@@ -471,16 +454,17 @@
         pair = keep + got.astype(F32)
         sent = jnp.where(side == 0, pair[1], pair[0]).astype(BF16)
         kept = jnp.where(side == 0, pair[0], pair[1])
+        started.append(sent)
         return kept + swap(sent, "tensor", 2).astype(F32)
 
     for chunk in range(count):
         common = (
-            info, near_base, pieces[chunk], output_maps, core_maps,
-            blocks_of(chunk, send if chunk else None), starts[chunk],
+            info, pace(chunk), pieces[chunk], output_maps, core_maps,
+            maps_of(chunk, started[chunk - 2] if chunk > 1 else send), starts[chunk],
         )
         if chunk == 0:
             keep, send, spread = combine(*common, build=(total, got, wide_ids))
-            moved.append(over_y(count - 1, send))
+            moved.append(start_maps(3, send))
         else:
             keep, send = combine(*common, spread=spread)
         if chunk + 1 < count:
@@ -488,7 +472,7 @@
         halves.append((keep, swap(send, "tensor", 1)))
         if chunk > 0:
             parts.append(finish(chunk - 1, send))
-    parts.append(finish(count - 1, None))
+    parts.append(finish(count - 1, started[-1]))
     return jnp.concatenate(parts, axis=1).astype(BF16)
 
 

time: 144 us -> 132 us (0.917)
  waiting for transfers between devices: 32.3 us -> 26.2 us
  Pallas kernels: 64 us -> 60.4 us
  starting transfers between devices: 32.3 us -> 30.4 us
    ppermute x37 -> x29, waiting for transfers between devices: 32.3 us -> 26.2 us  [swap(): return lax.ppermute(values, axis, partners(lax.axis_size(axis), step))]
    dynamic_slice x0 -> x1, local copies, waits for them, and re-layouts: none -> 2.9 us  [per_device_fast(): lax.dynamic_slice(output_maps, (0, (place ^ other) * width + start), (hel...]
    pallas_call x4, Pallas kernels: 9.03 us -> 7.03 us  [combine(): pl.pallas_call(lambda *refs: combine_kernel(bool(build), *refs), grid_spe...]
    ppermute x37 -> x29, starting transfers between devices: 32.3 us -> 30.4 us  [swap(): return lax.ppermute(values, axis, partners(lax.axis_size(axis), step))]
    another operation x2 -> x1, local copies, waits for them, and re-layouts: 1.66 us -> 0.09 us  [per_device_fast(): jnp.stack([parity, place] + [owner_first[j] + half_step * h for j in rang...]
    pallas_call x8 -> x7, Pallas kernels: 37.3 us -> 35.8 us  [product(): pl.pallas_call(lambda *refs: product_kernel(len(lower), len(upper), prior...]
  transfers between devices with their start and end apart: 37 -> 29, of which waited for: 10 -> 11; matrix products, arithmetic and copies ran while one was open for 5% -> 5% of each run, Pallas kernels for 44% -> 46%
where the time goes in v6:
time: 132 us
  Pallas kernels  60.4 us (46%)
  starting transfers between devices  30.4 us (23%)
  waiting for transfers between devices  26.2 us (20%)
  local copies, waits for them, and re-layouts  9.63 us (7%)
  other arithmetic  4.76 us (4%)
    pallas_call x7, Pallas kernels, product(): pl.pallas_call(lambda *refs: product_kernel(len(lower), len(upper), prior...  35.8 us
    ppermute x29, starting transfers between devices, swap(): return lax.ppermute(values, axis, partners(lax.axis_size(axis), step))  30.4 us
    ppermute x29, waiting for transfers between devices, swap(): return lax.ppermute(values, axis, partners(lax.axis_size(axis), step))  26.2 us
    pallas_call x3, Pallas kernels, scores(): pl.pallas_call(lambda *refs: scores_kernel(first, half * depth, len(lower...  16.4 us
    pallas_call x4, Pallas kernels, combine(): pl.pallas_call(lambda *refs: combine_kernel(bool(build), *refs), grid_spe...  7.03 us
    unnamed x42, local copies, waits for them, and re-layouts  6.33 us
    dynamic_slice x1, local copies, waits for them, and re-layouts, per_device_fast(): lax.dynamic_slice(output_maps, (0, (place ^ other) * width + start), (hel...  2.9 us
  transfers between devices with their start and end apart: 29, of which 11 were waited for; matrix products, arithmetic and copies ran while one was open for 5% of the time, Pallas kernels for 46%

profile of v6, /device:TPU:0, one launch (start us, length us, event | category | flops | bytes accessed | tf_op | source)
XLA Modules:
  0.0 131.9 jit_solution(14784891383462883496)
XLA Ops:
  0.5 1.5 %copy-done.6 = bf16[128,7168]{1,0:T(8,128)(2,1)S(1)} copy-done((bf16[128,7168]{1,0:T(8,128)(2,1)S(1)}, bf16[128,7168]{1,0:T(8,128)(2,1)}, u32[]{:S(2)}) %copy-start.6) | copy-done | bytes 1835032
  3.2 2.6 %collective-permute-start.2 = (bf16[128,1792]{1,0:T(8,128)(2,1)}, bf16[128,1792]{1,0:T(8,128)(2,1)S(1)}, u32[]{:S(2)}, u32[]{:S(2)}) collective-permute-start(bf16[128,1792]{1,0:T(8,128)(2,1)} %get-tuple-element.73), channel_id=1, source_target_pairs={{0,8},{4,12},{8,0},{12,4},{1,9},{5,13},{9,1},{13,5},{2,10},{6,14},... | collective-permute-start | bytes 1376264 | tf_op jit(solution)/shard_map/ppermute | solution.py:23
  5.9 1.9 %collective-permute-start.1 = (bf16[128,3584]{1,0:T(8,128)(2,1)}, bf16[128,3584]{1,0:T(8,128)(2,1)S(1)}, u32[]{:S(2)}, u32[]{:S(2)}) collective-permute-start(bf16[128,3584]{1,0:T(8,128)(2,1)} %get-tuple-element.72), channel_id=1, source_target_pairs={{0,8},{4,12},{8,0},{12,4},{1,9},{5,13},{9,1},{13,5},{2,10},{6,14},... | collective-permute-start | bytes 2752520 | tf_op jit(solution)/shard_map/ppermute | solution.py:23
  10.3 2.9 %constant_dynamic-slice_fusion.8 = (bf16[256,512]{1,0:T(8,128)(2,1)}, bf16[256,512]{1,0:T(8,128)(2,1)}, bf16[256,512]{1,0:T(8,128)(2,1)}, bf16[256,512]{1,0:T(8,...) fusion(bf16[256,8192]{1,0:T(8,128)(2,1)} %refs_4_.9, ...), kind=kLoop, calls=%fused_computation.41 | loop fusion | bytes 4194336 | tf_op jit(solution)/shard_map/dynamic_slice | solution.py:335
  13.4 7.1 %scores.3.refs_5_ = f32[2,64,128]{2,1,0:T(8,128)S(1)} custom-call(s32[17]{0:T(128)S(1)} %pad_add_fusion.refs_0_, bf16[128,7168]{1,0:T(8,128)(2,1)S(1)} %copy-done.7, bf16[128,7168]{1,0:T(8,128)(2,1)} %collective-permute-done.refs_2_.refs_1_, bf16[16,64,7168]{2,1,0:T(8,128)(2,1)} %refs_3_.5, s32[4,1,128]{2,1,0:T(1,128)S(1)} %bitcast.49), custom_call_target="tpu_custom_call" | custom-call | flops 939524 | bytes 11010 | tf_op jit(solution)/shard_map/scores/pallas_call | solution.py:211
  20.6 13.5 %base.7 = f32[256,2048]{1,0:T(8,128)S(1)} custom-call(bf16[128,7168]{1,0:T(8,128)(2,1)S(1)} %copy-done.8, bf16[128,7168]{1,0:T(8,128)(2,1)} %collective-permute-done.refs_2_.refs_1_, bf16[7168,2048]{1,0:T(8,128)(2,1)} %refs_6_.5), custom_call_target="tpu_custom_call" | custom-call | flops 7516192 | bytes 35127 | tf_op jit(solution)/shard_map/base/pallas_call | solution.py:97
  34.7 1.3 collective-permute-done.4.refs_3_.refs_2_
  36.8 4.8 %scores.4.refs_4_ = f32[2,256,128]{2,1,0:T(8,128)S(1)} custom-call(s32[17]{0:T(128)S(1)} %pad_add_fusion.refs_0_, bf16[128,1792]{1,0:T(8,128)(2,1)S(1)} %collective-permute-done.2.refs_1_.refs_0_, bf16[128,1792]{1,0:T(8,128)(2,1)} %collective-permute-done.3.refs_2_.refs_1_, bf16[128,1792]{1,0:T(8,128)(2,1)S(1)} %collective-permute-done.4.refs_3_.refs_2_, ...), custom_call_target="tpu_custom_call" | custom-call | flops 469762 | bytes 5505 | tf_op jit(solution)/shard_map/scores/pallas_call | solution.py:211
  41.6 3.3 %base.8.refs_2_ = f32[256,512]{1,0:T(8,128)S(1)} custom-call(bf16[128,1792]{1,0:T(8,128)(2,1)S(1)} %collective-permute-done.2.refs_1_.refs_0_, bf16[128,1792]{1,0:T(8,128)(2,1)} %collective-permute-done.3.refs_2_.refs_1_, bf16[128,1792]{1,0:T(8,128)(2,1)S(1)} %collective-permute-done.4.refs_3_.refs_2_, ...), custom_call_target="tpu_custom_call" | custom-call | flops 939524 | bytes 6029 | tf_op jit(solution)/shard_map/base/pallas_call | solution.py:97
  44.9 3.3 %base.9.refs_2_ = f32[256,512]{1,0:T(8,128)S(1)} custom-call(bf16[128,1792]{1,0:T(8,128)(2,1)S(1)} %collective-permute-done.2.refs_1_.refs_0_, bf16[128,1792]{1,0:T(8,128)(2,1)} %collective-permute-done.3.refs_2_.refs_1_, bf16[128,1792]{1,0:T(8,128)(2,1)S(1)} %collective-permute-done.4.refs_3_.refs_2_, ...), custom_call_target="tpu_custom_call" | custom-call | flops 939524 | bytes 6029 | tf_op jit(solution)/shard_map/base/pallas_call | solution.py:97
  49.5 2.0 %collective-permute-done.6.refs_2_.refs_1_.refs_5_ = bf16[128,3584]{1,0:T(8,128)(2,1)S(1)} collective-permute-done((bf16[128,3584]{1,0:T(8,128)(2,1)S(1)}, bf16[128,3584]{1,0:T(8,128)(2,1)S(1)}, u32[]{:S(2)}, u32[]{:S(2)}) %collective-permute-start.6) | collective-permute-done | bytes 917536 | tf_op jit(solution)/shard_map/ppermute | solution.py:23
  51.5 4.5 %scores.5 = (f32[4,64,128]{2,1,0:T(8,128)S(1)}, bf16[4,64,128]{2,1,0:T(8,128)(2,1)S(1)}) custom-call(s32[17]{0:T(128)S(1)} %pad_add_fusion.refs_0_, bf16[128,3584]{1,0:T(8,128)(2,1)S(1)} %collective-permute-done.1.refs_1_.refs_0_.refs_2_, bf16[128,3584]{1,0:T(8,128)(2,1)S(1)} %collective-permute-done.6.refs_2_.refs_1_.refs_5_, ...), custom_call_target="tpu_custom_call" | custom-call | flops 469762 | bytes 5505 | tf_op jit(solution)/shard_map/scores/pallas_call | solution.py:211
  56.3 2.0 %collective-permute-start.7 = (bf16[4,64,128]{2,1,0:T(8,128)(2,1)S(1)}, bf16[4,64,128]{2,1,0:T(8,128)(2,1)S(1)}, u32[]{:S(2)}, u32[]{:S(2)}) collective-permute-start(bf16[4,64,128]{2,1,0:T(8,128)(2,1)S(1)} %get-tuple-element.85), channel_id=1, source_target_pairs={{0,8},{4,12},{8,0},{12,4},{1,9},{5,13},{9,1},{13,5},{2,10},{6,14},... | collective-permute-start | bytes 196616 | tf_op jit(solution)/shard_map/ppermute | solution.py:23
  60.2 2.3 %collective-permute-done.7 = bf16[4,64,128]{2,1,0:T(8,128)(2,1)S(1)} collective-permute-done((bf16[4,64,128]{2,1,0:T(8,128)(2,1)S(1)}, bf16[4,64,128]{2,1,0:T(8,128)(2,1)S(1)}, u32[]{:S(2)}, u32[]{:S(2)}) %collective-permute-start.7) | collective-permute-done | bytes 65568 | tf_op jit(solution)/shard_map/ppermute | solution.py:23
  62.5 1.6 %collective-permute-start.10 = (bf16[4,64,128]{2,1,0:T(8,128)(2,1)S(1)}, bf16[4,64,128]{2,1,0:T(8,128)(2,1)S(1)}, u32[]{:S(2)}, u32[]{:S(2)}) collective-permute-start(bf16[4,64,128]{2,1,0:T(8,128)(2,1)S(1)} %fusion.8), channel_id=1, source_target_pairs={{0,1},{1,0},{2,3},{3,2},{4,5},{5,4},{6,7},{7,6},{8,9},{9,8},{10,11... | collective-permute-start | bytes 196616 | tf_op jit(solution)/shard_map/ppermute | solution.py:23
  64.2 3.0 %base.10 = f32[256,512]{1,0:T(8,128)S(1)} custom-call(bf16[128,3584]{1,0:T(8,128)(2,1)S(1)} %collective-permute-done.1.refs_1_.refs_0_.refs_2_, bf16[128,3584]{1,0:T(8,128)(2,1)S(1)} %collective-permute-done.6.refs_2_.refs_1_.refs_5_, f32[256,512]{1,0:T(8,128)S(1)} %base.8.refs_2_, bf16[7168,2048]{1,0:T(8,128)(2,1)} %refs_6_.5), custom_call_target="tpu_custom_call" | custom-call | flops 939524096 | bytes 6029312 | tf_op jit(solution)/shard_map/base/pallas_call | solution.py:97
  67.2 2.7 %collective-permute-start.11 = (bf16[4,64,128]{2,1,0:T(8,128)(2,1)S(1)}, bf16[4,64,128]{2,1,0:T(8,128)(2,1)S(1)}, u32[]{:S(2)}, u32[]{:S(2)}) collective-permute-start(bf16[4,64,128]{2,1,0:T(8,128)(2,1)S(1)} %get-tuple-element.135), channel_id=1, source_target_pairs={{0,2},{1,3},{2,0},{3,1},{4,6},{5,7},{6,4},{7,5},{8,10},{9,11},{10,... | collective-permute-start | bytes 196616 | tf_op jit(solution)/shard_map/ppermute | solution.py:23
  70.5 2.3 %collective-permute-done.13.refs_9_ = bf16[256,512]{1,0:T(8,128)(2,1)S(1)} collective-permute-done((bf16[256,512]{1,0:T(8,128)(2,1)S(1)}, bf16[256,512]{1,0:T(8,128)(2,1)S(1)}, u32[]{:S(2)}, u32[]{:S(2)}) %collective-permute-start.13) | collective-permute-done | bytes 262176 | tf_op jit(solution)/shard_map/ppermute | solution.py:23
  72.8 2.2 %combine.4 = (f32[2,128,512]{2,1,0:T(8,128)S(1)}, bf16[2,128,512]{2,1,0:T(8,128)(2,1)}, bf16[512,1024]{1,0:T(8,128)(2,1)S(1)}) custom-call(s32[10]{0:T(128)S(1)} %stack.40.refs_0_, f32[4,64,128]{2,1,0:T(8,128)S(1)} %get-tuple-element.136.refs_1_, bf16[4,64,128]{2,1,0:T(8,128)(2,1)S(1)} %collective-permute-done.11.refs_2_, ...), custom_call_target="tpu_custom_call" | custom-call | flops 536870 | bytes 2752 | tf_op jit(solution)/shard_map/combine/pallas_call | solution.py:299
  76.8 1.5 %collective-permute-start.15 = (bf16[2,128,512]{2,1,0:T(8,128)(2,1)}, bf16[2,128,512]{2,1,0:T(8,128)(2,1)}, u32[]{:S(2)}, u32[]{:S(2)}) collective-permute-start(bf16[2,128,512]{2,1,0:T(8,128)(2,1)} %get-tuple-element.100), channel_id=1, source_target_pairs={{0,1},{1,0},{2,3},{3,2},{4,5},{5,4},{6,7},{7,6},{8,9},{9,8},{10,11... | collective-permute-start | bytes 786440 | tf_op jit(solution)/shard_map/ppermute | solution.py:23
  78.8 1.4 %collective-permute-start.21 = (bf16[256,512]{1,0:T(8,128)(2,1)}, bf16[256,512]{1,0:T(8,128)(2,1)S(1)}, u32[]{:S(2)}, u32[]{:S(2)}) collective-permute-start(bf16[256,512]{1,0:T(8,128)(2,1)} %get-tuple-element.118), channel_id=1, source_target_pairs={{0,12},{4,8},{8,4},{12,0},{1,13},{5,9},{9,5},{13,1},{2,14},{6,10},... | collective-permute-start | bytes 786440 | tf_op jit(solution)/shard_map/ppermute | solution.py:23
  82.4 3.1 %base.11 = f32[256,512]{1,0:T(8,128)S(1)} custom-call(bf16[128,3584]{1,0:T(8,128)(2,1)S(1)} %collective-permute-done.1.refs_1_.refs_0_.refs_2_, bf16[128,3584]{1,0:T(8,128)(2,1)S(1)} %copy-done.3, f32[256,512]{1,0:T(8,128)S(1)} %copy-done.16, bf16[7168,2048]{1,0:T(8,128)(2,1)} %refs_6_.5), custom_call_target="tpu_custom_call" | custom-call | flops 939524 | bytes 6029 | tf_op jit(solution)/shard_map/base/pallas_call | solution.py:97
  87.3 2.4 %combine.5 = (f32[2,128,512]{2,1,0:T(8,128)S(1)}, bf16[2,128,512]{2,1,0:T(8,128)(2,1)S(1)}) custom-call(s32[10]{0:T(128)S(1)} %stack.40.refs_0_, bf16[512,1024]{1,0:T(8,128)(2,1)S(1)} %copy-done.14, f32[2,128,2048]{2,1,0:T(8,128)S(1)} %bitcast.42, f32[2,128,512]{2,1,0:T(8,128)S(1)} %bitcast.48, bf16[256,8192]{1,0:T(8,128)(2,1)S(1)} %copy-done.1, ...), custom_call_target="tpu_custom_call" | custom-call | flops 536870 | bytes 2752 | tf_op jit(solution)/shard_map/combine/pallas_call | solution.py:299
  89.7 4.9 %base.12 = f32[256,512]{1,0:T(8,128)S(1)} custom-call(bf16[128,1792]{1,0:T(8,128)(2,1)S(1)} %collective-permute-done.2.refs_1_.refs_0_, bf16[128,1792]{1,0:T(8,128)(2,1)} %collective-permute-done.3.refs_2_.refs_1_, bf16[128,3584]{1,0:T(8,128)(2,1)S(1)} %collective-permute-done.1.refs_1_.refs_0_.refs_2_, bf16[128,1792]{1,0:T(8,128)(2,1)S(1)} %copy-done.10, ...), custom_call_target="tpu_custom_call" | custom-call | flops 1879048 | bytes 11534 | tf_op jit(solution)/shard_map/base/pallas_call | solution.py:97
  96.6 2.7 %collective-permute-start.18 = (bf16[128,512]{1,0:T(8,128)(2,1)S(1)}, bf16[128,512]{1,0:T(8,128)(2,1)S(1)}, u32[]{:S(2)}, u32[]{:S(2)}) collective-permute-start(bf16[128,512]{1,0:T(8,128)(2,1)S(1)} %fusion.4), channel_id=1, source_target_pairs={{0,2},{1,3},{2,0},{3,1},{4,6},{5,7},{6,4},{7,5},{8,10},{9,11},{10,... | collective-permute-start | bytes 393224 | tf_op jit(solution)/shard_map/ppermute | solution.py:23
  101.8 4.7 %base.13 = f32[256,512]{1,0:T(8,128)S(1)} custom-call(bf16[128,1792]{1,0:T(8,128)(2,1)S(1)} %collective-permute-done.2.refs_1_.refs_0_, bf16[128,1792]{1,0:T(8,128)(2,1)} %collective-permute-done.3.refs_2_.refs_1_, bf16[128,3584]{1,0:T(8,128)(2,1)S(1)} %collective-permute-done.1.refs_1_.refs_0_.refs_2_, bf16[128,1792]{1,0:T(8,128)(2,1)S(1)} %copy-done.10, ...), custom_call_target="tpu_custom_call" | custom-call | flops 1879048 | bytes 11534 | tf_op jit(solution)/shard_map/base/pallas_call | solution.py:97
  108.9 2.7 %collective-permute-start.27 = (bf16[2,128,512]{2,1,0:T(8,128)(2,1)S(1)}, bf16[2,128,512]{2,1,0:T(8,128)(2,1)S(1)}, u32[]{:S(2)}, u32[]{:S(2)}) collective-permute-start(bf16[2,128,512]{2,1,0:T(8,128)(2,1)S(1)} %get-tuple-element.131), channel_id=1, source_target_pairs={{0,1},{1,0},{2,3},{3,2},{4,5},{5,4},{6,7},{7,6},{8,9},{9,8},{10,11... | collective-permute-start | bytes 786440 | tf_op jit(solution)/shard_map/ppermute | solution.py:23
  111.7 1.9 %collective-permute-done.22 = bf16[128,512]{1,0:T(8,128)(2,1)S(1)} collective-permute-done((bf16[128,512]{1,0:T(8,128)(2,1)S(1)}, bf16[128,512]{1,0:T(8,128)(2,1)S(1)}, u32[]{:S(2)}, u32[]{:S(2)}) %collective-permute-start.22) | collective-permute-done | bytes 131104 | tf_op jit(solution)/shard_map/ppermute | solution.py:23
  113.6 1.4 %collective-permute-done.23 = bf16[2,128,512]{2,1,0:T(8,128)(2,1)S(1)} collective-permute-done((bf16[2,128,512]{2,1,0:T(8,128)(2,1)S(1)}, bf16[2,128,512]{2,1,0:T(8,128)(2,1)S(1)}, u32[]{:S(2)}, u32[]{:S(2)}) %collective-permute-start.23) | collective-permute-done | bytes 262176 | tf_op jit(solution)/shard_map/ppermute | solution.py:23
  115.1 2.0 %collective-permute-start.26 = (bf16[128,512]{1,0:T(8,128)(2,1)S(1)}, bf16[128,512]{1,0:T(8,128)(2,1)S(1)}, u32[]{:S(2)}, u32[]{:S(2)}) collective-permute-start(bf16[128,512]{1,0:T(8,128)(2,1)S(1)} %fusion.6), channel_id=1, source_target_pairs={{0,2},{1,3},{2,0},{3,1},{4,6},{5,7},{6,4},{7,5},{8,10},{9,11},{10,... | collective-permute-start | bytes 393224 | tf_op jit(solution)/shard_map/ppermute | solution.py:23
  117.2 5.9 %collective-permute-done.27 = bf16[2,128,512]{2,1,0:T(8,128)(2,1)S(1)} collective-permute-done((bf16[2,128,512]{2,1,0:T(8,128)(2,1)S(1)}, bf16[2,128,512]{2,1,0:T(8,128)(2,1)S(1)}, u32[]{:S(2)}, u32[]{:S(2)}) %collective-permute-start.27) | collective-permute-done | bytes 262176 | tf_op jit(solution)/shard_map/ppermute | solution.py:23
  123.5 7.5 %collective-permute-done.28 = bf16[128,512]{1,0:T(8,128)(2,1)S(1)} collective-permute-done((bf16[128,512]{1,0:T(8,128)(2,1)S(1)}, bf16[128,512]{1,0:T(8,128)(2,1)S(1)}, u32[]{:S(2)}, u32[]{:S(2)}) %collective-permute-start.28) | collective-permute-done | bytes 131104 | tf_op jit(solution)/shard_map/ppermute | solution.py:23
  (115 shorter events, 24.9 us)
Async XLA Ops:
  0.0 13.3 %collective-permute-start = (bf16[128,7168]{1,0:T(8,128)(2,1)}, bf16[128,7168]{1,0:T(8,128)(2,1)}, u32[]{:S(2)}, u32[]{:S(2)}) collective-permute-start(bf16[128,7168]{1,0:T(8,128)(2,1)} %refs_0_), channel_id=1, source_target_pairs={{0,4},{4,0},{8,12},{12,8},{1,5},{5,1},{9,13},{13,9},{2,6},{6,2},{1... | collective-permute-start | bytes 5505032 | tf_op jit(solution)/shard_map/ppermute | solution.py:23
  2.0 11.5 %copy-start.7 = (bf16[128,7168]{1,0:T(8,128)(2,1)S(1)}, bf16[128,7168]{1,0:T(8,128)(2,1)}, u32[]{:S(2)}) copy-start(bf16[128,7168]{1,0:T(8,128)(2,1)} %refs_0_) | copy-start | bytes 5505028
  3.2 30.8 %collective-permute-start.2 = (bf16[128,1792]{1,0:T(8,128)(2,1)}, bf16[128,1792]{1,0:T(8,128)(2,1)S(1)}, u32[]{:S(2)}, u32[]{:S(2)}) collective-permute-start(bf16[128,1792]{1,0:T(8,128)(2,1)} %get-tuple-element.73), channel_id=1, source_target_pairs={{0,8},{4,12},{8,0},{12,4},{1,9},{5,13},{9,1},{13,5},{2,10},{6,14},... | collective-permute-start | bytes 1376264 | tf_op jit(solution)/shard_map/ppermute | solution.py:23
  5.8 28.3 %collective-permute-start.3 = (bf16[128,1792]{1,0:T(8,128)(2,1)}, bf16[128,1792]{1,0:T(8,128)(2,1)}, u32[]{:S(2)}, u32[]{:S(2)}) collective-permute-start(bf16[128,1792]{1,0:T(8,128)(2,1)} %get-tuple-element.74), channel_id=1, source_target_pairs={{0,8},{4,12},{8,0},{12,4},{1,9},{5,13},{9,1},{13,5},{2,10},{6,14},... | collective-permute-start | bytes 1376264 | tf_op jit(solution)/shard_map/ppermute | solution.py:23
  5.9 43.2 %collective-permute-start.1 = (bf16[128,3584]{1,0:T(8,128)(2,1)}, bf16[128,3584]{1,0:T(8,128)(2,1)S(1)}, u32[]{:S(2)}, u32[]{:S(2)}) collective-permute-start(bf16[128,3584]{1,0:T(8,128)(2,1)} %get-tuple-element.72), channel_id=1, source_target_pairs={{0,8},{4,12},{8,0},{12,4},{1,9},{5,13},{9,1},{13,5},{2,10},{6,14},... | collective-permute-start | bytes 2752520 | tf_op jit(solution)/shard_map/ppermute | solution.py:23
  34.1 1.9 %collective-permute-start.4 = (bf16[128,1792]{1,0:T(8,128)(2,1)S(1)}, bf16[128,1792]{1,0:T(8,128)(2,1)S(1)}, u32[]{:S(2)}, u32[]{:S(2)}) collective-permute-start(bf16[128,1792]{1,0:T(8,128)(2,1)S(1)} %collective-permute-done.2.refs_1_.refs_0_), channel_id=1, source_target_pairs={{0,4},{4,0},{8,12},{12,8},{1,5},{5,1},{9,13},{13,9},{2,6},{6,2},{1... | collective-permute-start | bytes 1376264 | tf_op jit(solution)/shard_map/ppermute | solution.py:23
  34.2 2.7 %collective-permute-start.5 = (bf16[128,1792]{1,0:T(8,128)(2,1)}, bf16[128,1792]{1,0:T(8,128)(2,1)S(1)}, u32[]{:S(2)}, u32[]{:S(2)}) collective-permute-start(bf16[128,1792]{1,0:T(8,128)(2,1)} %collective-permute-done.3.refs_2_.refs_1_), channel_id=1, source_target_pairs={{0,4},{4,0},{8,12},{12,8},{1,5},{5,1},{9,13},{13,9},{2,6},{6,2},{1... | collective-permute-start | bytes 1376264 | tf_op jit(solution)/shard_map/ppermute | solution.py:23
  49.0 2.5 %collective-permute-start.6 = (bf16[128,3584]{1,0:T(8,128)(2,1)S(1)}, bf16[128,3584]{1,0:T(8,128)(2,1)S(1)}, u32[]{:S(2)}, u32[]{:S(2)}) collective-permute-start(bf16[128,3584]{1,0:T(8,128)(2,1)S(1)} %collective-permute-done.1.refs_1_.refs_0_.refs_2_), channel_id=1, source_target_pairs={{0,4},{4,0},{8,12},{12,8},{1,5},{5,1},{9,13},{13,9},{2,6},{6,2},{1... | collective-permute-start | bytes 2752520 | tf_op jit(solution)/shard_map/ppermute | solution.py:23
  49.2 23.7 %collective-permute-start.14 = (bf16[256,2048]{1,0:T(8,128)(2,1)S(1)}, bf16[256,2048]{1,0:T(8,128)(2,1)S(1)}, u32[]{:S(2)}, u32[]{:S(2)}) collective-permute-start(bf16[256,2048]{1,0:T(8,128)(2,1)S(1)} %constant_dynamic-slice_fusion.7), channel_id=1, source_target_pairs={{0,4},{4,0},{8,12},{12,8},{1,5},{5,1},{9,13},{13,9},{2,6},{6,2},{1... | collective-permute-start | bytes 3145736 | tf_op jit(solution)/shard_map/ppermute | solution.py:23
  51.5 12.7 %copy-start.2 = (bf16[128,3584]{1,0:T(8,128)(2,1)}, bf16[128,3584]{1,0:T(8,128)(2,1)S(1)}, u32[]{:S(2)}) copy-start(bf16[128,3584]{1,0:T(8,128)(2,1)S(1)} %collective-permute-done.6.refs_2_.refs_1_.refs_5_) | copy-start | bytes 2752516
  56.0 2.3 %collective-permute-start.9 = (bf16[4,64,128]{2,1,0:T(8,128)(2,1)S(1)}, bf16[4,64,128]{2,1,0:T(8,128)(2,1)S(1)}, u32[]{:S(2)}, u32[]{:S(2)}) collective-permute-start(bf16[4,64,128]{2,1,0:T(8,128)(2,1)S(1)} %get-tuple-element.85), channel_id=1, source_target_pairs={{0,4},{4,0},{8,12},{12,8},{1,5},{5,1},{9,13},{13,9},{2,6},{6,2},{1... | collective-permute-start | bytes 196616 | tf_op jit(solution)/shard_map/ppermute | solution.py:23
  56.2 4.0 %collective-permute-start.8 = (bf16[4,64,128]{2,1,0:T(8,128)(2,1)S(1)}, bf16[4,64,128]{2,1,0:T(8,128)(2,1)S(1)}, u32[]{:S(2)}, u32[]{:S(2)}) collective-permute-start(bf16[4,64,128]{2,1,0:T(8,128)(2,1)S(1)} %get-tuple-element.85), channel_id=1, source_target_pairs={{0,12},{4,8},{8,4},{12,0},{1,13},{5,9},{9,5},{13,1},{2,14},{6,10},... | collective-permute-start | bytes 196616 | tf_op jit(solution)/shard_map/ppermute | solution.py:23
  56.3 6.2 %collective-permute-start.7 = (bf16[4,64,128]{2,1,0:T(8,128)(2,1)S(1)}, bf16[4,64,128]{2,1,0:T(8,128)(2,1)S(1)}, u32[]{:S(2)}, u32[]{:S(2)}) collective-permute-start(bf16[4,64,128]{2,1,0:T(8,128)(2,1)S(1)} %get-tuple-element.85), channel_id=1, source_target_pairs={{0,8},{4,12},{8,0},{12,4},{1,9},{5,13},{9,1},{13,5},{2,10},{6,14},... | collective-permute-start | bytes 196616 | tf_op jit(solution)/shard_map/ppermute | solution.py:23
  58.2 12.3 %collective-permute-start.12 = (bf16[256,512]{1,0:T(8,128)(2,1)S(1)}, bf16[256,512]{1,0:T(8,128)(2,1)S(1)}, u32[]{:S(2)}, u32[]{:S(2)}) collective-permute-start(bf16[256,512]{1,0:T(8,128)(2,1)S(1)} %get-tuple-element.89), channel_id=1, source_target_pairs={{0,8},{4,12},{8,0},{12,4},{1,9},{5,13},{9,1},{13,5},{2,10},{6,14},... | collective-permute-start | bytes 786440 | tf_op jit(solution)/shard_map/ppermute | solution.py:23
  58.3 14.5 %collective-permute-start.13 = (bf16[256,512]{1,0:T(8,128)(2,1)S(1)}, bf16[256,512]{1,0:T(8,128)(2,1)S(1)}, u32[]{:S(2)}, u32[]{:S(2)}) collective-permute-start(bf16[256,512]{1,0:T(8,128)(2,1)S(1)} %get-tuple-element.93), channel_id=1, source_target_pairs={{0,12},{4,8},{8,4},{12,0},{1,13},{5,9},{9,5},{13,1},{2,14},{6,10},... | collective-permute-start | bytes 786440 | tf_op jit(solution)/shard_map/ppermute | solution.py:23
  62.5 4.6 %collective-permute-start.10 = (bf16[4,64,128]{2,1,0:T(8,128)(2,1)S(1)}, bf16[4,64,128]{2,1,0:T(8,128)(2,1)S(1)}, u32[]{:S(2)}, u32[]{:S(2)}) collective-permute-start(bf16[4,64,128]{2,1,0:T(8,128)(2,1)S(1)} %fusion.8), channel_id=1, source_target_pairs={{0,1},{1,0},{2,3},{3,2},{4,5},{5,4},{6,7},{7,6},{8,9},{9,8},{10,11... | collective-permute-start | bytes 196616 | tf_op jit(solution)/shard_map/ppermute | solution.py:23
  67.2 5.6 %collective-permute-start.11 = (bf16[4,64,128]{2,1,0:T(8,128)(2,1)S(1)}, bf16[4,64,128]{2,1,0:T(8,128)(2,1)S(1)}, u32[]{:S(2)}, u32[]{:S(2)}) collective-permute-start(bf16[4,64,128]{2,1,0:T(8,128)(2,1)S(1)} %get-tuple-element.135), channel_id=1, source_target_pairs={{0,2},{1,3},{2,0},{3,1},{4,6},{5,7},{6,4},{7,5},{8,10},{9,11},{10,... | collective-permute-start | bytes 196616 | tf_op jit(solution)/shard_map/ppermute | solution.py:23
  69.9 16.4 %collective-permute-start.16 = (bf16[256,512]{1,0:T(8,128)(2,1)}, bf16[256,512]{1,0:T(8,128)(2,1)}, u32[]{:S(2)}, u32[]{:S(2)}) collective-permute-start(bf16[256,512]{1,0:T(8,128)(2,1)} %get-tuple-element.104), channel_id=1, source_target_pairs={{0,8},{4,12},{8,0},{12,4},{1,9},{5,13},{9,1},{13,5},{2,10},{6,14},... | collective-permute-start | bytes 786440 | tf_op jit(solution)/shard_map/ppermute | solution.py:23
  70.5 15.0 %collective-permute-start.17 = (bf16[256,512]{1,0:T(8,128)(2,1)}, bf16[256,512]{1,0:T(8,128)(2,1)}, u32[]{:S(2)}, u32[]{:S(2)}) collective-permute-start(bf16[256,512]{1,0:T(8,128)(2,1)} %get-tuple-element.107), channel_id=1, source_target_pairs={{0,12},{4,8},{8,4},{12,0},{1,13},{5,9},{9,5},{13,1},{2,14},{6,10},... | collective-permute-start | bytes 786440 | tf_op jit(solution)/shard_map/ppermute | solution.py:23
  76.8 17.9 %collective-permute-start.15 = (bf16[2,128,512]{2,1,0:T(8,128)(2,1)}, bf16[2,128,512]{2,1,0:T(8,128)(2,1)}, u32[]{:S(2)}, u32[]{:S(2)}) collective-permute-start(bf16[2,128,512]{2,1,0:T(8,128)(2,1)} %get-tuple-element.100), channel_id=1, source_target_pairs={{0,1},{1,0},{2,3},{3,2},{4,5},{5,4},{6,7},{7,6},{8,9},{9,8},{10,11... | collective-permute-start | bytes 786440 | tf_op jit(solution)/shard_map/ppermute | solution.py:23
  78.3 9.0 %copy-start.1 = (bf16[256,8192]{1,0:T(8,128)(2,1)S(1)}, bf16[256,8192]{1,0:T(8,128)(2,1)}, u32[]{:S(2)}) copy-start(bf16[256,8192]{1,0:T(8,128)(2,1)} %refs_4_.9) | copy-start | bytes 12582916
  78.3 21.0 %collective-permute-start.20 = (bf16[256,512]{1,0:T(8,128)(2,1)}, bf16[256,512]{1,0:T(8,128)(2,1)S(1)}, u32[]{:S(2)}, u32[]{:S(2)}) collective-permute-start(bf16[256,512]{1,0:T(8,128)(2,1)} %get-tuple-element.115), channel_id=1, source_target_pairs={{0,8},{4,12},{8,0},{12,4},{1,9},{5,13},{9,1},{13,5},{2,10},{6,14},... | collective-permute-start | bytes 786440 | tf_op jit(solution)/shard_map/ppermute | solution.py:23
  78.8 17.8 %collective-permute-start.21 = (bf16[256,512]{1,0:T(8,128)(2,1)}, bf16[256,512]{1,0:T(8,128)(2,1)S(1)}, u32[]{:S(2)}, u32[]{:S(2)}) collective-permute-start(bf16[256,512]{1,0:T(8,128)(2,1)} %get-tuple-element.118), channel_id=1, source_target_pairs={{0,12},{4,8},{8,4},{12,0},{1,13},{5,9},{9,5},{13,1},{2,14},{6,10},... | collective-permute-start | bytes 786440 | tf_op jit(solution)/shard_map/ppermute | solution.py:23
  85.5 22.1 %collective-permute-start.24 = (bf16[256,512]{1,0:T(8,128)(2,1)S(1)}, bf16[256,512]{1,0:T(8,128)(2,1)S(1)}, u32[]{:S(2)}, u32[]{:S(2)}) collective-permute-start(bf16[256,512]{1,0:T(8,128)(2,1)S(1)} %copy-done.19), channel_id=1, source_target_pairs={{0,8},{4,12},{8,0},{12,4},{1,9},{5,13},{9,1},{13,5},{2,10},{6,14},... | collective-permute-start | bytes 786440 | tf_op jit(solution)/shard_map/ppermute | solution.py:23
  86.3 21.4 %collective-permute-start.25 = (bf16[256,512]{1,0:T(8,128)(2,1)S(1)}, bf16[256,512]{1,0:T(8,128)(2,1)S(1)}, u32[]{:S(2)}, u32[]{:S(2)}) collective-permute-start(bf16[256,512]{1,0:T(8,128)(2,1)S(1)} %copy-done.20), channel_id=1, source_target_pairs={{0,12},{4,8},{8,4},{12,0},{1,13},{5,9},{9,5},{13,1},{2,14},{6,10},... | collective-permute-start | bytes 786440 | tf_op jit(solution)/shard_map/ppermute | solution.py:23
  94.6 12.0 %collective-permute-start.19 = (bf16[2,128,512]{2,1,0:T(8,128)(2,1)S(1)}, bf16[2,128,512]{2,1,0:T(8,128)(2,1)S(1)}, u32[]{:S(2)}, u32[]{:S(2)}) collective-permute-start(bf16[2,128,512]{2,1,0:T(8,128)(2,1)S(1)} %get-tuple-element.109), channel_id=1, source_target_pairs={{0,1},{1,0},{2,3},{3,2},{4,5},{5,4},{6,7},{7,6},{8,9},{9,8},{10,11... | collective-permute-start | bytes 786440 | tf_op jit(solution)/shard_map/ppermute | solution.py:23
  96.6 15.0 %collective-permute-start.18 = (bf16[128,512]{1,0:T(8,128)(2,1)S(1)}, bf16[128,512]{1,0:T(8,128)(2,1)S(1)}, u32[]{:S(2)}, u32[]{:S(2)}) collective-permute-start(bf16[128,512]{1,0:T(8,128)(2,1)S(1)} %fusion.4), channel_id=1, source_target_pairs={{0,2},{1,3},{2,0},{3,1},{4,6},{5,7},{6,4},{7,5},{8,10},{9,11},{10,... | collective-permute-start | bytes 393224 | tf_op jit(solution)/shard_map/ppermute | solution.py:23
  100.5 14.5 %collective-permute-start.23 = (bf16[2,128,512]{2,1,0:T(8,128)(2,1)S(1)}, bf16[2,128,512]{2,1,0:T(8,128)(2,1)S(1)}, u32[]{:S(2)}, u32[]{:S(2)}) collective-permute-start(bf16[2,128,512]{2,1,0:T(8,128)(2,1)S(1)} %get-tuple-element.120), channel_id=1, source_target_pairs={{0,1},{1,0},{2,3},{3,2},{4,5},{5,4},{6,7},{7,6},{8,9},{9,8},{10,11... | collective-permute-start | bytes 786440 | tf_op jit(solution)/shard_map/ppermute | solution.py:23
  106.7 6.8 %collective-permute-start.22 = (bf16[128,512]{1,0:T(8,128)(2,1)S(1)}, bf16[128,512]{1,0:T(8,128)(2,1)S(1)}, u32[]{:S(2)}, u32[]{:S(2)}) collective-permute-start(bf16[128,512]{1,0:T(8,128)(2,1)S(1)} %fusion.5), channel_id=1, source_target_pairs={{0,2},{1,3},{2,0},{3,1},{4,6},{5,7},{6,4},{7,5},{8,10},{9,11},{10,... | collective-permute-start | bytes 393224 | tf_op jit(solution)/shard_map/ppermute | solution.py:23
  108.9 14.1 %collective-permute-start.27 = (bf16[2,128,512]{2,1,0:T(8,128)(2,1)S(1)}, bf16[2,128,512]{2,1,0:T(8,128)(2,1)S(1)}, u32[]{:S(2)}, u32[]{:S(2)}) collective-permute-start(bf16[2,128,512]{2,1,0:T(8,128)(2,1)S(1)} %get-tuple-element.131), channel_id=1, source_target_pairs={{0,1},{1,0},{2,3},{3,2},{4,5},{5,4},{6,7},{7,6},{8,9},{9,8},{10,11... | collective-permute-start | bytes 786440 | tf_op jit(solution)/shard_map/ppermute | solution.py:23
  115.1 8.3 %collective-permute-start.26 = (bf16[128,512]{1,0:T(8,128)(2,1)S(1)}, bf16[128,512]{1,0:T(8,128)(2,1)S(1)}, u32[]{:S(2)}, u32[]{:S(2)}) collective-permute-start(bf16[128,512]{1,0:T(8,128)(2,1)S(1)} %fusion.6), channel_id=1, source_target_pairs={{0,2},{1,3},{2,0},{3,1},{4,6},{5,7},{6,4},{7,5},{8,10},{9,11},{10,... | collective-permute-start | bytes 393224 | tf_op jit(solution)/shard_map/ppermute | solution.py:23
  123.2 7.9 %collective-permute-start.28 = (bf16[128,512]{1,0:T(8,128)(2,1)S(1)}, bf16[128,512]{1,0:T(8,128)(2,1)S(1)}, u32[]{:S(2)}, u32[]{:S(2)}) collective-permute-start(bf16[128,512]{1,0:T(8,128)(2,1)S(1)} %fusion.7), channel_id=1, source_target_pairs={{0,2},{1,3},{2,0},{3,1},{4,6},{5,7},{6,4},{7,5},{8,10},{9,11},{10,... | collective-permute-start | bytes 393224 | tf_op jit(solution)/shard_map/ppermute | solution.py:23
  (18 other events, 64.1 us)

commit v7 on v6

--- a/solution.py
+++ b/solution.py
@@ -7,9 +7,8 @@
 
 F32 = jnp.float32
 BF16 = jnp.bfloat16
-VMEM_LIMIT = 40 * 1024 * 1024
+VMEM_LIMIT = 60 * 1024 * 1024
 WIDTHS = (512, 512, 512, 512)
-EARLY = 2
 CAP = 4
 HALVES = 2
 HINT = 1000
@@ -63,47 +62,61 @@
     )(array)
 
 
-def product_kernel(lower, upper, has_prior, *refs):
-    pieces, refs = refs[: lower + upper], refs[lower + upper :]
+def product_kernel(counts, has_prior, *refs):
+    pieces, refs = refs[: sum(counts)], refs[sum(counts) :]
     if has_prior:
         prior_ref, refs = refs[0], refs[1:]
     w_ref, out_ref, rows = refs
 
     @pl.when(pl.program_id(0) == 0)
     def _():
-        half = rows.shape[0] // 2
-        for top, group in ((0, pieces[:lower]), (half, pieces[lower:])):
+        height = rows.shape[0] // len(counts)
+        spot = 0
+        for group, count in enumerate(counts):
             start = 0
-            for piece in group:
-                rows[top : top + half, start : start + piece.shape[1]] = piece[...]
-                start += piece.shape[1]
+            for piece in pieces[spot : spot + count]:
+                wide = piece.shape[1]
+                rows[group * height : (group + 1) * height, start : start + wide] = piece[...]
+                start += wide
+            spot += count
 
     value = jnp.dot(rows[...], w_ref[...], preferred_element_type=F32)
     if has_prior:
-        value += prior_ref[...]
-    out_ref[...] = value
-
-
-def product(lower, upper, weight, depth_block, prior, first, width, tile, hint=HINT):
-    rows = lower[0].shape[0]
-    depth = sum(x.shape[1] for x in lower)
-    args = [*lower, *upper]
-    in_specs = [pl.BlockSpec(x.shape, lambda n: (0, 0)) for x in args]
+        top = prior_ref.shape[0]
+        out_ref[:top, :] = value[:top] + prior_ref[...]
+        if top < value.shape[0]:
+            out_ref[top:, :] = value[top:]
+    else:
+        out_ref[...] = value
+
+
+def product(groups, weight, depth_block, first, width, tile, prior=None, prior_block=0, hint=HINT):
+    rows = groups[0][0][0].shape[0]
+    depth = sum(wide for _, wide, _ in groups[0])
+    total = rows * len(groups)
+    in_specs, args = [], []
+    for group in groups:
+        for array, wide, block in group:
+            in_specs.append(pl.BlockSpec((rows, wide), lambda n, block=block: (0, block)))
+            args.append(array)
     if prior is not None:
-        in_specs.append(pl.BlockSpec((2 * rows, tile), lambda n: (0, n)))
+        in_specs.append(
+            pl.BlockSpec((2 * rows, tile), lambda n: (prior_block, first // tile + n))
+        )
         args.append(prior)
     in_specs.append(pl.BlockSpec((depth, tile), lambda n: (depth_block, first // tile + n)))
     args.append(weight)
+    counts = [len(group) for group in groups]
     return pl.pallas_call(
-        lambda *refs: product_kernel(len(lower), len(upper), prior is not None, *refs),
+        lambda *refs: product_kernel(counts, prior is not None, *refs),
         grid=(width // tile,),
         in_specs=in_specs,
-        out_specs=pl.BlockSpec((2 * rows, tile), lambda n: (0, n)),
-        out_shape=jax.ShapeDtypeStruct((2 * rows, width), F32),
-        scratch_shapes=[pltpu.VMEM((2 * rows, depth), BF16)],
+        out_specs=pl.BlockSpec((total, tile), lambda n: (0, n)),
+        out_shape=jax.ShapeDtypeStruct((total, width), F32),
+        scratch_shapes=[pltpu.VMEM((total, depth), BF16)],
         compiler_params=params(),
         cost_estimate=cost(
-            4 * rows * depth * width, 2 * depth * (width + 2 * rows) + 8 * rows * width, hint
+            2 * total * depth * width, 2 * depth * (width + total) + 8 * total * width, hint
         ),
         name="base",
     )(*args)
@@ -377,63 +390,60 @@
     core_maps = swap(core_block, "pool", 1)
 
     (near_lowrank,) = scores(picks, 0, [own_rows], [near_b], input_maps, 0, ids=owned_ids)
-    near_base = product(
-        [tie(own_rows, near_lowrank)], [near_b], weight, 0, None, 0, width, 512
-    )
-
-    first_a, first_b = lax.optimization_barrier((first_a, first_b, near_base))[:2]
+    near_late = product(
+        [[(tie(own_rows, near_lowrank), part, 1)], [(near_b, part, 1)]],
+        weight, 1, 0, width, 512,
+    )
+
+    first_a, first_b = lax.optimization_barrier((first_a, first_b, near_late))[:2]
     a0 = [first_a, first_b]
     b0 = [swap(x, "pool", 1) for x in a0]
     (raw,) = scores(picks, 2, a0, b0, input_maps, 0)
-    begun = []
-    after = raw
-    for index in range(EARLY):
-        begun.append(
-            product(
-                [tie(first_a, after), first_b], b0, weight, 0, None, starts[index], WIDTHS[index], 512
-            )
-        )
-        after = begun[-1]
-    a1 = [tie(second, after)]
-    b1 = [swap(a1[0], "pool", 1)]
+    base = product(
+        [
+            [(tie(own_rows, raw), part, 0)],
+            [(near_b, part, 0)],
+            [(x, part // 2, 0) for x in a0],
+            [(x, part // 2, 0) for x in b0],
+        ],
+        weight, 0, 0, width, 512, near_late,
+    )
+    a1 = tie(second, base)
+    b1 = swap(a1, "pool", 1)
     total, sent = scores(
-        picks, 2, a1, b1, input_maps, 1, prior=raw, near=near_lowrank, ids=owned_ids
+        picks, 2, [a1], [b1], input_maps, 1, prior=raw, near=near_lowrank, ids=owned_ids
     )
 
     def far_piece(index, after, hint=HINT):
-        left = [tie(a1[0], after)]
-        if index < EARLY:
-            piece = product(
-                left, b1, weight, 1, begun[index], starts[index], WIDTHS[index], 256, hint
-            )
-        else:
-            piece = product(
-                a0 + left, b0 + b1, weight, 0, None, starts[index], WIDTHS[index], 256, hint
-            )
-        return piece.reshape(2, rows, WIDTHS[index])
+        return product(
+            [[(tie(a1, after), part, 0)], [(b1, part, 0)]],
+            weight, 1, starts[index], WIDTHS[index], 256, base, 1, hint,
+        ).reshape(2, rows, WIDTHS[index])
 
     got = [swap(sent, "pool", step) for step in (2, 3, 1)]
+    pieces = [far_piece(0, sent, 1)]
+
+    def start_maps(index, after):
+        pair = blocks[2 * index : 2 * index + 2]
+        return [swap(tie(x, after), "pool", 2 + k) for k, x in enumerate(pair)]
+
+    moved = [[swap(blocks[0], "pool", 2), swap(tie(blocks[1], sent), "pool", 3)]]
+    moved[0][0] = tie(moved[0][0], sent)
+    got = lax.optimization_barrier((*got, moved[0][0], pieces[0]))[:3]
     total = total + sum(x.astype(F32) for x in got)
-
-    def start_maps(index, after):
-        pair = [tie(x, after) for x in blocks[2 * index : 2 * index + 2]]
-        return [swap(x, "pool", 2 + k) for k, x in enumerate(pair)]
-
-    moved = [start_maps(0, sent)]
     sent = total.astype(BF16)
     got = swap(sent, "tensor", 1)
     moved.append(start_maps(1, sent))
-    pieces = [far_piece(0, sent, 1)]
-    moved[0] = [tie(x, pieces[0]) for x in moved[0]]
-    got = lax.optimization_barrier((got, pieces[0]))[0]
+    pieces.append(far_piece(1, sent, 1))
+    got = tie(got, pieces[1])
     total = total + got.astype(F32)
     sent = total.astype(BF16)
     got = swap(sent, "tensor", 2)
     moved.append(start_maps(2, sent))
-    moved[0] = [tie(x, sent) for x in moved[0]]
+    moved[0][1] = tie(moved[0][1], sent)
     got = lax.optimization_barrier((got, *moved[0]))[0]
 
-    near_base = near_base.reshape(2, rows, width)
+    near_base = base.reshape(4, rows, width)
     side = ((place ^ t) >> 1) & 1
     parts = []
     spread = send = None
@@ -467,11 +477,13 @@
             moved.append(start_maps(3, send))
         else:
             keep, send = combine(*common, spread=spread)
-        if chunk + 1 < count:
-            pieces.append(far_piece(chunk + 1, send))
+        if chunk == 0:
+            pieces.append(far_piece(2, send))
         halves.append((keep, swap(send, "tensor", 1)))
         if chunk > 0:
             parts.append(finish(chunk - 1, send))
+        if chunk == 1:
+            pieces.append(far_piece(3, started[0]))
     parts.append(finish(count - 1, started[-1]))
     return jnp.concatenate(parts, axis=1).astype(BF16)
 

time: 132 us -> 207 us (1.57)
  Pallas kernels: 60.4 us -> 137 us
  starting transfers between devices: 30.4 us -> 25.4 us
  local copies, waits for them, and re-layouts: 9.63 us -> 11.9 us
    pallas_call x1, Pallas kernels: 1.25 us -> 56.7 us  [cut_columns(): pl.pallas_call(cut_kernel, in_specs=[pl.BlockSpec(memory_space=pl.ANY)],...]
    pallas_call x4, Pallas kernels: 7.03 us -> 17 us  [combine(): pl.pallas_call(lambda *refs: combine_kernel(bool(build), *refs), grid_spe...]
    pallas_call x3, Pallas kernels: 16.4 us -> 23.2 us  [scores(): pl.pallas_call(lambda *refs: scores_kernel(first, half * depth, len(lower...]
    ppermute x29, starting transfers between devices: 30.4 us -> 25.4 us  [swap(): return lax.ppermute(values, axis, partners(lax.axis_size(axis), step))]
    pallas_call x7 -> x6, Pallas kernels: 35.8 us -> 40.3 us  [product(): pl.pallas_call(lambda *refs: product_kernel(counts, prior is not None, *r...]
    dynamic_slice x1, local copies, waits for them, and re-layouts: 0.11 us -> 2.37 us  [per_device_fast(): lax.dynamic_slice(output_maps, (0, (place ^ 1) * width), (held, width))]
    unnamed x42 -> x50, local copies, waits for them, and re-layouts: 6.33 us -> 4.92 us
  transfers between devices with their start and end apart: 29 -> 29, of which waited for: 11 -> 9; matrix products, arithmetic and copies ran while one was open for 5% -> 6% of each run, Pallas kernels for 46% -> 66%
where the time goes in v7:
time: 207 us
  Pallas kernels  137 us (66%)
  starting transfers between devices  25.4 us (12%)
  waiting for transfers between devices  25.3 us (12%)
  local copies, waits for them, and re-layouts  11.9 us (6%)
  other arithmetic  6.49 us (3%)
    pallas_call x1, Pallas kernels, cut_columns(): pl.pallas_call(cut_kernel, in_specs=[pl.BlockSpec(memory_space=pl.ANY)],...  56.7 us
    pallas_call x6, Pallas kernels, product(): pl.pallas_call(lambda *refs: product_kernel(counts, prior is not None, *r...  40.3 us
    ppermute x29, starting transfers between devices, swap(): return lax.ppermute(values, axis, partners(lax.axis_size(axis), step))  25.4 us
    ppermute x29, waiting for transfers between devices, swap(): return lax.ppermute(values, axis, partners(lax.axis_size(axis), step))  25.3 us
    pallas_call x3, Pallas kernels, scores(): pl.pallas_call(lambda *refs: scores_kernel(first, half * depth, len(lower...  23.2 us
    pallas_call x4, Pallas kernels, combine(): pl.pallas_call(lambda *refs: combine_kernel(bool(build), *refs), grid_spe...  17 us
    unnamed x50, local copies, waits for them, and re-layouts  4.92 us
  transfers between devices with their start and end apart: 29, of which 9 were waited for; matrix products, arithmetic and copies ran while one was open for 6% of the time, Pallas kernels for 66%

profile of v7, /device:TPU:0, one launch (start us, length us, event | category | flops | bytes accessed | tf_op | source)
XLA Modules:
  0.0 206.7 jit_solution(7741948473488926621)
XLA Ops:
  0.5 56.7 %cut.1 = (bf16[128,1792]{1,0:T(8,128)(2,1)}, bf16[128,1792]{1,0:T(8,128)(2,1)}, bf16[128,3584]{1,0:T(8,128)(2,1)}) custom-call(bf16[128,7168]{1,0:T(8,128)(2,1)} %refs_0_.1), custom_call_target="tpu_custom_call" | custom-call | bytes 3670 | tf_op jit(solution)/shard_map/cut/pallas_call | solution.py:53
  57.2 2.6 %collective-permute-start.2 = (bf16[128,1792]{1,0:T(8,128)(2,1)}, bf16[128,1792]{1,0:T(8,128)(2,1)S(1)}, u32[]{:S(2)}, u32[]{:S(2)}) collective-permute-start(bf16[128,1792]{1,0:T(8,128)(2,1)} %get-tuple-element.73), channel_id=1, source_target_pairs={{0,8},{4,12},{8,0},{12,4},{1,9},{5,13},{9,1},{13,5},{2,10},{6,14},... | collective-permute-start | bytes 1376264 | tf_op jit(solution)/shard_map/ppermute | solution.py:22
  59.8 1.9 collective-permute-start.1
  65.1 3.0 %constant_dynamic-slice_fusion.8 = (bf16[256,512]{1,0:T(8,128)(2,1)}, bf16[256,512]{1,0:T(8,128)(2,1)}, bf16[256,512]{1,0:T(8,128)(2,1)}, bf16[256,512]{1,0:T(8,...) fusion(bf16[256,8192]{1,0:T(8,128)(2,1)} %refs_4_.5, ...), kind=kLoop, calls=%fused_computation.41 | loop fusion | bytes 4194336 | tf_op jit(solution)/shard_map/dynamic_slice | solution.py:348
  68.7 2.4 %constant_dynamic-slice_fusion.7 = bf16[256,2048]{1,0:T(8,128)(2,1)} fusion(bf16[256,8192]{1,0:T(8,128)(2,1)} %refs_4_.5, s32[]{:T(128)S(6)} %select_n.100), kind=kLoop, calls=%fused_computation.40 | loop fusion | bytes 2097156 | tf_op jit(solution)/shard_map/dynamic_slice | solution.py:346
  72.4 10.0 %scores.3.refs_5_ = f32[2,64,128]{2,1,0:T(8,128)} custom-call(s32[17]{0:T(128)} %pad_add_fusion.refs_0_, bf16[128,7168]{1,0:T(8,128)(2,1)} %refs_0_.1, bf16[128,7168]{1,0:T(8,128)(2,1)} %copy-done.3, bf16[16,64,7168]{2,1,0:T(8,128)(2,1)} %refs_3_.7, s32[4,1,128]{2,1,0:T(1,128)} %bitcast.49), custom_call_target="tpu_custom_call" | custom-call | flops 939524 | bytes 11010 | tf_op jit(solution)/shard_map/scores/pallas_call | solution.py:224
  82.5 9.7 %base.6.refs_6_ = f32[256,2048]{1,0:T(8,128)} custom-call(bf16[128,7168]{1,0:T(8,128)(2,1)} %refs_0_.1, bf16[128,7168]{1,0:T(8,128)(2,1)} %copy-done.3, bf16[7168,2048]{1,0:T(8,128)(2,1)} %refs_3_.11), custom_call_target="tpu_custom_call" | custom-call | flops 3758096 | bytes 20709 | tf_op jit(solution)/shard_map/base/pallas_call | solution.py:110
  95.7 6.1 %scores.4.refs_4_ = f32[2,256,128]{2,1,0:T(8,128)} custom-call(s32[17]{0:T(128)} %pad_add_fusion.refs_0_, bf16[128,1792]{1,0:T(8,128)(2,1)} %copy-done.4, bf16[128,1792]{1,0:T(8,128)(2,1)} %collective-permute-done.3.refs_2_.refs_3_, bf16[128,1792]{1,0:T(8,128)(2,1)} %copy-done.5, bf16[128,1792]{1,0:T(8,128)(2,1)} %copy-done.6, bf16[16,64,7168]{2,1,0:T(8,128)(2,1)} %refs_3_.7), custom_call_target="tpu_custom_call" | custom-call | flops 469762 | bytes 5505 | tf_op jit(solution)/shard_map/scores/pallas_call | solution.py:224
  101.8 13.5 %base.7.refs_2_ = f32[512,2048]{1,0:T(8,128)} custom-call(bf16[128,7168]{1,0:T(8,128)(2,1)} %refs_0_.1, bf16[128,7168]{1,0:T(8,128)(2,1)} %copy-done.3, bf16[128,1792]{1,0:T(8,128)(2,1)} %copy-done.4, bf16[128,1792]{1,0:T(8,128)(2,1)} %collective-permute-done.3.refs_2_.refs_3_, bf16[128,1792]{1,0:T(8,128)(2,1)} %copy-done.5, bf16[128,1792]{1,0:T(8,128)(2,1)} %copy-done.6, ...), custom_call_target="tpu_custom_call" | custom-call | flops 7516192 | bytes 26738 | tf_op jit(solution)/shard_map/base/pallas_call | solution.py:110
  116.0 1.9 collective-permute-done.6.refs_2_.refs_1_
  118.9 7.1 %scores.5 = (f32[4,64,128]{2,1,0:T(8,128)}, bf16[4,64,128]{2,1,0:T(8,128)(2,1)}) custom-call(s32[17]{0:T(128)} %pad_add_fusion.refs_0_, bf16[128,3584]{1,0:T(8,128)(2,1)} %copy-done, bf16[128,3584]{1,0:T(8,128)(2,1)} %copy-done.1, bf16[16,64,7168]{2,1,0:T(8,128)(2,1)} %refs_3_.7, f32[2,256,128]{2,1,0:T(8,128)} %scores.4.refs_4_, ...), custom_call_target="tpu_custom_call" | custom-call | flops 469762 | bytes 5505 | tf_op jit(solution)/shard_map/scores/pallas_call | solution.py:224
  126.3 2.0 collective-permute-start.7
  128.3 4.3 %base.8 = f32[256,512]{1,0:T(8,128)} custom-call(bf16[128,3584]{1,0:T(8,128)(2,1)} %copy-done, bf16[128,3584]{1,0:T(8,128)(2,1)} %copy-done.1, f32[512,2048]{1,0:T(8,128)} %base.7.refs_2_, bf16[7168,2048]{1,0:T(8,128)(2,1)} %refs_3_.11), custom_call_target="tpu_custom_call" | custom-call | flops 939524096 | bytes 6553600 | tf_op jit(solution)/shard_map/base/pallas_call | solution.py:110
  132.8 1.6 collective-permute-start.11
  134.4 4.3 %base.9 = f32[256,512]{1,0:T(8,128)} custom-call(bf16[128,3584]{1,0:T(8,128)(2,1)} %copy-done, bf16[128,3584]{1,0:T(8,128)(2,1)} %copy-done.1, f32[512,2048]{1,0:T(8,128)} %base.7.refs_2_, bf16[7168,2048]{1,0:T(8,128)(2,1)} %refs_3_.11), custom_call_target="tpu_custom_call" | custom-call | flops 939524096 | bytes 6553600 | tf_op jit(solution)/shard_map/base/pallas_call | solution.py:110
  139.4 2.6 %collective-permute-start.12 = (bf16[4,64,128]{2,1,0:T(8,128)(2,1)S(1)}, bf16[4,64,128]{2,1,0:T(8,128)(2,1)S(1)}, u32[]{:S(2)}, u32[]{:S(2)}) collective-permute-start(bf16[4,64,128]{2,1,0:T(8,128)(2,1)S(1)} %get-tuple-element.133), channel_id=1, source_target_pairs={{0,2},{1,3},{2,0},{3,1},{4,6},{5,7},{6,4},{7,5},{8,10},{9,11},{10,... | collective-permute-start | bytes 196616 | tf_op jit(solution)/shard_map/ppermute | solution.py:22
  142.0 1.3 collective-permute-start.16
  143.3 2.4 %collective-permute-done.12.refs_2_ = bf16[4,64,128]{2,1,0:T(8,128)(2,1)S(1)} collective-permute-done((bf16[4,64,128]{2,1,0:T(8,128)(2,1)S(1)}, bf16[4,64,128]{2,1,0:T(8,128)(2,1)S(1)}, u32[]{:S(2)}, u32[]{:S(2)}) %collective-permute-start.12) | collective-permute-done | bytes 65568 | tf_op jit(solution)/shard_map/ppermute | solution.py:22
  146.8 4.5 %combine.4 = (f32[2,128,512]{2,1,0:T(8,128)}, bf16[2,128,512]{2,1,0:T(8,128)(2,1)}, bf16[512,1024]{1,0:T(8,128)(2,1)}) custom-call(s32[10]{0:T(128)} %stack.40.refs_0_, f32[4,64,128]{2,1,0:T(8,128)} %get-tuple-element.134.refs_1_, bf16[4,64,128]{2,1,0:T(8,128)(2,1)} %copy-done.24, s32[4,128,128]{2,1,0:T(8,128)} %broadcast_in_dim.96.refs_3_, ...), custom_call_target="tpu_custom_call" | custom-call | flops 536870 | bytes 2752 | tf_op jit(solution)/shard_map/combine/pallas_call | solution.py:312
  151.3 1.6 collective-permute-start.20
  153.0 4.3 %base.10 = f32[256,512]{1,0:T(8,128)} custom-call(bf16[128,3584]{1,0:T(8,128)(2,1)} %copy-done, bf16[128,3584]{1,0:T(8,128)(2,1)} %copy-done.1, f32[512,2048]{1,0:T(8,128)} %base.7.refs_2_, bf16[7168,2048]{1,0:T(8,128)(2,1)} %refs_3_.11), custom_call_target="tpu_custom_call" | custom-call | flops 939524 | bytes 6553 | tf_op jit(solution)/shard_map/base/pallas_call | solution.py:110
  157.3 1.4 collective-permute-start.24
  159.4 4.3 %combine.5 = (f32[2,128,512]{2,1,0:T(8,128)}, bf16[2,128,512]{2,1,0:T(8,128)(2,1)}) custom-call(s32[10]{0:T(128)} %stack.40.refs_0_, bf16[512,1024]{1,0:T(8,128)(2,1)} %get-tuple-element.100.refs_1_, f32[4,128,2048]{2,1,0:T(8,128)} %bitcast.42, f32[2,128,512]{2,1,0:T(8,128)} %bitcast.45, bf16[256,8192]{1,0:T(8,128)(2,1)} %refs_4_.5, ...), custom_call_target="tpu_custom_call" | custom-call | flops 536870 | bytes 2752 | tf_op jit(solution)/shard_map/combine/pallas_call | solution.py:312
  163.7 1.8 collective-permute-start.19
  166.9 1.5 collective-permute-start.18
  169.1 4.1 %combine.6 = (f32[2,128,512]{2,1,0:T(8,128)}, bf16[2,128,512]{2,1,0:T(8,128)(2,1)}) custom-call(s32[10]{0:T(128)} %stack.40.refs_0_, bf16[512,1024]{1,0:T(8,128)(2,1)} %get-tuple-element.100.refs_1_, f32[4,128,2048]{2,1,0:T(8,128)} %bitcast.43, f32[2,128,512]{2,1,0:T(8,128)} %bitcast.47, bf16[256,8192]{1,0:T(8,128)(2,1)} %refs_4_.5, ...), custom_call_target="tpu_custom_call" | custom-call | flops 536870 | bytes 2752 | tf_op jit(solution)/shard_map/combine/pallas_call | solution.py:312
  173.9 4.3 %base.11 = f32[256,512]{1,0:T(8,128)} custom-call(bf16[128,3584]{1,0:T(8,128)(2,1)} %copy-done, bf16[128,3584]{1,0:T(8,128)(2,1)} %copy-done.1, f32[512,2048]{1,0:T(8,128)} %base.7.refs_2_, bf16[7168,2048]{1,0:T(8,128)(2,1)} %refs_3_.11), custom_call_target="tpu_custom_call" | custom-call | flops 939524 | bytes 6553 | tf_op jit(solution)/shard_map/base/pallas_call | solution.py:110
  180.2 4.1 %combine.7 = (f32[2,128,512]{2,1,0:T(8,128)}, bf16[2,128,512]{2,1,0:T(8,128)(2,1)}) custom-call(s32[10]{0:T(128)} %stack.40.refs_0_, bf16[512,1024]{1,0:T(8,128)(2,1)} %get-tuple-element.100.refs_1_, f32[4,128,2048]{2,1,0:T(8,128)} %bitcast.44, f32[2,128,512]{2,1,0:T(8,128)} %bitcast.48, bf16[256,8192]{1,0:T(8,128)(2,1)} %refs_4_.5, ...), custom_call_target="tpu_custom_call" | custom-call | flops 536870 | bytes 2752 | tf_op jit(solution)/shard_map/combine/pallas_call | solution.py:312
  184.4 1.7 collective-permute-start.27
  186.1 1.4 collective-permute-done.22
  187.9 8.1 %collective-permute-done.27 = bf16[2,128,512]{2,1,0:T(8,128)(2,1)S(1)} collective-permute-done((bf16[2,128,512]{2,1,0:T(8,128)(2,1)}, bf16[2,128,512]{2,1,0:T(8,128)(2,1)S(1)}, u32[]{:S(2)}, u32[]{:S(2)}) %collective-permute-start.27) | collective-permute-done | bytes 262176 | tf_op jit(solution)/shard_map/ppermute | solution.py:22
  198.0 7.8 %collective-permute-done.28 = bf16[128,512]{1,0:T(8,128)(2,1)S(1)} collective-permute-done((bf16[128,512]{1,0:T(8,128)(2,1)S(1)}, bf16[128,512]{1,0:T(8,128)(2,1)S(1)}, u32[]{:S(2)}, u32[]{:S(2)}) %collective-permute-start.28) | collective-permute-done | bytes 131104 | tf_op jit(solution)/shard_map/ppermute | solution.py:22
  (122 shorter events, 22.0 us)
Async XLA Ops:
  0.0 71.0 %collective-permute-start = (bf16[128,7168]{1,0:T(8,128)(2,1)}, bf16[128,7168]{1,0:T(8,128)(2,1)S(1)}, u32[]{:S(2)}, u32[]{:S(2)}) collective-permute-start(bf16[128,7168]{1,0:T(8,128)(2,1)} %refs_0_.1), channel_id=1, source_target_pairs={{0,4},{4,0},{8,12},{12,8},{1,5},{5,1},{9,13},{13,9},{2,6},{6,2},{1... | collective-permute-start | bytes 5505032 | tf_op jit(solution)/shard_map/ppermute | solution.py:22
  57.2 35.0 %collective-permute-start.2 = (bf16[128,1792]{1,0:T(8,128)(2,1)}, bf16[128,1792]{1,0:T(8,128)(2,1)S(1)}, u32[]{:S(2)}, u32[]{:S(2)}) collective-permute-start(bf16[128,1792]{1,0:T(8,128)(2,1)} %get-tuple-element.73), channel_id=1, source_target_pairs={{0,8},{4,12},{8,0},{12,4},{1,9},{5,13},{9,1},{13,5},{2,10},{6,14},... | collective-permute-start | bytes 1376264 | tf_op jit(solution)/shard_map/ppermute | solution.py:22
  59.7 32.4 %collective-permute-start.3 = (bf16[128,1792]{1,0:T(8,128)(2,1)}, bf16[128,1792]{1,0:T(8,128)(2,1)}, u32[]{:S(2)}, u32[]{:S(2)}) collective-permute-start(bf16[128,1792]{1,0:T(8,128)(2,1)} %get-tuple-element.74), channel_id=1, source_target_pairs={{0,8},{4,12},{8,0},{12,4},{1,9},{5,13},{9,1},{13,5},{2,10},{6,14},... | collective-permute-start | bytes 1376264 | tf_op jit(solution)/shard_map/ppermute | solution.py:22
  59.8 55.6 %collective-permute-start.1 = (bf16[128,3584]{1,0:T(8,128)(2,1)}, bf16[128,3584]{1,0:T(8,128)(2,1)S(1)}, u32[]{:S(2)}, u32[]{:S(2)}) collective-permute-start(bf16[128,3584]{1,0:T(8,128)(2,1)} %get-tuple-element.71), channel_id=1, source_target_pairs={{0,8},{4,12},{8,0},{12,4},{1,9},{5,13},{9,1},{13,5},{2,10},{6,14},... | collective-permute-start | bytes 2752520 | tf_op jit(solution)/shard_map/ppermute | solution.py:22
  92.2 1.9 collective-permute-start.4
  92.3 2.7 %collective-permute-start.5 = (bf16[128,1792]{1,0:T(8,128)(2,1)}, bf16[128,1792]{1,0:T(8,128)(2,1)S(1)}, u32[]{:S(2)}, u32[]{:S(2)}) collective-permute-start(bf16[128,1792]{1,0:T(8,128)(2,1)} %collective-permute-done.3.refs_2_.refs_3_), channel_id=1, source_target_pairs={{0,4},{4,0},{8,12},{12,8},{1,5},{5,1},{9,13},{13,9},{2,6},{6,2},{1... | collective-permute-start | bytes 1376264 | tf_op jit(solution)/shard_map/ppermute | solution.py:22
  101.8 13.7 %copy-start.7 = (bf16[256,2048]{1,0:T(8,128)(2,1)S(1)}, bf16[256,2048]{1,0:T(8,128)(2,1)}, u32[]{:S(2)}) copy-start(bf16[256,2048]{1,0:T(8,128)(2,1)} %constant_dynamic-slice_fusion.7) | copy-start | bytes 3145732
  115.4 2.5 %collective-permute-start.6 = (bf16[128,3584]{1,0:T(8,128)(2,1)S(1)}, bf16[128,3584]{1,0:T(8,128)(2,1)S(1)}, u32[]{:S(2)}, u32[]{:S(2)}) collective-permute-start(bf16[128,3584]{1,0:T(8,128)(2,1)S(1)} %collective-permute-done.1.refs_1_.refs_0_), channel_id=1, source_target_pairs={{0,4},{4,0},{8,12},{12,8},{1,5},{5,1},{9,13},{13,9},{2,6},{6,2},{1... | collective-permute-start | bytes 2752520 | tf_op jit(solution)/shard_map/ppermute | solution.py:22
  115.6 30.2 %collective-permute-start.14 = (bf16[256,2048]{1,0:T(8,128)(2,1)S(1)}, bf16[256,2048]{1,0:T(8,128)(2,1)S(1)}, u32[]{:S(2)}, u32[]{:S(2)}) collective-permute-start(bf16[256,2048]{1,0:T(8,128)(2,1)S(1)} %copy-done.7), channel_id=1, source_target_pairs={{0,4},{4,0},{8,12},{12,8},{1,5},{5,1},{9,13},{13,9},{2,6},{6,2},{1... | collective-permute-start | bytes 3145736 | tf_op jit(solution)/shard_map/ppermute | solution.py:22
  115.9 12.3 %collective-permute-start.10 = (bf16[256,512]{1,0:T(8,128)(2,1)}, bf16[256,512]{1,0:T(8,128)(2,1)}, u32[]{:S(2)}, u32[]{:S(2)}) collective-permute-start(bf16[256,512]{1,0:T(8,128)(2,1)} %get-tuple-element.84), channel_id=1, source_target_pairs={{0,8},{4,12},{8,0},{12,4},{1,9},{5,13},{9,1},{13,5},{2,10},{6,14},... | collective-permute-start | bytes 786440 | tf_op jit(solution)/shard_map/ppermute | solution.py:22
  126.0 6.5 %collective-permute-start.9 = (bf16[4,64,128]{2,1,0:T(8,128)(2,1)}, bf16[4,64,128]{2,1,0:T(8,128)(2,1)S(1)}, u32[]{:S(2)}, u32[]{:S(2)}) collective-permute-start(bf16[4,64,128]{2,1,0:T(8,128)(2,1)} %get-tuple-element.83), channel_id=1, source_target_pairs={{0,4},{4,0},{8,12},{12,8},{1,5},{5,1},{9,13},{13,9},{2,6},{6,2},{1... | collective-permute-start | bytes 196616 | tf_op jit(solution)/shard_map/ppermute | solution.py:22
  126.2 6.3 %collective-permute-start.8 = (bf16[4,64,128]{2,1,0:T(8,128)(2,1)}, bf16[4,64,128]{2,1,0:T(8,128)(2,1)S(1)}, u32[]{:S(2)}, u32[]{:S(2)}) collective-permute-start(bf16[4,64,128]{2,1,0:T(8,128)(2,1)} %get-tuple-element.83), channel_id=1, source_target_pairs={{0,12},{4,8},{8,4},{12,0},{1,13},{5,9},{9,5},{13,1},{2,14},{6,10},... | collective-permute-start | bytes 196616 | tf_op jit(solution)/shard_map/ppermute | solution.py:22
  126.3 6.4 %collective-permute-start.7 = (bf16[4,64,128]{2,1,0:T(8,128)(2,1)}, bf16[4,64,128]{2,1,0:T(8,128)(2,1)S(1)}, u32[]{:S(2)}, u32[]{:S(2)}) collective-permute-start(bf16[4,64,128]{2,1,0:T(8,128)(2,1)} %get-tuple-element.83), channel_id=1, source_target_pairs={{0,8},{4,12},{8,0},{12,4},{1,9},{5,13},{9,1},{13,5},{2,10},{6,14},... | collective-permute-start | bytes 196616 | tf_op jit(solution)/shard_map/ppermute | solution.py:22
  128.2 15.1 %collective-permute-start.13 = (bf16[256,512]{1,0:T(8,128)(2,1)}, bf16[256,512]{1,0:T(8,128)(2,1)S(1)}, u32[]{:S(2)}, u32[]{:S(2)}) collective-permute-start(bf16[256,512]{1,0:T(8,128)(2,1)} %get-tuple-element.93), channel_id=1, source_target_pairs={{0,12},{4,8},{8,4},{12,0},{1,13},{5,9},{9,5},{13,1},{2,14},{6,10},... | collective-permute-start | bytes 786440 | tf_op jit(solution)/shard_map/ppermute | solution.py:22
  132.8 9.2 %copy-start.16 = (bf16[256,512]{1,0:T(8,128)(2,1)S(1)}, bf16[256,512]{1,0:T(8,128)(2,1)}, u32[]{:S(2)}) copy-start(bf16[256,512]{1,0:T(8,128)(2,1)} %get-tuple-element.102) | copy-start | bytes 786436
  132.8 6.0 %collective-permute-start.11 = (bf16[4,64,128]{2,1,0:T(8,128)(2,1)S(1)}, bf16[4,64,128]{2,1,0:T(8,128)(2,1)S(1)}, u32[]{:S(2)}, u32[]{:S(2)}) collective-permute-start(bf16[4,64,128]{2,1,0:T(8,128)(2,1)S(1)} %fusion.8), channel_id=1, source_target_pairs={{0,1},{1,0},{2,3},{3,2},{4,5},{5,4},{6,7},{7,6},{8,9},{9,8},{10,11... | collective-permute-start | bytes 196616 | tf_op jit(solution)/shard_map/ppermute | solution.py:22
  139.4 6.3 %collective-permute-start.12 = (bf16[4,64,128]{2,1,0:T(8,128)(2,1)S(1)}, bf16[4,64,128]{2,1,0:T(8,128)(2,1)S(1)}, u32[]{:S(2)}, u32[]{:S(2)}) collective-permute-start(bf16[4,64,128]{2,1,0:T(8,128)(2,1)S(1)} %get-tuple-element.133), channel_id=1, source_target_pairs={{0,2},{1,3},{2,0},{3,1},{4,6},{5,7},{6,4},{7,5},{8,10},{9,11},{10,... | collective-permute-start | bytes 196616 | tf_op jit(solution)/shard_map/ppermute | solution.py:22
  142.0 16.7 %collective-permute-start.16 = (bf16[256,512]{1,0:T(8,128)(2,1)S(1)}, bf16[256,512]{1,0:T(8,128)(2,1)S(1)}, u32[]{:S(2)}, u32[]{:S(2)}) collective-permute-start(bf16[256,512]{1,0:T(8,128)(2,1)S(1)} %copy-done.16), channel_id=1, source_target_pairs={{0,8},{4,12},{8,0},{12,4},{1,9},{5,13},{9,1},{13,5},{2,10},{6,14},... | collective-permute-start | bytes 786440 | tf_op jit(solution)/shard_map/ppermute | solution.py:22
  143.3 13.9 %collective-permute-start.17 = (bf16[256,512]{1,0:T(8,128)(2,1)}, bf16[256,512]{1,0:T(8,128)(2,1)S(1)}, u32[]{:S(2)}, u32[]{:S(2)}) collective-permute-start(bf16[256,512]{1,0:T(8,128)(2,1)} %get-tuple-element.105), channel_id=1, source_target_pairs={{0,12},{4,8},{8,4},{12,0},{1,13},{5,9},{9,5},{13,1},{2,14},{6,10},... | collective-permute-start | bytes 786440 | tf_op jit(solution)/shard_map/ppermute | solution.py:22
  151.3 12.4 %collective-permute-start.15 = (bf16[2,128,512]{2,1,0:T(8,128)(2,1)}, bf16[2,128,512]{2,1,0:T(8,128)(2,1)S(1)}, u32[]{:S(2)}, u32[]{:S(2)}) collective-permute-start(bf16[2,128,512]{2,1,0:T(8,128)(2,1)} %get-tuple-element.99), channel_id=1, source_target_pairs={{0,1},{1,0},{2,3},{3,2},{4,5},{5,4},{6,7},{7,6},{8,9},{9,8},{10,11... | collective-permute-start | bytes 786440 | tf_op jit(solution)/shard_map/ppermute | solution.py:22
  151.3 7.4 %copy-start.13 = (bf16[256,512]{1,0:T(8,128)(2,1)S(1)}, bf16[256,512]{1,0:T(8,128)(2,1)}, u32[]{:S(2)}) copy-start(bf16[256,512]{1,0:T(8,128)(2,1)} %get-tuple-element.127) | copy-start | bytes 786436
  151.3 17.1 %collective-permute-start.20 = (bf16[256,512]{1,0:T(8,128)(2,1)S(1)}, bf16[256,512]{1,0:T(8,128)(2,1)S(1)}, u32[]{:S(2)}, u32[]{:S(2)}) collective-permute-start(bf16[256,512]{1,0:T(8,128)(2,1)S(1)} %copy-done.14), channel_id=1, source_target_pairs={{0,8},{4,12},{8,0},{12,4},{1,9},{5,13},{9,1},{13,5},{2,10},{6,14},... | collective-permute-start | bytes 786440 | tf_op jit(solution)/shard_map/ppermute | solution.py:22
  153.0 13.9 %collective-permute-start.21 = (bf16[256,512]{1,0:T(8,128)(2,1)S(1)}, bf16[256,512]{1,0:T(8,128)(2,1)S(1)}, u32[]{:S(2)}, u32[]{:S(2)}) collective-permute-start(bf16[256,512]{1,0:T(8,128)(2,1)S(1)} %copy-done.15), channel_id=1, source_target_pairs={{0,12},{4,8},{8,4},{12,0},{1,13},{5,9},{9,5},{13,1},{2,14},{6,10},... | collective-permute-start | bytes 786440 | tf_op jit(solution)/shard_map/ppermute | solution.py:22
  157.3 22.2 %collective-permute-start.24 = (bf16[256,512]{1,0:T(8,128)(2,1)S(1)}, bf16[256,512]{1,0:T(8,128)(2,1)S(1)}, u32[]{:S(2)}, u32[]{:S(2)}) collective-permute-start(bf16[256,512]{1,0:T(8,128)(2,1)S(1)} %copy-done.12), channel_id=1, source_target_pairs={{0,8},{4,12},{8,0},{12,4},{1,9},{5,13},{9,1},{13,5},{2,10},{6,14},... | collective-permute-start | bytes 786440 | tf_op jit(solution)/shard_map/ppermute | solution.py:22
  158.7 20.7 %collective-permute-start.25 = (bf16[256,512]{1,0:T(8,128)(2,1)S(1)}, bf16[256,512]{1,0:T(8,128)(2,1)S(1)}, u32[]{:S(2)}, u32[]{:S(2)}) collective-permute-start(bf16[256,512]{1,0:T(8,128)(2,1)S(1)} %copy-done.13), channel_id=1, source_target_pairs={{0,12},{4,8},{8,4},{12,0},{1,13},{5,9},{9,5},{13,1},{2,14},{6,10},... | collective-permute-start | bytes 786440 | tf_op jit(solution)/shard_map/ppermute | solution.py:22
  163.7 14.4 %collective-permute-start.19 = (bf16[2,128,512]{2,1,0:T(8,128)(2,1)}, bf16[2,128,512]{2,1,0:T(8,128)(2,1)S(1)}, u32[]{:S(2)}, u32[]{:S(2)}) collective-permute-start(bf16[2,128,512]{2,1,0:T(8,128)(2,1)} %get-tuple-element.107), channel_id=1, source_target_pairs={{0,1},{1,0},{2,3},{3,2},{4,5},{5,4},{6,7},{7,6},{8,9},{9,8},{10,11... | collective-permute-start | bytes 786440 | tf_op jit(solution)/shard_map/ppermute | solution.py:22
  166.9 19.2 %collective-permute-start.18 = (bf16[128,512]{1,0:T(8,128)(2,1)S(1)}, bf16[128,512]{1,0:T(8,128)(2,1)S(1)}, u32[]{:S(2)}, u32[]{:S(2)}) collective-permute-start(bf16[128,512]{1,0:T(8,128)(2,1)S(1)} %fusion.4), channel_id=1, source_target_pairs={{0,2},{1,3},{2,0},{3,1},{4,6},{5,7},{6,4},{7,5},{8,10},{9,11},{10,... | collective-permute-start | bytes 393224 | tf_op jit(solution)/shard_map/ppermute | solution.py:22
  173.2 14.4 %collective-permute-start.23 = (bf16[2,128,512]{2,1,0:T(8,128)(2,1)}, bf16[2,128,512]{2,1,0:T(8,128)(2,1)S(1)}, u32[]{:S(2)}, u32[]{:S(2)}) collective-permute-start(bf16[2,128,512]{2,1,0:T(8,128)(2,1)} %get-tuple-element.118), channel_id=1, source_target_pairs={{0,1},{1,0},{2,3},{3,2},{4,5},{5,4},{6,7},{7,6},{8,9},{9,8},{10,11... | collective-permute-start | bytes 786440 | tf_op jit(solution)/shard_map/ppermute | solution.py:22
  178.3 9.3 %collective-permute-start.22 = (bf16[128,512]{1,0:T(8,128)(2,1)S(1)}, bf16[128,512]{1,0:T(8,128)(2,1)S(1)}, u32[]{:S(2)}, u32[]{:S(2)}) collective-permute-start(bf16[128,512]{1,0:T(8,128)(2,1)S(1)} %fusion.5), channel_id=1, source_target_pairs={{0,2},{1,3},{2,0},{3,1},{4,6},{5,7},{6,4},{7,5},{8,10},{9,11},{10,... | collective-permute-start | bytes 393224 | tf_op jit(solution)/shard_map/ppermute | solution.py:22
  184.4 11.7 %collective-permute-start.27 = (bf16[2,128,512]{2,1,0:T(8,128)(2,1)}, bf16[2,128,512]{2,1,0:T(8,128)(2,1)S(1)}, u32[]{:S(2)}, u32[]{:S(2)}) collective-permute-start(bf16[2,128,512]{2,1,0:T(8,128)(2,1)} %get-tuple-element.129), channel_id=1, source_target_pairs={{0,1},{1,0},{2,3},{3,2},{4,5},{5,4},{6,7},{7,6},{8,9},{9,8},{10,11... | collective-permute-start | bytes 786440 | tf_op jit(solution)/shard_map/ppermute | solution.py:22
  187.7 10.2 %collective-permute-start.26 = (bf16[128,512]{1,0:T(8,128)(2,1)S(1)}, bf16[128,512]{1,0:T(8,128)(2,1)S(1)}, u32[]{:S(2)}, u32[]{:S(2)}) collective-permute-start(bf16[128,512]{1,0:T(8,128)(2,1)S(1)} %fusion.6), channel_id=1, source_target_pairs={{0,2},{1,3},{2,0},{3,1},{4,6},{5,7},{6,4},{7,5},{8,10},{9,11},{10,... | collective-permute-start | bytes 393224 | tf_op jit(solution)/shard_map/ppermute | solution.py:22
  197.2 8.6 %collective-permute-start.28 = (bf16[128,512]{1,0:T(8,128)(2,1)S(1)}, bf16[128,512]{1,0:T(8,128)(2,1)S(1)}, u32[]{:S(2)}, u32[]{:S(2)}) collective-permute-start(bf16[128,512]{1,0:T(8,128)(2,1)S(1)} %fusion.7), channel_id=1, source_target_pairs={{0,2},{1,3},{2,0},{3,1},{4,6},{5,7},{6,4},{7,5},{8,10},{9,11},{10,... | collective-permute-start | bytes 393224 | tf_op jit(solution)/shard_map/ppermute | solution.py:22
  (22 other events, 61.7 us)

commit v8 on v7

--- a/solution.py
+++ b/solution.py
@@ -7,7 +7,6 @@
 
 F32 = jnp.float32
 BF16 = jnp.bfloat16
-VMEM_LIMIT = 60 * 1024 * 1024
 WIDTHS = (512, 512, 512, 512)
 CAP = 4
 HALVES = 2
@@ -30,22 +29,26 @@
     return pl.CostEstimate(flops=flops // hint, bytes_accessed=moved // hint, transcendentals=0)
 
 
-def params():
-    return pltpu.CompilerParams(vmem_limit_bytes=VMEM_LIMIT)
+def params(mebibytes):
+    return pltpu.CompilerParams(vmem_limit_bytes=mebibytes * 1024 * 1024)
 
 
 def cut_kernel(ref, *refs):
-    outs, sems = refs[:-1], refs[-1]
-    copies, start = [], 0
+    outs, (stage, sems) = refs[:-2], refs[-2:]
+    inward, outward, start = [], [], 0
     for index, out in enumerate(outs):
-        wide = out.shape[1]
-        copies.append(
-            pltpu.make_async_copy(ref.at[:, pl.ds(start, wide)], out, sems.at[index])
+        spot = pl.ds(start, out.shape[1])
+        inward.append(
+            pltpu.make_async_copy(ref.at[:, spot], stage.at[:, spot], sems.at[0, index])
         )
-        start += wide
-    for copy in copies:
+        outward.append(pltpu.make_async_copy(stage.at[:, spot], out, sems.at[1, index]))
+        start += out.shape[1]
+    for copy in inward:
         copy.start()
-    for copy in copies:
+    for copy, after in zip(inward, outward):
+        copy.wait()
+        after.start()
+    for copy in outward:
         copy.wait()
 
 
@@ -55,8 +58,11 @@
         in_specs=[pl.BlockSpec(memory_space=pl.ANY)],
         out_specs=[pl.BlockSpec(memory_space=pl.ANY)] * len(widths),
         out_shape=[jax.ShapeDtypeStruct((array.shape[0], w), array.dtype) for w in widths],
-        scratch_shapes=[pltpu.SemaphoreType.DMA((len(widths),))],
-        compiler_params=params(),
+        scratch_shapes=[
+            pltpu.VMEM(array.shape, array.dtype),
+            pltpu.SemaphoreType.DMA((2, len(widths))),
+        ],
+        compiler_params=params(4),
         cost_estimate=cost(0, 4 * array.size),
         name="cut",
     )(array)
@@ -94,6 +100,7 @@
     rows = groups[0][0][0].shape[0]
     depth = sum(wide for _, wide, _ in groups[0])
     total = rows * len(groups)
+    limit = 28 if len(groups) > 2 else 20 if tile > 256 else 14
     in_specs, args = [], []
     for group in groups:
         for array, wide, block in group:
@@ -114,7 +121,7 @@
         out_specs=pl.BlockSpec((total, tile), lambda n: (0, n)),
         out_shape=jax.ShapeDtypeStruct((total, width), F32),
         scratch_shapes=[pltpu.VMEM((total, depth), BF16)],
-        compiler_params=params(),
+        compiler_params=params(limit),
         cost_estimate=cost(
             2 * total * depth * width, 2 * depth * (width + total) + 8 * total * width, hint
         ),
@@ -236,7 +243,7 @@
             ],
         ),
         out_shape=out_shape,
-        compiler_params=params(),
+        compiler_params=params(18 if first == 0 else 12),
         cost_estimate=cost(4 * rows * depth * CAP * rank, 4 * depth * (CAP * rank + rows)),
         name="scores",
     )(info, *args)
@@ -319,7 +326,7 @@
             scratch_shapes=[pltpu.VMEM((4 * held, tile), BF16)],
         ),
         out_shape=out_shape,
-        compiler_params=params(),
+        compiler_params=params(14),
         cost_estimate=cost(
             32 * rows * held * width, 26 * rows * width + 8 * held * width
         ),

time: 207 us -> 171 us (0.83)
  Pallas kernels: 137 us -> 49.4 us
  local copies, waits for them, and re-layouts: 11.9 us -> 63.9 us
    pallas_call x1, Pallas kernels: 56.7 us -> 1.46 us  [cut_columns(): pl.pallas_call(cut_kernel, in_specs=[pl.BlockSpec(memory_space=pl.ANY)],...]
    unnamed x50 -> x42, local copies, waits for them, and re-layouts: 4.92 us -> 58.4 us
    pallas_call x6, Pallas kernels: 40.3 us -> 26.6 us  [product(): pl.pallas_call(lambda *refs: product_kernel(counts, prior is not None, *r...]
    pallas_call x4, Pallas kernels: 17 us -> 6.96 us  [combine(): pl.pallas_call(lambda *refs: combine_kernel(bool(build), *refs), grid_spe...]
    pallas_call x3, Pallas kernels: 23.2 us -> 14.4 us  [scores(): pl.pallas_call(lambda *refs: scores_kernel(first, half * depth, len(lower...]
  transfers between devices with their start and end apart: 29 -> 29, of which waited for: 9 -> 9; matrix products, arithmetic and copies ran while one was open for 6% -> 5% of each run, Pallas kernels for 66% -> 29%
where the time goes in v8:
time: 171 us; the launch traced here: 170 us
  local copies, waits for them, and re-layouts  63.9 us (37%)
  Pallas kernels  49.4 us (29%)
  starting transfers between devices  26.7 us (16%)
  waiting for transfers between devices  24.9 us (15%)
  other arithmetic  4.62 us (3%)
    unnamed x42, local copies, waits for them, and re-layouts  58.4 us
    ppermute x29, starting transfers between devices, swap(): return lax.ppermute(values, axis, partners(lax.axis_size(axis), step))  26.7 us
    pallas_call x6, Pallas kernels, product(): pl.pallas_call(lambda *refs: product_kernel(counts, prior is not None, *r...  26.6 us
    ppermute x29, waiting for transfers between devices, swap(): return lax.ppermute(values, axis, partners(lax.axis_size(axis), step))  24.9 us
    pallas_call x3, Pallas kernels, scores(): pl.pallas_call(lambda *refs: scores_kernel(first, half * depth, len(lower...  14.4 us
    pallas_call x4, Pallas kernels, combine(): pl.pallas_call(lambda *refs: combine_kernel(bool(build), *refs), grid_spe...  6.96 us
  transfers between devices with their start and end apart: 29, of which 9 were waited for; matrix products, arithmetic and copies ran while one was open for 5% of the time, Pallas kernels for 29%

profile of v8, /device:TPU:0, one launch (start us, length us, event | category | flops | bytes accessed | tf_op | source)
XLA Modules:
  0.0 169.9 jit_solution(1926669736758509176)
XLA Ops:
  3.4 2.6 %collective-permute-start.2 = (bf16[128,1792]{1,0:T(8,128)(2,1)}, bf16[128,1792]{1,0:T(8,128)(2,1)S(1)}, u32[]{:S(2)}, u32[]{:S(2)}) collective-permute-start(bf16[128,1792]{1,0:T(8,128)(2,1)} %get-tuple-element.73), channel_id=1, source_target_pairs={{0,8},{4,12},{8,0},{12,4},{1,9},{5,13},{9,1},{13,5},{2,10},{6,14},... | collective-permute-start | bytes 1376264 | tf_op jit(solution)/shard_map/ppermute | solution.py:21
  6.1 1.9 %collective-permute-start.1 = (bf16[128,3584]{1,0:T(8,128)(2,1)}, bf16[128,3584]{1,0:T(8,128)(2,1)S(1)}, u32[]{:S(2)}, u32[]{:S(2)}) collective-permute-start(bf16[128,3584]{1,0:T(8,128)(2,1)} %get-tuple-element.71), channel_id=1, source_target_pairs={{0,8},{4,12},{8,0},{12,4},{1,9},{5,13},{9,1},{13,5},{2,10},{6,14},... | collective-permute-start | bytes 2752520 | tf_op jit(solution)/shard_map/ppermute | solution.py:21
  10.3 2.8 %constant_dynamic-slice_fusion.8 = (bf16[256,512]{1,0:T(8,128)(2,1)}, bf16[256,512]{1,0:T(8,128)(2,1)}, bf16[256,512]{1,0:T(8,128)(2,1)}, bf16[256,512]{1,0:T(8,...) fusion(bf16[256,8192]{1,0:T(8,128)(2,1)} %refs_4_.5, ...), kind=kLoop, calls=%fused_computation.41 | loop fusion | bytes 4194336 | tf_op jit(solution)/shard_map/dynamic_slice | solution.py:355
  13.1 2.3 %constant_dynamic-slice_fusion.7 = bf16[256,2048]{1,0:T(8,128)(2,1)} fusion(bf16[256,8192]{1,0:T(8,128)(2,1)} %refs_4_.5, s32[]{:T(128)S(6)} %select_n.100), kind=kLoop, calls=%fused_computation.40 | loop fusion | bytes 2097156 | tf_op jit(solution)/shard_map/dynamic_slice | solution.py:353
  15.6 5.2 %copy-done.6 = bf16[16,64,7168]{2,1,0:T(8,128)(2,1)S(1)} copy-done((bf16[16,64,7168]{2,1,0:T(8,128)(2,1)S(1)}, bf16[16,64,7168]{2,1,0:T(8,128)(2,1)}, u32[]{:S(2)}) %copy-start.6) | copy-done | bytes 14680088
  20.8 6.2 %scores.3.refs_5_ = f32[2,64,128]{2,1,0:T(8,128)S(1)} custom-call(s32[17]{0:T(128)S(1)} %pad_add_fusion.refs_0_, bf16[128,7168]{1,0:T(8,128)(2,1)S(1)} %copy-done.12, bf16[128,7168]{1,0:T(8,128)(2,1)} %collective-permute-done.refs_2_.refs_1_, bf16[16,64,7168]{2,1,0:T(8,128)(2,1)S(1)} %copy-done.6, s32[4,1,128]{2,1,0:T(1,128)S(1)} %bitcast.49), custom_call_target="tpu_custom_call" | custom-call | flops 939524 | bytes 11010 | tf_op jit(solution)/shard_map/scores/pallas_call | solution.py:231
  27.0 9.3 %copy-done = bf16[7168,2048]{1,0:T(8,128)(2,1)S(1)} copy-done((bf16[7168,2048]{1,0:T(8,128)(2,1)S(1)}, bf16[7168,2048]{1,0:T(8,128)(2,1)}, u32[]{:S(2)}) %copy-start) | copy-done | bytes 29360152
  36.3 6.9 %base.6.refs_6_ = f32[256,2048]{1,0:T(8,128)S(1)} custom-call(bf16[128,7168]{1,0:T(8,128)(2,1)S(1)} %copy-done.12, bf16[128,7168]{1,0:T(8,128)(2,1)} %collective-permute-done.refs_2_.refs_1_, bf16[7168,2048]{1,0:T(8,128)(2,1)S(1)} %copy-done), custom_call_target="tpu_custom_call" | custom-call | flops 3758096 | bytes 20709 | tf_op jit(solution)/shard_map/base/pallas_call | solution.py:117
  46.0 5.2 %copy-done.7 = bf16[16,64,7168]{2,1,0:T(8,128)(2,1)S(1)} copy-done((bf16[16,64,7168]{2,1,0:T(8,128)(2,1)S(1)}, bf16[16,64,7168]{2,1,0:T(8,128)(2,1)}, u32[]{:S(2)}) %copy-start.7) | copy-done | bytes 14680088
  51.1 4.1 %scores.4.refs_4_ = f32[2,256,128]{2,1,0:T(8,128)S(1)} custom-call(s32[17]{0:T(128)S(1)} %pad_add_fusion.refs_0_, bf16[128,1792]{1,0:T(8,128)(2,1)S(1)} %collective-permute-done.2.refs_1_.refs_2_, bf16[128,1792]{1,0:T(8,128)(2,1)} %collective-permute-done.3.refs_2_.refs_3_, bf16[128,1792]{1,0:T(8,128)(2,1)S(1)} %collective-permute-done.4.refs_3_.refs_4_, ...), custom_call_target="tpu_custom_call" | custom-call | flops 469762 | bytes 5505 | tf_op jit(solution)/shard_map/scores/pallas_call | solution.py:231
  55.3 11.3 %base.7.refs_2_ = f32[512,2048]{1,0:T(8,128)S(1)} custom-call(bf16[128,7168]{1,0:T(8,128)(2,1)S(1)} %copy-done.12, bf16[128,7168]{1,0:T(8,128)(2,1)} %collective-permute-done.refs_2_.refs_1_, bf16[128,1792]{1,0:T(8,128)(2,1)S(1)} %collective-permute-done.2.refs_1_.refs_2_, bf16[128,1792]{1,0:T(8,128)(2,1)} %collective-permute-done.3.refs_2_.refs_3_, ...), custom_call_target="tpu_custom_call" | custom-call | flops 7516192 | bytes 26738 | tf_op jit(solution)/shard_map/base/pallas_call | solution.py:117
  67.3 1.9 %collective-permute-done.6.refs_2_.refs_1_ = bf16[128,3584]{1,0:T(8,128)(2,1)S(1)} collective-permute-done((bf16[128,3584]{1,0:T(8,128)(2,1)S(1)}, bf16[128,3584]{1,0:T(8,128)(2,1)S(1)}, u32[]{:S(2)}, u32[]{:S(2)}) %collective-permute-start.6) | collective-permute-done | bytes 917536 | tf_op jit(solution)/shard_map/ppermute | solution.py:21
  69.2 5.2 %copy-done.8 = bf16[16,64,7168]{2,1,0:T(8,128)(2,1)S(1)} copy-done((bf16[16,64,7168]{2,1,0:T(8,128)(2,1)S(1)}, bf16[16,64,7168]{2,1,0:T(8,128)(2,1)}, u32[]{:S(2)}) %copy-start.8) | copy-done | bytes 14680088
  74.4 4.1 %scores.5 = (f32[4,64,128]{2,1,0:T(8,128)S(1)}, bf16[4,64,128]{2,1,0:T(8,128)(2,1)S(1)}) custom-call(s32[17]{0:T(128)S(1)} %pad_add_fusion.refs_0_, bf16[128,3584]{1,0:T(8,128)(2,1)S(1)} %collective-permute-done.1.refs_1_.refs_0_, bf16[128,3584]{1,0:T(8,128)(2,1)S(1)} %collective-permute-done.6.refs_2_.refs_1_, bf16[16,64,7168]{2,1,0:T(8,128)(2,1)S(1)} %copy-done.8, ...), custom_call_target="tpu_custom_call" | custom-call | flops 469762 | bytes 5505 | tf_op jit(solution)/shard_map/scores/pallas_call | solution.py:231
  78.7 2.0 %collective-permute-start.7 = (bf16[4,64,128]{2,1,0:T(8,128)(2,1)S(1)}, bf16[4,64,128]{2,1,0:T(8,128)(2,1)S(1)}, u32[]{:S(2)}, u32[]{:S(2)}) collective-permute-start(bf16[4,64,128]{2,1,0:T(8,128)(2,1)S(1)} %get-tuple-element.83), channel_id=1, source_target_pairs={{0,8},{4,12},{8,0},{12,4},{1,9},{5,13},{9,1},{13,5},{2,10},{6,14},... | collective-permute-start | bytes 196616 | tf_op jit(solution)/shard_map/ppermute | solution.py:21
  80.7 9.3 %copy-done.1 = bf16[7168,2048]{1,0:T(8,128)(2,1)S(1)} copy-done((bf16[7168,2048]{1,0:T(8,128)(2,1)S(1)}, bf16[7168,2048]{1,0:T(8,128)(2,1)}, u32[]{:S(2)}) %copy-start.1) | copy-done | bytes 29360152
  90.1 2.0 %base.8 = f32[256,512]{1,0:T(8,128)S(1)} custom-call(bf16[128,3584]{1,0:T(8,128)(2,1)S(1)} %collective-permute-done.1.refs_1_.refs_0_, bf16[128,3584]{1,0:T(8,128)(2,1)S(1)} %collective-permute-done.6.refs_2_.refs_1_, f32[512,2048]{1,0:T(8,128)S(1)} %base.7.refs_2_, bf16[7168,2048]{1,0:T(8,128)(2,1)S(1)} %copy-done.1), custom_call_target="tpu_custom_call" | custom-call | flops 939524096 | bytes 6553600 | tf_op jit(solution)/shard_map/base/pallas_call | solution.py:117
  93.9 2.0 %base.9 = f32[256,512]{1,0:T(8,128)S(1)} custom-call(bf16[128,3584]{1,0:T(8,128)(2,1)S(1)} %collective-permute-done.1.refs_1_.refs_0_, bf16[128,3584]{1,0:T(8,128)(2,1)S(1)} %collective-permute-done.6.refs_2_.refs_1_, f32[512,2048]{1,0:T(8,128)S(1)} %base.7.refs_2_, bf16[7168,2048]{1,0:T(8,128)(2,1)S(1)} %copy-done.1), custom_call_target="tpu_custom_call" | custom-call | flops 939524096 | bytes 6553600 | tf_op jit(solution)/shard_map/base/pallas_call | solution.py:117
  96.8 2.8 %collective-permute-start.12 = (bf16[4,64,128]{2,1,0:T(8,128)(2,1)S(1)}, bf16[4,64,128]{2,1,0:T(8,128)(2,1)S(1)}, u32[]{:S(2)}, u32[]{:S(2)}) collective-permute-start(bf16[4,64,128]{2,1,0:T(8,128)(2,1)S(1)} %get-tuple-element.133), channel_id=1, source_target_pairs={{0,2},{1,3},{2,0},{3,1},{4,6},{5,7},{6,4},{7,5},{8,10},{9,11},{10,... | collective-permute-start | bytes 196616 | tf_op jit(solution)/shard_map/ppermute | solution.py:21
  101.1 2.3 %collective-permute-done.12.refs_2_ = bf16[4,64,128]{2,1,0:T(8,128)(2,1)S(1)} collective-permute-done((bf16[4,64,128]{2,1,0:T(8,128)(2,1)S(1)}, bf16[4,64,128]{2,1,0:T(8,128)(2,1)S(1)}, u32[]{:S(2)}, u32[]{:S(2)}) %collective-permute-start.12) | collective-permute-done | bytes 65568 | tf_op jit(solution)/shard_map/ppermute | solution.py:21
  103.4 2.2 %combine.4 = (f32[2,128,512]{2,1,0:T(8,128)S(1)}, bf16[2,128,512]{2,1,0:T(8,128)(2,1)}, bf16[512,1024]{1,0:T(8,128)(2,1)S(1)}) custom-call(s32[10]{0:T(128)S(1)} %stack.40.refs_0_, f32[4,64,128]{2,1,0:T(8,128)S(1)} %get-tuple-element.134.refs_1_, bf16[4,64,128]{2,1,0:T(8,128)(2,1)S(1)} %collective-permute-done.12.refs_2_, ...), custom_call_target="tpu_custom_call" | custom-call | flops 536870 | bytes 2752 | tf_op jit(solution)/shard_map/combine/pallas_call | solution.py:319
  109.3 9.3 %copy-done.2 = bf16[7168,2048]{1,0:T(8,128)(2,1)S(1)} copy-done((bf16[7168,2048]{1,0:T(8,128)(2,1)S(1)}, bf16[7168,2048]{1,0:T(8,128)(2,1)}, u32[]{:S(2)}) %copy-start.2) | copy-done | bytes 29360152
  118.6 2.2 %copy-done.5 = f32[512,2048]{1,0:T(8,128)S(1)} copy-done((f32[512,2048]{1,0:T(8,128)S(1)}, f32[512,2048]{1,0:T(8,128)}, u32[]{:S(2)}) %copy-start.5) | copy-done | bytes 4194328
  120.8 2.2 %base.10 = f32[256,512]{1,0:T(8,128)S(1)} custom-call(bf16[128,3584]{1,0:T(8,128)(2,1)S(1)} %collective-permute-done.1.refs_1_.refs_0_, bf16[128,3584]{1,0:T(8,128)(2,1)S(1)} %collective-permute-done.6.refs_2_.refs_1_, f32[512,2048]{1,0:T(8,128)S(1)} %copy-done.5, bf16[7168,2048]{1,0:T(8,128)(2,1)S(1)} %copy-done.2), custom_call_target="tpu_custom_call" | custom-call | flops 939524 | bytes 6553 | tf_op jit(solution)/shard_map/base/pallas_call | solution.py:117
  125.2 2.3 %combine.5 = (f32[2,128,512]{2,1,0:T(8,128)S(1)}, bf16[2,128,512]{2,1,0:T(8,128)(2,1)S(1)}) custom-call(s32[10]{0:T(128)S(1)} %stack.40.refs_0_, bf16[512,1024]{1,0:T(8,128)(2,1)S(1)} %copy-done.16, f32[4,128,2048]{2,1,0:T(8,128)S(1)} %bitcast.42, f32[2,128,512]{2,1,0:T(8,128)S(1)} %bitcast.45, bf16[256,8192]{1,0:T(8,128)(2,1)S(1)} %copy-done.10, ...), custom_call_target="tpu_custom_call" | custom-call | flops 536870 | bytes 2752 | tf_op jit(solution)/shard_map/combine/pallas_call | solution.py:319
  133.4 2.1 %collective-permute-start.23 = (bf16[2,128,512]{2,1,0:T(8,128)(2,1)S(1)}, bf16[2,128,512]{2,1,0:T(8,128)(2,1)S(1)}, u32[]{:S(2)}, u32[]{:S(2)}) collective-permute-start(bf16[2,128,512]{2,1,0:T(8,128)(2,1)S(1)} %get-tuple-element.118), channel_id=1, source_target_pairs={{0,1},{1,0},{2,3},{3,2},{4,5},{5,4},{6,7},{7,6},{8,9},{9,8},{10,11... | collective-permute-start | bytes 786440 | tf_op jit(solution)/shard_map/ppermute | solution.py:21
  135.5 9.3 %copy-done.3 = bf16[7168,2048]{1,0:T(8,128)(2,1)S(1)} copy-done((bf16[7168,2048]{1,0:T(8,128)(2,1)S(1)}, bf16[7168,2048]{1,0:T(8,128)(2,1)}, u32[]{:S(2)}) %copy-start.3) | copy-done | bytes 29360152
  144.8 2.0 %base.11 = f32[256,512]{1,0:T(8,128)S(1)} custom-call(bf16[128,3584]{1,0:T(8,128)(2,1)S(1)} %collective-permute-done.1.refs_1_.refs_0_, bf16[128,3584]{1,0:T(8,128)(2,1)S(1)} %collective-permute-done.6.refs_2_.refs_1_, f32[512,2048]{1,0:T(8,128)S(1)} %copy-done.5, bf16[7168,2048]{1,0:T(8,128)(2,1)S(1)} %copy-done.3), custom_call_target="tpu_custom_call" | custom-call | flops 939524 | bytes 6553 | tf_op jit(solution)/shard_map/base/pallas_call | solution.py:117
  149.6 5.6 %collective-permute-done.22 = bf16[128,512]{1,0:T(8,128)(2,1)S(1)} collective-permute-done((bf16[128,512]{1,0:T(8,128)(2,1)S(1)}, bf16[128,512]{1,0:T(8,128)(2,1)S(1)}, u32[]{:S(2)}, u32[]{:S(2)}) %collective-permute-start.22) | collective-permute-done | bytes 131104 | tf_op jit(solution)/shard_map/ppermute | solution.py:21
  155.5 3.1 %collective-permute-done.27 = bf16[2,128,512]{2,1,0:T(8,128)(2,1)S(1)} collective-permute-done((bf16[2,128,512]{2,1,0:T(8,128)(2,1)S(1)}, bf16[2,128,512]{2,1,0:T(8,128)(2,1)S(1)}, u32[]{:S(2)}, u32[]{:S(2)}) %collective-permute-start.27) | collective-permute-done | bytes 262176 | tf_op jit(solution)/shard_map/ppermute | solution.py:21
  160.1 6.4 %collective-permute-done.26 = bf16[128,512]{1,0:T(8,128)(2,1)S(1)} collective-permute-done((bf16[128,512]{1,0:T(8,128)(2,1)S(1)}, bf16[128,512]{1,0:T(8,128)(2,1)S(1)}, u32[]{:S(2)}, u32[]{:S(2)}) %collective-permute-start.26) | collective-permute-done | bytes 131104 | tf_op jit(solution)/shard_map/ppermute | solution.py:21
  166.6 2.4 %collective-permute-done.28 = bf16[128,512]{1,0:T(8,128)(2,1)S(1)} collective-permute-done((bf16[128,512]{1,0:T(8,128)(2,1)S(1)}, bf16[128,512]{1,0:T(8,128)(2,1)S(1)}, u32[]{:S(2)}, u32[]{:S(2)}) %collective-permute-start.28) | collective-permute-done | bytes 131104 | tf_op jit(solution)/shard_map/ppermute | solution.py:21
  (114 shorter events, 30.7 us)
Async XLA Ops:
  0.0 15.4 %collective-permute-start = (bf16[128,7168]{1,0:T(8,128)(2,1)}, bf16[128,7168]{1,0:T(8,128)(2,1)}, u32[]{:S(2)}, u32[]{:S(2)}) collective-permute-start(bf16[128,7168]{1,0:T(8,128)(2,1)} %refs_0_.1), channel_id=1, source_target_pairs={{0,4},{4,0},{8,12},{12,8},{1,5},{5,1},{9,13},{13,9},{2,6},{6,2},{1... | collective-permute-start | bytes 5505032 | tf_op jit(solution)/shard_map/ppermute | solution.py:21
  2.0 13.6 %copy-start.12 = (bf16[128,7168]{1,0:T(8,128)(2,1)S(1)}, bf16[128,7168]{1,0:T(8,128)(2,1)}, u32[]{:S(2)}) copy-start(bf16[128,7168]{1,0:T(8,128)(2,1)} %refs_0_.1) | copy-start | bytes 5505028
  3.4 39.8 %collective-permute-start.2 = (bf16[128,1792]{1,0:T(8,128)(2,1)}, bf16[128,1792]{1,0:T(8,128)(2,1)S(1)}, u32[]{:S(2)}, u32[]{:S(2)}) collective-permute-start(bf16[128,1792]{1,0:T(8,128)(2,1)} %get-tuple-element.73), channel_id=1, source_target_pairs={{0,8},{4,12},{8,0},{12,4},{1,9},{5,13},{9,1},{13,5},{2,10},{6,14},... | collective-permute-start | bytes 1376264 | tf_op jit(solution)/shard_map/ppermute | solution.py:21
  6.0 37.2 %collective-permute-start.3 = (bf16[128,1792]{1,0:T(8,128)(2,1)}, bf16[128,1792]{1,0:T(8,128)(2,1)}, u32[]{:S(2)}, u32[]{:S(2)}) collective-permute-start(bf16[128,1792]{1,0:T(8,128)(2,1)} %get-tuple-element.74), channel_id=1, source_target_pairs={{0,8},{4,12},{8,0},{12,4},{1,9},{5,13},{9,1},{13,5},{2,10},{6,14},... | collective-permute-start | bytes 1376264 | tf_op jit(solution)/shard_map/ppermute | solution.py:21
  6.1 60.6 %collective-permute-start.1 = (bf16[128,3584]{1,0:T(8,128)(2,1)}, bf16[128,3584]{1,0:T(8,128)(2,1)S(1)}, u32[]{:S(2)}, u32[]{:S(2)}) collective-permute-start(bf16[128,3584]{1,0:T(8,128)(2,1)} %get-tuple-element.71), channel_id=1, source_target_pairs={{0,8},{4,12},{8,0},{12,4},{1,9},{5,13},{9,1},{13,5},{2,10},{6,14},... | collective-permute-start | bytes 2752520 | tf_op jit(solution)/shard_map/ppermute | solution.py:21
  43.2 1.9 %collective-permute-start.4 = (bf16[128,1792]{1,0:T(8,128)(2,1)S(1)}, bf16[128,1792]{1,0:T(8,128)(2,1)S(1)}, u32[]{:S(2)}, u32[]{:S(2)}) collective-permute-start(bf16[128,1792]{1,0:T(8,128)(2,1)S(1)} %collective-permute-done.2.refs_1_.refs_2_), channel_id=1, source_target_pairs={{0,4},{4,0},{8,12},{12,8},{1,5},{5,1},{9,13},{13,9},{2,6},{6,2},{1... | collective-permute-start | bytes 1376264 | tf_op jit(solution)/shard_map/ppermute | solution.py:21
  43.3 2.7 %collective-permute-start.5 = (bf16[128,1792]{1,0:T(8,128)(2,1)}, bf16[128,1792]{1,0:T(8,128)(2,1)S(1)}, u32[]{:S(2)}, u32[]{:S(2)}) collective-permute-start(bf16[128,1792]{1,0:T(8,128)(2,1)} %collective-permute-done.3.refs_2_.refs_3_), channel_id=1, source_target_pairs={{0,4},{4,0},{8,12},{12,8},{1,5},{5,1},{9,13},{13,9},{2,6},{6,2},{1... | collective-permute-start | bytes 1376264 | tf_op jit(solution)/shard_map/ppermute | solution.py:21
  66.6 36.8 %copy-start.4 = (f32[512,2048]{1,0:T(8,128)}, f32[512,2048]{1,0:T(8,128)S(1)}, u32[]{:S(2)}) copy-start(f32[512,2048]{1,0:T(8,128)S(1)} %base.7.refs_2_) | copy-start | bytes 12582916
  66.7 2.5 %collective-permute-start.6 = (bf16[128,3584]{1,0:T(8,128)(2,1)S(1)}, bf16[128,3584]{1,0:T(8,128)(2,1)S(1)}, u32[]{:S(2)}, u32[]{:S(2)}) collective-permute-start(bf16[128,3584]{1,0:T(8,128)(2,1)S(1)} %collective-permute-done.1.refs_1_.refs_0_), channel_id=1, source_target_pairs={{0,4},{4,0},{8,12},{12,8},{1,5},{5,1},{9,13},{13,9},{2,6},{6,2},{1... | collective-permute-start | bytes 2752520 | tf_op jit(solution)/shard_map/ppermute | solution.py:21
  66.9 36.6 %collective-permute-start.14 = (bf16[256,2048]{1,0:T(8,128)(2,1)}, bf16[256,2048]{1,0:T(8,128)(2,1)S(1)}, u32[]{:S(2)}, u32[]{:S(2)}) collective-permute-start(bf16[256,2048]{1,0:T(8,128)(2,1)} %constant_dynamic-slice_fusion.7), channel_id=1, source_target_pairs={{0,4},{4,0},{8,12},{12,8},{1,5},{5,1},{9,13},{13,9},{2,6},{6,2},{1... | collective-permute-start | bytes 3145736 | tf_op jit(solution)/shard_map/ppermute | solution.py:21
  67.2 13.5 %collective-permute-start.10 = (bf16[256,512]{1,0:T(8,128)(2,1)S(1)}, bf16[256,512]{1,0:T(8,128)(2,1)S(1)}, u32[]{:S(2)}, u32[]{:S(2)}) collective-permute-start(bf16[256,512]{1,0:T(8,128)(2,1)S(1)} %get-tuple-element.84), channel_id=1, source_target_pairs={{0,8},{4,12},{8,0},{12,4},{1,9},{5,13},{9,1},{13,5},{2,10},{6,14},... | collective-permute-start | bytes 786440 | tf_op jit(solution)/shard_map/ppermute | solution.py:21
  78.5 13.6 %collective-permute-start.9 = (bf16[4,64,128]{2,1,0:T(8,128)(2,1)S(1)}, bf16[4,64,128]{2,1,0:T(8,128)(2,1)S(1)}, u32[]{:S(2)}, u32[]{:S(2)}) collective-permute-start(bf16[4,64,128]{2,1,0:T(8,128)(2,1)S(1)} %get-tuple-element.83), channel_id=1, source_target_pairs={{0,4},{4,0},{8,12},{12,8},{1,5},{5,1},{9,13},{13,9},{2,6},{6,2},{1... | collective-permute-start | bytes 196616 | tf_op jit(solution)/shard_map/ppermute | solution.py:21
  78.7 13.4 %collective-permute-start.8 = (bf16[4,64,128]{2,1,0:T(8,128)(2,1)S(1)}, bf16[4,64,128]{2,1,0:T(8,128)(2,1)S(1)}, u32[]{:S(2)}, u32[]{:S(2)}) collective-permute-start(bf16[4,64,128]{2,1,0:T(8,128)(2,1)S(1)} %get-tuple-element.83), channel_id=1, source_target_pairs={{0,12},{4,8},{8,4},{12,0},{1,13},{5,9},{9,5},{13,1},{2,14},{6,10},... | collective-permute-start | bytes 196616 | tf_op jit(solution)/shard_map/ppermute | solution.py:21
  78.7 13.4 %collective-permute-start.7 = (bf16[4,64,128]{2,1,0:T(8,128)(2,1)S(1)}, bf16[4,64,128]{2,1,0:T(8,128)(2,1)S(1)}, u32[]{:S(2)}, u32[]{:S(2)}) collective-permute-start(bf16[4,64,128]{2,1,0:T(8,128)(2,1)S(1)} %get-tuple-element.83), channel_id=1, source_target_pairs={{0,8},{4,12},{8,0},{12,4},{1,9},{5,13},{9,1},{13,5},{2,10},{6,14},... | collective-permute-start | bytes 196616 | tf_op jit(solution)/shard_map/ppermute | solution.py:21
  80.7 20.4 %collective-permute-start.13 = (bf16[256,512]{1,0:T(8,128)(2,1)}, bf16[256,512]{1,0:T(8,128)(2,1)S(1)}, u32[]{:S(2)}, u32[]{:S(2)}) collective-permute-start(bf16[256,512]{1,0:T(8,128)(2,1)} %get-tuple-element.93), channel_id=1, source_target_pairs={{0,12},{4,8},{8,4},{12,0},{1,13},{5,9},{9,5},{13,1},{2,14},{6,10},... | collective-permute-start | bytes 786440 | tf_op jit(solution)/shard_map/ppermute | solution.py:21
  92.2 11.3 %copy-start.9 = (bf16[256,8192]{1,0:T(8,128)(2,1)S(1)}, bf16[256,8192]{1,0:T(8,128)(2,1)}, u32[]{:S(2)}) copy-start(bf16[256,8192]{1,0:T(8,128)(2,1)} %refs_4_.5) | copy-start | bytes 12582916
  92.2 4.5 %collective-permute-start.11 = (bf16[4,64,128]{2,1,0:T(8,128)(2,1)S(1)}, bf16[4,64,128]{2,1,0:T(8,128)(2,1)S(1)}, u32[]{:S(2)}, u32[]{:S(2)}) collective-permute-start(bf16[4,64,128]{2,1,0:T(8,128)(2,1)S(1)} %fusion.8), channel_id=1, source_target_pairs={{0,1},{1,0},{2,3},{3,2},{4,5},{5,4},{6,7},{7,6},{8,9},{9,8},{10,11... | collective-permute-start | bytes 196616 | tf_op jit(solution)/shard_map/ppermute | solution.py:21
  96.8 6.6 %collective-permute-start.12 = (bf16[4,64,128]{2,1,0:T(8,128)(2,1)S(1)}, bf16[4,64,128]{2,1,0:T(8,128)(2,1)S(1)}, u32[]{:S(2)}, u32[]{:S(2)}) collective-permute-start(bf16[4,64,128]{2,1,0:T(8,128)(2,1)S(1)} %get-tuple-element.133), channel_id=1, source_target_pairs={{0,2},{1,3},{2,0},{3,1},{4,6},{5,7},{6,4},{7,5},{8,10},{9,11},{10,... | collective-permute-start | bytes 196616 | tf_op jit(solution)/shard_map/ppermute | solution.py:21
  99.6 24.2 %collective-permute-start.16 = (bf16[256,512]{1,0:T(8,128)(2,1)}, bf16[256,512]{1,0:T(8,128)(2,1)S(1)}, u32[]{:S(2)}, u32[]{:S(2)}) collective-permute-start(bf16[256,512]{1,0:T(8,128)(2,1)} %get-tuple-element.102), channel_id=1, source_target_pairs={{0,8},{4,12},{8,0},{12,4},{1,9},{5,13},{9,1},{13,5},{2,10},{6,14},... | collective-permute-start | bytes 786440 | tf_op jit(solution)/shard_map/ppermute | solution.py:21
  101.1 22.0 %collective-permute-start.17 = (bf16[256,512]{1,0:T(8,128)(2,1)}, bf16[256,512]{1,0:T(8,128)(2,1)}, u32[]{:S(2)}, u32[]{:S(2)}) collective-permute-start(bf16[256,512]{1,0:T(8,128)(2,1)} %get-tuple-element.105), channel_id=1, source_target_pairs={{0,12},{4,8},{8,4},{12,0},{1,13},{5,9},{9,5},{13,1},{2,14},{6,10},... | collective-permute-start | bytes 786440 | tf_op jit(solution)/shard_map/ppermute | solution.py:21
  107.4 20.1 %collective-permute-start.15 = (bf16[2,128,512]{2,1,0:T(8,128)(2,1)}, bf16[2,128,512]{2,1,0:T(8,128)(2,1)}, u32[]{:S(2)}, u32[]{:S(2)}) collective-permute-start(bf16[2,128,512]{2,1,0:T(8,128)(2,1)} %get-tuple-element.99), channel_id=1, source_target_pairs={{0,1},{1,0},{2,3},{3,2},{4,5},{5,4},{6,7},{7,6},{8,9},{9,8},{10,11... | collective-permute-start | bytes 786440 | tf_op jit(solution)/shard_map/ppermute | solution.py:21
  107.8 24.3 %collective-permute-start.20 = (bf16[256,512]{1,0:T(8,128)(2,1)}, bf16[256,512]{1,0:T(8,128)(2,1)S(1)}, u32[]{:S(2)}, u32[]{:S(2)}) collective-permute-start(bf16[256,512]{1,0:T(8,128)(2,1)} %get-tuple-element.113), channel_id=1, source_target_pairs={{0,8},{4,12},{8,0},{12,4},{1,9},{5,13},{9,1},{13,5},{2,10},{6,14},... | collective-permute-start | bytes 786440 | tf_op jit(solution)/shard_map/ppermute | solution.py:21
  109.2 21.0 %collective-permute-start.21 = (bf16[256,512]{1,0:T(8,128)(2,1)}, bf16[256,512]{1,0:T(8,128)(2,1)S(1)}, u32[]{:S(2)}, u32[]{:S(2)}) collective-permute-start(bf16[256,512]{1,0:T(8,128)(2,1)} %get-tuple-element.116), channel_id=1, source_target_pairs={{0,12},{4,8},{8,4},{12,0},{1,13},{5,9},{9,5},{13,1},{2,14},{6,10},... | collective-permute-start | bytes 786440 | tf_op jit(solution)/shard_map/ppermute | solution.py:21
  123.1 24.0 %collective-permute-start.24 = (bf16[256,512]{1,0:T(8,128)(2,1)S(1)}, bf16[256,512]{1,0:T(8,128)(2,1)S(1)}, u32[]{:S(2)}, u32[]{:S(2)}) collective-permute-start(bf16[256,512]{1,0:T(8,128)(2,1)S(1)} %copy-done.19), channel_id=1, source_target_pairs={{0,8},{4,12},{8,0},{12,4},{1,9},{5,13},{9,1},{13,5},{2,10},{6,14},... | collective-permute-start | bytes 786440 | tf_op jit(solution)/shard_map/ppermute | solution.py:21
  123.8 23.3 %collective-permute-start.25 = (bf16[256,512]{1,0:T(8,128)(2,1)S(1)}, bf16[256,512]{1,0:T(8,128)(2,1)S(1)}, u32[]{:S(2)}, u32[]{:S(2)}) collective-permute-start(bf16[256,512]{1,0:T(8,128)(2,1)S(1)} %copy-done.20), channel_id=1, source_target_pairs={{0,12},{4,8},{8,4},{12,0},{1,13},{5,9},{9,5},{13,1},{2,14},{6,10},... | collective-permute-start | bytes 786440 | tf_op jit(solution)/shard_map/ppermute | solution.py:21
  127.5 19.3 %collective-permute-start.19 = (bf16[2,128,512]{2,1,0:T(8,128)(2,1)S(1)}, bf16[2,128,512]{2,1,0:T(8,128)(2,1)S(1)}, u32[]{:S(2)}, u32[]{:S(2)}) collective-permute-start(bf16[2,128,512]{2,1,0:T(8,128)(2,1)S(1)} %get-tuple-element.107), channel_id=1, source_target_pairs={{0,1},{1,0},{2,3},{3,2},{4,5},{5,4},{6,7},{7,6},{8,9},{9,8},{10,11... | collective-permute-start | bytes 786440 | tf_op jit(solution)/shard_map/ppermute | solution.py:21
  130.3 19.3 %collective-permute-start.18 = (bf16[128,512]{1,0:T(8,128)(2,1)S(1)}, bf16[128,512]{1,0:T(8,128)(2,1)S(1)}, u32[]{:S(2)}, u32[]{:S(2)}) collective-permute-start(bf16[128,512]{1,0:T(8,128)(2,1)S(1)} %fusion.4), channel_id=1, source_target_pairs={{0,2},{1,3},{2,0},{3,1},{4,6},{5,7},{6,4},{7,5},{8,10},{9,11},{10,... | collective-permute-start | bytes 393224 | tf_op jit(solution)/shard_map/ppermute | solution.py:21
  133.4 21.9 %collective-permute-start.23 = (bf16[2,128,512]{2,1,0:T(8,128)(2,1)S(1)}, bf16[2,128,512]{2,1,0:T(8,128)(2,1)S(1)}, u32[]{:S(2)}, u32[]{:S(2)}) collective-permute-start(bf16[2,128,512]{2,1,0:T(8,128)(2,1)S(1)} %get-tuple-element.118), channel_id=1, source_target_pairs={{0,1},{1,0},{2,3},{3,2},{4,5},{5,4},{6,7},{7,6},{8,9},{9,8},{10,11... | collective-permute-start | bytes 786440 | tf_op jit(solution)/shard_map/ppermute | solution.py:21
  147.0 8.2 %collective-permute-start.22 = (bf16[128,512]{1,0:T(8,128)(2,1)S(1)}, bf16[128,512]{1,0:T(8,128)(2,1)S(1)}, u32[]{:S(2)}, u32[]{:S(2)}) collective-permute-start(bf16[128,512]{1,0:T(8,128)(2,1)S(1)} %fusion.5), channel_id=1, source_target_pairs={{0,2},{1,3},{2,0},{3,1},{4,6},{5,7},{6,4},{7,5},{8,10},{9,11},{10,... | collective-permute-start | bytes 393224 | tf_op jit(solution)/shard_map/ppermute | solution.py:21
  148.4 10.3 %collective-permute-start.27 = (bf16[2,128,512]{2,1,0:T(8,128)(2,1)S(1)}, bf16[2,128,512]{2,1,0:T(8,128)(2,1)S(1)}, u32[]{:S(2)}, u32[]{:S(2)}) collective-permute-start(bf16[2,128,512]{2,1,0:T(8,128)(2,1)S(1)} %get-tuple-element.129), channel_id=1, source_target_pairs={{0,1},{1,0},{2,3},{3,2},{4,5},{5,4},{6,7},{7,6},{8,9},{9,8},{10,11... | collective-permute-start | bytes 786440 | tf_op jit(solution)/shard_map/ppermute | solution.py:21
  155.4 11.1 %collective-permute-start.26 = (bf16[128,512]{1,0:T(8,128)(2,1)S(1)}, bf16[128,512]{1,0:T(8,128)(2,1)S(1)}, u32[]{:S(2)}, u32[]{:S(2)}) collective-permute-start(bf16[128,512]{1,0:T(8,128)(2,1)S(1)} %fusion.6), channel_id=1, source_target_pairs={{0,2},{1,3},{2,0},{3,1},{4,6},{5,7},{6,4},{7,5},{8,10},{9,11},{10,... | collective-permute-start | bytes 393224 | tf_op jit(solution)/shard_map/ppermute | solution.py:21
  158.7 10.3 %collective-permute-start.28 = (bf16[128,512]{1,0:T(8,128)(2,1)S(1)}, bf16[128,512]{1,0:T(8,128)(2,1)S(1)}, u32[]{:S(2)}, u32[]{:S(2)}) collective-permute-start(bf16[128,512]{1,0:T(8,128)(2,1)S(1)} %fusion.7), channel_id=1, source_target_pairs={{0,2},{1,3},{2,0},{3,1},{4,6},{5,7},{6,4},{7,5},{8,10},{9,11},{10,... | collective-permute-start | bytes 393224 | tf_op jit(solution)/shard_map/ppermute | solution.py:21
  (18 other events, 83.1 us)

commit v9 on v8

--- a/solution.py
+++ b/solution.py
@@ -7,6 +7,7 @@
 
 F32 = jnp.float32
 BF16 = jnp.bfloat16
+VMEM_LIMIT = 48 * 1024 * 1024
 WIDTHS = (512, 512, 512, 512)
 CAP = 4
 HALVES = 2
@@ -29,8 +30,8 @@
     return pl.CostEstimate(flops=flops // hint, bytes_accessed=moved // hint, transcendentals=0)
 
 
-def params(mebibytes):
-    return pltpu.CompilerParams(vmem_limit_bytes=mebibytes * 1024 * 1024)
+def params():
+    return pltpu.CompilerParams(vmem_limit_bytes=VMEM_LIMIT)
 
 
 def cut_kernel(ref, *refs):
@@ -62,7 +63,7 @@
             pltpu.VMEM(array.shape, array.dtype),
             pltpu.SemaphoreType.DMA((2, len(widths))),
         ],
-        compiler_params=params(4),
+        compiler_params=params(),
         cost_estimate=cost(0, 4 * array.size),
         name="cut",
     )(array)
@@ -100,7 +101,6 @@
     rows = groups[0][0][0].shape[0]
     depth = sum(wide for _, wide, _ in groups[0])
     total = rows * len(groups)
-    limit = 28 if len(groups) > 2 else 20 if tile > 256 else 14
     in_specs, args = [], []
     for group in groups:
         for array, wide, block in group:
@@ -121,7 +121,7 @@
         out_specs=pl.BlockSpec((total, tile), lambda n: (0, n)),
         out_shape=jax.ShapeDtypeStruct((total, width), F32),
         scratch_shapes=[pltpu.VMEM((total, depth), BF16)],
-        compiler_params=params(limit),
+        compiler_params=params(),
         cost_estimate=cost(
             2 * total * depth * width, 2 * depth * (width + total) + 8 * total * width, hint
         ),
@@ -243,7 +243,7 @@
             ],
         ),
         out_shape=out_shape,
-        compiler_params=params(18 if first == 0 else 12),
+        compiler_params=params(),
         cost_estimate=cost(4 * rows * depth * CAP * rank, 4 * depth * (CAP * rank + rows)),
         name="scores",
     )(info, *args)
@@ -326,7 +326,7 @@
             scratch_shapes=[pltpu.VMEM((4 * held, tile), BF16)],
         ),
         out_shape=out_shape,
-        compiler_params=params(14),
+        compiler_params=params(),
         cost_estimate=cost(
             32 * rows * held * width, 26 * rows * width + 8 * held * width
         ),

time: 171 us -> 131 us (0.77)
  local copies, waits for them, and re-layouts: 63.9 us -> 9.95 us
  Pallas kernels: 49.4 us -> 61.8 us
  waiting for transfers between devices: 24.9 us -> 28.4 us
    unnamed x42 -> x22, local copies, waits for them, and re-layouts: 58.4 us -> 5.59 us
    pallas_call x6, Pallas kernels: 26.6 us -> 33.5 us  [product(): pl.pallas_call(lambda *refs: product_kernel(counts, prior is not None, *r...]
    ppermute x29, waiting for transfers between devices: 24.9 us -> 28.4 us  [swap(): return lax.ppermute(values, axis, partners(lax.axis_size(axis), step))]
    pallas_call x4, Pallas kernels: 6.96 us -> 10.4 us  [combine(): pl.pallas_call(lambda *refs: combine_kernel(bool(build), *refs), grid_spe...]
    pallas_call x3, Pallas kernels: 14.4 us -> 16.4 us  [scores(): pl.pallas_call(lambda *refs: scores_kernel(first, half * depth, len(lower...]
  transfers between devices with their start and end apart: 29 -> 29, of which waited for: 9 -> 11; matrix products, arithmetic and copies ran while one was open for 5% -> 6% of each run, Pallas kernels for 29% -> 47%
where the time goes in v9:
time: 131 us; the launch traced here: 130 us
  Pallas kernels  61.8 us (47%)
  waiting for transfers between devices  28.4 us (22%)
  starting transfers between devices  25.3 us (19%)
  local copies, waits for them, and re-layouts  9.95 us (8%)
  other arithmetic  4.62 us (4%)
    pallas_call x6, Pallas kernels, product(): pl.pallas_call(lambda *refs: product_kernel(counts, prior is not None, *r...  33.5 us
    ppermute x29, waiting for transfers between devices, swap(): return lax.ppermute(values, axis, partners(lax.axis_size(axis), step))  28.4 us
    ppermute x29, starting transfers between devices, swap(): return lax.ppermute(values, axis, partners(lax.axis_size(axis), step))  25.3 us
    pallas_call x3, Pallas kernels, scores(): pl.pallas_call(lambda *refs: scores_kernel(first, half * depth, len(lower...  16.4 us
    pallas_call x4, Pallas kernels, combine(): pl.pallas_call(lambda *refs: combine_kernel(bool(build), *refs), grid_spe...  10.4 us
    unnamed x22, local copies, waits for them, and re-layouts  5.59 us
    dynamic_slice x1, local copies, waits for them, and re-layouts, per_device_fast(): lax.dynamic_slice(output_maps, (0, (place ^ other) * width + start), (hel...  2.74 us
  transfers between devices with their start and end apart: 29, of which 11 were waited for; matrix products, arithmetic and copies ran while one was open for 6% of the time, Pallas kernels for 47%

profile of v9, /device:TPU:0, one launch (start us, length us, event | category | flops | bytes accessed | tf_op | source)
XLA Modules:
  0.0 130.3 jit_solution(4108055899524571415)
XLA Ops:
  0.5 1.5 %copy-done = bf16[128,7168]{1,0:T(8,128)(2,1)S(1)} copy-done((bf16[128,7168]{1,0:T(8,128)(2,1)S(1)}, bf16[128,7168]{1,0:T(8,128)(2,1)}, u32[]{:S(2)}) %copy-start) | copy-done | bytes 1835032
  2.0 1.5 %cut.1 = (bf16[128,1792]{1,0:T(8,128)(2,1)}, bf16[128,1792]{1,0:T(8,128)(2,1)}, bf16[128,3584]{1,0:T(8,128)(2,1)}) custom-call(bf16[128,7168]{1,0:T(8,128)(2,1)S(1)} %copy-done), custom_call_target="tpu_custom_call" | custom-call | bytes 3670 | tf_op jit(solution)/shard_map/cut/pallas_call | solution.py:57
  3.5 2.6 %collective-permute-start.2 = (bf16[128,1792]{1,0:T(8,128)(2,1)}, bf16[128,1792]{1,0:T(8,128)(2,1)S(1)}, u32[]{:S(2)}, u32[]{:S(2)}) collective-permute-start(bf16[128,1792]{1,0:T(8,128)(2,1)} %get-tuple-element.73), channel_id=1, source_target_pairs={{0,8},{4,12},{8,0},{12,4},{1,9},{5,13},{9,1},{13,5},{2,10},{6,14},... | collective-permute-start | bytes 1376264 | tf_op jit(solution)/shard_map/ppermute | solution.py:22
  6.1 1.9 %collective-permute-start.1 = (bf16[128,3584]{1,0:T(8,128)(2,1)}, bf16[128,3584]{1,0:T(8,128)(2,1)S(1)}, u32[]{:S(2)}, u32[]{:S(2)}) collective-permute-start(bf16[128,3584]{1,0:T(8,128)(2,1)} %get-tuple-element.71), channel_id=1, source_target_pairs={{0,8},{4,12},{8,0},{12,4},{1,9},{5,13},{9,1},{13,5},{2,10},{6,14},... | collective-permute-start | bytes 2752520 | tf_op jit(solution)/shard_map/ppermute | solution.py:22
  10.4 2.7 %constant_dynamic-slice_fusion.8 = (bf16[256,512]{1,0:T(8,128)(2,1)}, bf16[256,512]{1,0:T(8,128)(2,1)}, bf16[256,512]{1,0:T(8,128)(2,1)}, bf16[256,512]{1,0:T(8,...) fusion(bf16[256,8192]{1,0:T(8,128)(2,1)} %refs_4_.5, ...), kind=kLoop, calls=%fused_computation.41 | loop fusion | bytes 4194336 | tf_op jit(solution)/shard_map/dynamic_slice | solution.py:355
  14.6 7.1 %scores.3.refs_5_ = f32[2,64,128]{2,1,0:T(8,128)S(1)} custom-call(s32[17]{0:T(128)S(1)} %pad_add_fusion.refs_0_, bf16[128,7168]{1,0:T(8,128)(2,1)S(1)} %copy-done.1, bf16[128,7168]{1,0:T(8,128)(2,1)} %collective-permute-done.refs_2_.refs_1_, bf16[16,64,7168]{2,1,0:T(8,128)(2,1)} %refs_3_.7, s32[4,1,128]{2,1,0:T(1,128)S(1)} %bitcast.45), custom_call_target="tpu_custom_call" | custom-call | flops 939524 | bytes 11010 | tf_op jit(solution)/shard_map/scores/pallas_call | solution.py:231
  21.7 8.2 %base.6.refs_6_ = f32[256,2048]{1,0:T(8,128)S(1)} custom-call(bf16[128,7168]{1,0:T(8,128)(2,1)S(1)} %copy-done.1, bf16[128,7168]{1,0:T(8,128)(2,1)} %collective-permute-done.refs_2_.refs_1_, bf16[7168,2048]{1,0:T(8,128)(2,1)} %refs_3_.11), custom_call_target="tpu_custom_call" | custom-call | flops 3758096 | bytes 20709 | tf_op jit(solution)/shard_map/base/pallas_call | solution.py:117
  29.9 1.4 %copy-done.6 = f32[256,2048]{1,0:T(8,128)} copy-done((f32[256,2048]{1,0:T(8,128)}, f32[256,2048]{1,0:T(8,128)S(1)}, u32[]{:S(2)}) %copy-start.6) | copy-done | bytes 2097176
  34.0 4.8 %scores.4.refs_4_ = f32[2,256,128]{2,1,0:T(8,128)S(1)} custom-call(s32[17]{0:T(128)S(1)} %pad_add_fusion.refs_0_, bf16[128,1792]{1,0:T(8,128)(2,1)S(1)} %collective-permute-done.2.refs_1_.refs_2_, bf16[128,1792]{1,0:T(8,128)(2,1)} %collective-permute-done.3.refs_2_.refs_3_, bf16[128,1792]{1,0:T(8,128)(2,1)S(1)} %collective-permute-done.4.refs_3_.refs_4_, ...), custom_call_target="tpu_custom_call" | custom-call | flops 469762 | bytes 5505 | tf_op jit(solution)/shard_map/scores/pallas_call | solution.py:231
  38.8 12.9 %base.7.refs_2_ = f32[512,2048]{1,0:T(8,128)} custom-call(bf16[128,7168]{1,0:T(8,128)(2,1)S(1)} %copy-done.1, bf16[128,7168]{1,0:T(8,128)(2,1)} %collective-permute-done.refs_2_.refs_1_, bf16[128,1792]{1,0:T(8,128)(2,1)S(1)} %collective-permute-done.2.refs_1_.refs_2_, bf16[128,1792]{1,0:T(8,128)(2,1)} %collective-permute-done.3.refs_2_.refs_3_, ...), custom_call_target="tpu_custom_call" | custom-call | flops 7516192 | bytes 26738 | tf_op jit(solution)/shard_map/base/pallas_call | solution.py:117
  52.2 1.9 %collective-permute-done.6.refs_2_.refs_1_ = bf16[128,3584]{1,0:T(8,128)(2,1)S(1)} collective-permute-done((bf16[128,3584]{1,0:T(8,128)(2,1)S(1)}, bf16[128,3584]{1,0:T(8,128)(2,1)S(1)}, u32[]{:S(2)}, u32[]{:S(2)}) %collective-permute-start.6) | collective-permute-done | bytes 917536 | tf_op jit(solution)/shard_map/ppermute | solution.py:22
  54.1 4.5 %scores.5 = (f32[4,64,128]{2,1,0:T(8,128)S(1)}, bf16[4,64,128]{2,1,0:T(8,128)(2,1)S(1)}) custom-call(s32[17]{0:T(128)S(1)} %pad_add_fusion.refs_0_, bf16[128,3584]{1,0:T(8,128)(2,1)S(1)} %collective-permute-done.1.refs_1_.refs_0_, bf16[128,3584]{1,0:T(8,128)(2,1)S(1)} %collective-permute-done.6.refs_2_.refs_1_, bf16[16,64,7168]{2,1,0:T(8,128)(2,1)} %refs_3_.7, ...), custom_call_target="tpu_custom_call" | custom-call | flops 469762 | bytes 5505 | tf_op jit(solution)/shard_map/scores/pallas_call | solution.py:231
  58.9 1.9 %collective-permute-start.7 = (bf16[4,64,128]{2,1,0:T(8,128)(2,1)S(1)}, bf16[4,64,128]{2,1,0:T(8,128)(2,1)S(1)}, u32[]{:S(2)}, u32[]{:S(2)}) collective-permute-start(bf16[4,64,128]{2,1,0:T(8,128)(2,1)S(1)} %get-tuple-element.83), channel_id=1, source_target_pairs={{0,8},{4,12},{8,0},{12,4},{1,9},{5,13},{9,1},{13,5},{2,10},{6,14},... | collective-permute-start | bytes 196616 | tf_op jit(solution)/shard_map/ppermute | solution.py:22
  60.8 3.1 %base.8 = f32[256,512]{1,0:T(8,128)S(1)} custom-call(bf16[128,3584]{1,0:T(8,128)(2,1)S(1)} %collective-permute-done.1.refs_1_.refs_0_, bf16[128,3584]{1,0:T(8,128)(2,1)S(1)} %collective-permute-done.6.refs_2_.refs_1_, f32[512,2048]{1,0:T(8,128)} %base.7.refs_2_, bf16[7168,2048]{1,0:T(8,128)(2,1)} %refs_3_.11), custom_call_target="tpu_custom_call" | custom-call | flops 939524096 | bytes 6553600 | tf_op jit(solution)/shard_map/base/pallas_call | solution.py:117
  65.1 1.6 %collective-permute-start.11 = (bf16[4,64,128]{2,1,0:T(8,128)(2,1)S(1)}, bf16[4,64,128]{2,1,0:T(8,128)(2,1)S(1)}, u32[]{:S(2)}, u32[]{:S(2)}) collective-permute-start(bf16[4,64,128]{2,1,0:T(8,128)(2,1)S(1)} %fusion.8), channel_id=1, source_target_pairs={{0,1},{1,0},{2,3},{3,2},{4,5},{5,4},{6,7},{7,6},{8,9},{9,8},{10,11... | collective-permute-start | bytes 196616 | tf_op jit(solution)/shard_map/ppermute | solution.py:22
  66.8 3.1 %base.9 = f32[256,512]{1,0:T(8,128)S(1)} custom-call(bf16[128,3584]{1,0:T(8,128)(2,1)S(1)} %collective-permute-done.1.refs_1_.refs_0_, bf16[128,3584]{1,0:T(8,128)(2,1)S(1)} %collective-permute-done.6.refs_2_.refs_1_, f32[512,2048]{1,0:T(8,128)} %base.7.refs_2_, bf16[7168,2048]{1,0:T(8,128)(2,1)} %refs_3_.11), custom_call_target="tpu_custom_call" | custom-call | flops 939524096 | bytes 6553600 | tf_op jit(solution)/shard_map/base/pallas_call | solution.py:117
  69.9 2.7 %collective-permute-start.12 = (bf16[4,64,128]{2,1,0:T(8,128)(2,1)S(1)}, bf16[4,64,128]{2,1,0:T(8,128)(2,1)S(1)}, u32[]{:S(2)}, u32[]{:S(2)}) collective-permute-start(bf16[4,64,128]{2,1,0:T(8,128)(2,1)S(1)} %get-tuple-element.133), channel_id=1, source_target_pairs={{0,2},{1,3},{2,0},{3,1},{4,6},{5,7},{6,4},{7,5},{8,10},{9,11},{10,... | collective-permute-start | bytes 196616 | tf_op jit(solution)/shard_map/ppermute | solution.py:22
  73.2 1.9 %collective-permute-done.12.refs_2_ = bf16[4,64,128]{2,1,0:T(8,128)(2,1)S(1)} collective-permute-done((bf16[4,64,128]{2,1,0:T(8,128)(2,1)S(1)}, bf16[4,64,128]{2,1,0:T(8,128)(2,1)S(1)}, u32[]{:S(2)}, u32[]{:S(2)}) %collective-permute-start.12) | collective-permute-done | bytes 65568 | tf_op jit(solution)/shard_map/ppermute | solution.py:22
  75.2 3.3 %combine.4 = (f32[2,128,512]{2,1,0:T(8,128)S(1)}, bf16[2,128,512]{2,1,0:T(8,128)(2,1)}, bf16[512,1024]{1,0:T(8,128)(2,1)S(1)}) custom-call(s32[10]{0:T(128)S(1)} %stack.40.refs_0_, f32[4,64,128]{2,1,0:T(8,128)S(1)} %get-tuple-element.134.refs_1_, bf16[4,64,128]{2,1,0:T(8,128)(2,1)S(1)} %collective-permute-done.12.refs_2_, ...), custom_call_target="tpu_custom_call" | custom-call | flops 536870 | bytes 2752 | tf_op jit(solution)/shard_map/combine/pallas_call | solution.py:319
  81.5 3.2 %base.10 = f32[256,512]{1,0:T(8,128)S(1)} custom-call(bf16[128,3584]{1,0:T(8,128)(2,1)S(1)} %collective-permute-done.1.refs_1_.refs_0_, bf16[128,3584]{1,0:T(8,128)(2,1)S(1)} %collective-permute-done.6.refs_2_.refs_1_, f32[512,2048]{1,0:T(8,128)} %base.7.refs_2_, bf16[7168,2048]{1,0:T(8,128)(2,1)} %refs_3_.11), custom_call_target="tpu_custom_call" | custom-call | flops 939524 | bytes 6553 | tf_op jit(solution)/shard_map/base/pallas_call | solution.py:117
  86.6 1.4 %collective-permute-start.24 = (bf16[256,512]{1,0:T(8,128)(2,1)S(1)}, bf16[256,512]{1,0:T(8,128)(2,1)S(1)}, u32[]{:S(2)}, u32[]{:S(2)}) collective-permute-start(bf16[256,512]{1,0:T(8,128)(2,1)S(1)} %copy-done.9), channel_id=1, source_target_pairs={{0,8},{4,12},{8,0},{12,4},{1,9},{5,13},{9,1},{13,5},{2,10},{6,14},... | collective-permute-start | bytes 786440 | tf_op jit(solution)/shard_map/ppermute | solution.py:22
  88.0 1.7 %collective-permute-start.25 = (bf16[256,512]{1,0:T(8,128)(2,1)S(1)}, bf16[256,512]{1,0:T(8,128)(2,1)S(1)}, u32[]{:S(2)}, u32[]{:S(2)}) collective-permute-start(bf16[256,512]{1,0:T(8,128)(2,1)S(1)} %copy-done.10), channel_id=1, source_target_pairs={{0,12},{4,8},{8,4},{12,0},{1,13},{5,9},{9,5},{13,1},{2,14},{6,10},... | collective-permute-start | bytes 786440 | tf_op jit(solution)/shard_map/ppermute | solution.py:22
  90.7 2.4 %combine.5 = (f32[2,128,512]{2,1,0:T(8,128)S(1)}, bf16[2,128,512]{2,1,0:T(8,128)(2,1)S(1)}) custom-call(s32[10]{0:T(128)S(1)} %stack.40.refs_0_, bf16[512,1024]{1,0:T(8,128)(2,1)S(1)} %copy-done.5, f32[4,128,2048]{2,1,0:T(8,128)} %bitcast.48, f32[2,128,512]{2,1,0:T(8,128)S(1)} %bitcast.41, bf16[256,8192]{1,0:T(8,128)(2,1)} %refs_4_.5, ...), custom_call_target="tpu_custom_call" | custom-call | flops 536870 | bytes 2752 | tf_op jit(solution)/shard_map/combine/pallas_call | solution.py:319
  94.9 2.2 %collective-permute-done.21.refs_7_ = bf16[256,512]{1,0:T(8,128)(2,1)S(1)} collective-permute-done((bf16[256,512]{1,0:T(8,128)(2,1)}, bf16[256,512]{1,0:T(8,128)(2,1)S(1)}, u32[]{:S(2)}, u32[]{:S(2)}) %collective-permute-start.21) | collective-permute-done | bytes 262176 | tf_op jit(solution)/shard_map/ppermute | solution.py:22
  97.5 2.4 %combine.6 = (f32[2,128,512]{2,1,0:T(8,128)S(1)}, bf16[2,128,512]{2,1,0:T(8,128)(2,1)S(1)}) custom-call(s32[10]{0:T(128)S(1)} %stack.40.refs_0_, bf16[512,1024]{1,0:T(8,128)(2,1)S(1)} %copy-done.5, f32[4,128,2048]{2,1,0:T(8,128)} %bitcast.49, f32[2,128,512]{2,1,0:T(8,128)S(1)} %bitcast.43, bf16[256,8192]{1,0:T(8,128)(2,1)} %refs_4_.5, ...), custom_call_target="tpu_custom_call" | custom-call | flops 536870 | bytes 2752 | tf_op jit(solution)/shard_map/combine/pallas_call | solution.py:319
  101.1 3.1 %base.11 = f32[256,512]{1,0:T(8,128)S(1)} custom-call(bf16[128,3584]{1,0:T(8,128)(2,1)S(1)} %collective-permute-done.1.refs_1_.refs_0_, bf16[128,3584]{1,0:T(8,128)(2,1)S(1)} %collective-permute-done.6.refs_2_.refs_1_, f32[512,2048]{1,0:T(8,128)} %base.7.refs_2_, bf16[7168,2048]{1,0:T(8,128)(2,1)} %refs_3_.11), custom_call_target="tpu_custom_call" | custom-call | flops 939524 | bytes 6553 | tf_op jit(solution)/shard_map/base/pallas_call | solution.py:117
  104.3 2.7 %collective-permute-start.22 = (bf16[128,512]{1,0:T(8,128)(2,1)S(1)}, bf16[128,512]{1,0:T(8,128)(2,1)S(1)}, u32[]{:S(2)}, u32[]{:S(2)}) collective-permute-start(bf16[128,512]{1,0:T(8,128)(2,1)S(1)} %fusion.5), channel_id=1, source_target_pairs={{0,2},{1,3},{2,0},{3,1},{4,6},{5,7},{6,4},{7,5},{8,10},{9,11},{10,... | collective-permute-start | bytes 393224 | tf_op jit(solution)/shard_map/ppermute | solution.py:22
  107.0 2.4 %combine.7 = (f32[2,128,512]{2,1,0:T(8,128)S(1)}, bf16[2,128,512]{2,1,0:T(8,128)(2,1)S(1)}) custom-call(s32[10]{0:T(128)S(1)} %stack.40.refs_0_, bf16[512,1024]{1,0:T(8,128)(2,1)S(1)} %copy-done.5, f32[4,128,2048]{2,1,0:T(8,128)} %bitcast.50, f32[2,128,512]{2,1,0:T(8,128)S(1)} %bitcast.44, bf16[256,8192]{1,0:T(8,128)(2,1)} %refs_4_.5, ...), custom_call_target="tpu_custom_call" | custom-call | flops 536870 | bytes 2752 | tf_op jit(solution)/shard_map/combine/pallas_call | solution.py:319
  110.3 3.4 %collective-permute-done.22 = bf16[128,512]{1,0:T(8,128)(2,1)S(1)} collective-permute-done((bf16[128,512]{1,0:T(8,128)(2,1)S(1)}, bf16[128,512]{1,0:T(8,128)(2,1)S(1)}, u32[]{:S(2)}, u32[]{:S(2)}) %collective-permute-start.22) | collective-permute-done | bytes 131104 | tf_op jit(solution)/shard_map/ppermute | solution.py:22
  114.4 6.0 %collective-permute-done.27 = bf16[2,128,512]{2,1,0:T(8,128)(2,1)S(1)} collective-permute-done((bf16[2,128,512]{2,1,0:T(8,128)(2,1)S(1)}, bf16[2,128,512]{2,1,0:T(8,128)(2,1)S(1)}, u32[]{:S(2)}, u32[]{:S(2)}) %collective-permute-start.27) | collective-permute-done | bytes 262176 | tf_op jit(solution)/shard_map/ppermute | solution.py:22
  120.9 5.8 %collective-permute-done.26 = bf16[128,512]{1,0:T(8,128)(2,1)S(1)} collective-permute-done((bf16[128,512]{1,0:T(8,128)(2,1)S(1)}, bf16[128,512]{1,0:T(8,128)(2,1)S(1)}, u32[]{:S(2)}, u32[]{:S(2)}) %collective-permute-start.26) | collective-permute-done | bytes 131104 | tf_op jit(solution)/shard_map/ppermute | solution.py:22
  126.7 2.7 %collective-permute-done.28 = bf16[128,512]{1,0:T(8,128)(2,1)S(1)} collective-permute-done((bf16[128,512]{1,0:T(8,128)(2,1)S(1)}, bf16[128,512]{1,0:T(8,128)(2,1)S(1)}, u32[]{:S(2)}, u32[]{:S(2)}) %collective-permute-start.28) | collective-permute-done | bytes 131104 | tf_op jit(solution)/shard_map/ppermute | solution.py:22
  (94 shorter events, 22.2 us)
Async XLA Ops:
  0.0 14.4 %collective-permute-start = (bf16[128,7168]{1,0:T(8,128)(2,1)}, bf16[128,7168]{1,0:T(8,128)(2,1)}, u32[]{:S(2)}, u32[]{:S(2)}) collective-permute-start(bf16[128,7168]{1,0:T(8,128)(2,1)} %refs_0_.1), channel_id=1, source_target_pairs={{0,4},{4,0},{8,12},{12,8},{1,5},{5,1},{9,13},{13,9},{2,6},{6,2},{1... | collective-permute-start | bytes 5505032 | tf_op jit(solution)/shard_map/ppermute | solution.py:22
  2.0 12.6 %copy-start.1 = (bf16[128,7168]{1,0:T(8,128)(2,1)S(1)}, bf16[128,7168]{1,0:T(8,128)(2,1)}, u32[]{:S(2)}) copy-start(bf16[128,7168]{1,0:T(8,128)(2,1)} %refs_0_.1) | copy-start | bytes 5505028
  3.5 27.8 %collective-permute-start.2 = (bf16[128,1792]{1,0:T(8,128)(2,1)}, bf16[128,1792]{1,0:T(8,128)(2,1)S(1)}, u32[]{:S(2)}, u32[]{:S(2)}) collective-permute-start(bf16[128,1792]{1,0:T(8,128)(2,1)} %get-tuple-element.73), channel_id=1, source_target_pairs={{0,8},{4,12},{8,0},{12,4},{1,9},{5,13},{9,1},{13,5},{2,10},{6,14},... | collective-permute-start | bytes 1376264 | tf_op jit(solution)/shard_map/ppermute | solution.py:22
  6.0 25.3 %collective-permute-start.3 = (bf16[128,1792]{1,0:T(8,128)(2,1)}, bf16[128,1792]{1,0:T(8,128)(2,1)}, u32[]{:S(2)}, u32[]{:S(2)}) collective-permute-start(bf16[128,1792]{1,0:T(8,128)(2,1)} %get-tuple-element.74), channel_id=1, source_target_pairs={{0,8},{4,12},{8,0},{12,4},{1,9},{5,13},{9,1},{13,5},{2,10},{6,14},... | collective-permute-start | bytes 1376264 | tf_op jit(solution)/shard_map/ppermute | solution.py:22
  6.1 45.5 %collective-permute-start.1 = (bf16[128,3584]{1,0:T(8,128)(2,1)}, bf16[128,3584]{1,0:T(8,128)(2,1)S(1)}, u32[]{:S(2)}, u32[]{:S(2)}) collective-permute-start(bf16[128,3584]{1,0:T(8,128)(2,1)} %get-tuple-element.71), channel_id=1, source_target_pairs={{0,8},{4,12},{8,0},{12,4},{1,9},{5,13},{9,1},{13,5},{2,10},{6,14},... | collective-permute-start | bytes 2752520 | tf_op jit(solution)/shard_map/ppermute | solution.py:22
  31.3 1.8 %collective-permute-start.4 = (bf16[128,1792]{1,0:T(8,128)(2,1)S(1)}, bf16[128,1792]{1,0:T(8,128)(2,1)S(1)}, u32[]{:S(2)}, u32[]{:S(2)}) collective-permute-start(bf16[128,1792]{1,0:T(8,128)(2,1)S(1)} %collective-permute-done.2.refs_1_.refs_2_), channel_id=1, source_target_pairs={{0,4},{4,0},{8,12},{12,8},{1,5},{5,1},{9,13},{13,9},{2,6},{6,2},{1... | collective-permute-start | bytes 1376264 | tf_op jit(solution)/shard_map/ppermute | solution.py:22
  31.3 2.7 %collective-permute-start.5 = (bf16[128,1792]{1,0:T(8,128)(2,1)}, bf16[128,1792]{1,0:T(8,128)(2,1)S(1)}, u32[]{:S(2)}, u32[]{:S(2)}) collective-permute-start(bf16[128,1792]{1,0:T(8,128)(2,1)} %collective-permute-done.3.refs_2_.refs_3_), channel_id=1, source_target_pairs={{0,4},{4,0},{8,12},{12,8},{1,5},{5,1},{9,13},{13,9},{2,6},{6,2},{1... | collective-permute-start | bytes 1376264 | tf_op jit(solution)/shard_map/ppermute | solution.py:22
  51.6 2.5 %collective-permute-start.6 = (bf16[128,3584]{1,0:T(8,128)(2,1)S(1)}, bf16[128,3584]{1,0:T(8,128)(2,1)S(1)}, u32[]{:S(2)}, u32[]{:S(2)}) collective-permute-start(bf16[128,3584]{1,0:T(8,128)(2,1)S(1)} %collective-permute-done.1.refs_1_.refs_0_), channel_id=1, source_target_pairs={{0,4},{4,0},{8,12},{12,8},{1,5},{5,1},{9,13},{13,9},{2,6},{6,2},{1... | collective-permute-start | bytes 2752520 | tf_op jit(solution)/shard_map/ppermute | solution.py:22
  51.8 23.4 %collective-permute-start.14 = (bf16[256,2048]{1,0:T(8,128)(2,1)S(1)}, bf16[256,2048]{1,0:T(8,128)(2,1)S(1)}, u32[]{:S(2)}, u32[]{:S(2)}) collective-permute-start(bf16[256,2048]{1,0:T(8,128)(2,1)S(1)} %constant_dynamic-slice_fusion.7), channel_id=1, source_target_pairs={{0,4},{4,0},{8,12},{12,8},{1,5},{5,1},{9,13},{13,9},{2,6},{6,2},{1... | collective-permute-start | bytes 3145736 | tf_op jit(solution)/shard_map/ppermute | solution.py:22
  52.2 8.7 %collective-permute-start.10 = (bf16[256,512]{1,0:T(8,128)(2,1)S(1)}, bf16[256,512]{1,0:T(8,128)(2,1)S(1)}, u32[]{:S(2)}, u32[]{:S(2)}) collective-permute-start(bf16[256,512]{1,0:T(8,128)(2,1)S(1)} %get-tuple-element.84), channel_id=1, source_target_pairs={{0,8},{4,12},{8,0},{12,4},{1,9},{5,13},{9,1},{13,5},{2,10},{6,14},... | collective-permute-start | bytes 786440 | tf_op jit(solution)/shard_map/ppermute | solution.py:22
  58.6 5.3 %collective-permute-start.9 = (bf16[4,64,128]{2,1,0:T(8,128)(2,1)S(1)}, bf16[4,64,128]{2,1,0:T(8,128)(2,1)S(1)}, u32[]{:S(2)}, u32[]{:S(2)}) collective-permute-start(bf16[4,64,128]{2,1,0:T(8,128)(2,1)S(1)} %get-tuple-element.83), channel_id=1, source_target_pairs={{0,4},{4,0},{8,12},{12,8},{1,5},{5,1},{9,13},{13,9},{2,6},{6,2},{1... | collective-permute-start | bytes 196616 | tf_op jit(solution)/shard_map/ppermute | solution.py:22
  58.8 5.1 %collective-permute-start.8 = (bf16[4,64,128]{2,1,0:T(8,128)(2,1)S(1)}, bf16[4,64,128]{2,1,0:T(8,128)(2,1)S(1)}, u32[]{:S(2)}, u32[]{:S(2)}) collective-permute-start(bf16[4,64,128]{2,1,0:T(8,128)(2,1)S(1)} %get-tuple-element.83), channel_id=1, source_target_pairs={{0,12},{4,8},{8,4},{12,0},{1,13},{5,9},{9,5},{13,1},{2,14},{6,10},... | collective-permute-start | bytes 196616 | tf_op jit(solution)/shard_map/ppermute | solution.py:22
  58.9 6.2 %collective-permute-start.7 = (bf16[4,64,128]{2,1,0:T(8,128)(2,1)S(1)}, bf16[4,64,128]{2,1,0:T(8,128)(2,1)S(1)}, u32[]{:S(2)}, u32[]{:S(2)}) collective-permute-start(bf16[4,64,128]{2,1,0:T(8,128)(2,1)S(1)} %get-tuple-element.83), channel_id=1, source_target_pairs={{0,8},{4,12},{8,0},{12,4},{1,9},{5,13},{9,1},{13,5},{2,10},{6,14},... | collective-permute-start | bytes 196616 | tf_op jit(solution)/shard_map/ppermute | solution.py:22
  60.8 12.4 %collective-permute-start.13 = (bf16[256,512]{1,0:T(8,128)(2,1)S(1)}, bf16[256,512]{1,0:T(8,128)(2,1)S(1)}, u32[]{:S(2)}, u32[]{:S(2)}) collective-permute-start(bf16[256,512]{1,0:T(8,128)(2,1)S(1)} %get-tuple-element.93), channel_id=1, source_target_pairs={{0,12},{4,8},{8,4},{12,0},{1,13},{5,9},{9,5},{13,1},{2,14},{6,10},... | collective-permute-start | bytes 786440 | tf_op jit(solution)/shard_map/ppermute | solution.py:22
  65.1 4.7 %collective-permute-start.11 = (bf16[4,64,128]{2,1,0:T(8,128)(2,1)S(1)}, bf16[4,64,128]{2,1,0:T(8,128)(2,1)S(1)}, u32[]{:S(2)}, u32[]{:S(2)}) collective-permute-start(bf16[4,64,128]{2,1,0:T(8,128)(2,1)S(1)} %fusion.8), channel_id=1, source_target_pairs={{0,1},{1,0},{2,3},{3,2},{4,5},{5,4},{6,7},{7,6},{8,9},{9,8},{10,11... | collective-permute-start | bytes 196616 | tf_op jit(solution)/shard_map/ppermute | solution.py:22
  69.9 5.2 %collective-permute-start.12 = (bf16[4,64,128]{2,1,0:T(8,128)(2,1)S(1)}, bf16[4,64,128]{2,1,0:T(8,128)(2,1)S(1)}, u32[]{:S(2)}, u32[]{:S(2)}) collective-permute-start(bf16[4,64,128]{2,1,0:T(8,128)(2,1)S(1)} %get-tuple-element.133), channel_id=1, source_target_pairs={{0,2},{1,3},{2,0},{3,1},{4,6},{5,7},{6,4},{7,5},{8,10},{9,11},{10,... | collective-permute-start | bytes 196616 | tf_op jit(solution)/shard_map/ppermute | solution.py:22
  72.6 15.5 %collective-permute-start.16 = (bf16[256,512]{1,0:T(8,128)(2,1)}, bf16[256,512]{1,0:T(8,128)(2,1)S(1)}, u32[]{:S(2)}, u32[]{:S(2)}) collective-permute-start(bf16[256,512]{1,0:T(8,128)(2,1)} %get-tuple-element.102), channel_id=1, source_target_pairs={{0,8},{4,12},{8,0},{12,4},{1,9},{5,13},{9,1},{13,5},{2,10},{6,14},... | collective-permute-start | bytes 786440 | tf_op jit(solution)/shard_map/ppermute | solution.py:22
  73.2 12.7 %collective-permute-start.17 = (bf16[256,512]{1,0:T(8,128)(2,1)}, bf16[256,512]{1,0:T(8,128)(2,1)S(1)}, u32[]{:S(2)}, u32[]{:S(2)}) collective-permute-start(bf16[256,512]{1,0:T(8,128)(2,1)} %get-tuple-element.105), channel_id=1, source_target_pairs={{0,12},{4,8},{8,4},{12,0},{1,13},{5,9},{9,5},{13,1},{2,14},{6,10},... | collective-permute-start | bytes 786440 | tf_op jit(solution)/shard_map/ppermute | solution.py:22
  79.5 13.6 %collective-permute-start.15 = (bf16[2,128,512]{2,1,0:T(8,128)(2,1)}, bf16[2,128,512]{2,1,0:T(8,128)(2,1)}, u32[]{:S(2)}, u32[]{:S(2)}) collective-permute-start(bf16[2,128,512]{2,1,0:T(8,128)(2,1)} %get-tuple-element.99), channel_id=1, source_target_pairs={{0,1},{1,0},{2,3},{3,2},{4,5},{5,4},{6,7},{7,6},{8,9},{9,8},{10,11... | collective-permute-start | bytes 786440 | tf_op jit(solution)/shard_map/ppermute | solution.py:22
  80.7 9.0 %copy-start.3 = (bf16[256,2048]{1,0:T(8,128)(2,1)S(1)}, bf16[256,2048]{1,0:T(8,128)(2,1)}, u32[]{:S(2)}) copy-start(bf16[256,2048]{1,0:T(8,128)(2,1)} %copy-done.2) | copy-start | bytes 3145732
  80.7 9.0 %copy-start.5 = (bf16[512,1024]{1,0:T(8,128)(2,1)S(1)}, bf16[512,1024]{1,0:T(8,128)(2,1)}, u32[]{:S(2)}) copy-start(bf16[512,1024]{1,0:T(8,128)(2,1)} %copy-done.4) | copy-start | bytes 3145732
  80.7 16.7 %collective-permute-start.20 = (bf16[256,512]{1,0:T(8,128)(2,1)}, bf16[256,512]{1,0:T(8,128)(2,1)S(1)}, u32[]{:S(2)}, u32[]{:S(2)}) collective-permute-start(bf16[256,512]{1,0:T(8,128)(2,1)} %get-tuple-element.113), channel_id=1, source_target_pairs={{0,8},{4,12},{8,0},{12,4},{1,9},{5,13},{9,1},{13,5},{2,10},{6,14},... | collective-permute-start | bytes 786440 | tf_op jit(solution)/shard_map/ppermute | solution.py:22
  81.5 15.6 %collective-permute-start.21 = (bf16[256,512]{1,0:T(8,128)(2,1)}, bf16[256,512]{1,0:T(8,128)(2,1)S(1)}, u32[]{:S(2)}, u32[]{:S(2)}) collective-permute-start(bf16[256,512]{1,0:T(8,128)(2,1)} %get-tuple-element.116), channel_id=1, source_target_pairs={{0,12},{4,8},{8,4},{12,0},{1,13},{5,9},{9,5},{13,1},{2,14},{6,10},... | collective-permute-start | bytes 786440 | tf_op jit(solution)/shard_map/ppermute | solution.py:22
  86.6 20.4 %collective-permute-start.24 = (bf16[256,512]{1,0:T(8,128)(2,1)S(1)}, bf16[256,512]{1,0:T(8,128)(2,1)S(1)}, u32[]{:S(2)}, u32[]{:S(2)}) collective-permute-start(bf16[256,512]{1,0:T(8,128)(2,1)S(1)} %copy-done.9), channel_id=1, source_target_pairs={{0,8},{4,12},{8,0},{12,4},{1,9},{5,13},{9,1},{13,5},{2,10},{6,14},... | collective-permute-start | bytes 786440 | tf_op jit(solution)/shard_map/ppermute | solution.py:22
  88.0 19.0 %collective-permute-start.25 = (bf16[256,512]{1,0:T(8,128)(2,1)S(1)}, bf16[256,512]{1,0:T(8,128)(2,1)S(1)}, u32[]{:S(2)}, u32[]{:S(2)}) collective-permute-start(bf16[256,512]{1,0:T(8,128)(2,1)S(1)} %copy-done.10), channel_id=1, source_target_pairs={{0,12},{4,8},{8,4},{12,0},{1,13},{5,9},{9,5},{13,1},{2,14},{6,10},... | collective-permute-start | bytes 786440 | tf_op jit(solution)/shard_map/ppermute | solution.py:22
  93.1 11.1 %collective-permute-start.19 = (bf16[2,128,512]{2,1,0:T(8,128)(2,1)S(1)}, bf16[2,128,512]{2,1,0:T(8,128)(2,1)S(1)}, u32[]{:S(2)}, u32[]{:S(2)}) collective-permute-start(bf16[2,128,512]{2,1,0:T(8,128)(2,1)S(1)} %get-tuple-element.107), channel_id=1, source_target_pairs={{0,1},{1,0},{2,3},{3,2},{4,5},{5,4},{6,7},{7,6},{8,9},{9,8},{10,11... | collective-permute-start | bytes 786440 | tf_op jit(solution)/shard_map/ppermute | solution.py:22
  97.1 13.1 %collective-permute-start.18 = (bf16[128,512]{1,0:T(8,128)(2,1)S(1)}, bf16[128,512]{1,0:T(8,128)(2,1)S(1)}, u32[]{:S(2)}, u32[]{:S(2)}) collective-permute-start(bf16[128,512]{1,0:T(8,128)(2,1)S(1)} %fusion.4), channel_id=1, source_target_pairs={{0,2},{1,3},{2,0},{3,1},{4,6},{5,7},{6,4},{7,5},{8,10},{9,11},{10,... | collective-permute-start | bytes 393224 | tf_op jit(solution)/shard_map/ppermute | solution.py:22
  99.8 13.9 %collective-permute-start.23 = (bf16[2,128,512]{2,1,0:T(8,128)(2,1)S(1)}, bf16[2,128,512]{2,1,0:T(8,128)(2,1)S(1)}, u32[]{:S(2)}, u32[]{:S(2)}) collective-permute-start(bf16[2,128,512]{2,1,0:T(8,128)(2,1)S(1)} %get-tuple-element.118), channel_id=1, source_target_pairs={{0,1},{1,0},{2,3},{3,2},{4,5},{5,4},{6,7},{7,6},{8,9},{9,8},{10,11... | collective-permute-start | bytes 786440 | tf_op jit(solution)/shard_map/ppermute | solution.py:22
  104.3 9.3 %collective-permute-start.22 = (bf16[128,512]{1,0:T(8,128)(2,1)S(1)}, bf16[128,512]{1,0:T(8,128)(2,1)S(1)}, u32[]{:S(2)}, u32[]{:S(2)}) collective-permute-start(bf16[128,512]{1,0:T(8,128)(2,1)S(1)} %fusion.5), channel_id=1, source_target_pairs={{0,2},{1,3},{2,0},{3,1},{4,6},{5,7},{6,4},{7,5},{8,10},{9,11},{10,... | collective-permute-start | bytes 393224 | tf_op jit(solution)/shard_map/ppermute | solution.py:22
  109.4 11.0 %collective-permute-start.27 = (bf16[2,128,512]{2,1,0:T(8,128)(2,1)S(1)}, bf16[2,128,512]{2,1,0:T(8,128)(2,1)S(1)}, u32[]{:S(2)}, u32[]{:S(2)}) collective-permute-start(bf16[2,128,512]{2,1,0:T(8,128)(2,1)S(1)} %get-tuple-element.129), channel_id=1, source_target_pairs={{0,1},{1,0},{2,3},{3,2},{4,5},{5,4},{6,7},{7,6},{8,9},{9,8},{10,11... | collective-permute-start | bytes 786440 | tf_op jit(solution)/shard_map/ppermute | solution.py:22
  113.8 12.8 %collective-permute-start.26 = (bf16[128,512]{1,0:T(8,128)(2,1)S(1)}, bf16[128,512]{1,0:T(8,128)(2,1)S(1)}, u32[]{:S(2)}, u32[]{:S(2)}) collective-permute-start(bf16[128,512]{1,0:T(8,128)(2,1)S(1)} %fusion.6), channel_id=1, source_target_pairs={{0,2},{1,3},{2,0},{3,1},{4,6},{5,7},{6,4},{7,5},{8,10},{9,11},{10,... | collective-permute-start | bytes 393224 | tf_op jit(solution)/shard_map/ppermute | solution.py:22
  120.5 8.9 %collective-permute-start.28 = (bf16[128,512]{1,0:T(8,128)(2,1)S(1)}, bf16[128,512]{1,0:T(8,128)(2,1)S(1)}, u32[]{:S(2)}, u32[]{:S(2)}) collective-permute-start(bf16[128,512]{1,0:T(8,128)(2,1)S(1)} %fusion.7), channel_id=1, source_target_pairs={{0,2},{1,3},{2,0},{3,1},{4,6},{5,7},{6,4},{7,5},{8,10},{9,11},{10,... | collective-permute-start | bytes 393224 | tf_op jit(solution)/shard_map/ppermute | solution.py:22
  (8 other events, 22.1 us)

commit v10 on v9

--- a/solution.py
+++ b/solution.py
@@ -346,16 +346,17 @@
 
     part = depth // HALVES
     near_b = swap(hidden, "pool", 1)
-    first_a, first_b, second = (
-        swap(block, "pool", 2) for block in cut_columns(hidden, (part // 2, part // 2, part))
-    )
+    *early, late = cut_columns(hidden, (part // 2, part // 2, part))
+    first_a, first_b = (swap(block, "pool", 2) for block in early)
 
     core_block = lax.dynamic_slice(output_maps, (0, (place ^ 1) * width), (held, width))
-    blocks = [
-        lax.dynamic_slice(output_maps, (0, (place ^ other) * width + start), (held, wide))
-        for start, wide in zip(starts, WIDTHS)
-        for other in (2, 3)
-    ]
+
+    def block_for(index, other, source):
+        return lax.dynamic_slice(
+            source, (0, (place ^ other) * width + starts[index]), (held, WIDTHS[index])
+        )
+
+    blocks = [block_for(index, other, output_maps) for index in range(2) for other in (2, 3)]
 
     order = place ^ jnp.arange(4, dtype=jnp.int32)
     hot = order[:, None] == jnp.arange(4, dtype=jnp.int32)[None, :]
@@ -397,6 +398,7 @@
     core_maps = swap(core_block, "pool", 1)
 
     (near_lowrank,) = scores(picks, 0, [own_rows], [near_b], input_maps, 0, ids=owned_ids)
+    second = swap(tie(late, near_lowrank), "pool", 2)
     near_late = product(
         [[(tie(own_rows, near_lowrank), part, 1)], [(near_b, part, 1)]],
         weight, 1, 0, width, 512,
@@ -431,24 +433,28 @@
     pieces = [far_piece(0, sent, 1)]
 
     def start_maps(index, after):
-        pair = blocks[2 * index : 2 * index + 2]
+        pair = later[2 * (index - 2) : 2 * (index - 2) + 2]
         return [swap(tie(x, after), "pool", 2 + k) for k, x in enumerate(pair)]
 
     moved = [[swap(blocks[0], "pool", 2), swap(tie(blocks[1], sent), "pool", 3)]]
+    moved.append([swap(tie(blocks[k], sent), "pool", k) for k in (2, 3)])
     moved[0][0] = tie(moved[0][0], sent)
     got = lax.optimization_barrier((*got, moved[0][0], pieces[0]))[:3]
     total = total + sum(x.astype(F32) for x in got)
     sent = total.astype(BF16)
     got = swap(sent, "tensor", 1)
-    moved.append(start_maps(1, sent))
     pieces.append(far_piece(1, sent, 1))
-    got = tie(got, pieces[1])
+    moved[0][1] = tie(moved[0][1], sent)
+    got = lax.optimization_barrier((got, pieces[1], moved[0][1]))[0]
     total = total + got.astype(F32)
     sent = total.astype(BF16)
     got = swap(sent, "tensor", 2)
+    source = tie(output_maps, sent)
+    later = [block_for(index, other, source) for index in (2, 3) for other in (2, 3)]
+    got, *later = lax.optimization_barrier((got, *later))
     moved.append(start_maps(2, sent))
-    moved[0][1] = tie(moved[0][1], sent)
-    got = lax.optimization_barrier((got, *moved[0]))[0]
+    moved[1][0] = tie(moved[1][0], sent)
+    got = lax.optimization_barrier((got, *moved[0], moved[1][0]))[0]
 
     near_base = base.reshape(4, rows, width)
     side = ((place ^ t) >> 1) & 1
@@ -459,6 +465,9 @@
         return moved[index] if after is None else [tie(x, after) for x in moved[index]]
 
     def pace(index):
+        if index == 1:
+            moved[2][0] = tie(moved[2][0], send)
+            return tie(near_base, moved[2][0])
         return near_base if index < 2 else tie(near_base, started[index - 2])
 
     started = []
@@ -467,7 +476,9 @@
 
     def finish(index, after):
         keep, got = halves[index]
-        got = got if after is None else tie(got, after)
+        got = tie(got, after)
+        if index == 2:
+            got = tie(got, parts[1])
         pair = keep + got.astype(F32)
         sent = jnp.where(side == 0, pair[1], pair[0]).astype(BF16)
         kept = jnp.where(side == 0, pair[0], pair[1])

time: 131 us -> 131 us (level)
  waiting for transfers between devices: 28.4 us -> 19.1 us
  starting transfers between devices: 25.3 us -> 31.5 us
  local copies, waits for them, and re-layouts: 9.95 us -> 12.7 us
    ppermute x29, waiting for transfers between devices: 28.4 us -> 19.1 us  [swap(): return lax.ppermute(values, axis, partners(lax.axis_size(axis), step))]
    ppermute x29, starting transfers between devices: 25.3 us -> 31.5 us  [swap(): return lax.ppermute(values, axis, partners(lax.axis_size(axis), step))]
    dynamic_slice x1 -> x2, local copies, waits for them, and re-layouts: 2.74 us -> 4.46 us  [block_for(): lax.dynamic_slice(source, (0, (place ^ other) * width + starts[index]), (...]
    unnamed x22 -> x20, local copies, waits for them, and re-layouts: 5.59 us -> 4.82 us
  transfers between devices with their start and end apart: 29 -> 29, of which waited for: 11 -> 8; matrix products, arithmetic and copies ran while one was open for 6% -> 9% of each run, Pallas kernels for 47% -> 48%
where the time goes in v10:
time: 131 us; the launch traced here: 130 us
  Pallas kernels  61.9 us (47%)
  starting transfers between devices  31.5 us (24%)
  waiting for transfers between devices  19.1 us (15%)
  local copies, waits for them, and re-layouts  12.7 us (10%)
  other arithmetic  4.63 us (4%)
    pallas_call x6, Pallas kernels, product(): pl.pallas_call(lambda *refs: product_kernel(counts, prior is not None, *r...  33.5 us
    ppermute x29, starting transfers between devices, swap(): return lax.ppermute(values, axis, partners(lax.axis_size(axis), step))  31.5 us
    ppermute x29, waiting for transfers between devices, swap(): return lax.ppermute(values, axis, partners(lax.axis_size(axis), step))  19.1 us
    pallas_call x3, Pallas kernels, scores(): pl.pallas_call(lambda *refs: scores_kernel(first, half * depth, len(lower...  16.4 us
    pallas_call x4, Pallas kernels, combine(): pl.pallas_call(lambda *refs: combine_kernel(bool(build), *refs), grid_spe...  10.9 us
    unnamed x20, local copies, waits for them, and re-layouts  4.82 us
    dynamic_slice x2, local copies, waits for them, and re-layouts, block_for(): lax.dynamic_slice(source, (0, (place ^ other) * width + starts[index]), (...  4.46 us
  transfers between devices with their start and end apart: 29, of which 8 were waited for; matrix products, arithmetic and copies ran while one was open for 9% of the time, Pallas kernels for 48%

profile of v10, /device:TPU:0, one launch (start us, length us, event | category | flops | bytes accessed | tf_op | source)
XLA Modules:
  0.0 130.2 jit_solution(6370052595362676379)
XLA Ops:
  0.5 1.5 %copy-done = bf16[128,7168]{1,0:T(8,128)(2,1)S(1)} copy-done((bf16[128,7168]{1,0:T(8,128)(2,1)S(1)}, bf16[128,7168]{1,0:T(8,128)(2,1)}, u32[]{:S(2)}) %copy-start) | copy-done | bytes 1835032
  4.0 2.5 %collective-permute-start.2 = (bf16[128,1792]{1,0:T(8,128)(2,1)}, bf16[128,1792]{1,0:T(8,128)(2,1)S(1)}, u32[]{:S(2)}, u32[]{:S(2)}) collective-permute-start(bf16[128,1792]{1,0:T(8,128)(2,1)} %get-tuple-element.83), channel_id=1, source_target_pairs={{0,8},{4,12},{8,0},{12,4},{1,9},{5,13},{9,1},{13,5},{2,10},{6,14},... | collective-permute-start | bytes 1376264 | tf_op jit(solution)/shard_map/ppermute | solution.py:22
  8.8 2.2 %constant_dynamic-slice_fusion.3 = (bf16[256,512]{1,0:T(8,128)(2,1)}, bf16[256,512]{1,0:T(8,128)(2,1)}, bf16[256,512]{1,0:T(8,128)(2,1)}, bf16[256,512]{1,0:T(8,128)(2,1)}) fusion(bf16[256,8192]{1,0:T(8,128)(2,1)} %refs_4_.5, s32[]{:T(128)S(6)} %select_n.104, s32[]{:T(128)S(6)} %select_n.103, s32[]{:T(128)S(6)} %select_n.102, s32[]{:T(128)S(6)} %select_n.101), kind=kLoop, calls=%fused_computation.35 | loop fusion | bytes 2097168 | tf_op jit(solution)/shard_map/dynamic_slice | solution.py:355
  11.0 2.4 %constant_dynamic-slice_fusion.7 = bf16[256,2048]{1,0:T(8,128)(2,1)} fusion(bf16[256,8192]{1,0:T(8,128)(2,1)} %refs_4_.5, s32[]{:T(128)S(6)} %select_n.100), kind=kLoop, calls=%fused_computation.39 | loop fusion | bytes 2097156 | tf_op jit(solution)/shard_map/dynamic_slice | solution.py:352
  14.3 7.1 %scores.3.refs_5_ = f32[2,64,128]{2,1,0:T(8,128)S(1)} custom-call(s32[17]{0:T(128)S(1)} %pad_add_fusion.refs_0_, bf16[128,7168]{1,0:T(8,128)(2,1)S(1)} %copy-done.1, bf16[128,7168]{1,0:T(8,128)(2,1)} %collective-permute-done.refs_2_.refs_1_, bf16[16,64,7168]{2,1,0:T(8,128)(2,1)} %refs_3_.7, s32[4,1,128]{2,1,0:T(1,128)S(1)} %bitcast.43), custom_call_target="tpu_custom_call" | custom-call | flops 939524 | bytes 11010 | tf_op jit(solution)/shard_map/scores/pallas_call | solution.py:231
  21.4 2.1 %collective-permute-start.1 = (bf16[128,3584]{1,0:T(8,128)(2,1)S(1)}, bf16[128,3584]{1,0:T(8,128)(2,1)S(1)}, u32[]{:S(2)}, u32[]{:S(2)}) collective-permute-start(bf16[128,3584]{1,0:T(8,128)(2,1)S(1)} %copy-done.7), channel_id=1, source_target_pairs={{0,8},{4,12},{8,0},{12,4},{1,9},{5,13},{9,1},{13,5},{2,10},{6,14},... | collective-permute-start | bytes 2752520 | tf_op jit(solution)/shard_map/ppermute | solution.py:22
  23.5 8.2 %base.6.refs_6_ = f32[256,2048]{1,0:T(8,128)S(1)} custom-call(bf16[128,7168]{1,0:T(8,128)(2,1)S(1)} %copy-done.1, bf16[128,7168]{1,0:T(8,128)(2,1)} %collective-permute-done.refs_2_.refs_1_, bf16[7168,2048]{1,0:T(8,128)(2,1)} %refs_3_.11), custom_call_target="tpu_custom_call" | custom-call | flops 3758096 | bytes 20709 | tf_op jit(solution)/shard_map/base/pallas_call | solution.py:117
  35.8 4.8 %scores.4.refs_4_ = f32[2,256,128]{2,1,0:T(8,128)S(1)} custom-call(s32[17]{0:T(128)S(1)} %pad_add_fusion.refs_0_, bf16[128,1792]{1,0:T(8,128)(2,1)S(1)} %collective-permute-done.2.refs_1_.refs_2_, bf16[128,1792]{1,0:T(8,128)(2,1)} %collective-permute-done.3.refs_2_.refs_3_, bf16[128,1792]{1,0:T(8,128)(2,1)S(1)} %collective-permute-done.4.refs_3_.refs_4_, ...), custom_call_target="tpu_custom_call" | custom-call | flops 469762 | bytes 5505 | tf_op jit(solution)/shard_map/scores/pallas_call | solution.py:231
  40.5 12.9 %base.7.refs_2_ = f32[512,2048]{1,0:T(8,128)} custom-call(bf16[128,7168]{1,0:T(8,128)(2,1)S(1)} %copy-done.1, bf16[128,7168]{1,0:T(8,128)(2,1)} %collective-permute-done.refs_2_.refs_1_, bf16[128,1792]{1,0:T(8,128)(2,1)S(1)} %collective-permute-done.2.refs_1_.refs_2_, bf16[128,1792]{1,0:T(8,128)(2,1)} %collective-permute-done.3.refs_2_.refs_3_, ...), custom_call_target="tpu_custom_call" | custom-call | flops 7516192 | bytes 26738 | tf_op jit(solution)/shard_map/base/pallas_call | solution.py:117
  53.9 2.0 %collective-permute-done.6.refs_2_.refs_1_ = bf16[128,3584]{1,0:T(8,128)(2,1)S(1)} collective-permute-done((bf16[128,3584]{1,0:T(8,128)(2,1)S(1)}, bf16[128,3584]{1,0:T(8,128)(2,1)S(1)}, u32[]{:S(2)}, u32[]{:S(2)}) %collective-permute-start.6) | collective-permute-done | bytes 917536 | tf_op jit(solution)/shard_map/ppermute | solution.py:22
  55.9 4.5 %scores.5 = (f32[4,64,128]{2,1,0:T(8,128)S(1)}, bf16[4,64,128]{2,1,0:T(8,128)(2,1)S(1)}) custom-call(s32[17]{0:T(128)S(1)} %pad_add_fusion.refs_0_, bf16[128,3584]{1,0:T(8,128)(2,1)S(1)} %collective-permute-done.1.refs_1_.refs_0_, bf16[128,3584]{1,0:T(8,128)(2,1)S(1)} %collective-permute-done.6.refs_2_.refs_1_, bf16[16,64,7168]{2,1,0:T(8,128)(2,1)} %refs_3_.7, ...), custom_call_target="tpu_custom_call" | custom-call | flops 469762 | bytes 5505 | tf_op jit(solution)/shard_map/scores/pallas_call | solution.py:231
  62.6 3.1 %base.8 = f32[256,512]{1,0:T(8,128)S(1)} custom-call(bf16[128,3584]{1,0:T(8,128)(2,1)S(1)} %collective-permute-done.1.refs_1_.refs_0_, bf16[128,3584]{1,0:T(8,128)(2,1)S(1)} %collective-permute-done.6.refs_2_.refs_1_, f32[512,2048]{1,0:T(8,128)} %base.7.refs_2_, bf16[7168,2048]{1,0:T(8,128)(2,1)} %refs_3_.11), custom_call_target="tpu_custom_call" | custom-call | flops 939524096 | bytes 6553600 | tf_op jit(solution)/shard_map/base/pallas_call | solution.py:117
  65.7 1.7 %collective-permute-start.14 = (bf16[256,512]{1,0:T(8,128)(2,1)S(1)}, bf16[256,512]{1,0:T(8,128)(2,1)S(1)}, u32[]{:S(2)}, u32[]{:S(2)}) collective-permute-start(bf16[256,512]{1,0:T(8,128)(2,1)S(1)} %copy-done.8), channel_id=1, source_target_pairs={{0,8},{4,12},{8,0},{12,4},{1,9},{5,13},{9,1},{13,5},{2,10},{6,14},... | collective-permute-start | bytes 786440 | tf_op jit(solution)/shard_map/ppermute | solution.py:22
  67.6 1.8 %collective-permute-start.11 = (bf16[4,64,128]{2,1,0:T(8,128)(2,1)S(1)}, bf16[4,64,128]{2,1,0:T(8,128)(2,1)S(1)}, u32[]{:S(2)}, u32[]{:S(2)}) collective-permute-start(bf16[4,64,128]{2,1,0:T(8,128)(2,1)S(1)} %fusion.7), channel_id=1, source_target_pairs={{0,1},{1,0},{2,3},{3,2},{4,5},{5,4},{6,7},{7,6},{8,9},{9,8},{10,11... | collective-permute-start | bytes 196616 | tf_op jit(solution)/shard_map/ppermute | solution.py:22
  69.5 3.1 %base.9 = f32[256,512]{1,0:T(8,128)S(1)} custom-call(bf16[128,3584]{1,0:T(8,128)(2,1)S(1)} %collective-permute-done.1.refs_1_.refs_0_, bf16[128,3584]{1,0:T(8,128)(2,1)S(1)} %collective-permute-done.6.refs_2_.refs_1_, f32[512,2048]{1,0:T(8,128)} %base.7.refs_2_, bf16[7168,2048]{1,0:T(8,128)(2,1)} %refs_3_.11), custom_call_target="tpu_custom_call" | custom-call | flops 939524096 | bytes 6553600 | tf_op jit(solution)/shard_map/base/pallas_call | solution.py:117
  72.6 2.7 %collective-permute-start.13 = (bf16[4,64,128]{2,1,0:T(8,128)(2,1)S(1)}, bf16[4,64,128]{2,1,0:T(8,128)(2,1)S(1)}, u32[]{:S(2)}, u32[]{:S(2)}) collective-permute-start(bf16[4,64,128]{2,1,0:T(8,128)(2,1)S(1)} %get-tuple-element.147), channel_id=1, source_target_pairs={{0,2},{1,3},{2,0},{3,1},{4,6},{5,7},{6,4},{7,5},{8,10},{9,11},{10,... | collective-permute-start | bytes 196616 | tf_op jit(solution)/shard_map/ppermute | solution.py:22
  75.3 2.2 %constant_dynamic-slice_fusion.8 = (bf16[256,512]{1,0:T(8,128)(2,1)}, bf16[256,512]{1,0:T(8,128)(2,1)}, bf16[256,512]{1,0:T(8,128)(2,1)}, bf16[256,512]{1,0:T(8,128)(2,1)}) fusion(bf16[256,8192]{1,0:T(8,128)(2,1)} %refs_4_.5, s32[]{:T(128)S(6)} %select_n.108, s32[]{:T(128)S(6)} %select_n.107, s32[]{:T(128)S(6)} %select_n.106, s32[]{:T(128)S(6)} %select_n.105), kind=kLoop, calls=%fused_computation.40 | loop fusion | bytes 2097168 | tf_op jit(solution)/shard_map/dynamic_slice | solution.py:355
  80.5 3.4 %combine.4 = (f32[2,128,512]{2,1,0:T(8,128)S(1)}, bf16[2,128,512]{2,1,0:T(8,128)(2,1)}, bf16[512,1024]{1,0:T(8,128)(2,1)S(1)}) custom-call(s32[10]{0:T(128)S(1)} %stack.40.refs_0_, f32[4,64,128]{2,1,0:T(8,128)S(1)} %get-tuple-element.148.refs_1_, bf16[4,64,128]{2,1,0:T(8,128)(2,1)S(1)} %collective-permute-done.13.refs_2_, s32[4,128,128]{2,1,0:T(8,128)S(1)} %copy-done.5, ...), custom_call_target="tpu_custom_call" | custom-call | flops 536870 | bytes 2752 | tf_op jit(solution)/shard_map/combine/pallas_call | solution.py:319
  87.3 3.2 %base.10 = f32[256,512]{1,0:T(8,128)S(1)} custom-call(bf16[128,3584]{1,0:T(8,128)(2,1)S(1)} %collective-permute-done.1.refs_1_.refs_0_, bf16[128,3584]{1,0:T(8,128)(2,1)S(1)} %collective-permute-done.6.refs_2_.refs_1_, f32[512,2048]{1,0:T(8,128)} %base.7.refs_2_, bf16[7168,2048]{1,0:T(8,128)(2,1)} %refs_3_.11), custom_call_target="tpu_custom_call" | custom-call | flops 939524 | bytes 6553 | tf_op jit(solution)/shard_map/base/pallas_call | solution.py:117
  90.6 2.5 %combine.5 = (f32[2,128,512]{2,1,0:T(8,128)S(1)}, bf16[2,128,512]{2,1,0:T(8,128)(2,1)S(1)}) custom-call(s32[10]{0:T(128)S(1)} %stack.40.refs_0_, bf16[512,1024]{1,0:T(8,128)(2,1)S(1)} %copy-done.3, f32[4,128,2048]{2,1,0:T(8,128)} %bitcast.46, f32[2,128,512]{2,1,0:T(8,128)S(1)} %bitcast.39, bf16[256,8192]{1,0:T(8,128)(2,1)} %refs_4_.5, ...), custom_call_target="tpu_custom_call" | custom-call | flops 536870 | bytes 2752 | tf_op jit(solution)/shard_map/combine/pallas_call | solution.py:319
  93.1 1.7 %collective-permute-start.20 = (bf16[2,128,512]{2,1,0:T(8,128)(2,1)S(1)}, bf16[2,128,512]{2,1,0:T(8,128)(2,1)S(1)}, u32[]{:S(2)}, u32[]{:S(2)}) collective-permute-start(bf16[2,128,512]{2,1,0:T(8,128)(2,1)S(1)} %get-tuple-element.122), channel_id=1, source_target_pairs={{0,1},{1,0},{2,3},{3,2},{4,5},{5,4},{6,7},{7,6},{8,9},{9,8},{10,11... | collective-permute-start | bytes 786440 | tf_op jit(solution)/shard_map/ppermute | solution.py:22
  95.9 1.9 %collective-permute-start.19 = (bf16[128,512]{1,0:T(8,128)(2,1)S(1)}, bf16[128,512]{1,0:T(8,128)(2,1)S(1)}, u32[]{:S(2)}, u32[]{:S(2)}) collective-permute-start(bf16[128,512]{1,0:T(8,128)(2,1)S(1)} %fusion.3), channel_id=1, source_target_pairs={{0,2},{1,3},{2,0},{3,1},{4,6},{5,7},{6,4},{7,5},{8,10},{9,11},{10,... | collective-permute-start | bytes 393224 | tf_op jit(solution)/shard_map/ppermute | solution.py:22
  97.7 2.5 %combine.6 = (f32[2,128,512]{2,1,0:T(8,128)S(1)}, bf16[2,128,512]{2,1,0:T(8,128)(2,1)S(1)}) custom-call(s32[10]{0:T(128)S(1)} %stack.40.refs_0_, bf16[512,1024]{1,0:T(8,128)(2,1)S(1)} %copy-done.3, f32[4,128,2048]{2,1,0:T(8,128)} %bitcast.47, f32[2,128,512]{2,1,0:T(8,128)S(1)} %bitcast.42, bf16[256,8192]{1,0:T(8,128)(2,1)} %refs_4_.5, ...), custom_call_target="tpu_custom_call" | custom-call | flops 536870 | bytes 2752 | tf_op jit(solution)/shard_map/combine/pallas_call | solution.py:319
  100.3 2.0 %collective-permute-start.23 = (bf16[2,128,512]{2,1,0:T(8,128)(2,1)S(1)}, bf16[2,128,512]{2,1,0:T(8,128)(2,1)S(1)}, u32[]{:S(2)}, u32[]{:S(2)}) collective-permute-start(bf16[2,128,512]{2,1,0:T(8,128)(2,1)S(1)} %get-tuple-element.131), channel_id=1, source_target_pairs={{0,1},{1,0},{2,3},{3,2},{4,5},{5,4},{6,7},{7,6},{8,9},{9,8},{10,11... | collective-permute-start | bytes 786440 | tf_op jit(solution)/shard_map/ppermute | solution.py:22
  102.3 3.1 %base.11 = f32[256,512]{1,0:T(8,128)S(1)} custom-call(bf16[128,3584]{1,0:T(8,128)(2,1)S(1)} %collective-permute-done.1.refs_1_.refs_0_, bf16[128,3584]{1,0:T(8,128)(2,1)S(1)} %collective-permute-done.6.refs_2_.refs_1_, f32[512,2048]{1,0:T(8,128)} %base.7.refs_2_, bf16[7168,2048]{1,0:T(8,128)(2,1)} %refs_3_.11), custom_call_target="tpu_custom_call" | custom-call | flops 939524 | bytes 6553 | tf_op jit(solution)/shard_map/base/pallas_call | solution.py:117
  106.4 2.5 %combine.7 = (f32[2,128,512]{2,1,0:T(8,128)S(1)}, bf16[2,128,512]{2,1,0:T(8,128)(2,1)S(1)}) custom-call(s32[10]{0:T(128)S(1)} %stack.40.refs_0_, bf16[512,1024]{1,0:T(8,128)(2,1)S(1)} %copy-done.3, f32[4,128,2048]{2,1,0:T(8,128)} %bitcast.48, f32[2,128,512]{2,1,0:T(8,128)S(1)} %bitcast.41, bf16[256,8192]{1,0:T(8,128)(2,1)} %refs_4_.5, ...), custom_call_target="tpu_custom_call" | custom-call | flops 536870 | bytes 2752 | tf_op jit(solution)/shard_map/combine/pallas_call | solution.py:319
  108.8 2.5 %collective-permute-start.27 = (bf16[2,128,512]{2,1,0:T(8,128)(2,1)S(1)}, bf16[2,128,512]{2,1,0:T(8,128)(2,1)S(1)}, u32[]{:S(2)}, u32[]{:S(2)}) collective-permute-start(bf16[2,128,512]{2,1,0:T(8,128)(2,1)S(1)} %get-tuple-element.142), channel_id=1, source_target_pairs={{0,1},{1,0},{2,3},{3,2},{4,5},{5,4},{6,7},{7,6},{8,9},{9,8},{10,11... | collective-permute-start | bytes 786440 | tf_op jit(solution)/shard_map/ppermute | solution.py:22
  111.4 2.2 %collective-permute-done.23 = bf16[2,128,512]{2,1,0:T(8,128)(2,1)S(1)} collective-permute-done((bf16[2,128,512]{2,1,0:T(8,128)(2,1)S(1)}, bf16[2,128,512]{2,1,0:T(8,128)(2,1)S(1)}, u32[]{:S(2)}, u32[]{:S(2)}) %collective-permute-start.23) | collective-permute-done | bytes 262176 | tf_op jit(solution)/shard_map/ppermute | solution.py:22
  113.7 2.6 %collective-permute-start.26 = (bf16[128,512]{1,0:T(8,128)(2,1)S(1)}, bf16[128,512]{1,0:T(8,128)(2,1)S(1)}, u32[]{:S(2)}, u32[]{:S(2)}) collective-permute-start(bf16[128,512]{1,0:T(8,128)(2,1)S(1)} %fusion.5), channel_id=1, source_target_pairs={{0,2},{1,3},{2,0},{3,1},{4,6},{5,7},{6,4},{7,5},{8,10},{9,11},{10,... | collective-permute-start | bytes 393224 | tf_op jit(solution)/shard_map/ppermute | solution.py:22
  116.4 4.8 %collective-permute-done.27 = bf16[2,128,512]{2,1,0:T(8,128)(2,1)S(1)} collective-permute-done((bf16[2,128,512]{2,1,0:T(8,128)(2,1)S(1)}, bf16[2,128,512]{2,1,0:T(8,128)(2,1)S(1)}, u32[]{:S(2)}, u32[]{:S(2)}) %collective-permute-start.27) | collective-permute-done | bytes 262176 | tf_op jit(solution)/shard_map/ppermute | solution.py:22
  121.3 1.5 %collective-permute-start.28 = (bf16[128,512]{1,0:T(8,128)(2,1)S(1)}, bf16[128,512]{1,0:T(8,128)(2,1)S(1)}, u32[]{:S(2)}, u32[]{:S(2)}) collective-permute-start(bf16[128,512]{1,0:T(8,128)(2,1)S(1)} %fusion.6), channel_id=1, source_target_pairs={{0,2},{1,3},{2,0},{3,1},{4,6},{5,7},{6,4},{7,5},{8,10},{9,11},{10,... | collective-permute-start | bytes 393224 | tf_op jit(solution)/shard_map/ppermute | solution.py:22
  122.8 6.5 %collective-permute-done.28 = bf16[128,512]{1,0:T(8,128)(2,1)S(1)} collective-permute-done((bf16[128,512]{1,0:T(8,128)(2,1)S(1)}, bf16[128,512]{1,0:T(8,128)(2,1)S(1)}, u32[]{:S(2)}, u32[]{:S(2)}) %collective-permute-start.28) | collective-permute-done | bytes 131104 | tf_op jit(solution)/shard_map/ppermute | solution.py:22
  (93 shorter events, 22.4 us)
Async XLA Ops:
  0.0 13.5 %collective-permute-start = (bf16[128,7168]{1,0:T(8,128)(2,1)}, bf16[128,7168]{1,0:T(8,128)(2,1)}, u32[]{:S(2)}, u32[]{:S(2)}) collective-permute-start(bf16[128,7168]{1,0:T(8,128)(2,1)} %refs_0_.1), channel_id=1, source_target_pairs={{0,4},{4,0},{8,12},{12,8},{1,5},{5,1},{9,13},{13,9},{2,6},{6,2},{1... | collective-permute-start | bytes 5505032 | tf_op jit(solution)/shard_map/ppermute | solution.py:22
  2.0 12.4 %copy-start.1 = (bf16[128,7168]{1,0:T(8,128)(2,1)S(1)}, bf16[128,7168]{1,0:T(8,128)(2,1)}, u32[]{:S(2)}) copy-start(bf16[128,7168]{1,0:T(8,128)(2,1)} %refs_0_.1) | copy-start | bytes 5505028
  4.0 29.0 %collective-permute-start.2 = (bf16[128,1792]{1,0:T(8,128)(2,1)}, bf16[128,1792]{1,0:T(8,128)(2,1)S(1)}, u32[]{:S(2)}, u32[]{:S(2)}) collective-permute-start(bf16[128,1792]{1,0:T(8,128)(2,1)} %get-tuple-element.83), channel_id=1, source_target_pairs={{0,8},{4,12},{8,0},{12,4},{1,9},{5,13},{9,1},{13,5},{2,10},{6,14},... | collective-permute-start | bytes 1376264 | tf_op jit(solution)/shard_map/ppermute | solution.py:22
  6.5 26.5 %collective-permute-start.3 = (bf16[128,1792]{1,0:T(8,128)(2,1)}, bf16[128,1792]{1,0:T(8,128)(2,1)}, u32[]{:S(2)}, u32[]{:S(2)}) collective-permute-start(bf16[128,1792]{1,0:T(8,128)(2,1)} %get-tuple-element.84), channel_id=1, source_target_pairs={{0,8},{4,12},{8,0},{12,4},{1,9},{5,13},{9,1},{13,5},{2,10},{6,14},... | collective-permute-start | bytes 1376264 | tf_op jit(solution)/shard_map/ppermute | solution.py:22
  21.4 32.0 %collective-permute-start.1 = (bf16[128,3584]{1,0:T(8,128)(2,1)S(1)}, bf16[128,3584]{1,0:T(8,128)(2,1)S(1)}, u32[]{:S(2)}, u32[]{:S(2)}) collective-permute-start(bf16[128,3584]{1,0:T(8,128)(2,1)S(1)} %copy-done.7), channel_id=1, source_target_pairs={{0,8},{4,12},{8,0},{12,4},{1,9},{5,13},{9,1},{13,5},{2,10},{6,14},... | collective-permute-start | bytes 2752520 | tf_op jit(solution)/shard_map/ppermute | solution.py:22
  33.1 1.8 %collective-permute-start.4 = (bf16[128,1792]{1,0:T(8,128)(2,1)S(1)}, bf16[128,1792]{1,0:T(8,128)(2,1)S(1)}, u32[]{:S(2)}, u32[]{:S(2)}) collective-permute-start(bf16[128,1792]{1,0:T(8,128)(2,1)S(1)} %collective-permute-done.2.refs_1_.refs_2_), channel_id=1, source_target_pairs={{0,4},{4,0},{8,12},{12,8},{1,5},{5,1},{9,13},{13,9},{2,6},{6,2},{1... | collective-permute-start | bytes 1376264 | tf_op jit(solution)/shard_map/ppermute | solution.py:22
  33.1 2.7 %collective-permute-start.5 = (bf16[128,1792]{1,0:T(8,128)(2,1)}, bf16[128,1792]{1,0:T(8,128)(2,1)S(1)}, u32[]{:S(2)}, u32[]{:S(2)}) collective-permute-start(bf16[128,1792]{1,0:T(8,128)(2,1)} %collective-permute-done.3.refs_2_.refs_3_), channel_id=1, source_target_pairs={{0,4},{4,0},{8,12},{12,8},{1,5},{5,1},{9,13},{13,9},{2,6},{6,2},{1... | collective-permute-start | bytes 1376264 | tf_op jit(solution)/shard_map/ppermute | solution.py:22
  53.4 2.5 %collective-permute-start.6 = (bf16[128,3584]{1,0:T(8,128)(2,1)S(1)}, bf16[128,3584]{1,0:T(8,128)(2,1)S(1)}, u32[]{:S(2)}, u32[]{:S(2)}) collective-permute-start(bf16[128,3584]{1,0:T(8,128)(2,1)S(1)} %collective-permute-done.1.refs_1_.refs_0_), channel_id=1, source_target_pairs={{0,4},{4,0},{8,12},{12,8},{1,5},{5,1},{9,13},{13,9},{2,6},{6,2},{1... | collective-permute-start | bytes 2752520 | tf_op jit(solution)/shard_map/ppermute | solution.py:22
  53.5 9.0 %collective-permute-start.10 = (bf16[256,512]{1,0:T(8,128)(2,1)}, bf16[256,512]{1,0:T(8,128)(2,1)S(1)}, u32[]{:S(2)}, u32[]{:S(2)}) collective-permute-start(bf16[256,512]{1,0:T(8,128)(2,1)} %get-tuple-element.92), channel_id=1, source_target_pairs={{0,8},{4,12},{8,0},{12,4},{1,9},{5,13},{9,1},{13,5},{2,10},{6,14},... | collective-permute-start | bytes 786440 | tf_op jit(solution)/shard_map/ppermute | solution.py:22
  53.6 26.9 %collective-permute-start.15 = (bf16[256,2048]{1,0:T(8,128)(2,1)}, bf16[256,2048]{1,0:T(8,128)(2,1)}, u32[]{:S(2)}, u32[]{:S(2)}) collective-permute-start(bf16[256,2048]{1,0:T(8,128)(2,1)} %constant_dynamic-slice_fusion.7), channel_id=1, source_target_pairs={{0,4},{4,0},{8,12},{12,8},{1,5},{5,1},{9,13},{13,9},{2,6},{6,2},{1... | collective-permute-start | bytes 3145736 | tf_op jit(solution)/shard_map/ppermute | solution.py:22
  53.9 8.7 %copy-start.9 = (bf16[256,512]{1,0:T(8,128)(2,1)S(1)}, bf16[256,512]{1,0:T(8,128)(2,1)}, u32[]{:S(2)}) copy-start(bf16[256,512]{1,0:T(8,128)(2,1)} %get-tuple-element.100) | copy-start | bytes 786436
  60.4 5.3 %collective-permute-start.7 = (bf16[4,64,128]{2,1,0:T(8,128)(2,1)S(1)}, bf16[4,64,128]{2,1,0:T(8,128)(2,1)S(1)}, u32[]{:S(2)}, u32[]{:S(2)}) collective-permute-start(bf16[4,64,128]{2,1,0:T(8,128)(2,1)S(1)} %get-tuple-element.91), channel_id=1, source_target_pairs={{0,8},{4,12},{8,0},{12,4},{1,9},{5,13},{9,1},{13,5},{2,10},{6,14},... | collective-permute-start | bytes 196616 | tf_op jit(solution)/shard_map/ppermute | solution.py:22
  60.5 7.0 %collective-permute-start.8 = (bf16[4,64,128]{2,1,0:T(8,128)(2,1)S(1)}, bf16[4,64,128]{2,1,0:T(8,128)(2,1)S(1)}, u32[]{:S(2)}, u32[]{:S(2)}) collective-permute-start(bf16[4,64,128]{2,1,0:T(8,128)(2,1)S(1)} %get-tuple-element.91), channel_id=1, source_target_pairs={{0,12},{4,8},{8,4},{12,0},{1,13},{5,9},{9,5},{13,1},{2,14},{6,10},... | collective-permute-start | bytes 196616 | tf_op jit(solution)/shard_map/ppermute | solution.py:22
  61.9 5.6 %collective-permute-start.9 = (bf16[4,64,128]{2,1,0:T(8,128)(2,1)S(1)}, bf16[4,64,128]{2,1,0:T(8,128)(2,1)S(1)}, u32[]{:S(2)}, u32[]{:S(2)}) collective-permute-start(bf16[4,64,128]{2,1,0:T(8,128)(2,1)S(1)} %get-tuple-element.91), channel_id=1, source_target_pairs={{0,4},{4,0},{8,12},{12,8},{1,5},{5,1},{9,13},{13,9},{2,6},{6,2},{1... | collective-permute-start | bytes 196616 | tf_op jit(solution)/shard_map/ppermute | solution.py:22
  62.6 9.9 %collective-permute-start.12 = (bf16[256,512]{1,0:T(8,128)(2,1)S(1)}, bf16[256,512]{1,0:T(8,128)(2,1)S(1)}, u32[]{:S(2)}, u32[]{:S(2)}) collective-permute-start(bf16[256,512]{1,0:T(8,128)(2,1)S(1)} %copy-done.9), channel_id=1, source_target_pairs={{0,12},{4,8},{8,4},{12,0},{1,13},{5,9},{9,5},{13,1},{2,14},{6,10},... | collective-permute-start | bytes 786440 | tf_op jit(solution)/shard_map/ppermute | solution.py:22
  65.7 11.9 %collective-permute-start.14 = (bf16[256,512]{1,0:T(8,128)(2,1)S(1)}, bf16[256,512]{1,0:T(8,128)(2,1)S(1)}, u32[]{:S(2)}, u32[]{:S(2)}) collective-permute-start(bf16[256,512]{1,0:T(8,128)(2,1)S(1)} %copy-done.8), channel_id=1, source_target_pairs={{0,8},{4,12},{8,0},{12,4},{1,9},{5,13},{9,1},{13,5},{2,10},{6,14},... | collective-permute-start | bytes 786440 | tf_op jit(solution)/shard_map/ppermute | solution.py:22
  67.5 17.6 %collective-permute-start.18 = (bf16[256,512]{1,0:T(8,128)(2,1)}, bf16[256,512]{1,0:T(8,128)(2,1)}, u32[]{:S(2)}, u32[]{:S(2)}) collective-permute-start(bf16[256,512]{1,0:T(8,128)(2,1)} %get-tuple-element.120), channel_id=1, source_target_pairs={{0,12},{4,8},{8,4},{12,0},{1,13},{5,9},{9,5},{13,1},{2,14},{6,10},... | collective-permute-start | bytes 786440 | tf_op jit(solution)/shard_map/ppermute | solution.py:22
  67.6 12.9 %copy-start.5 = (s32[4,128,128]{2,1,0:T(8,128)S(1)}, s32[4,128,128]{2,1,0:T(8,128)}, u32[]{:S(2)}) copy-start(s32[4,128,128]{2,1,0:T(8,128)} %broadcast_in_dim.96.refs_3_) | copy-start | bytes 786436
  67.6 4.9 %collective-permute-start.11 = (bf16[4,64,128]{2,1,0:T(8,128)(2,1)S(1)}, bf16[4,64,128]{2,1,0:T(8,128)(2,1)S(1)}, u32[]{:S(2)}, u32[]{:S(2)}) collective-permute-start(bf16[4,64,128]{2,1,0:T(8,128)(2,1)S(1)} %fusion.7), channel_id=1, source_target_pairs={{0,1},{1,0},{2,3},{3,2},{4,5},{5,4},{6,7},{7,6},{8,9},{9,8},{10,11... | collective-permute-start | bytes 196616 | tf_op jit(solution)/shard_map/ppermute | solution.py:22
  72.6 6.4 %collective-permute-start.13 = (bf16[4,64,128]{2,1,0:T(8,128)(2,1)S(1)}, bf16[4,64,128]{2,1,0:T(8,128)(2,1)S(1)}, u32[]{:S(2)}, u32[]{:S(2)}) collective-permute-start(bf16[4,64,128]{2,1,0:T(8,128)(2,1)S(1)} %get-tuple-element.147), channel_id=1, source_target_pairs={{0,2},{1,3},{2,0},{3,1},{4,6},{5,7},{6,4},{7,5},{8,10},{9,11},{10,... | collective-permute-start | bytes 196616 | tf_op jit(solution)/shard_map/ppermute | solution.py:22
  79.0 11.5 %collective-permute-start.17 = (bf16[256,512]{1,0:T(8,128)(2,1)}, bf16[256,512]{1,0:T(8,128)(2,1)}, u32[]{:S(2)}, u32[]{:S(2)}) collective-permute-start(bf16[256,512]{1,0:T(8,128)(2,1)} %get-tuple-element.115), channel_id=1, source_target_pairs={{0,8},{4,12},{8,0},{12,4},{1,9},{5,13},{9,1},{13,5},{2,10},{6,14},... | collective-permute-start | bytes 786440 | tf_op jit(solution)/shard_map/ppermute | solution.py:22
  84.9 9.9 %collective-permute-start.16 = (bf16[2,128,512]{2,1,0:T(8,128)(2,1)}, bf16[2,128,512]{2,1,0:T(8,128)(2,1)}, u32[]{:S(2)}, u32[]{:S(2)}) collective-permute-start(bf16[2,128,512]{2,1,0:T(8,128)(2,1)} %get-tuple-element.112), channel_id=1, source_target_pairs={{0,1},{1,0},{2,3},{3,2},{4,5},{5,4},{6,7},{7,6},{8,9},{9,8},{10,11... | collective-permute-start | bytes 786440 | tf_op jit(solution)/shard_map/ppermute | solution.py:22
  85.0 12.7 %collective-permute-start.21 = (bf16[256,512]{1,0:T(8,128)(2,1)}, bf16[256,512]{1,0:T(8,128)(2,1)S(1)}, u32[]{:S(2)}, u32[]{:S(2)}) collective-permute-start(bf16[256,512]{1,0:T(8,128)(2,1)} %get-tuple-element.129), channel_id=1, source_target_pairs={{0,12},{4,8},{8,4},{12,0},{1,13},{5,9},{9,5},{13,1},{2,14},{6,10},... | collective-permute-start | bytes 786440 | tf_op jit(solution)/shard_map/ppermute | solution.py:22
  85.0 21.3 %collective-permute-start.24 = (bf16[256,512]{1,0:T(8,128)(2,1)}, bf16[256,512]{1,0:T(8,128)(2,1)S(1)}, u32[]{:S(2)}, u32[]{:S(2)}) collective-permute-start(bf16[256,512]{1,0:T(8,128)(2,1)} %get-tuple-element.137), channel_id=1, source_target_pairs={{0,8},{4,12},{8,0},{12,4},{1,9},{5,13},{9,1},{13,5},{2,10},{6,14},... | collective-permute-start | bytes 786440 | tf_op jit(solution)/shard_map/ppermute | solution.py:22
  86.2 20.2 %collective-permute-start.25 = (bf16[256,512]{1,0:T(8,128)(2,1)}, bf16[256,512]{1,0:T(8,128)(2,1)S(1)}, u32[]{:S(2)}, u32[]{:S(2)}) collective-permute-start(bf16[256,512]{1,0:T(8,128)(2,1)} %get-tuple-element.140), channel_id=1, source_target_pairs={{0,12},{4,8},{8,4},{12,0},{1,13},{5,9},{9,5},{13,1},{2,14},{6,10},... | collective-permute-start | bytes 786440 | tf_op jit(solution)/shard_map/ppermute | solution.py:22
  93.1 12.3 %collective-permute-start.20 = (bf16[2,128,512]{2,1,0:T(8,128)(2,1)S(1)}, bf16[2,128,512]{2,1,0:T(8,128)(2,1)S(1)}, u32[]{:S(2)}, u32[]{:S(2)}) collective-permute-start(bf16[2,128,512]{2,1,0:T(8,128)(2,1)S(1)} %get-tuple-element.122), channel_id=1, source_target_pairs={{0,1},{1,0},{2,3},{3,2},{4,5},{5,4},{6,7},{7,6},{8,9},{9,8},{10,11... | collective-permute-start | bytes 786440 | tf_op jit(solution)/shard_map/ppermute | solution.py:22
  95.9 10.4 %collective-permute-start.19 = (bf16[128,512]{1,0:T(8,128)(2,1)S(1)}, bf16[128,512]{1,0:T(8,128)(2,1)S(1)}, u32[]{:S(2)}, u32[]{:S(2)}) collective-permute-start(bf16[128,512]{1,0:T(8,128)(2,1)S(1)} %fusion.3), channel_id=1, source_target_pairs={{0,2},{1,3},{2,0},{3,1},{4,6},{5,7},{6,4},{7,5},{8,10},{9,11},{10,... | collective-permute-start | bytes 393224 | tf_op jit(solution)/shard_map/ppermute | solution.py:22
  100.3 13.3 %collective-permute-start.23 = (bf16[2,128,512]{2,1,0:T(8,128)(2,1)S(1)}, bf16[2,128,512]{2,1,0:T(8,128)(2,1)S(1)}, u32[]{:S(2)}, u32[]{:S(2)}) collective-permute-start(bf16[2,128,512]{2,1,0:T(8,128)(2,1)S(1)} %get-tuple-element.131), channel_id=1, source_target_pairs={{0,1},{1,0},{2,3},{3,2},{4,5},{5,4},{6,7},{7,6},{8,9},{9,8},{10,11... | collective-permute-start | bytes 786440 | tf_op jit(solution)/shard_map/ppermute | solution.py:22
  105.5 8.0 %collective-permute-start.22 = (bf16[128,512]{1,0:T(8,128)(2,1)S(1)}, bf16[128,512]{1,0:T(8,128)(2,1)S(1)}, u32[]{:S(2)}, u32[]{:S(2)}) collective-permute-start(bf16[128,512]{1,0:T(8,128)(2,1)S(1)} %fusion.4), channel_id=1, source_target_pairs={{0,2},{1,3},{2,0},{3,1},{4,6},{5,7},{6,4},{7,5},{8,10},{9,11},{10,... | collective-permute-start | bytes 393224 | tf_op jit(solution)/shard_map/ppermute | solution.py:22
  108.8 12.3 %collective-permute-start.27 = (bf16[2,128,512]{2,1,0:T(8,128)(2,1)S(1)}, bf16[2,128,512]{2,1,0:T(8,128)(2,1)S(1)}, u32[]{:S(2)}, u32[]{:S(2)}) collective-permute-start(bf16[2,128,512]{2,1,0:T(8,128)(2,1)S(1)} %get-tuple-element.142), channel_id=1, source_target_pairs={{0,1},{1,0},{2,3},{3,2},{4,5},{5,4},{6,7},{7,6},{8,9},{9,8},{10,11... | collective-permute-start | bytes 786440 | tf_op jit(solution)/shard_map/ppermute | solution.py:22
  113.7 9.0 %collective-permute-start.26 = (bf16[128,512]{1,0:T(8,128)(2,1)S(1)}, bf16[128,512]{1,0:T(8,128)(2,1)S(1)}, u32[]{:S(2)}, u32[]{:S(2)}) collective-permute-start(bf16[128,512]{1,0:T(8,128)(2,1)S(1)} %fusion.5), channel_id=1, source_target_pairs={{0,2},{1,3},{2,0},{3,1},{4,6},{5,7},{6,4},{7,5},{8,10},{9,11},{10,... | collective-permute-start | bytes 393224 | tf_op jit(solution)/shard_map/ppermute | solution.py:22
  121.3 8.0 %collective-permute-start.28 = (bf16[128,512]{1,0:T(8,128)(2,1)S(1)}, bf16[128,512]{1,0:T(8,128)(2,1)S(1)}, u32[]{:S(2)}, u32[]{:S(2)}) collective-permute-start(bf16[128,512]{1,0:T(8,128)(2,1)S(1)} %fusion.6), channel_id=1, source_target_pairs={{0,2},{1,3},{2,0},{3,1},{4,6},{5,7},{6,4},{7,5},{8,10},{9,11},{10,... | collective-permute-start | bytes 393224 | tf_op jit(solution)/shard_map/ppermute | solution.py:22
  (7 other events, 22.8 us)

commit v11 on v10

--- a/solution.py
+++ b/solution.py
@@ -349,14 +349,11 @@
     *early, late = cut_columns(hidden, (part // 2, part // 2, part))
     first_a, first_b = (swap(block, "pool", 2) for block in early)
 
-    core_block = lax.dynamic_slice(output_maps, (0, (place ^ 1) * width), (held, width))
 
     def block_for(index, other, source):
         return lax.dynamic_slice(
             source, (0, (place ^ other) * width + starts[index]), (held, WIDTHS[index])
         )
-
-    blocks = [block_for(index, other, output_maps) for index in range(2) for other in (2, 3)]
 
     order = place ^ jnp.arange(4, dtype=jnp.int32)
     hot = order[:, None] == jnp.arange(4, dtype=jnp.int32)[None, :]
@@ -366,7 +363,6 @@
     ids = jnp.sum(
         jnp.where(slots_local[:, :, None] == positions, lists_local[:, None, :], 0), axis=2
     )
-    wide_ids = jnp.broadcast_to(ids[:, :, None], (4, rows, 128))
     owned_ids = (ids - place * holding).reshape(4, 1, rows)
     owned = (lists_local >= place * holding) & (lists_local < (place + 1) * holding)
     earlier = positions[None, :] < positions[:, None]
@@ -391,11 +387,9 @@
         + [owner_first[j] + half_step * h for j in range(4) for h in range(2)]
     ).astype(jnp.int32)
 
-    ready = lax.optimization_barrier(
-        (hidden, near_b, picks, info, wide_ids, owned_ids, core_block, *blocks)
-    )
-    own_rows, near_b, picks, info, wide_ids, owned_ids, core_block, *blocks = ready
-    core_maps = swap(core_block, "pool", 1)
+    own_rows, near_b, picks, info, ids, owned_ids = lax.optimization_barrier(
+        (hidden, near_b, picks, info, ids, owned_ids)
+    )
 
     (near_lowrank,) = scores(picks, 0, [own_rows], [near_b], input_maps, 0, ids=owned_ids)
     second = swap(tie(late, near_lowrank), "pool", 2)
@@ -407,6 +401,12 @@
     first_a, first_b = lax.optimization_barrier((first_a, first_b, near_late))[:2]
     a0 = [first_a, first_b]
     b0 = [swap(x, "pool", 1) for x in a0]
+    source, kept_ids, _ = lax.optimization_barrier((output_maps, ids, first_a))
+    blocks = [block_for(index, other, source) for index in range(2) for other in (2, 3)]
+    wide_ids = jnp.broadcast_to(kept_ids[:, :, None], (4, rows, 128))
+    *b0, wide_ids, blocks[0], blocks[1], blocks[2], blocks[3] = lax.optimization_barrier(
+        (*b0, wide_ids, *blocks)
+    )
     (raw,) = scores(picks, 2, a0, b0, input_maps, 0)
     base = product(
         [
@@ -419,6 +419,11 @@
     )
     a1 = tie(second, base)
     b1 = swap(a1, "pool", 1)
+    core_block = lax.dynamic_slice(
+        tie(output_maps, a1), (0, (place ^ 1) * width), (held, width)
+    )
+    b1, core_block = lax.optimization_barrier((b1, core_block))
+    core_maps = swap(core_block, "pool", 1)
     total, sent = scores(
         picks, 2, [a1], [b1], input_maps, 1, prior=raw, near=near_lowrank, ids=owned_ids
     )
@@ -468,6 +473,8 @@
         if index == 1:
             moved[2][0] = tie(moved[2][0], send)
             return tie(near_base, moved[2][0])
+        if index == 3:
+            return lax.optimization_barrier((near_base, started[1], parts[0]))[0]
         return near_base if index < 2 else tie(near_base, started[index - 2])
 
     started = []

time: 131 us -> 134 us (1.023)
  starting transfers between devices: 31.5 us -> 24.6 us
  waiting for transfers between devices: 19.1 us -> 24.9 us
  local copies, waits for them, and re-layouts: 12.7 us -> 16.8 us
    ppermute x29, starting transfers between devices: 31.5 us -> 24.6 us  [swap(): return lax.ppermute(values, axis, partners(lax.axis_size(axis), step))]
    ppermute x29, waiting for transfers between devices: 19.1 us -> 24.9 us  [swap(): return lax.ppermute(values, axis, partners(lax.axis_size(axis), step))]
    unnamed x20 -> x34, local copies, waits for them, and re-layouts: 4.82 us -> 9.08 us
  transfers between devices with their start and end apart: 29 -> 29, of which waited for: 8 -> 9; matrix products, arithmetic and copies ran while one was open for 9% -> 9% of each run, Pallas kernels for 48% -> 46%
where the time goes in v11:
time: 134 us; the launch traced here: 133 us
  Pallas kernels  61.9 us (46%)
  waiting for transfers between devices  24.9 us (19%)
  starting transfers between devices  24.6 us (18%)
  local copies, waits for them, and re-layouts  16.8 us (13%)
  other arithmetic  4.63 us (3%)
    pallas_call x6, Pallas kernels, product(): pl.pallas_call(lambda *refs: product_kernel(counts, prior is not None, *r...  33.2 us
    ppermute x29, waiting for transfers between devices, swap(): return lax.ppermute(values, axis, partners(lax.axis_size(axis), step))  24.9 us
    ppermute x29, starting transfers between devices, swap(): return lax.ppermute(values, axis, partners(lax.axis_size(axis), step))  24.6 us
    pallas_call x3, Pallas kernels, scores(): pl.pallas_call(lambda *refs: scores_kernel(first, half * depth, len(lower...  16.8 us
    pallas_call x4, Pallas kernels, combine(): pl.pallas_call(lambda *refs: combine_kernel(bool(build), *refs), grid_spe...  10.5 us
    unnamed x34, local copies, waits for them, and re-layouts  9.08 us
    dynamic_slice x2, local copies, waits for them, and re-layouts, block_for(): lax.dynamic_slice(source, (0, (place ^ other) * width + starts[index]), (...  4.36 us
  transfers between devices with their start and end apart: 29, of which 9 were waited for; matrix products, arithmetic and copies ran while one was open for 9% of the time, Pallas kernels for 46%

profile of v11, /device:TPU:0, one launch (start us, length us, event | category | flops | bytes accessed | tf_op | source)
XLA Modules:
  0.0 133.2 jit_solution(16569192720565184832)
XLA Ops:
  0.5 1.5 %copy-done = bf16[128,7168]{1,0:T(8,128)(2,1)S(1)} copy-done((bf16[128,7168]{1,0:T(8,128)(2,1)S(1)}, bf16[128,7168]{1,0:T(8,128)(2,1)}, u32[]{:S(2)}) %copy-start) | copy-done | bytes 1835032
  2.0 1.4 %cut.1 = (bf16[128,1792]{1,0:T(8,128)(2,1)}, bf16[128,1792]{1,0:T(8,128)(2,1)}, bf16[128,3584]{1,0:T(8,128)(2,1)}) custom-call(bf16[128,7168]{1,0:T(8,128)(2,1)S(1)} %copy-done), custom_call_target="tpu_custom_call" | custom-call | bytes 3670 | tf_op jit(solution)/shard_map/cut/pallas_call | solution.py:57
  3.4 2.6 %collective-permute-start.2 = (bf16[128,1792]{1,0:T(8,128)(2,1)}, bf16[128,1792]{1,0:T(8,128)(2,1)S(1)}, u32[]{:S(2)}, u32[]{:S(2)}) collective-permute-start(bf16[128,1792]{1,0:T(8,128)(2,1)} %get-tuple-element.90), channel_id=1, source_target_pairs={{0,8},{4,12},{8,0},{12,4},{1,9},{5,13},{9,1},{13,5},{2,10},{6,14},... | collective-permute-start | bytes 1376264 | tf_op jit(solution)/shard_map/ppermute | solution.py:22
  8.4 1.5 %copy-done.1 = bf16[128,7168]{1,0:T(8,128)(2,1)S(1)} copy-done((bf16[128,7168]{1,0:T(8,128)(2,1)S(1)}, bf16[128,7168]{1,0:T(8,128)(2,1)}, u32[]{:S(2)}) %copy-start.1) | copy-done | bytes 1835032
  9.9 7.1 %scores.3.refs_5_ = f32[2,64,128]{2,1,0:T(8,128)S(1)} custom-call(s32[17]{0:T(128)S(1)} %pad_add_fusion.refs_0_, bf16[128,7168]{1,0:T(8,128)(2,1)S(1)} %copy-done.1, bf16[128,7168]{1,0:T(8,128)(2,1)S(1)} %collective-permute-done.refs_2_.refs_1_, bf16[16,64,7168]{2,1,0:T(8,128)(2,1)} %refs_3_.7, s32[4,1,128]{2,1,0:T(1,128)S(1)} %bitcast.41), custom_call_target="tpu_custom_call" | custom-call | flops 939524 | bytes 11010 | tf_op jit(solution)/shard_map/scores/pallas_call | solution.py:231
  17.0 2.0 %collective-permute-start.1 = (bf16[128,3584]{1,0:T(8,128)(2,1)}, bf16[128,3584]{1,0:T(8,128)(2,1)S(1)}, u32[]{:S(2)}, u32[]{:S(2)}) collective-permute-start(bf16[128,3584]{1,0:T(8,128)(2,1)} %get-tuple-element.89), channel_id=1, source_target_pairs={{0,8},{4,12},{8,0},{12,4},{1,9},{5,13},{9,1},{13,5},{2,10},{6,14},... | collective-permute-start | bytes 2752520 | tf_op jit(solution)/shard_map/ppermute | solution.py:22
  19.0 7.9 %base.6.refs_6_ = f32[256,2048]{1,0:T(8,128)S(1)} custom-call(bf16[128,7168]{1,0:T(8,128)(2,1)S(1)} %copy-done.1, bf16[128,7168]{1,0:T(8,128)(2,1)S(1)} %collective-permute-done.refs_2_.refs_1_, bf16[7168,2048]{1,0:T(8,128)(2,1)} %refs_3_.11), custom_call_target="tpu_custom_call" | custom-call | flops 3758096 | bytes 20709 | tf_op jit(solution)/shard_map/base/pallas_call | solution.py:117
  28.8 2.2 %constant_dynamic-slice_fusion.4 = (bf16[256,512]{1,0:T(8,128)(2,1)}, bf16[256,512]{1,0:T(8,128)(2,1)}, bf16[256,512]{1,0:T(8,128)(2,1)}, bf16[256,512]{1,0:T(8,128)(2,1)}) fusion(bf16[256,8192]{1,0:T(8,128)(2,1)} %refs_4_.5, s32[]{:T(128)S(6)} %select_n.103, s32[]{:T(128)S(6)} %select_n.102, s32[]{:T(128)S(6)} %select_n.101, s32[]{:T(128)S(6)} %select_n.100), kind=kLoop, calls=%fused_computation.35 | loop fusion | bytes 2097168 | tf_op jit(solution)/shard_map/dynamic_slice | solution.py:354
  31.8 5.2 %scores.4.refs_4_ = f32[2,256,128]{2,1,0:T(8,128)S(1)} custom-call(s32[17]{0:T(128)S(1)} %pad_add_fusion.refs_0_, bf16[128,1792]{1,0:T(8,128)(2,1)S(1)} %collective-permute-done.2.refs_1_.refs_2_, bf16[128,1792]{1,0:T(8,128)(2,1)} %collective-permute-done.3.refs_2_.refs_3_, bf16[128,1792]{1,0:T(8,128)(2,1)} %collective-permute-done.4.refs_3_.refs_4_, ...), custom_call_target="tpu_custom_call" | custom-call | flops 469762 | bytes 5505 | tf_op jit(solution)/shard_map/scores/pallas_call | solution.py:231
  37.0 12.8 %base.7.refs_2_ = f32[512,2048]{1,0:T(8,128)} custom-call(bf16[128,7168]{1,0:T(8,128)(2,1)S(1)} %copy-done.2, bf16[128,7168]{1,0:T(8,128)(2,1)S(1)} %collective-permute-done.refs_2_.refs_1_, bf16[128,1792]{1,0:T(8,128)(2,1)S(1)} %collective-permute-done.2.refs_1_.refs_2_, bf16[128,1792]{1,0:T(8,128)(2,1)} %collective-permute-done.3.refs_2_.refs_3_, ...), custom_call_target="tpu_custom_call" | custom-call | flops 7516192 | bytes 26738 | tf_op jit(solution)/shard_map/base/pallas_call | solution.py:117
  51.2 2.3 %constant_dynamic-slice_fusion.3 = bf16[256,2048]{1,0:T(8,128)(2,1)} fusion(bf16[256,8192]{1,0:T(8,128)(2,1)} %refs_4_.5, s32[]{:T(128)S(6)} %select_n.104), kind=kLoop, calls=%fused_computation.34 | loop fusion | bytes 2097156 | tf_op jit(solution)/shard_map/dynamic_slice | solution.py:422
  53.7 4.5 %scores.5 = (f32[4,64,128]{2,1,0:T(8,128)S(1)}, bf16[4,64,128]{2,1,0:T(8,128)(2,1)S(1)}) custom-call(s32[17]{0:T(128)S(1)} %pad_add_fusion.refs_0_, bf16[128,3584]{1,0:T(8,128)(2,1)S(1)} %collective-permute-done.1.refs_1_.refs_0_, bf16[128,3584]{1,0:T(8,128)(2,1)S(1)} %collective-permute-done.6.refs_2_.refs_1_, bf16[16,64,7168]{2,1,0:T(8,128)(2,1)} %refs_3_.7, ...), custom_call_target="tpu_custom_call" | custom-call | flops 469762 | bytes 5505 | tf_op jit(solution)/shard_map/scores/pallas_call | solution.py:231
  61.0 3.1 %base.8 = f32[256,512]{1,0:T(8,128)S(1)} custom-call(bf16[128,3584]{1,0:T(8,128)(2,1)S(1)} %collective-permute-done.1.refs_1_.refs_0_, bf16[128,3584]{1,0:T(8,128)(2,1)S(1)} %collective-permute-done.6.refs_2_.refs_1_, f32[512,2048]{1,0:T(8,128)} %base.7.refs_2_, bf16[7168,2048]{1,0:T(8,128)(2,1)} %refs_3_.11), custom_call_target="tpu_custom_call" | custom-call | flops 939524096 | bytes 6553600 | tf_op jit(solution)/shard_map/base/pallas_call | solution.py:117
  66.0 1.6 %collective-permute-start.11 = (bf16[4,64,128]{2,1,0:T(8,128)(2,1)S(1)}, bf16[4,64,128]{2,1,0:T(8,128)(2,1)S(1)}, u32[]{:S(2)}, u32[]{:S(2)}) collective-permute-start(bf16[4,64,128]{2,1,0:T(8,128)(2,1)S(1)} %fusion.6), channel_id=1, source_target_pairs={{0,1},{1,0},{2,3},{3,2},{4,5},{5,4},{6,7},{7,6},{8,9},{9,8},{10,11... | collective-permute-start | bytes 196616 | tf_op jit(solution)/shard_map/ppermute | solution.py:22
  67.6 3.1 %base.9 = f32[256,512]{1,0:T(8,128)S(1)} custom-call(bf16[128,3584]{1,0:T(8,128)(2,1)S(1)} %collective-permute-done.1.refs_1_.refs_0_, bf16[128,3584]{1,0:T(8,128)(2,1)S(1)} %collective-permute-done.6.refs_2_.refs_1_, f32[512,2048]{1,0:T(8,128)} %base.7.refs_2_, bf16[7168,2048]{1,0:T(8,128)(2,1)} %refs_3_.11), custom_call_target="tpu_custom_call" | custom-call | flops 939524096 | bytes 6553600 | tf_op jit(solution)/shard_map/base/pallas_call | solution.py:117
  70.8 2.7 %collective-permute-start.13 = (bf16[4,64,128]{2,1,0:T(8,128)(2,1)S(1)}, bf16[4,64,128]{2,1,0:T(8,128)(2,1)S(1)}, u32[]{:S(2)}, u32[]{:S(2)}) collective-permute-start(bf16[4,64,128]{2,1,0:T(8,128)(2,1)S(1)} %get-tuple-element.161), channel_id=1, source_target_pairs={{0,2},{1,3},{2,0},{3,1},{4,6},{5,7},{6,4},{7,5},{8,10},{9,11},{10,... | collective-permute-start | bytes 196616 | tf_op jit(solution)/shard_map/ppermute | solution.py:22
  73.4 2.2 %constant_dynamic-slice_fusion.8 = (bf16[256,512]{1,0:T(8,128)(2,1)}, bf16[256,512]{1,0:T(8,128)(2,1)}, bf16[256,512]{1,0:T(8,128)(2,1)}, bf16[256,512]{1,0:T(8,128)(2,1)}) fusion(bf16[256,8192]{1,0:T(8,128)(2,1)} %refs_4_.5, s32[]{:T(128)S(6)} %select_n.108, s32[]{:T(128)S(6)} %select_n.107, s32[]{:T(128)S(6)} %select_n.106, s32[]{:T(128)S(6)} %select_n.105), kind=kLoop, calls=%fused_computation.39 | loop fusion | bytes 2097168 | tf_op jit(solution)/shard_map/dynamic_slice | solution.py:354
  75.6 1.6 %collective-permute-done.13.refs_2_ = bf16[4,64,128]{2,1,0:T(8,128)(2,1)S(1)} collective-permute-done((bf16[4,64,128]{2,1,0:T(8,128)(2,1)S(1)}, bf16[4,64,128]{2,1,0:T(8,128)(2,1)S(1)}, u32[]{:S(2)}, u32[]{:S(2)}) %collective-permute-start.13) | collective-permute-done | bytes 65568 | tf_op jit(solution)/shard_map/ppermute | solution.py:22
  79.2 3.3 %combine.4 = (f32[2,128,512]{2,1,0:T(8,128)S(1)}, bf16[2,128,512]{2,1,0:T(8,128)(2,1)}, bf16[512,1024]{1,0:T(8,128)(2,1)S(1)}) custom-call(s32[10]{0:T(128)S(1)} %stack.40.refs_0_, f32[4,64,128]{2,1,0:T(8,128)S(1)} %get-tuple-element.162.refs_1_, bf16[4,64,128]{2,1,0:T(8,128)(2,1)S(1)} %collective-permute-done.13.refs_2_, s32[4,128,128]{2,1,0:T(8,128)S(1)} %copy-done.6, ...), custom_call_target="tpu_custom_call" | custom-call | flops 536870 | bytes 2752 | tf_op jit(solution)/shard_map/combine/pallas_call | solution.py:319
  84.4 2.6 %collective-permute-done.17.refs_6_ = bf16[256,512]{1,0:T(8,128)(2,1)} collective-permute-done((bf16[256,512]{1,0:T(8,128)(2,1)}, bf16[256,512]{1,0:T(8,128)(2,1)}, u32[]{:S(2)}, u32[]{:S(2)}) %collective-permute-start.17) | collective-permute-done | bytes 262176 | tf_op jit(solution)/shard_map/ppermute | solution.py:22
  89.2 2.4 %combine.5 = (f32[2,128,512]{2,1,0:T(8,128)S(1)}, bf16[2,128,512]{2,1,0:T(8,128)(2,1)S(1)}) custom-call(s32[10]{0:T(128)S(1)} %stack.40.refs_0_, bf16[512,1024]{1,0:T(8,128)(2,1)S(1)} %copy-done.4, f32[4,128,2048]{2,1,0:T(8,128)} %bitcast.44, f32[2,128,512]{2,1,0:T(8,128)S(1)} %bitcast.37, bf16[256,8192]{1,0:T(8,128)(2,1)} %refs_4_.5, ...), custom_call_target="tpu_custom_call" | custom-call | flops 536870 | bytes 2752 | tf_op jit(solution)/shard_map/combine/pallas_call | solution.py:319
  91.7 1.6 %collective-permute-start.20 = (bf16[2,128,512]{2,1,0:T(8,128)(2,1)S(1)}, bf16[2,128,512]{2,1,0:T(8,128)(2,1)S(1)}, u32[]{:S(2)}, u32[]{:S(2)}) collective-permute-start(bf16[2,128,512]{2,1,0:T(8,128)(2,1)S(1)} %get-tuple-element.136), channel_id=1, source_target_pairs={{0,1},{1,0},{2,3},{3,2},{4,5},{5,4},{6,7},{7,6},{8,9},{9,8},{10,11... | collective-permute-start | bytes 786440 | tf_op jit(solution)/shard_map/ppermute | solution.py:22
  94.3 3.2 %base.10 = f32[256,512]{1,0:T(8,128)S(1)} custom-call(bf16[128,3584]{1,0:T(8,128)(2,1)S(1)} %collective-permute-done.1.refs_1_.refs_0_, bf16[128,3584]{1,0:T(8,128)(2,1)S(1)} %collective-permute-done.6.refs_2_.refs_1_, f32[512,2048]{1,0:T(8,128)} %base.7.refs_2_, bf16[7168,2048]{1,0:T(8,128)(2,1)} %refs_3_.11), custom_call_target="tpu_custom_call" | custom-call | flops 939524 | bytes 6553 | tf_op jit(solution)/shard_map/base/pallas_call | solution.py:117
  98.6 2.7 %collective-permute-start.19 = (bf16[128,512]{1,0:T(8,128)(2,1)S(1)}, bf16[128,512]{1,0:T(8,128)(2,1)S(1)}, u32[]{:S(2)}, u32[]{:S(2)}) collective-permute-start(bf16[128,512]{1,0:T(8,128)(2,1)S(1)} %fusion.2), channel_id=1, source_target_pairs={{0,2},{1,3},{2,0},{3,1},{4,6},{5,7},{6,4},{7,5},{8,10},{9,11},{10,... | collective-permute-start | bytes 393224 | tf_op jit(solution)/shard_map/ppermute | solution.py:22
  101.3 2.4 %combine.6 = (f32[2,128,512]{2,1,0:T(8,128)S(1)}, bf16[2,128,512]{2,1,0:T(8,128)(2,1)S(1)}) custom-call(s32[10]{0:T(128)S(1)} %stack.40.refs_0_, bf16[512,1024]{1,0:T(8,128)(2,1)S(1)} %copy-done.4, f32[4,128,2048]{2,1,0:T(8,128)} %bitcast.45, f32[2,128,512]{2,1,0:T(8,128)S(1)} %bitcast.39, bf16[256,8192]{1,0:T(8,128)(2,1)} %refs_4_.5, ...), custom_call_target="tpu_custom_call" | custom-call | flops 536870 | bytes 2752 | tf_op jit(solution)/shard_map/combine/pallas_call | solution.py:319
  105.3 3.1 %base.11 = f32[256,512]{1,0:T(8,128)S(1)} custom-call(bf16[128,3584]{1,0:T(8,128)(2,1)S(1)} %collective-permute-done.1.refs_1_.refs_0_, bf16[128,3584]{1,0:T(8,128)(2,1)S(1)} %collective-permute-done.6.refs_2_.refs_1_, f32[512,2048]{1,0:T(8,128)} %base.7.refs_2_, bf16[7168,2048]{1,0:T(8,128)(2,1)} %refs_3_.11), custom_call_target="tpu_custom_call" | custom-call | flops 939524 | bytes 6553 | tf_op jit(solution)/shard_map/base/pallas_call | solution.py:117
  108.8 2.4 %combine.7 = (f32[2,128,512]{2,1,0:T(8,128)S(1)}, bf16[2,128,512]{2,1,0:T(8,128)(2,1)S(1)}) custom-call(s32[10]{0:T(128)S(1)} %stack.40.refs_0_, bf16[512,1024]{1,0:T(8,128)(2,1)S(1)} %copy-done.4, f32[4,128,2048]{2,1,0:T(8,128)} %bitcast.46, f32[2,128,512]{2,1,0:T(8,128)S(1)} %bitcast.40, bf16[256,8192]{1,0:T(8,128)(2,1)} %refs_4_.5, ...), custom_call_target="tpu_custom_call" | custom-call | flops 536870 | bytes 2752 | tf_op jit(solution)/shard_map/combine/pallas_call | solution.py:319
  111.9 1.8 %collective-permute-done.22 = bf16[128,512]{1,0:T(8,128)(2,1)S(1)} collective-permute-done((bf16[128,512]{1,0:T(8,128)(2,1)S(1)}, bf16[128,512]{1,0:T(8,128)(2,1)S(1)}, u32[]{:S(2)}, u32[]{:S(2)}) %collective-permute-start.22) | collective-permute-done | bytes 131104 | tf_op jit(solution)/shard_map/ppermute | solution.py:22
  113.8 3.3 %collective-permute-done.23 = bf16[2,128,512]{2,1,0:T(8,128)(2,1)S(1)} collective-permute-done((bf16[2,128,512]{2,1,0:T(8,128)(2,1)S(1)}, bf16[2,128,512]{2,1,0:T(8,128)(2,1)S(1)}, u32[]{:S(2)}, u32[]{:S(2)}) %collective-permute-start.23) | collective-permute-done | bytes 262176 | tf_op jit(solution)/shard_map/ppermute | solution.py:22
  117.4 6.5 %collective-permute-done.27 = bf16[2,128,512]{2,1,0:T(8,128)(2,1)S(1)} collective-permute-done((bf16[2,128,512]{2,1,0:T(8,128)(2,1)S(1)}, bf16[2,128,512]{2,1,0:T(8,128)(2,1)S(1)}, u32[]{:S(2)}, u32[]{:S(2)}) %collective-permute-start.27) | collective-permute-done | bytes 262176 | tf_op jit(solution)/shard_map/ppermute | solution.py:22
  124.1 2.4 %collective-permute-done.26 = bf16[128,512]{1,0:T(8,128)(2,1)S(1)} collective-permute-done((bf16[128,512]{1,0:T(8,128)(2,1)S(1)}, bf16[128,512]{1,0:T(8,128)(2,1)S(1)}, u32[]{:S(2)}, u32[]{:S(2)}) %collective-permute-start.26) | collective-permute-done | bytes 131104 | tf_op jit(solution)/shard_map/ppermute | solution.py:22
  126.5 5.7 %collective-permute-done.28 = bf16[128,512]{1,0:T(8,128)(2,1)S(1)} collective-permute-done((bf16[128,512]{1,0:T(8,128)(2,1)S(1)}, bf16[128,512]{1,0:T(8,128)(2,1)S(1)}, u32[]{:S(2)}, u32[]{:S(2)}) %collective-permute-start.28) | collective-permute-done | bytes 131104 | tf_op jit(solution)/shard_map/ppermute | solution.py:22
  (107 shorter events, 24.1 us)
Async XLA Ops:
  0.0 8.4 %collective-permute-start = (bf16[128,7168]{1,0:T(8,128)(2,1)}, bf16[128,7168]{1,0:T(8,128)(2,1)S(1)}, u32[]{:S(2)}, u32[]{:S(2)}) collective-permute-start(bf16[128,7168]{1,0:T(8,128)(2,1)} %refs_0_.1), channel_id=1, source_target_pairs={{0,4},{4,0},{8,12},{12,8},{1,5},{5,1},{9,13},{13,9},{2,6},{6,2},{1... | collective-permute-start | bytes 5505032 | tf_op jit(solution)/shard_map/ppermute | solution.py:22
  3.4 24.9 %collective-permute-start.2 = (bf16[128,1792]{1,0:T(8,128)(2,1)}, bf16[128,1792]{1,0:T(8,128)(2,1)S(1)}, u32[]{:S(2)}, u32[]{:S(2)}) collective-permute-start(bf16[128,1792]{1,0:T(8,128)(2,1)} %get-tuple-element.90), channel_id=1, source_target_pairs={{0,8},{4,12},{8,0},{12,4},{1,9},{5,13},{9,1},{13,5},{2,10},{6,14},... | collective-permute-start | bytes 1376264 | tf_op jit(solution)/shard_map/ppermute | solution.py:22
  6.0 22.3 %collective-permute-start.3 = (bf16[128,1792]{1,0:T(8,128)(2,1)}, bf16[128,1792]{1,0:T(8,128)(2,1)}, u32[]{:S(2)}, u32[]{:S(2)}) collective-permute-start(bf16[128,1792]{1,0:T(8,128)(2,1)} %get-tuple-element.91), channel_id=1, source_target_pairs={{0,8},{4,12},{8,0},{12,4},{1,9},{5,13},{9,1},{13,5},{2,10},{6,14},... | collective-permute-start | bytes 1376264 | tf_op jit(solution)/shard_map/ppermute | solution.py:22
  17.0 32.9 %collective-permute-start.1 = (bf16[128,3584]{1,0:T(8,128)(2,1)}, bf16[128,3584]{1,0:T(8,128)(2,1)S(1)}, u32[]{:S(2)}, u32[]{:S(2)}) collective-permute-start(bf16[128,3584]{1,0:T(8,128)(2,1)} %get-tuple-element.89), channel_id=1, source_target_pairs={{0,8},{4,12},{8,0},{12,4},{1,9},{5,13},{9,1},{13,5},{2,10},{6,14},... | collective-permute-start | bytes 2752520 | tf_op jit(solution)/shard_map/ppermute | solution.py:22
  28.3 2.7 %collective-permute-start.5 = (bf16[128,1792]{1,0:T(8,128)(2,1)}, bf16[128,1792]{1,0:T(8,128)(2,1)}, u32[]{:S(2)}, u32[]{:S(2)}) collective-permute-start(bf16[128,1792]{1,0:T(8,128)(2,1)} %collective-permute-done.3.refs_2_.refs_3_), channel_id=1, source_target_pairs={{0,4},{4,0},{8,12},{12,8},{1,5},{5,1},{9,13},{13,9},{2,6},{6,2},{1... | collective-permute-start | bytes 1376264 | tf_op jit(solution)/shard_map/ppermute | solution.py:22
  28.3 2.7 %collective-permute-start.4 = (bf16[128,1792]{1,0:T(8,128)(2,1)S(1)}, bf16[128,1792]{1,0:T(8,128)(2,1)}, u32[]{:S(2)}, u32[]{:S(2)}) collective-permute-start(bf16[128,1792]{1,0:T(8,128)(2,1)S(1)} %collective-permute-done.2.refs_1_.refs_2_), channel_id=1, source_target_pairs={{0,4},{4,0},{8,12},{12,8},{1,5},{5,1},{9,13},{13,9},{2,6},{6,2},{1... | collective-permute-start | bytes 1376264 | tf_op jit(solution)/shard_map/ppermute | solution.py:22
  49.9 3.7 %collective-permute-start.6 = (bf16[128,3584]{1,0:T(8,128)(2,1)S(1)}, bf16[128,3584]{1,0:T(8,128)(2,1)S(1)}, u32[]{:S(2)}, u32[]{:S(2)}) collective-permute-start(bf16[128,3584]{1,0:T(8,128)(2,1)S(1)} %collective-permute-done.1.refs_1_.refs_0_), channel_id=1, source_target_pairs={{0,4},{4,0},{8,12},{12,8},{1,5},{5,1},{9,13},{13,9},{2,6},{6,2},{1... | collective-permute-start | bytes 2752520 | tf_op jit(solution)/shard_map/ppermute | solution.py:22
  50.0 10.4 %collective-permute-start.10 = (bf16[256,512]{1,0:T(8,128)(2,1)}, bf16[256,512]{1,0:T(8,128)(2,1)S(1)}, u32[]{:S(2)}, u32[]{:S(2)}) collective-permute-start(bf16[256,512]{1,0:T(8,128)(2,1)} %get-tuple-element.106), channel_id=1, source_target_pairs={{0,8},{4,12},{8,0},{12,4},{1,9},{5,13},{9,1},{13,5},{2,10},{6,14},... | collective-permute-start | bytes 786440 | tf_op jit(solution)/shard_map/ppermute | solution.py:22
  53.6 25.6 %collective-permute-start.15 = (bf16[256,2048]{1,0:T(8,128)(2,1)}, bf16[256,2048]{1,0:T(8,128)(2,1)S(1)}, u32[]{:S(2)}, u32[]{:S(2)}) collective-permute-start(bf16[256,2048]{1,0:T(8,128)(2,1)} %constant_dynamic-slice_fusion.3), channel_id=1, source_target_pairs={{0,4},{4,0},{8,12},{12,8},{1,5},{5,1},{9,13},{13,9},{2,6},{6,2},{1... | collective-permute-start | bytes 3145736 | tf_op jit(solution)/shard_map/ppermute | solution.py:22
  53.7 6.7 %copy-start.14 = (bf16[256,512]{1,0:T(8,128)(2,1)S(1)}, bf16[256,512]{1,0:T(8,128)(2,1)}, u32[]{:S(2)}) copy-start(bf16[256,512]{1,0:T(8,128)(2,1)} %get-tuple-element.114) | copy-start | bytes 786436
  58.2 5.9 %collective-permute-start.9 = (bf16[4,64,128]{2,1,0:T(8,128)(2,1)S(1)}, bf16[4,64,128]{2,1,0:T(8,128)(2,1)S(1)}, u32[]{:S(2)}, u32[]{:S(2)}) collective-permute-start(bf16[4,64,128]{2,1,0:T(8,128)(2,1)S(1)} %get-tuple-element.105), channel_id=1, source_target_pairs={{0,4},{4,0},{8,12},{12,8},{1,5},{5,1},{9,13},{13,9},{2,6},{6,2},{1... | collective-permute-start | bytes 196616 | tf_op jit(solution)/shard_map/ppermute | solution.py:22
  58.7 6.7 %collective-permute-start.8 = (bf16[4,64,128]{2,1,0:T(8,128)(2,1)S(1)}, bf16[4,64,128]{2,1,0:T(8,128)(2,1)S(1)}, u32[]{:S(2)}, u32[]{:S(2)}) collective-permute-start(bf16[4,64,128]{2,1,0:T(8,128)(2,1)S(1)} %get-tuple-element.105), channel_id=1, source_target_pairs={{0,12},{4,8},{8,4},{12,0},{1,13},{5,9},{9,5},{13,1},{2,14},{6,10},... | collective-permute-start | bytes 196616 | tf_op jit(solution)/shard_map/ppermute | solution.py:22
  59.2 6.7 %collective-permute-start.7 = (bf16[4,64,128]{2,1,0:T(8,128)(2,1)S(1)}, bf16[4,64,128]{2,1,0:T(8,128)(2,1)S(1)}, u32[]{:S(2)}, u32[]{:S(2)}) collective-permute-start(bf16[4,64,128]{2,1,0:T(8,128)(2,1)S(1)} %get-tuple-element.105), channel_id=1, source_target_pairs={{0,8},{4,12},{8,0},{12,4},{1,9},{5,13},{9,1},{13,5},{2,10},{6,14},... | collective-permute-start | bytes 196616 | tf_op jit(solution)/shard_map/ppermute | solution.py:22
  60.4 10.3 %collective-permute-start.12 = (bf16[256,512]{1,0:T(8,128)(2,1)S(1)}, bf16[256,512]{1,0:T(8,128)(2,1)S(1)}, u32[]{:S(2)}, u32[]{:S(2)}) collective-permute-start(bf16[256,512]{1,0:T(8,128)(2,1)S(1)} %copy-done.14), channel_id=1, source_target_pairs={{0,12},{4,8},{8,4},{12,0},{1,13},{5,9},{9,5},{13,1},{2,14},{6,10},... | collective-permute-start | bytes 786440 | tf_op jit(solution)/shard_map/ppermute | solution.py:22
  64.1 14.4 %collective-permute-start.14 = (bf16[256,512]{1,0:T(8,128)(2,1)S(1)}, bf16[256,512]{1,0:T(8,128)(2,1)S(1)}, u32[]{:S(2)}, u32[]{:S(2)}) collective-permute-start(bf16[256,512]{1,0:T(8,128)(2,1)S(1)} %copy-done.13), channel_id=1, source_target_pairs={{0,8},{4,12},{8,0},{12,4},{1,9},{5,13},{9,1},{13,5},{2,10},{6,14},... | collective-permute-start | bytes 786440 | tf_op jit(solution)/shard_map/ppermute | solution.py:22
  65.4 19.0 %collective-permute-start.18 = (bf16[256,512]{1,0:T(8,128)(2,1)}, bf16[256,512]{1,0:T(8,128)(2,1)}, u32[]{:S(2)}, u32[]{:S(2)}) collective-permute-start(bf16[256,512]{1,0:T(8,128)(2,1)} %get-tuple-element.134), channel_id=1, source_target_pairs={{0,12},{4,8},{8,4},{12,0},{1,13},{5,9},{9,5},{13,1},{2,14},{6,10},... | collective-permute-start | bytes 786440 | tf_op jit(solution)/shard_map/ppermute | solution.py:22
  66.0 13.2 %copy-start.6 = (s32[4,128,128]{2,1,0:T(8,128)S(1)}, s32[4,128,128]{2,1,0:T(8,128)}, u32[]{:S(2)}) copy-start(s32[4,128,128]{2,1,0:T(8,128)} %broadcast_in_dim.96.refs_3_) | copy-start | bytes 786436
  66.0 13.2 %copy-start.10 = (bf16[256,512]{1,0:T(8,128)(2,1)S(1)}, bf16[256,512]{1,0:T(8,128)(2,1)}, u32[]{:S(2)}) copy-start(bf16[256,512]{1,0:T(8,128)(2,1)} %copy-done.9) | copy-start | bytes 786436
  66.0 4.7 %collective-permute-start.11 = (bf16[4,64,128]{2,1,0:T(8,128)(2,1)S(1)}, bf16[4,64,128]{2,1,0:T(8,128)(2,1)S(1)}, u32[]{:S(2)}, u32[]{:S(2)}) collective-permute-start(bf16[4,64,128]{2,1,0:T(8,128)(2,1)S(1)} %fusion.6), channel_id=1, source_target_pairs={{0,1},{1,0},{2,3},{3,2},{4,5},{5,4},{6,7},{7,6},{8,9},{9,8},{10,11... | collective-permute-start | bytes 196616 | tf_op jit(solution)/shard_map/ppermute | solution.py:22
  70.8 6.4 %collective-permute-start.13 = (bf16[4,64,128]{2,1,0:T(8,128)(2,1)S(1)}, bf16[4,64,128]{2,1,0:T(8,128)(2,1)S(1)}, u32[]{:S(2)}, u32[]{:S(2)}) collective-permute-start(bf16[4,64,128]{2,1,0:T(8,128)(2,1)S(1)} %get-tuple-element.161), channel_id=1, source_target_pairs={{0,2},{1,3},{2,0},{3,1},{4,6},{5,7},{6,4},{7,5},{8,10},{9,11},{10,... | collective-permute-start | bytes 196616 | tf_op jit(solution)/shard_map/ppermute | solution.py:22
  77.2 9.8 %collective-permute-start.17 = (bf16[256,512]{1,0:T(8,128)(2,1)}, bf16[256,512]{1,0:T(8,128)(2,1)}, u32[]{:S(2)}, u32[]{:S(2)}) collective-permute-start(bf16[256,512]{1,0:T(8,128)(2,1)} %get-tuple-element.129), channel_id=1, source_target_pairs={{0,8},{4,12},{8,0},{12,4},{1,9},{5,13},{9,1},{13,5},{2,10},{6,14},... | collective-permute-start | bytes 786440 | tf_op jit(solution)/shard_map/ppermute | solution.py:22
  84.3 13.2 %collective-permute-start.16 = (bf16[2,128,512]{2,1,0:T(8,128)(2,1)}, bf16[2,128,512]{2,1,0:T(8,128)(2,1)}, u32[]{:S(2)}, u32[]{:S(2)}) collective-permute-start(bf16[2,128,512]{2,1,0:T(8,128)(2,1)} %get-tuple-element.126), channel_id=1, source_target_pairs={{0,1},{1,0},{2,3},{3,2},{4,5},{5,4},{6,7},{7,6},{8,9},{9,8},{10,11... | collective-permute-start | bytes 786440 | tf_op jit(solution)/shard_map/ppermute | solution.py:22
  84.4 16.8 %collective-permute-start.21 = (bf16[256,512]{1,0:T(8,128)(2,1)}, bf16[256,512]{1,0:T(8,128)(2,1)S(1)}, u32[]{:S(2)}, u32[]{:S(2)}) collective-permute-start(bf16[256,512]{1,0:T(8,128)(2,1)} %get-tuple-element.143), channel_id=1, source_target_pairs={{0,12},{4,8},{8,4},{12,0},{1,13},{5,9},{9,5},{13,1},{2,14},{6,10},... | collective-permute-start | bytes 786440 | tf_op jit(solution)/shard_map/ppermute | solution.py:22
  91.7 12.5 %collective-permute-start.20 = (bf16[2,128,512]{2,1,0:T(8,128)(2,1)S(1)}, bf16[2,128,512]{2,1,0:T(8,128)(2,1)S(1)}, u32[]{:S(2)}, u32[]{:S(2)}) collective-permute-start(bf16[2,128,512]{2,1,0:T(8,128)(2,1)S(1)} %get-tuple-element.136), channel_id=1, source_target_pairs={{0,1},{1,0},{2,3},{3,2},{4,5},{5,4},{6,7},{7,6},{8,9},{9,8},{10,11... | collective-permute-start | bytes 786440 | tf_op jit(solution)/shard_map/ppermute | solution.py:22
  93.3 11.9 %collective-permute-start.24 = (bf16[256,512]{1,0:T(8,128)(2,1)S(1)}, bf16[256,512]{1,0:T(8,128)(2,1)S(1)}, u32[]{:S(2)}, u32[]{:S(2)}) collective-permute-start(bf16[256,512]{1,0:T(8,128)(2,1)S(1)} %copy-done.15), channel_id=1, source_target_pairs={{0,8},{4,12},{8,0},{12,4},{1,9},{5,13},{9,1},{13,5},{2,10},{6,14},... | collective-permute-start | bytes 786440 | tf_op jit(solution)/shard_map/ppermute | solution.py:22
  94.1 11.2 %collective-permute-start.25 = (bf16[256,512]{1,0:T(8,128)(2,1)S(1)}, bf16[256,512]{1,0:T(8,128)(2,1)S(1)}, u32[]{:S(2)}, u32[]{:S(2)}) collective-permute-start(bf16[256,512]{1,0:T(8,128)(2,1)S(1)} %copy-done.16), channel_id=1, source_target_pairs={{0,12},{4,8},{8,4},{12,0},{1,13},{5,9},{9,5},{13,1},{2,14},{6,10},... | collective-permute-start | bytes 786440 | tf_op jit(solution)/shard_map/ppermute | solution.py:22
  98.6 10.1 %collective-permute-start.19 = (bf16[128,512]{1,0:T(8,128)(2,1)S(1)}, bf16[128,512]{1,0:T(8,128)(2,1)S(1)}, u32[]{:S(2)}, u32[]{:S(2)}) collective-permute-start(bf16[128,512]{1,0:T(8,128)(2,1)S(1)} %fusion.2), channel_id=1, source_target_pairs={{0,2},{1,3},{2,0},{3,1},{4,6},{5,7},{6,4},{7,5},{8,10},{9,11},{10,... | collective-permute-start | bytes 393224 | tf_op jit(solution)/shard_map/ppermute | solution.py:22
  103.7 13.3 %collective-permute-start.23 = (bf16[2,128,512]{2,1,0:T(8,128)(2,1)S(1)}, bf16[2,128,512]{2,1,0:T(8,128)(2,1)S(1)}, u32[]{:S(2)}, u32[]{:S(2)}) collective-permute-start(bf16[2,128,512]{2,1,0:T(8,128)(2,1)S(1)} %get-tuple-element.145), channel_id=1, source_target_pairs={{0,1},{1,0},{2,3},{3,2},{4,5},{5,4},{6,7},{7,6},{8,9},{9,8},{10,11... | collective-permute-start | bytes 786440 | tf_op jit(solution)/shard_map/ppermute | solution.py:22
  104.3 9.4 %collective-permute-start.22 = (bf16[128,512]{1,0:T(8,128)(2,1)S(1)}, bf16[128,512]{1,0:T(8,128)(2,1)S(1)}, u32[]{:S(2)}, u32[]{:S(2)}) collective-permute-start(bf16[128,512]{1,0:T(8,128)(2,1)S(1)} %fusion.3), channel_id=1, source_target_pairs={{0,2},{1,3},{2,0},{3,1},{4,6},{5,7},{6,4},{7,5},{8,10},{9,11},{10,... | collective-permute-start | bytes 393224 | tf_op jit(solution)/shard_map/ppermute | solution.py:22
  111.1 12.7 %collective-permute-start.27 = (bf16[2,128,512]{2,1,0:T(8,128)(2,1)S(1)}, bf16[2,128,512]{2,1,0:T(8,128)(2,1)S(1)}, u32[]{:S(2)}, u32[]{:S(2)}) collective-permute-start(bf16[2,128,512]{2,1,0:T(8,128)(2,1)S(1)} %get-tuple-element.156), channel_id=1, source_target_pairs={{0,1},{1,0},{2,3},{3,2},{4,5},{5,4},{6,7},{7,6},{8,9},{9,8},{10,11... | collective-permute-start | bytes 786440 | tf_op jit(solution)/shard_map/ppermute | solution.py:22
  117.2 9.3 %collective-permute-start.26 = (bf16[128,512]{1,0:T(8,128)(2,1)S(1)}, bf16[128,512]{1,0:T(8,128)(2,1)S(1)}, u32[]{:S(2)}, u32[]{:S(2)}) collective-permute-start(bf16[128,512]{1,0:T(8,128)(2,1)S(1)} %fusion.4), channel_id=1, source_target_pairs={{0,2},{1,3},{2,0},{3,1},{4,6},{5,7},{6,4},{7,5},{8,10},{9,11},{10,... | collective-permute-start | bytes 393224 | tf_op jit(solution)/shard_map/ppermute | solution.py:22
  124.0 8.3 %collective-permute-start.28 = (bf16[128,512]{1,0:T(8,128)(2,1)S(1)}, bf16[128,512]{1,0:T(8,128)(2,1)S(1)}, u32[]{:S(2)}, u32[]{:S(2)}) collective-permute-start(bf16[128,512]{1,0:T(8,128)(2,1)S(1)} %fusion.5), channel_id=1, source_target_pairs={{0,2},{1,3},{2,0},{3,1},{4,6},{5,7},{6,4},{7,5},{8,10},{9,11},{10,... | collective-permute-start | bytes 393224 | tf_op jit(solution)/shard_map/ppermute | solution.py:22
  (14 other events, 38.7 us)

commit v12 on v11

--- a/solution.py
+++ b/solution.py
@@ -470,9 +470,6 @@
         return moved[index] if after is None else [tie(x, after) for x in moved[index]]
 
     def pace(index):
-        if index == 1:
-            moved[2][0] = tie(moved[2][0], send)
-            return tie(near_base, moved[2][0])
         if index == 3:
             return lax.optimization_barrier((near_base, started[1], parts[0]))[0]
         return near_base if index < 2 else tie(near_base, started[index - 2])

time: 134 us -> 134 us (level)
  starting transfers between devices: 24.6 us -> 30.2 us
  waiting for transfers between devices: 24.9 us -> 20 us
    ppermute x29, starting transfers between devices: 24.6 us -> 30.2 us  [swap(): return lax.ppermute(values, axis, partners(lax.axis_size(axis), step))]
    ppermute x29, waiting for transfers between devices: 24.9 us -> 20 us  [swap(): return lax.ppermute(values, axis, partners(lax.axis_size(axis), step))]
  transfers between devices with their start and end apart: 29 -> 29, of which waited for: 9 -> 5; matrix products, arithmetic and copies ran while one was open for 9% -> 9% of each run, Pallas kernels for 46% -> 46%
where the time goes in v12:
time: 134 us
  Pallas kernels  61.9 us (46%)
  starting transfers between devices  30.2 us (23%)
  waiting for transfers between devices  20 us (15%)
  local copies, waits for them, and re-layouts  16.8 us (13%)
  other arithmetic  4.62 us (3%)
    pallas_call x6, Pallas kernels, product(): pl.pallas_call(lambda *refs: product_kernel(counts, prior is not None, *r...  33.2 us
    ppermute x29, starting transfers between devices, swap(): return lax.ppermute(values, axis, partners(lax.axis_size(axis), step))  30.2 us
    ppermute x29, waiting for transfers between devices, swap(): return lax.ppermute(values, axis, partners(lax.axis_size(axis), step))  20 us
    pallas_call x3, Pallas kernels, scores(): pl.pallas_call(lambda *refs: scores_kernel(first, half * depth, len(lower...  16.8 us
    pallas_call x4, Pallas kernels, combine(): pl.pallas_call(lambda *refs: combine_kernel(bool(build), *refs), grid_spe...  10.5 us
    unnamed x34, local copies, waits for them, and re-layouts  9.09 us
    dynamic_slice x2, local copies, waits for them, and re-layouts, block_for(): lax.dynamic_slice(source, (0, (place ^ other) * width + starts[index]), (...  4.38 us
  transfers between devices with their start and end apart: 29, of which 5 were waited for; matrix products, arithmetic and copies ran while one was open for 9% of the time, Pallas kernels for 46%

profile of v12, /device:TPU:0, one launch (start us, length us, event | category | flops | bytes accessed | tf_op | source)
XLA Modules:
  0.0 133.9 jit_solution(8011402273026396824)
XLA Ops:
  0.5 1.5 %copy-done = bf16[128,7168]{1,0:T(8,128)(2,1)S(1)} copy-done((bf16[128,7168]{1,0:T(8,128)(2,1)S(1)}, bf16[128,7168]{1,0:T(8,128)(2,1)}, u32[]{:S(2)}) %copy-start) | copy-done | bytes 1835032
  2.0 1.4 %cut.1 = (bf16[128,1792]{1,0:T(8,128)(2,1)}, bf16[128,1792]{1,0:T(8,128)(2,1)}, bf16[128,3584]{1,0:T(8,128)(2,1)}) custom-call(bf16[128,7168]{1,0:T(8,128)(2,1)S(1)} %copy-done), custom_call_target="tpu_custom_call" | custom-call | bytes 3670 | tf_op jit(solution)/shard_map/cut/pallas_call | solution.py:57
  3.4 2.6 %collective-permute-start.2 = (bf16[128,1792]{1,0:T(8,128)(2,1)}, bf16[128,1792]{1,0:T(8,128)(2,1)S(1)}, u32[]{:S(2)}, u32[]{:S(2)}) collective-permute-start(bf16[128,1792]{1,0:T(8,128)(2,1)} %get-tuple-element.88), channel_id=1, source_target_pairs={{0,8},{4,12},{8,0},{12,4},{1,9},{5,13},{9,1},{13,5},{2,10},{6,14},... | collective-permute-start | bytes 1376264 | tf_op jit(solution)/shard_map/ppermute | solution.py:22
  8.4 1.5 %copy-done.1 = bf16[128,7168]{1,0:T(8,128)(2,1)S(1)} copy-done((bf16[128,7168]{1,0:T(8,128)(2,1)S(1)}, bf16[128,7168]{1,0:T(8,128)(2,1)}, u32[]{:S(2)}) %copy-start.1) | copy-done | bytes 1835032
  9.9 7.1 %scores.3.refs_5_ = f32[2,64,128]{2,1,0:T(8,128)S(1)} custom-call(s32[17]{0:T(128)S(1)} %pad_add_fusion.refs_0_, bf16[128,7168]{1,0:T(8,128)(2,1)S(1)} %copy-done.1, bf16[128,7168]{1,0:T(8,128)(2,1)S(1)} %collective-permute-done.refs_2_.refs_1_, bf16[16,64,7168]{2,1,0:T(8,128)(2,1)} %refs_3_.7, s32[4,1,128]{2,1,0:T(1,128)S(1)} %bitcast.41), custom_call_target="tpu_custom_call" | custom-call | flops 939524 | bytes 11010 | tf_op jit(solution)/shard_map/scores/pallas_call | solution.py:231
  17.0 2.0 %collective-permute-start.1 = (bf16[128,3584]{1,0:T(8,128)(2,1)}, bf16[128,3584]{1,0:T(8,128)(2,1)S(1)}, u32[]{:S(2)}, u32[]{:S(2)}) collective-permute-start(bf16[128,3584]{1,0:T(8,128)(2,1)} %get-tuple-element.87), channel_id=1, source_target_pairs={{0,8},{4,12},{8,0},{12,4},{1,9},{5,13},{9,1},{13,5},{2,10},{6,14},... | collective-permute-start | bytes 2752520 | tf_op jit(solution)/shard_map/ppermute | solution.py:22
  19.0 7.9 %base.6.refs_6_ = f32[256,2048]{1,0:T(8,128)S(1)} custom-call(bf16[128,7168]{1,0:T(8,128)(2,1)S(1)} %copy-done.1, bf16[128,7168]{1,0:T(8,128)(2,1)S(1)} %collective-permute-done.refs_2_.refs_1_, bf16[7168,2048]{1,0:T(8,128)(2,1)} %refs_3_.11), custom_call_target="tpu_custom_call" | custom-call | flops 3758096 | bytes 20709 | tf_op jit(solution)/shard_map/base/pallas_call | solution.py:117
  28.8 2.2 %constant_dynamic-slice_fusion.4 = (bf16[256,512]{1,0:T(8,128)(2,1)}, bf16[256,512]{1,0:T(8,128)(2,1)}, bf16[256,512]{1,0:T(8,128)(2,1)}, bf16[256,512]{1,0:T(8,128)(2,1)}) fusion(bf16[256,8192]{1,0:T(8,128)(2,1)} %refs_4_.5, s32[]{:T(128)S(6)} %select_n.103, s32[]{:T(128)S(6)} %select_n.102, s32[]{:T(128)S(6)} %select_n.101, s32[]{:T(128)S(6)} %select_n.100), kind=kLoop, calls=%fused_computation.35 | loop fusion | bytes 2097168 | tf_op jit(solution)/shard_map/dynamic_slice | solution.py:354
  31.8 5.2 %scores.4.refs_4_ = f32[2,256,128]{2,1,0:T(8,128)S(1)} custom-call(s32[17]{0:T(128)S(1)} %pad_add_fusion.refs_0_, bf16[128,1792]{1,0:T(8,128)(2,1)S(1)} %collective-permute-done.2.refs_1_.refs_2_, bf16[128,1792]{1,0:T(8,128)(2,1)} %collective-permute-done.3.refs_2_.refs_3_, bf16[128,1792]{1,0:T(8,128)(2,1)} %collective-permute-done.4.refs_3_.refs_4_, ...), custom_call_target="tpu_custom_call" | custom-call | flops 469762 | bytes 5505 | tf_op jit(solution)/shard_map/scores/pallas_call | solution.py:231
  37.0 12.8 %base.7.refs_2_ = f32[512,2048]{1,0:T(8,128)} custom-call(bf16[128,7168]{1,0:T(8,128)(2,1)S(1)} %copy-done.2, bf16[128,7168]{1,0:T(8,128)(2,1)S(1)} %collective-permute-done.refs_2_.refs_1_, bf16[128,1792]{1,0:T(8,128)(2,1)S(1)} %collective-permute-done.2.refs_1_.refs_2_, bf16[128,1792]{1,0:T(8,128)(2,1)} %collective-permute-done.3.refs_2_.refs_3_, ...), custom_call_target="tpu_custom_call" | custom-call | flops 7516192 | bytes 26738 | tf_op jit(solution)/shard_map/base/pallas_call | solution.py:117
  51.2 2.3 %constant_dynamic-slice_fusion.3 = bf16[256,2048]{1,0:T(8,128)(2,1)} fusion(bf16[256,8192]{1,0:T(8,128)(2,1)} %refs_4_.5, s32[]{:T(128)S(6)} %select_n.104), kind=kLoop, calls=%fused_computation.34 | loop fusion | bytes 2097156 | tf_op jit(solution)/shard_map/dynamic_slice | solution.py:422
  53.7 4.5 %scores.5 = (f32[4,64,128]{2,1,0:T(8,128)S(1)}, bf16[4,64,128]{2,1,0:T(8,128)(2,1)S(1)}) custom-call(s32[17]{0:T(128)S(1)} %pad_add_fusion.refs_0_, bf16[128,3584]{1,0:T(8,128)(2,1)S(1)} %collective-permute-done.1.refs_1_.refs_0_, bf16[128,3584]{1,0:T(8,128)(2,1)S(1)} %collective-permute-done.6.refs_2_.refs_1_, bf16[16,64,7168]{2,1,0:T(8,128)(2,1)} %refs_3_.7, ...), custom_call_target="tpu_custom_call" | custom-call | flops 469762 | bytes 5505 | tf_op jit(solution)/shard_map/scores/pallas_call | solution.py:231
  61.0 3.1 %base.8 = f32[256,512]{1,0:T(8,128)S(1)} custom-call(bf16[128,3584]{1,0:T(8,128)(2,1)S(1)} %collective-permute-done.1.refs_1_.refs_0_, bf16[128,3584]{1,0:T(8,128)(2,1)S(1)} %collective-permute-done.6.refs_2_.refs_1_, f32[512,2048]{1,0:T(8,128)} %base.7.refs_2_, bf16[7168,2048]{1,0:T(8,128)(2,1)} %refs_3_.11), custom_call_target="tpu_custom_call" | custom-call | flops 939524096 | bytes 6553600 | tf_op jit(solution)/shard_map/base/pallas_call | solution.py:117
  66.0 1.6 %collective-permute-start.11 = (bf16[4,64,128]{2,1,0:T(8,128)(2,1)S(1)}, bf16[4,64,128]{2,1,0:T(8,128)(2,1)S(1)}, u32[]{:S(2)}, u32[]{:S(2)}) collective-permute-start(bf16[4,64,128]{2,1,0:T(8,128)(2,1)S(1)} %fusion.6), channel_id=1, source_target_pairs={{0,1},{1,0},{2,3},{3,2},{4,5},{5,4},{6,7},{7,6},{8,9},{9,8},{10,11... | collective-permute-start | bytes 196616 | tf_op jit(solution)/shard_map/ppermute | solution.py:22
  67.6 3.1 %base.9 = f32[256,512]{1,0:T(8,128)S(1)} custom-call(bf16[128,3584]{1,0:T(8,128)(2,1)S(1)} %collective-permute-done.1.refs_1_.refs_0_, bf16[128,3584]{1,0:T(8,128)(2,1)S(1)} %collective-permute-done.6.refs_2_.refs_1_, f32[512,2048]{1,0:T(8,128)} %base.7.refs_2_, bf16[7168,2048]{1,0:T(8,128)(2,1)} %refs_3_.11), custom_call_target="tpu_custom_call" | custom-call | flops 939524096 | bytes 6553600 | tf_op jit(solution)/shard_map/base/pallas_call | solution.py:117
  70.8 2.7 %collective-permute-start.13 = (bf16[4,64,128]{2,1,0:T(8,128)(2,1)S(1)}, bf16[4,64,128]{2,1,0:T(8,128)(2,1)S(1)}, u32[]{:S(2)}, u32[]{:S(2)}) collective-permute-start(bf16[4,64,128]{2,1,0:T(8,128)(2,1)S(1)} %get-tuple-element.157), channel_id=1, source_target_pairs={{0,2},{1,3},{2,0},{3,1},{4,6},{5,7},{6,4},{7,5},{8,10},{9,11},{10,... | collective-permute-start | bytes 196616 | tf_op jit(solution)/shard_map/ppermute | solution.py:22
  73.4 2.2 %constant_dynamic-slice_fusion.8 = (bf16[256,512]{1,0:T(8,128)(2,1)}, bf16[256,512]{1,0:T(8,128)(2,1)}, bf16[256,512]{1,0:T(8,128)(2,1)}, bf16[256,512]{1,0:T(8,128)(2,1)}) fusion(bf16[256,8192]{1,0:T(8,128)(2,1)} %refs_4_.5, s32[]{:T(128)S(6)} %select_n.108, s32[]{:T(128)S(6)} %select_n.107, s32[]{:T(128)S(6)} %select_n.106, s32[]{:T(128)S(6)} %select_n.105), kind=kLoop, calls=%fused_computation.39 | loop fusion | bytes 2097168 | tf_op jit(solution)/shard_map/dynamic_slice | solution.py:354
  77.2 3.3 %combine.4 = (f32[2,128,512]{2,1,0:T(8,128)S(1)}, bf16[2,128,512]{2,1,0:T(8,128)(2,1)}, bf16[512,1024]{1,0:T(8,128)(2,1)S(1)}) custom-call(s32[10]{0:T(128)S(1)} %stack.40.refs_0_, f32[4,64,128]{2,1,0:T(8,128)S(1)} %get-tuple-element.158.refs_1_, bf16[4,64,128]{2,1,0:T(8,128)(2,1)S(1)} %collective-permute-done.13.refs_2_, s32[4,128,128]{2,1,0:T(8,128)S(1)} %copy-done.6, ...), custom_call_target="tpu_custom_call" | custom-call | flops 536870 | bytes 2752 | tf_op jit(solution)/shard_map/combine/pallas_call | solution.py:319
  86.5 2.4 %combine.5 = (f32[2,128,512]{2,1,0:T(8,128)S(1)}, bf16[2,128,512]{2,1,0:T(8,128)(2,1)S(1)}) custom-call(s32[10]{0:T(128)S(1)} %stack.40.refs_0_, bf16[512,1024]{1,0:T(8,128)(2,1)S(1)} %copy-done.4, f32[4,128,2048]{2,1,0:T(8,128)} %bitcast.44, f32[2,128,512]{2,1,0:T(8,128)S(1)} %bitcast.37, bf16[256,8192]{1,0:T(8,128)(2,1)} %refs_4_.5, ...), custom_call_target="tpu_custom_call" | custom-call | flops 536870 | bytes 2752 | tf_op jit(solution)/shard_map/combine/pallas_call | solution.py:319
  89.0 1.4 %collective-permute-start.19 = (bf16[2,128,512]{2,1,0:T(8,128)(2,1)S(1)}, bf16[2,128,512]{2,1,0:T(8,128)(2,1)S(1)}, u32[]{:S(2)}, u32[]{:S(2)}) collective-permute-start(bf16[2,128,512]{2,1,0:T(8,128)(2,1)S(1)} %get-tuple-element.130), channel_id=1, source_target_pairs={{0,1},{1,0},{2,3},{3,2},{4,5},{5,4},{6,7},{7,6},{8,9},{9,8},{10,11... | collective-permute-start | bytes 786440 | tf_op jit(solution)/shard_map/ppermute | solution.py:22
  91.5 3.2 %base.10 = f32[256,512]{1,0:T(8,128)S(1)} custom-call(bf16[128,3584]{1,0:T(8,128)(2,1)S(1)} %collective-permute-done.1.refs_1_.refs_0_, bf16[128,3584]{1,0:T(8,128)(2,1)S(1)} %collective-permute-done.6.refs_2_.refs_1_, f32[512,2048]{1,0:T(8,128)} %base.7.refs_2_, bf16[7168,2048]{1,0:T(8,128)(2,1)} %refs_3_.11), custom_call_target="tpu_custom_call" | custom-call | flops 939524 | bytes 6553 | tf_op jit(solution)/shard_map/base/pallas_call | solution.py:117
  96.4 2.2 %collective-permute-start.18 = (bf16[128,512]{1,0:T(8,128)(2,1)S(1)}, bf16[128,512]{1,0:T(8,128)(2,1)S(1)}, u32[]{:S(2)}, u32[]{:S(2)}) collective-permute-start(bf16[128,512]{1,0:T(8,128)(2,1)S(1)} %fusion.2), channel_id=1, source_target_pairs={{0,2},{1,3},{2,0},{3,1},{4,6},{5,7},{6,4},{7,5},{8,10},{9,11},{10,... | collective-permute-start | bytes 393224 | tf_op jit(solution)/shard_map/ppermute | solution.py:22
  98.7 2.4 %combine.6 = (f32[2,128,512]{2,1,0:T(8,128)S(1)}, bf16[2,128,512]{2,1,0:T(8,128)(2,1)S(1)}) custom-call(s32[10]{0:T(128)S(1)} %stack.40.refs_0_, bf16[512,1024]{1,0:T(8,128)(2,1)S(1)} %copy-done.4, f32[4,128,2048]{2,1,0:T(8,128)} %bitcast.45, f32[2,128,512]{2,1,0:T(8,128)S(1)} %bitcast.39, bf16[256,8192]{1,0:T(8,128)(2,1)} %refs_4_.5, ...), custom_call_target="tpu_custom_call" | custom-call | flops 536870 | bytes 2752 | tf_op jit(solution)/shard_map/combine/pallas_call | solution.py:319
  101.0 1.7 %collective-permute-start.23 = (bf16[2,128,512]{2,1,0:T(8,128)(2,1)S(1)}, bf16[2,128,512]{2,1,0:T(8,128)(2,1)S(1)}, u32[]{:S(2)}, u32[]{:S(2)}) collective-permute-start(bf16[2,128,512]{2,1,0:T(8,128)(2,1)S(1)} %get-tuple-element.141), channel_id=1, source_target_pairs={{0,1},{1,0},{2,3},{3,2},{4,5},{5,4},{6,7},{7,6},{8,9},{9,8},{10,11... | collective-permute-start | bytes 786440 | tf_op jit(solution)/shard_map/ppermute | solution.py:22
  103.1 5.5 %collective-permute-done.25.refs_7_ = bf16[256,512]{1,0:T(8,128)(2,1)S(1)} collective-permute-done((bf16[256,512]{1,0:T(8,128)(2,1)S(1)}, bf16[256,512]{1,0:T(8,128)(2,1)S(1)}, u32[]{:S(2)}, u32[]{:S(2)}) %collective-permute-start.25) | collective-permute-done | bytes 262176 | tf_op jit(solution)/shard_map/ppermute | solution.py:22
  108.5 3.1 %base.11 = f32[256,512]{1,0:T(8,128)S(1)} custom-call(bf16[128,3584]{1,0:T(8,128)(2,1)S(1)} %collective-permute-done.1.refs_1_.refs_0_, bf16[128,3584]{1,0:T(8,128)(2,1)S(1)} %collective-permute-done.6.refs_2_.refs_1_, f32[512,2048]{1,0:T(8,128)} %base.7.refs_2_, bf16[7168,2048]{1,0:T(8,128)(2,1)} %refs_3_.11), custom_call_target="tpu_custom_call" | custom-call | flops 939524 | bytes 6553 | tf_op jit(solution)/shard_map/base/pallas_call | solution.py:117
  111.7 2.4 %combine.7 = (f32[2,128,512]{2,1,0:T(8,128)S(1)}, bf16[2,128,512]{2,1,0:T(8,128)(2,1)S(1)}) custom-call(s32[10]{0:T(128)S(1)} %stack.40.refs_0_, bf16[512,1024]{1,0:T(8,128)(2,1)S(1)} %copy-done.4, f32[4,128,2048]{2,1,0:T(8,128)} %bitcast.46, f32[2,128,512]{2,1,0:T(8,128)S(1)} %bitcast.40, bf16[256,8192]{1,0:T(8,128)(2,1)} %refs_4_.5, ...), custom_call_target="tpu_custom_call" | custom-call | flops 536870 | bytes 2752 | tf_op jit(solution)/shard_map/combine/pallas_call | solution.py:319
  114.0 1.4 %collective-permute-start.27 = (bf16[2,128,512]{2,1,0:T(8,128)(2,1)S(1)}, bf16[2,128,512]{2,1,0:T(8,128)(2,1)S(1)}, u32[]{:S(2)}, u32[]{:S(2)}) collective-permute-start(bf16[2,128,512]{2,1,0:T(8,128)(2,1)S(1)} %get-tuple-element.152), channel_id=1, source_target_pairs={{0,1},{1,0},{2,3},{3,2},{4,5},{5,4},{6,7},{7,6},{8,9},{9,8},{10,11... | collective-permute-start | bytes 786440 | tf_op jit(solution)/shard_map/ppermute | solution.py:22
  115.6 2.0 %collective-permute-start.26 = (bf16[128,512]{1,0:T(8,128)(2,1)S(1)}, bf16[128,512]{1,0:T(8,128)(2,1)S(1)}, u32[]{:S(2)}, u32[]{:S(2)}) collective-permute-start(bf16[128,512]{1,0:T(8,128)(2,1)S(1)} %fusion.4), channel_id=1, source_target_pairs={{0,2},{1,3},{2,0},{3,1},{4,6},{5,7},{6,4},{7,5},{8,10},{9,11},{10,... | collective-permute-start | bytes 393224 | tf_op jit(solution)/shard_map/ppermute | solution.py:22
  117.6 7.2 %collective-permute-done.27 = bf16[2,128,512]{2,1,0:T(8,128)(2,1)S(1)} collective-permute-done((bf16[2,128,512]{2,1,0:T(8,128)(2,1)S(1)}, bf16[2,128,512]{2,1,0:T(8,128)(2,1)S(1)}, u32[]{:S(2)}, u32[]{:S(2)}) %collective-permute-start.27) | collective-permute-done | bytes 262176 | tf_op jit(solution)/shard_map/ppermute | solution.py:22
  124.9 1.6 %collective-permute-start.28 = (bf16[128,512]{1,0:T(8,128)(2,1)S(1)}, bf16[128,512]{1,0:T(8,128)(2,1)S(1)}, u32[]{:S(2)}, u32[]{:S(2)}) collective-permute-start(bf16[128,512]{1,0:T(8,128)(2,1)S(1)} %fusion.5), channel_id=1, source_target_pairs={{0,2},{1,3},{2,0},{3,1},{4,6},{5,7},{6,4},{7,5},{8,10},{9,11},{10,... | collective-permute-start | bytes 393224 | tf_op jit(solution)/shard_map/ppermute | solution.py:22
  126.5 6.4 %collective-permute-done.28 = bf16[128,512]{1,0:T(8,128)(2,1)S(1)} collective-permute-done((bf16[128,512]{1,0:T(8,128)(2,1)S(1)}, bf16[128,512]{1,0:T(8,128)(2,1)S(1)}, u32[]{:S(2)}, u32[]{:S(2)}) %collective-permute-start.28) | collective-permute-done | bytes 131104 | tf_op jit(solution)/shard_map/ppermute | solution.py:22
  (107 shorter events, 23.6 us)
Async XLA Ops:
  0.0 8.4 %collective-permute-start = (bf16[128,7168]{1,0:T(8,128)(2,1)}, bf16[128,7168]{1,0:T(8,128)(2,1)S(1)}, u32[]{:S(2)}, u32[]{:S(2)}) collective-permute-start(bf16[128,7168]{1,0:T(8,128)(2,1)} %refs_0_.1), channel_id=1, source_target_pairs={{0,4},{4,0},{8,12},{12,8},{1,5},{5,1},{9,13},{13,9},{2,6},{6,2},{1... | collective-permute-start | bytes 5505032 | tf_op jit(solution)/shard_map/ppermute | solution.py:22
  3.4 24.9 %collective-permute-start.2 = (bf16[128,1792]{1,0:T(8,128)(2,1)}, bf16[128,1792]{1,0:T(8,128)(2,1)S(1)}, u32[]{:S(2)}, u32[]{:S(2)}) collective-permute-start(bf16[128,1792]{1,0:T(8,128)(2,1)} %get-tuple-element.88), channel_id=1, source_target_pairs={{0,8},{4,12},{8,0},{12,4},{1,9},{5,13},{9,1},{13,5},{2,10},{6,14},... | collective-permute-start | bytes 1376264 | tf_op jit(solution)/shard_map/ppermute | solution.py:22
  6.0 22.3 %collective-permute-start.3 = (bf16[128,1792]{1,0:T(8,128)(2,1)}, bf16[128,1792]{1,0:T(8,128)(2,1)}, u32[]{:S(2)}, u32[]{:S(2)}) collective-permute-start(bf16[128,1792]{1,0:T(8,128)(2,1)} %get-tuple-element.89), channel_id=1, source_target_pairs={{0,8},{4,12},{8,0},{12,4},{1,9},{5,13},{9,1},{13,5},{2,10},{6,14},... | collective-permute-start | bytes 1376264 | tf_op jit(solution)/shard_map/ppermute | solution.py:22
  17.0 32.9 %collective-permute-start.1 = (bf16[128,3584]{1,0:T(8,128)(2,1)}, bf16[128,3584]{1,0:T(8,128)(2,1)S(1)}, u32[]{:S(2)}, u32[]{:S(2)}) collective-permute-start(bf16[128,3584]{1,0:T(8,128)(2,1)} %get-tuple-element.87), channel_id=1, source_target_pairs={{0,8},{4,12},{8,0},{12,4},{1,9},{5,13},{9,1},{13,5},{2,10},{6,14},... | collective-permute-start | bytes 2752520 | tf_op jit(solution)/shard_map/ppermute | solution.py:22
  28.3 2.7 %collective-permute-start.5 = (bf16[128,1792]{1,0:T(8,128)(2,1)}, bf16[128,1792]{1,0:T(8,128)(2,1)}, u32[]{:S(2)}, u32[]{:S(2)}) collective-permute-start(bf16[128,1792]{1,0:T(8,128)(2,1)} %collective-permute-done.3.refs_2_.refs_3_), channel_id=1, source_target_pairs={{0,4},{4,0},{8,12},{12,8},{1,5},{5,1},{9,13},{13,9},{2,6},{6,2},{1... | collective-permute-start | bytes 1376264 | tf_op jit(solution)/shard_map/ppermute | solution.py:22
  28.3 2.7 %collective-permute-start.4 = (bf16[128,1792]{1,0:T(8,128)(2,1)S(1)}, bf16[128,1792]{1,0:T(8,128)(2,1)}, u32[]{:S(2)}, u32[]{:S(2)}) collective-permute-start(bf16[128,1792]{1,0:T(8,128)(2,1)S(1)} %collective-permute-done.2.refs_1_.refs_2_), channel_id=1, source_target_pairs={{0,4},{4,0},{8,12},{12,8},{1,5},{5,1},{9,13},{13,9},{2,6},{6,2},{1... | collective-permute-start | bytes 1376264 | tf_op jit(solution)/shard_map/ppermute | solution.py:22
  49.9 3.7 %collective-permute-start.6 = (bf16[128,3584]{1,0:T(8,128)(2,1)S(1)}, bf16[128,3584]{1,0:T(8,128)(2,1)S(1)}, u32[]{:S(2)}, u32[]{:S(2)}) collective-permute-start(bf16[128,3584]{1,0:T(8,128)(2,1)S(1)} %collective-permute-done.1.refs_1_.refs_0_), channel_id=1, source_target_pairs={{0,4},{4,0},{8,12},{12,8},{1,5},{5,1},{9,13},{13,9},{2,6},{6,2},{1... | collective-permute-start | bytes 2752520 | tf_op jit(solution)/shard_map/ppermute | solution.py:22
  50.0 10.4 %collective-permute-start.10 = (bf16[256,512]{1,0:T(8,128)(2,1)}, bf16[256,512]{1,0:T(8,128)(2,1)S(1)}, u32[]{:S(2)}, u32[]{:S(2)}) collective-permute-start(bf16[256,512]{1,0:T(8,128)(2,1)} %get-tuple-element.104), channel_id=1, source_target_pairs={{0,8},{4,12},{8,0},{12,4},{1,9},{5,13},{9,1},{13,5},{2,10},{6,14},... | collective-permute-start | bytes 786440 | tf_op jit(solution)/shard_map/ppermute | solution.py:22
  53.6 23.6 %collective-permute-start.15 = (bf16[256,2048]{1,0:T(8,128)(2,1)}, bf16[256,2048]{1,0:T(8,128)(2,1)S(1)}, u32[]{:S(2)}, u32[]{:S(2)}) collective-permute-start(bf16[256,2048]{1,0:T(8,128)(2,1)} %constant_dynamic-slice_fusion.3), channel_id=1, source_target_pairs={{0,4},{4,0},{8,12},{12,8},{1,5},{5,1},{9,13},{13,9},{2,6},{6,2},{1... | collective-permute-start | bytes 3145736 | tf_op jit(solution)/shard_map/ppermute | solution.py:22
  53.7 6.7 %copy-start.14 = (bf16[256,512]{1,0:T(8,128)(2,1)S(1)}, bf16[256,512]{1,0:T(8,128)(2,1)}, u32[]{:S(2)}) copy-start(bf16[256,512]{1,0:T(8,128)(2,1)} %get-tuple-element.112) | copy-start | bytes 786436
  58.2 5.9 %collective-permute-start.9 = (bf16[4,64,128]{2,1,0:T(8,128)(2,1)S(1)}, bf16[4,64,128]{2,1,0:T(8,128)(2,1)S(1)}, u32[]{:S(2)}, u32[]{:S(2)}) collective-permute-start(bf16[4,64,128]{2,1,0:T(8,128)(2,1)S(1)} %get-tuple-element.103), channel_id=1, source_target_pairs={{0,4},{4,0},{8,12},{12,8},{1,5},{5,1},{9,13},{13,9},{2,6},{6,2},{1... | collective-permute-start | bytes 196616 | tf_op jit(solution)/shard_map/ppermute | solution.py:22
  58.7 6.7 %collective-permute-start.8 = (bf16[4,64,128]{2,1,0:T(8,128)(2,1)S(1)}, bf16[4,64,128]{2,1,0:T(8,128)(2,1)S(1)}, u32[]{:S(2)}, u32[]{:S(2)}) collective-permute-start(bf16[4,64,128]{2,1,0:T(8,128)(2,1)S(1)} %get-tuple-element.103), channel_id=1, source_target_pairs={{0,12},{4,8},{8,4},{12,0},{1,13},{5,9},{9,5},{13,1},{2,14},{6,10},... | collective-permute-start | bytes 196616 | tf_op jit(solution)/shard_map/ppermute | solution.py:22
  59.2 6.7 %collective-permute-start.7 = (bf16[4,64,128]{2,1,0:T(8,128)(2,1)S(1)}, bf16[4,64,128]{2,1,0:T(8,128)(2,1)S(1)}, u32[]{:S(2)}, u32[]{:S(2)}) collective-permute-start(bf16[4,64,128]{2,1,0:T(8,128)(2,1)S(1)} %get-tuple-element.103), channel_id=1, source_target_pairs={{0,8},{4,12},{8,0},{12,4},{1,9},{5,13},{9,1},{13,5},{2,10},{6,14},... | collective-permute-start | bytes 196616 | tf_op jit(solution)/shard_map/ppermute | solution.py:22
  60.4 10.3 %collective-permute-start.12 = (bf16[256,512]{1,0:T(8,128)(2,1)S(1)}, bf16[256,512]{1,0:T(8,128)(2,1)S(1)}, u32[]{:S(2)}, u32[]{:S(2)}) collective-permute-start(bf16[256,512]{1,0:T(8,128)(2,1)S(1)} %copy-done.14), channel_id=1, source_target_pairs={{0,12},{4,8},{8,4},{12,0},{1,13},{5,9},{9,5},{13,1},{2,14},{6,10},... | collective-permute-start | bytes 786440 | tf_op jit(solution)/shard_map/ppermute | solution.py:22
  64.1 11.9 %collective-permute-start.14 = (bf16[256,512]{1,0:T(8,128)(2,1)S(1)}, bf16[256,512]{1,0:T(8,128)(2,1)S(1)}, u32[]{:S(2)}, u32[]{:S(2)}) collective-permute-start(bf16[256,512]{1,0:T(8,128)(2,1)S(1)} %copy-done.13), channel_id=1, source_target_pairs={{0,8},{4,12},{8,0},{12,4},{1,9},{5,13},{9,1},{13,5},{2,10},{6,14},... | collective-permute-start | bytes 786440 | tf_op jit(solution)/shard_map/ppermute | solution.py:22
  65.4 18.9 %collective-permute-start.17 = (bf16[256,512]{1,0:T(8,128)(2,1)}, bf16[256,512]{1,0:T(8,128)(2,1)}, u32[]{:S(2)}, u32[]{:S(2)}) collective-permute-start(bf16[256,512]{1,0:T(8,128)(2,1)} %get-tuple-element.128), channel_id=1, source_target_pairs={{0,12},{4,8},{8,4},{12,0},{1,13},{5,9},{9,5},{13,1},{2,14},{6,10},... | collective-permute-start | bytes 786440 | tf_op jit(solution)/shard_map/ppermute | solution.py:22
  66.0 11.3 %copy-start.6 = (s32[4,128,128]{2,1,0:T(8,128)S(1)}, s32[4,128,128]{2,1,0:T(8,128)}, u32[]{:S(2)}) copy-start(s32[4,128,128]{2,1,0:T(8,128)} %broadcast_in_dim.96.refs_3_) | copy-start | bytes 786436
  66.0 11.2 %copy-start.10 = (bf16[256,512]{1,0:T(8,128)(2,1)S(1)}, bf16[256,512]{1,0:T(8,128)(2,1)}, u32[]{:S(2)}) copy-start(bf16[256,512]{1,0:T(8,128)(2,1)} %copy-done.9) | copy-start | bytes 786436
  66.0 4.7 %collective-permute-start.11 = (bf16[4,64,128]{2,1,0:T(8,128)(2,1)S(1)}, bf16[4,64,128]{2,1,0:T(8,128)(2,1)S(1)}, u32[]{:S(2)}, u32[]{:S(2)}) collective-permute-start(bf16[4,64,128]{2,1,0:T(8,128)(2,1)S(1)} %fusion.6), channel_id=1, source_target_pairs={{0,1},{1,0},{2,3},{3,2},{4,5},{5,4},{6,7},{7,6},{8,9},{9,8},{10,11... | collective-permute-start | bytes 196616 | tf_op jit(solution)/shard_map/ppermute | solution.py:22
  70.8 6.4 %collective-permute-start.13 = (bf16[4,64,128]{2,1,0:T(8,128)(2,1)S(1)}, bf16[4,64,128]{2,1,0:T(8,128)(2,1)S(1)}, u32[]{:S(2)}, u32[]{:S(2)}) collective-permute-start(bf16[4,64,128]{2,1,0:T(8,128)(2,1)S(1)} %get-tuple-element.157), channel_id=1, source_target_pairs={{0,2},{1,3},{2,0},{3,1},{4,6},{5,7},{6,4},{7,5},{8,10},{9,11},{10,... | collective-permute-start | bytes 196616 | tf_op jit(solution)/shard_map/ppermute | solution.py:22
  82.3 12.4 %collective-permute-start.16 = (bf16[2,128,512]{2,1,0:T(8,128)(2,1)}, bf16[2,128,512]{2,1,0:T(8,128)(2,1)}, u32[]{:S(2)}, u32[]{:S(2)}) collective-permute-start(bf16[2,128,512]{2,1,0:T(8,128)(2,1)} %get-tuple-element.124), channel_id=1, source_target_pairs={{0,1},{1,0},{2,3},{3,2},{4,5},{5,4},{6,7},{7,6},{8,9},{9,8},{10,11... | collective-permute-start | bytes 786440 | tf_op jit(solution)/shard_map/ppermute | solution.py:22
  83.4 13.1 %collective-permute-start.21 = (bf16[256,512]{1,0:T(8,128)(2,1)}, bf16[256,512]{1,0:T(8,128)(2,1)S(1)}, u32[]{:S(2)}, u32[]{:S(2)}) collective-permute-start(bf16[256,512]{1,0:T(8,128)(2,1)} %get-tuple-element.139), channel_id=1, source_target_pairs={{0,12},{4,8},{8,4},{12,0},{1,13},{5,9},{9,5},{13,1},{2,14},{6,10},... | collective-permute-start | bytes 786440 | tf_op jit(solution)/shard_map/ppermute | solution.py:22
  83.4 15.3 %collective-permute-start.20 = (bf16[256,512]{1,0:T(8,128)(2,1)}, bf16[256,512]{1,0:T(8,128)(2,1)S(1)}, u32[]{:S(2)}, u32[]{:S(2)}) collective-permute-start(bf16[256,512]{1,0:T(8,128)(2,1)} %get-tuple-element.136), channel_id=1, source_target_pairs={{0,8},{4,12},{8,0},{12,4},{1,9},{5,13},{9,1},{13,5},{2,10},{6,14},... | collective-permute-start | bytes 786440 | tf_op jit(solution)/shard_map/ppermute | solution.py:22
  89.0 13.8 %collective-permute-start.19 = (bf16[2,128,512]{2,1,0:T(8,128)(2,1)S(1)}, bf16[2,128,512]{2,1,0:T(8,128)(2,1)S(1)}, u32[]{:S(2)}, u32[]{:S(2)}) collective-permute-start(bf16[2,128,512]{2,1,0:T(8,128)(2,1)S(1)} %get-tuple-element.130), channel_id=1, source_target_pairs={{0,1},{1,0},{2,3},{3,2},{4,5},{5,4},{6,7},{7,6},{8,9},{9,8},{10,11... | collective-permute-start | bytes 786440 | tf_op jit(solution)/shard_map/ppermute | solution.py:22
  90.4 18.1 %collective-permute-start.24 = (bf16[256,512]{1,0:T(8,128)(2,1)S(1)}, bf16[256,512]{1,0:T(8,128)(2,1)S(1)}, u32[]{:S(2)}, u32[]{:S(2)}) collective-permute-start(bf16[256,512]{1,0:T(8,128)(2,1)S(1)} %copy-done.15), channel_id=1, source_target_pairs={{0,8},{4,12},{8,0},{12,4},{1,9},{5,13},{9,1},{13,5},{2,10},{6,14},... | collective-permute-start | bytes 786440 | tf_op jit(solution)/shard_map/ppermute | solution.py:22
  94.8 13.8 %collective-permute-start.25 = (bf16[256,512]{1,0:T(8,128)(2,1)S(1)}, bf16[256,512]{1,0:T(8,128)(2,1)S(1)}, u32[]{:S(2)}, u32[]{:S(2)}) collective-permute-start(bf16[256,512]{1,0:T(8,128)(2,1)S(1)} %copy-done.16), channel_id=1, source_target_pairs={{0,12},{4,8},{8,4},{12,0},{1,13},{5,9},{9,5},{13,1},{2,14},{6,10},... | collective-permute-start | bytes 786440 | tf_op jit(solution)/shard_map/ppermute | solution.py:22
  96.4 15.2 %collective-permute-start.18 = (bf16[128,512]{1,0:T(8,128)(2,1)S(1)}, bf16[128,512]{1,0:T(8,128)(2,1)S(1)}, u32[]{:S(2)}, u32[]{:S(2)}) collective-permute-start(bf16[128,512]{1,0:T(8,128)(2,1)S(1)} %fusion.2), channel_id=1, source_target_pairs={{0,2},{1,3},{2,0},{3,1},{4,6},{5,7},{6,4},{7,5},{8,10},{9,11},{10,... | collective-permute-start | bytes 393224 | tf_op jit(solution)/shard_map/ppermute | solution.py:22
  101.0 14.5 %collective-permute-start.23 = (bf16[2,128,512]{2,1,0:T(8,128)(2,1)S(1)}, bf16[2,128,512]{2,1,0:T(8,128)(2,1)S(1)}, u32[]{:S(2)}, u32[]{:S(2)}) collective-permute-start(bf16[2,128,512]{2,1,0:T(8,128)(2,1)S(1)} %get-tuple-element.141), channel_id=1, source_target_pairs={{0,1},{1,0},{2,3},{3,2},{4,5},{5,4},{6,7},{7,6},{8,9},{9,8},{10,11... | collective-permute-start | bytes 786440 | tf_op jit(solution)/shard_map/ppermute | solution.py:22
  102.9 12.6 %collective-permute-start.22 = (bf16[128,512]{1,0:T(8,128)(2,1)S(1)}, bf16[128,512]{1,0:T(8,128)(2,1)S(1)}, u32[]{:S(2)}, u32[]{:S(2)}) collective-permute-start(bf16[128,512]{1,0:T(8,128)(2,1)S(1)} %fusion.3), channel_id=1, source_target_pairs={{0,2},{1,3},{2,0},{3,1},{4,6},{5,7},{6,4},{7,5},{8,10},{9,11},{10,... | collective-permute-start | bytes 393224 | tf_op jit(solution)/shard_map/ppermute | solution.py:22
  114.0 10.8 %collective-permute-start.27 = (bf16[2,128,512]{2,1,0:T(8,128)(2,1)S(1)}, bf16[2,128,512]{2,1,0:T(8,128)(2,1)S(1)}, u32[]{:S(2)}, u32[]{:S(2)}) collective-permute-start(bf16[2,128,512]{2,1,0:T(8,128)(2,1)S(1)} %get-tuple-element.152), channel_id=1, source_target_pairs={{0,1},{1,0},{2,3},{3,2},{4,5},{5,4},{6,7},{7,6},{8,9},{9,8},{10,11... | collective-permute-start | bytes 786440 | tf_op jit(solution)/shard_map/ppermute | solution.py:22
  115.6 10.9 %collective-permute-start.26 = (bf16[128,512]{1,0:T(8,128)(2,1)S(1)}, bf16[128,512]{1,0:T(8,128)(2,1)S(1)}, u32[]{:S(2)}, u32[]{:S(2)}) collective-permute-start(bf16[128,512]{1,0:T(8,128)(2,1)S(1)} %fusion.4), channel_id=1, source_target_pairs={{0,2},{1,3},{2,0},{3,1},{4,6},{5,7},{6,4},{7,5},{8,10},{9,11},{10,... | collective-permute-start | bytes 393224 | tf_op jit(solution)/shard_map/ppermute | solution.py:22
  124.9 8.1 %collective-permute-start.28 = (bf16[128,512]{1,0:T(8,128)(2,1)S(1)}, bf16[128,512]{1,0:T(8,128)(2,1)S(1)}, u32[]{:S(2)}, u32[]{:S(2)}) collective-permute-start(bf16[128,512]{1,0:T(8,128)(2,1)S(1)} %fusion.5), channel_id=1, source_target_pairs={{0,2},{1,3},{2,0},{3,1},{4,6},{5,7},{6,4},{7,5},{8,10},{9,11},{10,... | collective-permute-start | bytes 393224 | tf_op jit(solution)/shard_map/ppermute | solution.py:22
  (14 other events, 39.9 us)

commit v13 on v12

--- a/solution.py
+++ b/solution.py
@@ -7,7 +7,7 @@
 
 F32 = jnp.float32
 BF16 = jnp.bfloat16
-VMEM_LIMIT = 48 * 1024 * 1024
+VMEM_LIMIT = 52 * 1024 * 1024
 WIDTHS = (512, 512, 512, 512)
 CAP = 4
 HALVES = 2

time: 134 us -> 135 us (level)
  local copies, waits for them, and re-layouts: 16.8 us -> 11 us
  Pallas kernels: 61.9 us -> 66.4 us
  waiting for transfers between devices: 20 us -> 22.2 us
    unnamed x34 -> x18, local copies, waits for them, and re-layouts: 9.09 us -> 3.93 us
    pallas_call x6, Pallas kernels: 33.2 us -> 35.6 us  [product(): pl.pallas_call(lambda *refs: product_kernel(counts, prior is not None, *r...]
    ppermute x29, waiting for transfers between devices: 20 us -> 22.2 us  [swap(): return lax.ppermute(values, axis, partners(lax.axis_size(axis), step))]
    pallas_call x4, Pallas kernels: 10.5 us -> 12.1 us  [combine(): pl.pallas_call(lambda *refs: combine_kernel(bool(build), *refs), grid_spe...]
  transfers between devices with their start and end apart: 29 -> 29, of which waited for: 5 -> 5; matrix products, arithmetic and copies ran while one was open for 9% -> 7% of each run, Pallas kernels for 46% -> 50%
where the time goes in v13:
time: 135 us; the launch traced here: 134 us
  Pallas kernels  66.4 us (49%)
  starting transfers between devices  30.3 us (22%)
  waiting for transfers between devices  22.2 us (16%)
  local copies, waits for them, and re-layouts  11 us (8%)
  other arithmetic  3.67 us (3%)
    pallas_call x6, Pallas kernels, product(): pl.pallas_call(lambda *refs: product_kernel(counts, prior is not None, *r...  35.6 us
    ppermute x29, starting transfers between devices, swap(): return lax.ppermute(values, axis, partners(lax.axis_size(axis), step))  30.3 us
    ppermute x29, waiting for transfers between devices, swap(): return lax.ppermute(values, axis, partners(lax.axis_size(axis), step))  22.2 us
    pallas_call x3, Pallas kernels, scores(): pl.pallas_call(lambda *refs: scores_kernel(first, half * depth, len(lower...  16.2 us
    pallas_call x4, Pallas kernels, combine(): pl.pallas_call(lambda *refs: combine_kernel(bool(build), *refs), grid_spe...  12.1 us
    dynamic_slice x2, local copies, waits for them, and re-layouts, block_for(): lax.dynamic_slice(source, (0, (place ^ other) * width + starts[index]), (...  4.43 us
    unnamed x18, local copies, waits for them, and re-layouts  3.93 us
  transfers between devices with their start and end apart: 29, of which 5 were waited for; matrix products, arithmetic and copies ran while one was open for 7% of the time, Pallas kernels for 50%

profile of v13, /device:TPU:0, one launch (start us, length us, event | category | flops | bytes accessed | tf_op | source)
XLA Modules:
  0.0 134.0 jit_solution(11614674546767327375)
XLA Ops:
  0.5 2.5 %cut.1 = (bf16[128,1792]{1,0:T(8,128)(2,1)S(1)}, bf16[128,1792]{1,0:T(8,128)(2,1)S(1)}, bf16[128,3584]{1,0:T(8,128)(2,1)}) custom-call(bf16[128,7168]{1,0:T(8,128)(2,1)} %refs_0_.1), custom_call_target="tpu_custom_call" | custom-call | bytes 3670 | tf_op jit(solution)/shard_map/cut/pallas_call | solution.py:57
  3.0 2.6 %collective-permute-start.2 = (bf16[128,1792]{1,0:T(8,128)(2,1)S(1)}, bf16[128,1792]{1,0:T(8,128)(2,1)S(1)}, u32[]{:S(2)}, u32[]{:S(2)}) collective-permute-start(bf16[128,1792]{1,0:T(8,128)(2,1)S(1)} %get-tuple-element.88), channel_id=1, source_target_pairs={{0,8},{4,12},{8,0},{12,4},{1,9},{5,13},{9,1},{13,5},{2,10},{6,14},... | collective-permute-start | bytes 1376264 | tf_op jit(solution)/shard_map/ppermute | solution.py:22
  8.0 1.5 %copy-done = bf16[128,7168]{1,0:T(8,128)(2,1)S(1)} copy-done((bf16[128,7168]{1,0:T(8,128)(2,1)S(1)}, bf16[128,7168]{1,0:T(8,128)(2,1)}, u32[]{:S(2)}) %copy-start) | copy-done | bytes 1835032
  9.5 7.1 %scores.3.refs_5_ = f32[2,64,128]{2,1,0:T(8,128)S(1)} custom-call(s32[17]{0:T(128)S(1)} %pad_add_fusion.refs_0_, bf16[128,7168]{1,0:T(8,128)(2,1)S(1)} %copy-done, bf16[128,7168]{1,0:T(8,128)(2,1)} %collective-permute-done.refs_2_.refs_1_, bf16[16,64,7168]{2,1,0:T(8,128)(2,1)} %refs_3_.7, s32[4,1,128]{2,1,0:T(1,128)S(1)} %bitcast.41), custom_call_target="tpu_custom_call" | custom-call | flops 939524 | bytes 11010 | tf_op jit(solution)/shard_map/scores/pallas_call | solution.py:231
  16.6 2.0 %collective-permute-start.1 = (bf16[128,3584]{1,0:T(8,128)(2,1)}, bf16[128,3584]{1,0:T(8,128)(2,1)S(1)}, u32[]{:S(2)}, u32[]{:S(2)}) collective-permute-start(bf16[128,3584]{1,0:T(8,128)(2,1)} %get-tuple-element.87), channel_id=1, source_target_pairs={{0,8},{4,12},{8,0},{12,4},{1,9},{5,13},{9,1},{13,5},{2,10},{6,14},... | collective-permute-start | bytes 2752520 | tf_op jit(solution)/shard_map/ppermute | solution.py:22
  18.6 9.2 %base.6.refs_6_ = f32[256,2048]{1,0:T(8,128)} custom-call(bf16[128,7168]{1,0:T(8,128)(2,1)S(1)} %copy-done, bf16[128,7168]{1,0:T(8,128)(2,1)} %collective-permute-done.refs_2_.refs_1_, bf16[7168,2048]{1,0:T(8,128)(2,1)} %refs_3_.11), custom_call_target="tpu_custom_call" | custom-call | flops 3758096 | bytes 20709 | tf_op jit(solution)/shard_map/base/pallas_call | solution.py:117
  28.4 2.2 %constant_dynamic-slice_fusion.4 = (bf16[256,512]{1,0:T(8,128)(2,1)}, bf16[256,512]{1,0:T(8,128)(2,1)}, bf16[256,512]{1,0:T(8,128)(2,1)}, bf16[256,512]{1,0:T(8,128)(2,1)}) fusion(bf16[256,8192]{1,0:T(8,128)(2,1)} %refs_4_.5, s32[]{:T(128)S(6)} %select_n.103, s32[]{:T(128)S(6)} %select_n.102, s32[]{:T(128)S(6)} %select_n.101, s32[]{:T(128)S(6)} %select_n.100), kind=kLoop, calls=%fused_computation.35 | loop fusion | bytes 2097168 | tf_op jit(solution)/shard_map/dynamic_slice | solution.py:354
  31.3 4.6 %scores.4.refs_4_ = f32[2,256,128]{2,1,0:T(8,128)S(1)} custom-call(s32[17]{0:T(128)S(1)} %pad_add_fusion.refs_0_, bf16[128,1792]{1,0:T(8,128)(2,1)S(1)} %collective-permute-done.2.refs_1_.refs_2_, bf16[128,1792]{1,0:T(8,128)(2,1)S(1)} %collective-permute-done.3.refs_2_.refs_3_, bf16[128,1792]{1,0:T(8,128)(2,1)S(1)} %collective-permute-done.4.refs_3_.refs_4_, ...), custom_call_target="tpu_custom_call" | custom-call | flops 469762 | bytes 5505 | tf_op jit(solution)/shard_map/scores/pallas_call | solution.py:231
  37.0 12.9 %base.7.refs_2_ = f32[512,2048]{1,0:T(8,128)} custom-call(bf16[128,7168]{1,0:T(8,128)(2,1)} %refs_0_.1, bf16[128,7168]{1,0:T(8,128)(2,1)} %collective-permute-done.refs_2_.refs_1_, bf16[128,1792]{1,0:T(8,128)(2,1)S(1)} %collective-permute-done.2.refs_1_.refs_2_, bf16[128,1792]{1,0:T(8,128)(2,1)S(1)} %collective-permute-done.3.refs_2_.refs_3_, ...), custom_call_target="tpu_custom_call" | custom-call | flops 7516192 | bytes 26738 | tf_op jit(solution)/shard_map/base/pallas_call | solution.py:117
  50.8 2.3 %constant_dynamic-slice_fusion.3 = bf16[256,2048]{1,0:T(8,128)(2,1)} fusion(bf16[256,8192]{1,0:T(8,128)(2,1)} %refs_4_.5, s32[]{:T(128)S(6)} %select_n.104), kind=kLoop, calls=%fused_computation.34 | loop fusion | bytes 2097156 | tf_op jit(solution)/shard_map/dynamic_slice | solution.py:422
  54.1 4.5 %scores.5 = (f32[4,64,128]{2,1,0:T(8,128)S(1)}, bf16[4,64,128]{2,1,0:T(8,128)(2,1)S(1)}) custom-call(s32[17]{0:T(128)S(1)} %pad_add_fusion.refs_0_, bf16[128,3584]{1,0:T(8,128)(2,1)S(1)} %collective-permute-done.1.refs_1_.refs_0_, bf16[128,3584]{1,0:T(8,128)(2,1)} %copy-done.4, bf16[16,64,7168]{2,1,0:T(8,128)(2,1)} %refs_3_.7, ...), custom_call_target="tpu_custom_call" | custom-call | flops 469762 | bytes 5505 | tf_op jit(solution)/shard_map/scores/pallas_call | solution.py:231
  61.5 3.3 %base.8 = f32[256,512]{1,0:T(8,128)S(1)} custom-call(bf16[128,3584]{1,0:T(8,128)(2,1)S(1)} %collective-permute-done.1.refs_1_.refs_0_, bf16[128,3584]{1,0:T(8,128)(2,1)} %copy-done.4, f32[512,2048]{1,0:T(8,128)} %base.7.refs_2_, bf16[7168,2048]{1,0:T(8,128)(2,1)} %refs_3_.11), custom_call_target="tpu_custom_call" | custom-call | flops 939524096 | bytes 6553600 | tf_op jit(solution)/shard_map/base/pallas_call | solution.py:117
  66.9 1.6 %collective-permute-start.11 = (bf16[4,64,128]{2,1,0:T(8,128)(2,1)S(1)}, bf16[4,64,128]{2,1,0:T(8,128)(2,1)S(1)}, u32[]{:S(2)}, u32[]{:S(2)}) collective-permute-start(bf16[4,64,128]{2,1,0:T(8,128)(2,1)S(1)} %fusion.6), channel_id=1, source_target_pairs={{0,1},{1,0},{2,3},{3,2},{4,5},{5,4},{6,7},{7,6},{8,9},{9,8},{10,11... | collective-permute-start | bytes 196616 | tf_op jit(solution)/shard_map/ppermute | solution.py:22
  68.6 3.3 %base.9 = f32[256,512]{1,0:T(8,128)S(1)} custom-call(bf16[128,3584]{1,0:T(8,128)(2,1)S(1)} %collective-permute-done.1.refs_1_.refs_0_, bf16[128,3584]{1,0:T(8,128)(2,1)} %copy-done.4, f32[512,2048]{1,0:T(8,128)} %base.7.refs_2_, bf16[7168,2048]{1,0:T(8,128)(2,1)} %refs_3_.11), custom_call_target="tpu_custom_call" | custom-call | flops 939524096 | bytes 6553600 | tf_op jit(solution)/shard_map/base/pallas_call | solution.py:117
  72.0 2.7 %collective-permute-start.13 = (bf16[4,64,128]{2,1,0:T(8,128)(2,1)S(1)}, bf16[4,64,128]{2,1,0:T(8,128)(2,1)S(1)}, u32[]{:S(2)}, u32[]{:S(2)}) collective-permute-start(bf16[4,64,128]{2,1,0:T(8,128)(2,1)S(1)} %get-tuple-element.157), channel_id=1, source_target_pairs={{0,2},{1,3},{2,0},{3,1},{4,6},{5,7},{6,4},{7,5},{8,10},{9,11},{10,... | collective-permute-start | bytes 196616 | tf_op jit(solution)/shard_map/ppermute | solution.py:22
  74.7 2.3 %constant_dynamic-slice_fusion.8 = (bf16[256,512]{1,0:T(8,128)(2,1)}, bf16[256,512]{1,0:T(8,128)(2,1)}, bf16[256,512]{1,0:T(8,128)(2,1)}, bf16[256,512]{1,0:T(8,128)(2,1)}) fusion(bf16[256,8192]{1,0:T(8,128)(2,1)} %refs_4_.5, s32[]{:T(128)S(6)} %select_n.108, s32[]{:T(128)S(6)} %select_n.107, s32[]{:T(128)S(6)} %select_n.106, s32[]{:T(128)S(6)} %select_n.105), kind=kLoop, calls=%fused_computation.39 | loop fusion | bytes 2097168 | tf_op jit(solution)/shard_map/dynamic_slice | solution.py:354
  78.2 3.8 %combine.4 = (f32[2,128,512]{2,1,0:T(8,128)S(1)}, bf16[2,128,512]{2,1,0:T(8,128)(2,1)}, bf16[512,1024]{1,0:T(8,128)(2,1)}) custom-call(s32[10]{0:T(128)S(1)} %stack.40.refs_0_, f32[4,64,128]{2,1,0:T(8,128)S(1)} %get-tuple-element.158.refs_1_, bf16[4,64,128]{2,1,0:T(8,128)(2,1)S(1)} %collective-permute-done.13.refs_2_, ...), custom_call_target="tpu_custom_call" | custom-call | flops 536870 | bytes 2752 | tf_op jit(solution)/shard_map/combine/pallas_call | solution.py:319
  83.4 2.8 %combine.5 = (f32[2,128,512]{2,1,0:T(8,128)S(1)}, bf16[2,128,512]{2,1,0:T(8,128)(2,1)S(1)}) custom-call(s32[10]{0:T(128)S(1)} %stack.40.refs_0_, bf16[512,1024]{1,0:T(8,128)(2,1)} %get-tuple-element.125.refs_1_, f32[4,128,2048]{2,1,0:T(8,128)} %bitcast.44, f32[2,128,512]{2,1,0:T(8,128)S(1)} %bitcast.37, bf16[256,8192]{1,0:T(8,128)(2,1)} %refs_4_.5, ...), custom_call_target="tpu_custom_call" | custom-call | flops 536870 | bytes 2752 | tf_op jit(solution)/shard_map/combine/pallas_call | solution.py:319
  86.2 1.8 %collective-permute-start.19 = (bf16[2,128,512]{2,1,0:T(8,128)(2,1)S(1)}, bf16[2,128,512]{2,1,0:T(8,128)(2,1)S(1)}, u32[]{:S(2)}, u32[]{:S(2)}) collective-permute-start(bf16[2,128,512]{2,1,0:T(8,128)(2,1)S(1)} %get-tuple-element.130), channel_id=1, source_target_pairs={{0,1},{1,0},{2,3},{3,2},{4,5},{5,4},{6,7},{7,6},{8,9},{9,8},{10,11... | collective-permute-start | bytes 786440 | tf_op jit(solution)/shard_map/ppermute | solution.py:22
  89.0 3.5 %base.10 = f32[256,512]{1,0:T(8,128)S(1)} custom-call(bf16[128,3584]{1,0:T(8,128)(2,1)S(1)} %collective-permute-done.1.refs_1_.refs_0_, bf16[128,3584]{1,0:T(8,128)(2,1)} %copy-done.4, f32[512,2048]{1,0:T(8,128)} %base.7.refs_2_, bf16[7168,2048]{1,0:T(8,128)(2,1)} %refs_3_.11), custom_call_target="tpu_custom_call" | custom-call | flops 939524 | bytes 6553 | tf_op jit(solution)/shard_map/base/pallas_call | solution.py:117
  93.6 1.8 %collective-permute-start.18 = (bf16[128,512]{1,0:T(8,128)(2,1)S(1)}, bf16[128,512]{1,0:T(8,128)(2,1)S(1)}, u32[]{:S(2)}, u32[]{:S(2)}) collective-permute-start(bf16[128,512]{1,0:T(8,128)(2,1)S(1)} %fusion.2), channel_id=1, source_target_pairs={{0,2},{1,3},{2,0},{3,1},{4,6},{5,7},{6,4},{7,5},{8,10},{9,11},{10,... | collective-permute-start | bytes 393224 | tf_op jit(solution)/shard_map/ppermute | solution.py:22
  96.2 2.8 %combine.6 = (f32[2,128,512]{2,1,0:T(8,128)S(1)}, bf16[2,128,512]{2,1,0:T(8,128)(2,1)S(1)}) custom-call(s32[10]{0:T(128)S(1)} %stack.40.refs_0_, bf16[512,1024]{1,0:T(8,128)(2,1)} %get-tuple-element.125.refs_1_, f32[4,128,2048]{2,1,0:T(8,128)} %bitcast.45, f32[2,128,512]{2,1,0:T(8,128)S(1)} %bitcast.39, bf16[256,8192]{1,0:T(8,128)(2,1)} %refs_4_.5, ...), custom_call_target="tpu_custom_call" | custom-call | flops 536870 | bytes 2752 | tf_op jit(solution)/shard_map/combine/pallas_call | solution.py:319
  99.0 1.6 %collective-permute-start.23 = (bf16[2,128,512]{2,1,0:T(8,128)(2,1)S(1)}, bf16[2,128,512]{2,1,0:T(8,128)(2,1)S(1)}, u32[]{:S(2)}, u32[]{:S(2)}) collective-permute-start(bf16[2,128,512]{2,1,0:T(8,128)(2,1)S(1)} %get-tuple-element.141), channel_id=1, source_target_pairs={{0,1},{1,0},{2,3},{3,2},{4,5},{5,4},{6,7},{7,6},{8,9},{9,8},{10,11... | collective-permute-start | bytes 786440 | tf_op jit(solution)/shard_map/ppermute | solution.py:22
  100.7 1.3 collective-permute-start.22
  102.1 5.5 %collective-permute-done.25.refs_7_ = bf16[256,512]{1,0:T(8,128)(2,1)S(1)} collective-permute-done((bf16[256,512]{1,0:T(8,128)(2,1)S(1)}, bf16[256,512]{1,0:T(8,128)(2,1)S(1)}, u32[]{:S(2)}, u32[]{:S(2)}) %collective-permute-start.25) | collective-permute-done | bytes 262176 | tf_op jit(solution)/shard_map/ppermute | solution.py:22
  107.6 3.3 %base.11 = f32[256,512]{1,0:T(8,128)S(1)} custom-call(bf16[128,3584]{1,0:T(8,128)(2,1)S(1)} %collective-permute-done.1.refs_1_.refs_0_, bf16[128,3584]{1,0:T(8,128)(2,1)} %copy-done.4, f32[512,2048]{1,0:T(8,128)} %base.7.refs_2_, bf16[7168,2048]{1,0:T(8,128)(2,1)} %refs_3_.11), custom_call_target="tpu_custom_call" | custom-call | flops 939524 | bytes 6553 | tf_op jit(solution)/shard_map/base/pallas_call | solution.py:117
  111.0 2.8 %combine.7 = (f32[2,128,512]{2,1,0:T(8,128)S(1)}, bf16[2,128,512]{2,1,0:T(8,128)(2,1)S(1)}) custom-call(s32[10]{0:T(128)S(1)} %stack.40.refs_0_, bf16[512,1024]{1,0:T(8,128)(2,1)} %get-tuple-element.125.refs_1_, f32[4,128,2048]{2,1,0:T(8,128)} %bitcast.46, f32[2,128,512]{2,1,0:T(8,128)S(1)} %bitcast.40, bf16[256,8192]{1,0:T(8,128)(2,1)} %refs_4_.5, ...), custom_call_target="tpu_custom_call" | custom-call | flops 536870 | bytes 2752 | tf_op jit(solution)/shard_map/combine/pallas_call | solution.py:319
  113.8 1.8 %collective-permute-start.27 = (bf16[2,128,512]{2,1,0:T(8,128)(2,1)S(1)}, bf16[2,128,512]{2,1,0:T(8,128)(2,1)S(1)}, u32[]{:S(2)}, u32[]{:S(2)}) collective-permute-start(bf16[2,128,512]{2,1,0:T(8,128)(2,1)S(1)} %get-tuple-element.152), channel_id=1, source_target_pairs={{0,1},{1,0},{2,3},{3,2},{4,5},{5,4},{6,7},{7,6},{8,9},{9,8},{10,11... | collective-permute-start | bytes 786440 | tf_op jit(solution)/shard_map/ppermute | solution.py:22
  115.8 1.4 %collective-permute-start.26 = (bf16[128,512]{1,0:T(8,128)(2,1)S(1)}, bf16[128,512]{1,0:T(8,128)(2,1)S(1)}, u32[]{:S(2)}, u32[]{:S(2)}) collective-permute-start(bf16[128,512]{1,0:T(8,128)(2,1)S(1)} %fusion.4), channel_id=1, source_target_pairs={{0,2},{1,3},{2,0},{3,1},{4,6},{5,7},{6,4},{7,5},{8,10},{9,11},{10,... | collective-permute-start | bytes 393224 | tf_op jit(solution)/shard_map/ppermute | solution.py:22
  117.2 7.6 %collective-permute-done.27 = bf16[2,128,512]{2,1,0:T(8,128)(2,1)S(1)} collective-permute-done((bf16[2,128,512]{2,1,0:T(8,128)(2,1)S(1)}, bf16[2,128,512]{2,1,0:T(8,128)(2,1)S(1)}, u32[]{:S(2)}, u32[]{:S(2)}) %collective-permute-start.27) | collective-permute-done | bytes 262176 | tf_op jit(solution)/shard_map/ppermute | solution.py:22
  124.9 1.3 collective-permute-start.28
  126.3 6.8 %collective-permute-done.28 = bf16[128,512]{1,0:T(8,128)(2,1)S(1)} collective-permute-done((bf16[128,512]{1,0:T(8,128)(2,1)S(1)}, bf16[128,512]{1,0:T(8,128)(2,1)S(1)}, u32[]{:S(2)}, u32[]{:S(2)}) %collective-permute-start.28) | collective-permute-done | bytes 131104 | tf_op jit(solution)/shard_map/ppermute | solution.py:22
  (91 shorter events, 19.0 us)
Async XLA Ops:
  0.0 8.0 %collective-permute-start = (bf16[128,7168]{1,0:T(8,128)(2,1)}, bf16[128,7168]{1,0:T(8,128)(2,1)}, u32[]{:S(2)}, u32[]{:S(2)}) collective-permute-start(bf16[128,7168]{1,0:T(8,128)(2,1)} %refs_0_.1), channel_id=1, source_target_pairs={{0,4},{4,0},{8,12},{12,8},{1,5},{5,1},{9,13},{13,9},{2,6},{6,2},{1... | collective-permute-start | bytes 5505032 | tf_op jit(solution)/shard_map/ppermute | solution.py:22
  3.0 24.8 %collective-permute-start.2 = (bf16[128,1792]{1,0:T(8,128)(2,1)S(1)}, bf16[128,1792]{1,0:T(8,128)(2,1)S(1)}, u32[]{:S(2)}, u32[]{:S(2)}) collective-permute-start(bf16[128,1792]{1,0:T(8,128)(2,1)S(1)} %get-tuple-element.88), channel_id=1, source_target_pairs={{0,8},{4,12},{8,0},{12,4},{1,9},{5,13},{9,1},{13,5},{2,10},{6,14},... | collective-permute-start | bytes 1376264 | tf_op jit(solution)/shard_map/ppermute | solution.py:22
  5.6 22.3 %collective-permute-start.3 = (bf16[128,1792]{1,0:T(8,128)(2,1)S(1)}, bf16[128,1792]{1,0:T(8,128)(2,1)S(1)}, u32[]{:S(2)}, u32[]{:S(2)}) collective-permute-start(bf16[128,1792]{1,0:T(8,128)(2,1)S(1)} %get-tuple-element.89), channel_id=1, source_target_pairs={{0,8},{4,12},{8,0},{12,4},{1,9},{5,13},{9,1},{13,5},{2,10},{6,14},... | collective-permute-start | bytes 1376264 | tf_op jit(solution)/shard_map/ppermute | solution.py:22
  16.6 33.3 %collective-permute-start.1 = (bf16[128,3584]{1,0:T(8,128)(2,1)}, bf16[128,3584]{1,0:T(8,128)(2,1)S(1)}, u32[]{:S(2)}, u32[]{:S(2)}) collective-permute-start(bf16[128,3584]{1,0:T(8,128)(2,1)} %get-tuple-element.87), channel_id=1, source_target_pairs={{0,8},{4,12},{8,0},{12,4},{1,9},{5,13},{9,1},{13,5},{2,10},{6,14},... | collective-permute-start | bytes 2752520 | tf_op jit(solution)/shard_map/ppermute | solution.py:22
  27.8 2.7 %collective-permute-start.5 = (bf16[128,1792]{1,0:T(8,128)(2,1)S(1)}, bf16[128,1792]{1,0:T(8,128)(2,1)S(1)}, u32[]{:S(2)}, u32[]{:S(2)}) collective-permute-start(bf16[128,1792]{1,0:T(8,128)(2,1)S(1)} %collective-permute-done.3.refs_2_.refs_3_), channel_id=1, source_target_pairs={{0,4},{4,0},{8,12},{12,8},{1,5},{5,1},{9,13},{13,9},{2,6},{6,2},{1... | collective-permute-start | bytes 1376264 | tf_op jit(solution)/shard_map/ppermute | solution.py:22
  27.9 2.7 %collective-permute-start.4 = (bf16[128,1792]{1,0:T(8,128)(2,1)S(1)}, bf16[128,1792]{1,0:T(8,128)(2,1)S(1)}, u32[]{:S(2)}, u32[]{:S(2)}) collective-permute-start(bf16[128,1792]{1,0:T(8,128)(2,1)S(1)} %collective-permute-done.2.refs_1_.refs_2_), channel_id=1, source_target_pairs={{0,4},{4,0},{8,12},{12,8},{1,5},{5,1},{9,13},{13,9},{2,6},{6,2},{1... | collective-permute-start | bytes 1376264 | tf_op jit(solution)/shard_map/ppermute | solution.py:22
  49.9 3.2 %collective-permute-start.6 = (bf16[128,3584]{1,0:T(8,128)(2,1)S(1)}, bf16[128,3584]{1,0:T(8,128)(2,1)S(1)}, u32[]{:S(2)}, u32[]{:S(2)}) collective-permute-start(bf16[128,3584]{1,0:T(8,128)(2,1)S(1)} %collective-permute-done.1.refs_1_.refs_0_), channel_id=1, source_target_pairs={{0,4},{4,0},{8,12},{12,8},{1,5},{5,1},{9,13},{13,9},{2,6},{6,2},{1... | collective-permute-start | bytes 2752520 | tf_op jit(solution)/shard_map/ppermute | solution.py:22
  50.0 10.8 %collective-permute-start.10 = (bf16[256,512]{1,0:T(8,128)(2,1)}, bf16[256,512]{1,0:T(8,128)(2,1)S(1)}, u32[]{:S(2)}, u32[]{:S(2)}) collective-permute-start(bf16[256,512]{1,0:T(8,128)(2,1)} %get-tuple-element.104), channel_id=1, source_target_pairs={{0,8},{4,12},{8,0},{12,4},{1,9},{5,13},{9,1},{13,5},{2,10},{6,14},... | collective-permute-start | bytes 786440 | tf_op jit(solution)/shard_map/ppermute | solution.py:22
  53.1 25.1 %collective-permute-start.15 = (bf16[256,2048]{1,0:T(8,128)(2,1)}, bf16[256,2048]{1,0:T(8,128)(2,1)}, u32[]{:S(2)}, u32[]{:S(2)}) collective-permute-start(bf16[256,2048]{1,0:T(8,128)(2,1)} %constant_dynamic-slice_fusion.3), channel_id=1, source_target_pairs={{0,4},{4,0},{8,12},{12,8},{1,5},{5,1},{9,13},{13,9},{2,6},{6,2},{1... | collective-permute-start | bytes 3145736 | tf_op jit(solution)/shard_map/ppermute | solution.py:22
  54.1 6.7 %copy-start.6 = (bf16[256,512]{1,0:T(8,128)(2,1)S(1)}, bf16[256,512]{1,0:T(8,128)(2,1)}, u32[]{:S(2)}) copy-start(bf16[256,512]{1,0:T(8,128)(2,1)} %get-tuple-element.112) | copy-start | bytes 786436
  58.6 6.2 %collective-permute-start.9 = (bf16[4,64,128]{2,1,0:T(8,128)(2,1)S(1)}, bf16[4,64,128]{2,1,0:T(8,128)(2,1)S(1)}, u32[]{:S(2)}, u32[]{:S(2)}) collective-permute-start(bf16[4,64,128]{2,1,0:T(8,128)(2,1)S(1)} %get-tuple-element.103), channel_id=1, source_target_pairs={{0,4},{4,0},{8,12},{12,8},{1,5},{5,1},{9,13},{13,9},{2,6},{6,2},{1... | collective-permute-start | bytes 196616 | tf_op jit(solution)/shard_map/ppermute | solution.py:22
  58.8 6.9 %collective-permute-start.8 = (bf16[4,64,128]{2,1,0:T(8,128)(2,1)S(1)}, bf16[4,64,128]{2,1,0:T(8,128)(2,1)S(1)}, u32[]{:S(2)}, u32[]{:S(2)}) collective-permute-start(bf16[4,64,128]{2,1,0:T(8,128)(2,1)S(1)} %get-tuple-element.103), channel_id=1, source_target_pairs={{0,12},{4,8},{8,4},{12,0},{1,13},{5,9},{9,5},{13,1},{2,14},{6,10},... | collective-permute-start | bytes 196616 | tf_op jit(solution)/shard_map/ppermute | solution.py:22
  60.0 6.9 %collective-permute-start.7 = (bf16[4,64,128]{2,1,0:T(8,128)(2,1)S(1)}, bf16[4,64,128]{2,1,0:T(8,128)(2,1)S(1)}, u32[]{:S(2)}, u32[]{:S(2)}) collective-permute-start(bf16[4,64,128]{2,1,0:T(8,128)(2,1)S(1)} %get-tuple-element.103), channel_id=1, source_target_pairs={{0,8},{4,12},{8,0},{12,4},{1,9},{5,13},{9,1},{13,5},{2,10},{6,14},... | collective-permute-start | bytes 196616 | tf_op jit(solution)/shard_map/ppermute | solution.py:22
  60.8 11.1 %collective-permute-start.12 = (bf16[256,512]{1,0:T(8,128)(2,1)S(1)}, bf16[256,512]{1,0:T(8,128)(2,1)S(1)}, u32[]{:S(2)}, u32[]{:S(2)}) collective-permute-start(bf16[256,512]{1,0:T(8,128)(2,1)S(1)} %copy-done.6), channel_id=1, source_target_pairs={{0,12},{4,8},{8,4},{12,0},{1,13},{5,9},{9,5},{13,1},{2,14},{6,10},... | collective-permute-start | bytes 786440 | tf_op jit(solution)/shard_map/ppermute | solution.py:22
  64.8 7.1 %copy-start.1 = (f32[256,512]{1,0:T(8,128)}, f32[256,512]{1,0:T(8,128)S(1)}, u32[]{:S(2)}) copy-start(f32[256,512]{1,0:T(8,128)S(1)} %base.8) | copy-start | bytes 1572868
  64.9 12.1 %collective-permute-start.14 = (bf16[256,512]{1,0:T(8,128)(2,1)S(1)}, bf16[256,512]{1,0:T(8,128)(2,1)S(1)}, u32[]{:S(2)}, u32[]{:S(2)}) collective-permute-start(bf16[256,512]{1,0:T(8,128)(2,1)S(1)} %copy-done.5), channel_id=1, source_target_pairs={{0,8},{4,12},{8,0},{12,4},{1,9},{5,13},{9,1},{13,5},{2,10},{6,14},... | collective-permute-start | bytes 786440 | tf_op jit(solution)/shard_map/ppermute | solution.py:22
  65.7 17.6 %collective-permute-start.17 = (bf16[256,512]{1,0:T(8,128)(2,1)}, bf16[256,512]{1,0:T(8,128)(2,1)S(1)}, u32[]{:S(2)}, u32[]{:S(2)}) collective-permute-start(bf16[256,512]{1,0:T(8,128)(2,1)} %get-tuple-element.128), channel_id=1, source_target_pairs={{0,12},{4,8},{8,4},{12,0},{1,13},{5,9},{9,5},{13,1},{2,14},{6,10},... | collective-permute-start | bytes 786440 | tf_op jit(solution)/shard_map/ppermute | solution.py:22
  66.9 5.0 %collective-permute-start.11 = (bf16[4,64,128]{2,1,0:T(8,128)(2,1)S(1)}, bf16[4,64,128]{2,1,0:T(8,128)(2,1)S(1)}, u32[]{:S(2)}, u32[]{:S(2)}) collective-permute-start(bf16[4,64,128]{2,1,0:T(8,128)(2,1)S(1)} %fusion.6), channel_id=1, source_target_pairs={{0,1},{1,0},{2,3},{3,2},{4,5},{5,4},{6,7},{7,6},{8,9},{9,8},{10,11... | collective-permute-start | bytes 196616 | tf_op jit(solution)/shard_map/ppermute | solution.py:22
  72.0 6.2 %collective-permute-start.13 = (bf16[4,64,128]{2,1,0:T(8,128)(2,1)S(1)}, bf16[4,64,128]{2,1,0:T(8,128)(2,1)S(1)}, u32[]{:S(2)}, u32[]{:S(2)}) collective-permute-start(bf16[4,64,128]{2,1,0:T(8,128)(2,1)S(1)} %get-tuple-element.157), channel_id=1, source_target_pairs={{0,2},{1,3},{2,0},{3,1},{4,6},{5,7},{6,4},{7,5},{8,10},{9,11},{10,... | collective-permute-start | bytes 196616 | tf_op jit(solution)/shard_map/ppermute | solution.py:22
  82.0 10.4 %collective-permute-start.16 = (bf16[2,128,512]{2,1,0:T(8,128)(2,1)}, bf16[2,128,512]{2,1,0:T(8,128)(2,1)S(1)}, u32[]{:S(2)}, u32[]{:S(2)}) collective-permute-start(bf16[2,128,512]{2,1,0:T(8,128)(2,1)} %get-tuple-element.124), channel_id=1, source_target_pairs={{0,1},{1,0},{2,3},{3,2},{4,5},{5,4},{6,7},{7,6},{8,9},{9,8},{10,11... | collective-permute-start | bytes 786440 | tf_op jit(solution)/shard_map/ppermute | solution.py:22
  82.1 11.5 %collective-permute-start.21 = (bf16[256,512]{1,0:T(8,128)(2,1)}, bf16[256,512]{1,0:T(8,128)(2,1)S(1)}, u32[]{:S(2)}, u32[]{:S(2)}) collective-permute-start(bf16[256,512]{1,0:T(8,128)(2,1)} %get-tuple-element.139), channel_id=1, source_target_pairs={{0,12},{4,8},{8,4},{12,0},{1,13},{5,9},{9,5},{13,1},{2,14},{6,10},... | collective-permute-start | bytes 786440 | tf_op jit(solution)/shard_map/ppermute | solution.py:22
  82.1 14.1 %collective-permute-start.20 = (bf16[256,512]{1,0:T(8,128)(2,1)}, bf16[256,512]{1,0:T(8,128)(2,1)S(1)}, u32[]{:S(2)}, u32[]{:S(2)}) collective-permute-start(bf16[256,512]{1,0:T(8,128)(2,1)} %get-tuple-element.136), channel_id=1, source_target_pairs={{0,8},{4,12},{8,0},{12,4},{1,9},{5,13},{9,1},{13,5},{2,10},{6,14},... | collective-permute-start | bytes 786440 | tf_op jit(solution)/shard_map/ppermute | solution.py:22
  86.1 6.4 %copy-start.8 = (bf16[256,512]{1,0:T(8,128)(2,1)S(1)}, bf16[256,512]{1,0:T(8,128)(2,1)}, u32[]{:S(2)}) copy-start(bf16[256,512]{1,0:T(8,128)(2,1)} %get-tuple-element.150) | copy-start | bytes 786436
  86.2 14.5 %collective-permute-start.19 = (bf16[2,128,512]{2,1,0:T(8,128)(2,1)S(1)}, bf16[2,128,512]{2,1,0:T(8,128)(2,1)S(1)}, u32[]{:S(2)}, u32[]{:S(2)}) collective-permute-start(bf16[2,128,512]{2,1,0:T(8,128)(2,1)S(1)} %get-tuple-element.130), channel_id=1, source_target_pairs={{0,1},{1,0},{2,3},{3,2},{4,5},{5,4},{6,7},{7,6},{8,9},{9,8},{10,11... | collective-permute-start | bytes 786440 | tf_op jit(solution)/shard_map/ppermute | solution.py:22
  88.0 19.6 %collective-permute-start.24 = (bf16[256,512]{1,0:T(8,128)(2,1)S(1)}, bf16[256,512]{1,0:T(8,128)(2,1)S(1)}, u32[]{:S(2)}, u32[]{:S(2)}) collective-permute-start(bf16[256,512]{1,0:T(8,128)(2,1)S(1)} %copy-done.7), channel_id=1, source_target_pairs={{0,8},{4,12},{8,0},{12,4},{1,9},{5,13},{9,1},{13,5},{2,10},{6,14},... | collective-permute-start | bytes 786440 | tf_op jit(solution)/shard_map/ppermute | solution.py:22
  92.5 15.1 %collective-permute-start.25 = (bf16[256,512]{1,0:T(8,128)(2,1)S(1)}, bf16[256,512]{1,0:T(8,128)(2,1)S(1)}, u32[]{:S(2)}, u32[]{:S(2)}) collective-permute-start(bf16[256,512]{1,0:T(8,128)(2,1)S(1)} %copy-done.8), channel_id=1, source_target_pairs={{0,12},{4,8},{8,4},{12,0},{1,13},{5,9},{9,5},{13,1},{2,14},{6,10},... | collective-permute-start | bytes 786440 | tf_op jit(solution)/shard_map/ppermute | solution.py:22
  93.6 17.4 %collective-permute-start.18 = (bf16[128,512]{1,0:T(8,128)(2,1)S(1)}, bf16[128,512]{1,0:T(8,128)(2,1)S(1)}, u32[]{:S(2)}, u32[]{:S(2)}) collective-permute-start(bf16[128,512]{1,0:T(8,128)(2,1)S(1)} %fusion.2), channel_id=1, source_target_pairs={{0,2},{1,3},{2,0},{3,1},{4,6},{5,7},{6,4},{7,5},{8,10},{9,11},{10,... | collective-permute-start | bytes 393224 | tf_op jit(solution)/shard_map/ppermute | solution.py:22
  99.0 16.7 %collective-permute-start.23 = (bf16[2,128,512]{2,1,0:T(8,128)(2,1)S(1)}, bf16[2,128,512]{2,1,0:T(8,128)(2,1)S(1)}, u32[]{:S(2)}, u32[]{:S(2)}) collective-permute-start(bf16[2,128,512]{2,1,0:T(8,128)(2,1)S(1)} %get-tuple-element.141), channel_id=1, source_target_pairs={{0,1},{1,0},{2,3},{3,2},{4,5},{5,4},{6,7},{7,6},{8,9},{9,8},{10,11... | collective-permute-start | bytes 786440 | tf_op jit(solution)/shard_map/ppermute | solution.py:22
  100.7 14.8 %collective-permute-start.22 = (bf16[128,512]{1,0:T(8,128)(2,1)S(1)}, bf16[128,512]{1,0:T(8,128)(2,1)S(1)}, u32[]{:S(2)}, u32[]{:S(2)}) collective-permute-start(bf16[128,512]{1,0:T(8,128)(2,1)S(1)} %fusion.3), channel_id=1, source_target_pairs={{0,2},{1,3},{2,0},{3,1},{4,6},{5,7},{6,4},{7,5},{8,10},{9,11},{10,... | collective-permute-start | bytes 393224 | tf_op jit(solution)/shard_map/ppermute | solution.py:22
  113.8 11.1 %collective-permute-start.27 = (bf16[2,128,512]{2,1,0:T(8,128)(2,1)S(1)}, bf16[2,128,512]{2,1,0:T(8,128)(2,1)S(1)}, u32[]{:S(2)}, u32[]{:S(2)}) collective-permute-start(bf16[2,128,512]{2,1,0:T(8,128)(2,1)S(1)} %get-tuple-element.152), channel_id=1, source_target_pairs={{0,1},{1,0},{2,3},{3,2},{4,5},{5,4},{6,7},{7,6},{8,9},{9,8},{10,11... | collective-permute-start | bytes 786440 | tf_op jit(solution)/shard_map/ppermute | solution.py:22
  115.8 10.5 %collective-permute-start.26 = (bf16[128,512]{1,0:T(8,128)(2,1)S(1)}, bf16[128,512]{1,0:T(8,128)(2,1)S(1)}, u32[]{:S(2)}, u32[]{:S(2)}) collective-permute-start(bf16[128,512]{1,0:T(8,128)(2,1)S(1)} %fusion.4), channel_id=1, source_target_pairs={{0,2},{1,3},{2,0},{3,1},{4,6},{5,7},{6,4},{7,5},{8,10},{9,11},{10,... | collective-permute-start | bytes 393224 | tf_op jit(solution)/shard_map/ppermute | solution.py:22
  124.9 8.2 %collective-permute-start.28 = (bf16[128,512]{1,0:T(8,128)(2,1)S(1)}, bf16[128,512]{1,0:T(8,128)(2,1)S(1)}, u32[]{:S(2)}, u32[]{:S(2)}) collective-permute-start(bf16[128,512]{1,0:T(8,128)(2,1)S(1)} %fusion.5), channel_id=1, source_target_pairs={{0,2},{1,3},{2,0},{3,1},{4,6},{5,7},{6,4},{7,5},{8,10},{9,11},{10,... | collective-permute-start | bytes 393224 | tf_op jit(solution)/shard_map/ppermute | solution.py:22
  (6 other events, 15.1 us)

commit v14 on v12

--- a/solution.py
+++ b/solution.py
@@ -470,6 +470,9 @@
         return moved[index] if after is None else [tie(x, after) for x in moved[index]]
 
     def pace(index):
+        if index == 1:
+            moved[2][0] = tie(moved[2][0], pieces[2])
+            return lax.optimization_barrier((near_base, moved[2][0], pieces[2]))[0]
         if index == 3:
             return lax.optimization_barrier((near_base, started[1], parts[0]))[0]
         return near_base if index < 2 else tie(near_base, started[index - 2])

time: 134 us -> 130 us (0.970)
  waiting for transfers between devices: 20 us -> 16.2 us
  local copies, waits for them, and re-layouts: 16.8 us -> 14.6 us
  starting transfers between devices: 30.2 us -> 31.8 us
    ppermute x29, waiting for transfers between devices: 20 us -> 16.2 us  [swap(): return lax.ppermute(values, axis, partners(lax.axis_size(axis), step))]
    unnamed x34 -> x30, local copies, waits for them, and re-layouts: 9.09 us -> 6.9 us
    ppermute x29, starting transfers between devices: 30.2 us -> 31.8 us  [swap(): return lax.ppermute(values, axis, partners(lax.axis_size(axis), step))]
  transfers between devices with their start and end apart: 29 -> 29, of which waited for: 5 -> 5; matrix products, arithmetic and copies ran while one was open for 9% -> 9% of each run, Pallas kernels for 46% -> 48%
where the time goes in v14:
time: 130 us
  Pallas kernels  61.9 us (48%)
  starting transfers between devices  31.8 us (24%)
  waiting for transfers between devices  16.2 us (12%)
  local copies, waits for them, and re-layouts  14.6 us (11%)
  other arithmetic  4.62 us (4%)
    pallas_call x6, Pallas kernels, product(): pl.pallas_call(lambda *refs: product_kernel(counts, prior is not None, *r...  33.2 us
    ppermute x29, starting transfers between devices, swap(): return lax.ppermute(values, axis, partners(lax.axis_size(axis), step))  31.8 us
    pallas_call x3, Pallas kernels, scores(): pl.pallas_call(lambda *refs: scores_kernel(first, half * depth, len(lower...  16.8 us
    ppermute x29, waiting for transfers between devices, swap(): return lax.ppermute(values, axis, partners(lax.axis_size(axis), step))  16.2 us
    pallas_call x4, Pallas kernels, combine(): pl.pallas_call(lambda *refs: combine_kernel(bool(build), *refs), grid_spe...  10.5 us
    unnamed x30, local copies, waits for them, and re-layouts  6.9 us
    dynamic_slice x2, local copies, waits for them, and re-layouts, block_for(): lax.dynamic_slice(source, (0, (place ^ other) * width + starts[index]), (...  4.38 us
  transfers between devices with their start and end apart: 29, of which 5 were waited for; matrix products, arithmetic and copies ran while one was open for 9% of the time, Pallas kernels for 48%

profile of v14, /device:TPU:0, one launch (start us, length us, event | category | flops | bytes accessed | tf_op | source)
XLA Modules:
  0.0 129.5 jit_solution(11265325614683297540)
XLA Ops:
  0.5 1.5 %copy-done = bf16[128,7168]{1,0:T(8,128)(2,1)S(1)} copy-done((bf16[128,7168]{1,0:T(8,128)(2,1)S(1)}, bf16[128,7168]{1,0:T(8,128)(2,1)}, u32[]{:S(2)}) %copy-start) | copy-done | bytes 1835032
  2.0 1.4 %cut.1 = (bf16[128,1792]{1,0:T(8,128)(2,1)}, bf16[128,1792]{1,0:T(8,128)(2,1)}, bf16[128,3584]{1,0:T(8,128)(2,1)}) custom-call(bf16[128,7168]{1,0:T(8,128)(2,1)S(1)} %copy-done), custom_call_target="tpu_custom_call" | custom-call | bytes 3670 | tf_op jit(solution)/shard_map/cut/pallas_call | solution.py:57
  3.4 2.6 %collective-permute-start.2 = (bf16[128,1792]{1,0:T(8,128)(2,1)}, bf16[128,1792]{1,0:T(8,128)(2,1)S(1)}, u32[]{:S(2)}, u32[]{:S(2)}) collective-permute-start(bf16[128,1792]{1,0:T(8,128)(2,1)} %get-tuple-element.90), channel_id=1, source_target_pairs={{0,8},{4,12},{8,0},{12,4},{1,9},{5,13},{9,1},{13,5},{2,10},{6,14},... | collective-permute-start | bytes 1376264 | tf_op jit(solution)/shard_map/ppermute | solution.py:22
  8.4 1.5 %copy-done.1 = bf16[128,7168]{1,0:T(8,128)(2,1)S(1)} copy-done((bf16[128,7168]{1,0:T(8,128)(2,1)S(1)}, bf16[128,7168]{1,0:T(8,128)(2,1)}, u32[]{:S(2)}) %copy-start.1) | copy-done | bytes 1835032
  9.9 7.1 %scores.3.refs_5_ = f32[2,64,128]{2,1,0:T(8,128)S(1)} custom-call(s32[17]{0:T(128)S(1)} %pad_add_fusion.refs_0_, bf16[128,7168]{1,0:T(8,128)(2,1)S(1)} %copy-done.1, bf16[128,7168]{1,0:T(8,128)(2,1)S(1)} %collective-permute-done.refs_2_.refs_1_, bf16[16,64,7168]{2,1,0:T(8,128)(2,1)} %refs_3_.7, s32[4,1,128]{2,1,0:T(1,128)S(1)} %bitcast.41), custom_call_target="tpu_custom_call" | custom-call | flops 939524 | bytes 11010 | tf_op jit(solution)/shard_map/scores/pallas_call | solution.py:231
  17.0 2.0 %collective-permute-start.1 = (bf16[128,3584]{1,0:T(8,128)(2,1)}, bf16[128,3584]{1,0:T(8,128)(2,1)S(1)}, u32[]{:S(2)}, u32[]{:S(2)}) collective-permute-start(bf16[128,3584]{1,0:T(8,128)(2,1)} %get-tuple-element.89), channel_id=1, source_target_pairs={{0,8},{4,12},{8,0},{12,4},{1,9},{5,13},{9,1},{13,5},{2,10},{6,14},... | collective-permute-start | bytes 2752520 | tf_op jit(solution)/shard_map/ppermute | solution.py:22
  19.0 7.9 %base.6.refs_6_ = f32[256,2048]{1,0:T(8,128)S(1)} custom-call(bf16[128,7168]{1,0:T(8,128)(2,1)S(1)} %copy-done.1, bf16[128,7168]{1,0:T(8,128)(2,1)S(1)} %collective-permute-done.refs_2_.refs_1_, bf16[7168,2048]{1,0:T(8,128)(2,1)} %refs_3_.11), custom_call_target="tpu_custom_call" | custom-call | flops 3758096 | bytes 20709 | tf_op jit(solution)/shard_map/base/pallas_call | solution.py:117
  26.9 1.4 %copy-done.5 = f32[256,2048]{1,0:T(8,128)} copy-done((f32[256,2048]{1,0:T(8,128)}, f32[256,2048]{1,0:T(8,128)S(1)}, u32[]{:S(2)}) %copy-start.5) | copy-done | bytes 2097176
  28.8 2.2 %constant_dynamic-slice_fusion.4 = (bf16[256,512]{1,0:T(8,128)(2,1)}, bf16[256,512]{1,0:T(8,128)(2,1)}, bf16[256,512]{1,0:T(8,128)(2,1)}, bf16[256,512]{1,0:T(8,128)(2,1)}) fusion(bf16[256,8192]{1,0:T(8,128)(2,1)} %refs_4_.5, s32[]{:T(128)S(6)} %select_n.103, s32[]{:T(128)S(6)} %select_n.102, s32[]{:T(128)S(6)} %select_n.101, s32[]{:T(128)S(6)} %select_n.100), kind=kLoop, calls=%fused_computation.35 | loop fusion | bytes 2097168 | tf_op jit(solution)/shard_map/dynamic_slice | solution.py:354
  31.8 5.2 %scores.4.refs_4_ = f32[2,256,128]{2,1,0:T(8,128)S(1)} custom-call(s32[17]{0:T(128)S(1)} %pad_add_fusion.refs_0_, bf16[128,1792]{1,0:T(8,128)(2,1)S(1)} %collective-permute-done.2.refs_1_.refs_2_, bf16[128,1792]{1,0:T(8,128)(2,1)} %collective-permute-done.3.refs_2_.refs_3_, bf16[128,1792]{1,0:T(8,128)(2,1)} %collective-permute-done.4.refs_3_.refs_4_, ...), custom_call_target="tpu_custom_call" | custom-call | flops 469762 | bytes 5505 | tf_op jit(solution)/shard_map/scores/pallas_call | solution.py:231
  37.0 12.8 %base.7.refs_2_ = f32[512,2048]{1,0:T(8,128)} custom-call(bf16[128,7168]{1,0:T(8,128)(2,1)S(1)} %copy-done.2, bf16[128,7168]{1,0:T(8,128)(2,1)S(1)} %collective-permute-done.refs_2_.refs_1_, bf16[128,1792]{1,0:T(8,128)(2,1)S(1)} %collective-permute-done.2.refs_1_.refs_2_, bf16[128,1792]{1,0:T(8,128)(2,1)} %collective-permute-done.3.refs_2_.refs_3_, ...), custom_call_target="tpu_custom_call" | custom-call | flops 7516192 | bytes 26738 | tf_op jit(solution)/shard_map/base/pallas_call | solution.py:117
  51.2 2.4 %constant_dynamic-slice_fusion.3 = bf16[256,2048]{1,0:T(8,128)(2,1)} fusion(bf16[256,8192]{1,0:T(8,128)(2,1)} %refs_4_.5, s32[]{:T(128)S(6)} %select_n.104), kind=kLoop, calls=%fused_computation.34 | loop fusion | bytes 2097156 | tf_op jit(solution)/shard_map/dynamic_slice | solution.py:422
  53.6 4.5 %scores.5 = (f32[4,64,128]{2,1,0:T(8,128)S(1)}, bf16[4,64,128]{2,1,0:T(8,128)(2,1)S(1)}) custom-call(s32[17]{0:T(128)S(1)} %pad_add_fusion.refs_0_, bf16[128,3584]{1,0:T(8,128)(2,1)S(1)} %collective-permute-done.1.refs_1_.refs_0_, bf16[128,3584]{1,0:T(8,128)(2,1)S(1)} %collective-permute-done.6.refs_2_.refs_1_, bf16[16,64,7168]{2,1,0:T(8,128)(2,1)} %refs_3_.7, ...), custom_call_target="tpu_custom_call" | custom-call | flops 469762 | bytes 5505 | tf_op jit(solution)/shard_map/scores/pallas_call | solution.py:231
  60.9 3.1 %base.8 = f32[256,512]{1,0:T(8,128)S(1)} custom-call(bf16[128,3584]{1,0:T(8,128)(2,1)S(1)} %collective-permute-done.1.refs_1_.refs_0_, bf16[128,3584]{1,0:T(8,128)(2,1)S(1)} %collective-permute-done.6.refs_2_.refs_1_, f32[512,2048]{1,0:T(8,128)} %base.7.refs_2_, bf16[7168,2048]{1,0:T(8,128)(2,1)} %refs_3_.11), custom_call_target="tpu_custom_call" | custom-call | flops 939524096 | bytes 6553600 | tf_op jit(solution)/shard_map/base/pallas_call | solution.py:117
  66.0 1.6 %collective-permute-start.11 = (bf16[4,64,128]{2,1,0:T(8,128)(2,1)S(1)}, bf16[4,64,128]{2,1,0:T(8,128)(2,1)S(1)}, u32[]{:S(2)}, u32[]{:S(2)}) collective-permute-start(bf16[4,64,128]{2,1,0:T(8,128)(2,1)S(1)} %fusion.6), channel_id=1, source_target_pairs={{0,1},{1,0},{2,3},{3,2},{4,5},{5,4},{6,7},{7,6},{8,9},{9,8},{10,11... | collective-permute-start | bytes 196616 | tf_op jit(solution)/shard_map/ppermute | solution.py:22
  67.6 3.1 %base.9 = f32[256,512]{1,0:T(8,128)S(1)} custom-call(bf16[128,3584]{1,0:T(8,128)(2,1)S(1)} %collective-permute-done.1.refs_1_.refs_0_, bf16[128,3584]{1,0:T(8,128)(2,1)S(1)} %collective-permute-done.6.refs_2_.refs_1_, f32[512,2048]{1,0:T(8,128)} %base.7.refs_2_, bf16[7168,2048]{1,0:T(8,128)(2,1)} %refs_3_.11), custom_call_target="tpu_custom_call" | custom-call | flops 939524096 | bytes 6553600 | tf_op jit(solution)/shard_map/base/pallas_call | solution.py:117
  70.7 2.7 %collective-permute-start.13 = (bf16[4,64,128]{2,1,0:T(8,128)(2,1)S(1)}, bf16[4,64,128]{2,1,0:T(8,128)(2,1)S(1)}, u32[]{:S(2)}, u32[]{:S(2)}) collective-permute-start(bf16[4,64,128]{2,1,0:T(8,128)(2,1)S(1)} %get-tuple-element.161), channel_id=1, source_target_pairs={{0,2},{1,3},{2,0},{3,1},{4,6},{5,7},{6,4},{7,5},{8,10},{9,11},{10,... | collective-permute-start | bytes 196616 | tf_op jit(solution)/shard_map/ppermute | solution.py:22
  73.4 2.2 %constant_dynamic-slice_fusion.8 = (bf16[256,512]{1,0:T(8,128)(2,1)}, bf16[256,512]{1,0:T(8,128)(2,1)}, bf16[256,512]{1,0:T(8,128)(2,1)}, bf16[256,512]{1,0:T(8,128)(2,1)}) fusion(bf16[256,8192]{1,0:T(8,128)(2,1)} %refs_4_.5, s32[]{:T(128)S(6)} %select_n.108, s32[]{:T(128)S(6)} %select_n.107, s32[]{:T(128)S(6)} %select_n.106, s32[]{:T(128)S(6)} %select_n.105), kind=kLoop, calls=%fused_computation.39 | loop fusion | bytes 2097168 | tf_op jit(solution)/shard_map/dynamic_slice | solution.py:354
  78.5 3.3 %combine.4 = (f32[2,128,512]{2,1,0:T(8,128)S(1)}, bf16[2,128,512]{2,1,0:T(8,128)(2,1)}, bf16[512,1024]{1,0:T(8,128)(2,1)S(1)}) custom-call(s32[10]{0:T(128)S(1)} %stack.40.refs_0_, f32[4,64,128]{2,1,0:T(8,128)S(1)} %get-tuple-element.162.refs_1_, bf16[4,64,128]{2,1,0:T(8,128)(2,1)S(1)} %collective-permute-done.13.refs_2_, s32[4,128,128]{2,1,0:T(8,128)S(1)} %copy-done.6, ...), custom_call_target="tpu_custom_call" | custom-call | flops 536870 | bytes 2752 | tf_op jit(solution)/shard_map/combine/pallas_call | solution.py:319
  85.4 1.4 %collective-permute-start.25 = (bf16[256,512]{1,0:T(8,128)(2,1)}, bf16[256,512]{1,0:T(8,128)(2,1)S(1)}, u32[]{:S(2)}, u32[]{:S(2)}) collective-permute-start(bf16[256,512]{1,0:T(8,128)(2,1)} %get-tuple-element.154), channel_id=1, source_target_pairs={{0,12},{4,8},{8,4},{12,0},{1,13},{5,9},{9,5},{13,1},{2,14},{6,10},... | collective-permute-start | bytes 786440 | tf_op jit(solution)/shard_map/ppermute | solution.py:22
  86.8 3.2 %base.10 = f32[256,512]{1,0:T(8,128)S(1)} custom-call(bf16[128,3584]{1,0:T(8,128)(2,1)S(1)} %collective-permute-done.1.refs_1_.refs_0_, bf16[128,3584]{1,0:T(8,128)(2,1)S(1)} %collective-permute-done.6.refs_2_.refs_1_, f32[512,2048]{1,0:T(8,128)} %base.7.refs_2_, bf16[7168,2048]{1,0:T(8,128)(2,1)} %refs_3_.11), custom_call_target="tpu_custom_call" | custom-call | flops 939524 | bytes 6553 | tf_op jit(solution)/shard_map/base/pallas_call | solution.py:117
  90.1 2.5 %combine.5 = (f32[2,128,512]{2,1,0:T(8,128)S(1)}, bf16[2,128,512]{2,1,0:T(8,128)(2,1)S(1)}) custom-call(s32[10]{0:T(128)S(1)} %stack.40.refs_0_, bf16[512,1024]{1,0:T(8,128)(2,1)S(1)} %copy-done.4, f32[4,128,2048]{2,1,0:T(8,128)} %bitcast.44, f32[2,128,512]{2,1,0:T(8,128)S(1)} %bitcast.37, bf16[256,8192]{1,0:T(8,128)(2,1)} %refs_4_.5, ...), custom_call_target="tpu_custom_call" | custom-call | flops 536870 | bytes 2752 | tf_op jit(solution)/shard_map/combine/pallas_call | solution.py:319
  94.7 2.1 %collective-permute-start.19 = (bf16[128,512]{1,0:T(8,128)(2,1)S(1)}, bf16[128,512]{1,0:T(8,128)(2,1)S(1)}, u32[]{:S(2)}, u32[]{:S(2)}) collective-permute-start(bf16[128,512]{1,0:T(8,128)(2,1)S(1)} %fusion.2), channel_id=1, source_target_pairs={{0,2},{1,3},{2,0},{3,1},{4,6},{5,7},{6,4},{7,5},{8,10},{9,11},{10,... | collective-permute-start | bytes 393224 | tf_op jit(solution)/shard_map/ppermute | solution.py:22
  96.8 2.4 %combine.6 = (f32[2,128,512]{2,1,0:T(8,128)S(1)}, bf16[2,128,512]{2,1,0:T(8,128)(2,1)S(1)}) custom-call(s32[10]{0:T(128)S(1)} %stack.40.refs_0_, bf16[512,1024]{1,0:T(8,128)(2,1)S(1)} %copy-done.4, f32[4,128,2048]{2,1,0:T(8,128)} %bitcast.45, f32[2,128,512]{2,1,0:T(8,128)S(1)} %bitcast.39, bf16[256,8192]{1,0:T(8,128)(2,1)} %refs_4_.5, ...), custom_call_target="tpu_custom_call" | custom-call | flops 536870 | bytes 2752 | tf_op jit(solution)/shard_map/combine/pallas_call | solution.py:319
  99.3 1.9 %collective-permute-start.23 = (bf16[2,128,512]{2,1,0:T(8,128)(2,1)S(1)}, bf16[2,128,512]{2,1,0:T(8,128)(2,1)S(1)}, u32[]{:S(2)}, u32[]{:S(2)}) collective-permute-start(bf16[2,128,512]{2,1,0:T(8,128)(2,1)S(1)} %get-tuple-element.145), channel_id=1, source_target_pairs={{0,1},{1,0},{2,3},{3,2},{4,5},{5,4},{6,7},{7,6},{8,9},{9,8},{10,11... | collective-permute-start | bytes 786440 | tf_op jit(solution)/shard_map/ppermute | solution.py:22
  101.1 3.5 %collective-permute-done.20 = bf16[2,128,512]{2,1,0:T(8,128)(2,1)S(1)} collective-permute-done((bf16[2,128,512]{2,1,0:T(8,128)(2,1)S(1)}, bf16[2,128,512]{2,1,0:T(8,128)(2,1)S(1)}, u32[]{:S(2)}, u32[]{:S(2)}) %collective-permute-start.20) | collective-permute-done | bytes 262176 | tf_op jit(solution)/shard_map/ppermute | solution.py:22
  105.4 3.1 %base.11 = f32[256,512]{1,0:T(8,128)S(1)} custom-call(bf16[128,3584]{1,0:T(8,128)(2,1)S(1)} %collective-permute-done.1.refs_1_.refs_0_, bf16[128,3584]{1,0:T(8,128)(2,1)S(1)} %collective-permute-done.6.refs_2_.refs_1_, f32[512,2048]{1,0:T(8,128)} %base.7.refs_2_, bf16[7168,2048]{1,0:T(8,128)(2,1)} %refs_3_.11), custom_call_target="tpu_custom_call" | custom-call | flops 939524 | bytes 6553 | tf_op jit(solution)/shard_map/base/pallas_call | solution.py:117
  108.6 2.4 %combine.7 = (f32[2,128,512]{2,1,0:T(8,128)S(1)}, bf16[2,128,512]{2,1,0:T(8,128)(2,1)S(1)}) custom-call(s32[10]{0:T(128)S(1)} %stack.40.refs_0_, bf16[512,1024]{1,0:T(8,128)(2,1)S(1)} %copy-done.4, f32[4,128,2048]{2,1,0:T(8,128)} %bitcast.46, f32[2,128,512]{2,1,0:T(8,128)S(1)} %bitcast.40, bf16[256,8192]{1,0:T(8,128)(2,1)} %refs_4_.5, ...), custom_call_target="tpu_custom_call" | custom-call | flops 536870 | bytes 2752 | tf_op jit(solution)/shard_map/combine/pallas_call | solution.py:319
  110.9 2.5 %collective-permute-start.27 = (bf16[2,128,512]{2,1,0:T(8,128)(2,1)S(1)}, bf16[2,128,512]{2,1,0:T(8,128)(2,1)S(1)}, u32[]{:S(2)}, u32[]{:S(2)}) collective-permute-start(bf16[2,128,512]{2,1,0:T(8,128)(2,1)S(1)} %get-tuple-element.156), channel_id=1, source_target_pairs={{0,1},{1,0},{2,3},{3,2},{4,5},{5,4},{6,7},{7,6},{8,9},{9,8},{10,11... | collective-permute-start | bytes 786440 | tf_op jit(solution)/shard_map/ppermute | solution.py:22
  114.3 5.5 %collective-permute-done.27 = bf16[2,128,512]{2,1,0:T(8,128)(2,1)S(1)} collective-permute-done((bf16[2,128,512]{2,1,0:T(8,128)(2,1)S(1)}, bf16[2,128,512]{2,1,0:T(8,128)(2,1)S(1)}, u32[]{:S(2)}, u32[]{:S(2)}) %collective-permute-start.27) | collective-permute-done | bytes 262176 | tf_op jit(solution)/shard_map/ppermute | solution.py:22
  119.9 2.4 %collective-permute-start.28 = (bf16[128,512]{1,0:T(8,128)(2,1)S(1)}, bf16[128,512]{1,0:T(8,128)(2,1)S(1)}, u32[]{:S(2)}, u32[]{:S(2)}) collective-permute-start(bf16[128,512]{1,0:T(8,128)(2,1)S(1)} %fusion.5), channel_id=1, source_target_pairs={{0,2},{1,3},{2,0},{3,1},{4,6},{5,7},{6,4},{7,5},{8,10},{9,11},{10,... | collective-permute-start | bytes 393224 | tf_op jit(solution)/shard_map/ppermute | solution.py:22
  122.4 6.2 %collective-permute-done.28 = bf16[128,512]{1,0:T(8,128)(2,1)S(1)} collective-permute-done((bf16[128,512]{1,0:T(8,128)(2,1)S(1)}, bf16[128,512]{1,0:T(8,128)(2,1)S(1)}, u32[]{:S(2)}, u32[]{:S(2)}) %collective-permute-start.28) | collective-permute-done | bytes 131104 | tf_op jit(solution)/shard_map/ppermute | solution.py:22
  (103 shorter events, 21.7 us)
Async XLA Ops:
  0.0 8.4 %collective-permute-start = (bf16[128,7168]{1,0:T(8,128)(2,1)}, bf16[128,7168]{1,0:T(8,128)(2,1)S(1)}, u32[]{:S(2)}, u32[]{:S(2)}) collective-permute-start(bf16[128,7168]{1,0:T(8,128)(2,1)} %refs_0_.1), channel_id=1, source_target_pairs={{0,4},{4,0},{8,12},{12,8},{1,5},{5,1},{9,13},{13,9},{2,6},{6,2},{1... | collective-permute-start | bytes 5505032 | tf_op jit(solution)/shard_map/ppermute | solution.py:22
  3.4 24.9 %collective-permute-start.2 = (bf16[128,1792]{1,0:T(8,128)(2,1)}, bf16[128,1792]{1,0:T(8,128)(2,1)S(1)}, u32[]{:S(2)}, u32[]{:S(2)}) collective-permute-start(bf16[128,1792]{1,0:T(8,128)(2,1)} %get-tuple-element.90), channel_id=1, source_target_pairs={{0,8},{4,12},{8,0},{12,4},{1,9},{5,13},{9,1},{13,5},{2,10},{6,14},... | collective-permute-start | bytes 1376264 | tf_op jit(solution)/shard_map/ppermute | solution.py:22
  6.0 22.3 %collective-permute-start.3 = (bf16[128,1792]{1,0:T(8,128)(2,1)}, bf16[128,1792]{1,0:T(8,128)(2,1)}, u32[]{:S(2)}, u32[]{:S(2)}) collective-permute-start(bf16[128,1792]{1,0:T(8,128)(2,1)} %get-tuple-element.91), channel_id=1, source_target_pairs={{0,8},{4,12},{8,0},{12,4},{1,9},{5,13},{9,1},{13,5},{2,10},{6,14},... | collective-permute-start | bytes 1376264 | tf_op jit(solution)/shard_map/ppermute | solution.py:22
  17.0 32.9 %collective-permute-start.1 = (bf16[128,3584]{1,0:T(8,128)(2,1)}, bf16[128,3584]{1,0:T(8,128)(2,1)S(1)}, u32[]{:S(2)}, u32[]{:S(2)}) collective-permute-start(bf16[128,3584]{1,0:T(8,128)(2,1)} %get-tuple-element.89), channel_id=1, source_target_pairs={{0,8},{4,12},{8,0},{12,4},{1,9},{5,13},{9,1},{13,5},{2,10},{6,14},... | collective-permute-start | bytes 2752520 | tf_op jit(solution)/shard_map/ppermute | solution.py:22
  28.3 2.7 %collective-permute-start.5 = (bf16[128,1792]{1,0:T(8,128)(2,1)}, bf16[128,1792]{1,0:T(8,128)(2,1)}, u32[]{:S(2)}, u32[]{:S(2)}) collective-permute-start(bf16[128,1792]{1,0:T(8,128)(2,1)} %collective-permute-done.3.refs_2_.refs_3_), channel_id=1, source_target_pairs={{0,4},{4,0},{8,12},{12,8},{1,5},{5,1},{9,13},{13,9},{2,6},{6,2},{1... | collective-permute-start | bytes 1376264 | tf_op jit(solution)/shard_map/ppermute | solution.py:22
  28.3 2.7 %collective-permute-start.4 = (bf16[128,1792]{1,0:T(8,128)(2,1)S(1)}, bf16[128,1792]{1,0:T(8,128)(2,1)}, u32[]{:S(2)}, u32[]{:S(2)}) collective-permute-start(bf16[128,1792]{1,0:T(8,128)(2,1)S(1)} %collective-permute-done.2.refs_1_.refs_2_), channel_id=1, source_target_pairs={{0,4},{4,0},{8,12},{12,8},{1,5},{5,1},{9,13},{13,9},{2,6},{6,2},{1... | collective-permute-start | bytes 1376264 | tf_op jit(solution)/shard_map/ppermute | solution.py:22
  49.8 3.7 %collective-permute-start.6 = (bf16[128,3584]{1,0:T(8,128)(2,1)S(1)}, bf16[128,3584]{1,0:T(8,128)(2,1)S(1)}, u32[]{:S(2)}, u32[]{:S(2)}) collective-permute-start(bf16[128,3584]{1,0:T(8,128)(2,1)S(1)} %collective-permute-done.1.refs_1_.refs_0_), channel_id=1, source_target_pairs={{0,4},{4,0},{8,12},{12,8},{1,5},{5,1},{9,13},{13,9},{2,6},{6,2},{1... | collective-permute-start | bytes 2752520 | tf_op jit(solution)/shard_map/ppermute | solution.py:22
  49.9 10.4 %collective-permute-start.10 = (bf16[256,512]{1,0:T(8,128)(2,1)}, bf16[256,512]{1,0:T(8,128)(2,1)S(1)}, u32[]{:S(2)}, u32[]{:S(2)}) collective-permute-start(bf16[256,512]{1,0:T(8,128)(2,1)} %get-tuple-element.106), channel_id=1, source_target_pairs={{0,8},{4,12},{8,0},{12,4},{1,9},{5,13},{9,1},{13,5},{2,10},{6,14},... | collective-permute-start | bytes 786440 | tf_op jit(solution)/shard_map/ppermute | solution.py:22
  53.6 24.9 %collective-permute-start.15 = (bf16[256,2048]{1,0:T(8,128)(2,1)}, bf16[256,2048]{1,0:T(8,128)(2,1)S(1)}, u32[]{:S(2)}, u32[]{:S(2)}) collective-permute-start(bf16[256,2048]{1,0:T(8,128)(2,1)} %constant_dynamic-slice_fusion.3), channel_id=1, source_target_pairs={{0,4},{4,0},{8,12},{12,8},{1,5},{5,1},{9,13},{13,9},{2,6},{6,2},{1... | collective-permute-start | bytes 3145736 | tf_op jit(solution)/shard_map/ppermute | solution.py:22
  53.6 6.7 %copy-start.14 = (bf16[256,512]{1,0:T(8,128)(2,1)S(1)}, bf16[256,512]{1,0:T(8,128)(2,1)}, u32[]{:S(2)}) copy-start(bf16[256,512]{1,0:T(8,128)(2,1)} %get-tuple-element.114) | copy-start | bytes 786436
  58.1 5.9 %collective-permute-start.9 = (bf16[4,64,128]{2,1,0:T(8,128)(2,1)S(1)}, bf16[4,64,128]{2,1,0:T(8,128)(2,1)S(1)}, u32[]{:S(2)}, u32[]{:S(2)}) collective-permute-start(bf16[4,64,128]{2,1,0:T(8,128)(2,1)S(1)} %get-tuple-element.105), channel_id=1, source_target_pairs={{0,4},{4,0},{8,12},{12,8},{1,5},{5,1},{9,13},{13,9},{2,6},{6,2},{1... | collective-permute-start | bytes 196616 | tf_op jit(solution)/shard_map/ppermute | solution.py:22
  58.6 6.7 %collective-permute-start.8 = (bf16[4,64,128]{2,1,0:T(8,128)(2,1)S(1)}, bf16[4,64,128]{2,1,0:T(8,128)(2,1)S(1)}, u32[]{:S(2)}, u32[]{:S(2)}) collective-permute-start(bf16[4,64,128]{2,1,0:T(8,128)(2,1)S(1)} %get-tuple-element.105), channel_id=1, source_target_pairs={{0,12},{4,8},{8,4},{12,0},{1,13},{5,9},{9,5},{13,1},{2,14},{6,10},... | collective-permute-start | bytes 196616 | tf_op jit(solution)/shard_map/ppermute | solution.py:22
  59.2 6.7 %collective-permute-start.7 = (bf16[4,64,128]{2,1,0:T(8,128)(2,1)S(1)}, bf16[4,64,128]{2,1,0:T(8,128)(2,1)S(1)}, u32[]{:S(2)}, u32[]{:S(2)}) collective-permute-start(bf16[4,64,128]{2,1,0:T(8,128)(2,1)S(1)} %get-tuple-element.105), channel_id=1, source_target_pairs={{0,8},{4,12},{8,0},{12,4},{1,9},{5,13},{9,1},{13,5},{2,10},{6,14},... | collective-permute-start | bytes 196616 | tf_op jit(solution)/shard_map/ppermute | solution.py:22
  60.4 10.3 %collective-permute-start.12 = (bf16[256,512]{1,0:T(8,128)(2,1)S(1)}, bf16[256,512]{1,0:T(8,128)(2,1)S(1)}, u32[]{:S(2)}, u32[]{:S(2)}) collective-permute-start(bf16[256,512]{1,0:T(8,128)(2,1)S(1)} %copy-done.14), channel_id=1, source_target_pairs={{0,12},{4,8},{8,4},{12,0},{1,13},{5,9},{9,5},{13,1},{2,14},{6,10},... | collective-permute-start | bytes 786440 | tf_op jit(solution)/shard_map/ppermute | solution.py:22
  64.0 11.9 %collective-permute-start.14 = (bf16[256,512]{1,0:T(8,128)(2,1)S(1)}, bf16[256,512]{1,0:T(8,128)(2,1)S(1)}, u32[]{:S(2)}, u32[]{:S(2)}) collective-permute-start(bf16[256,512]{1,0:T(8,128)(2,1)S(1)} %copy-done.13), channel_id=1, source_target_pairs={{0,8},{4,12},{8,0},{12,4},{1,9},{5,13},{9,1},{13,5},{2,10},{6,14},... | collective-permute-start | bytes 786440 | tf_op jit(solution)/shard_map/ppermute | solution.py:22
  65.4 18.8 %collective-permute-start.18 = (bf16[256,512]{1,0:T(8,128)(2,1)}, bf16[256,512]{1,0:T(8,128)(2,1)}, u32[]{:S(2)}, u32[]{:S(2)}) collective-permute-start(bf16[256,512]{1,0:T(8,128)(2,1)} %get-tuple-element.135), channel_id=1, source_target_pairs={{0,12},{4,8},{8,4},{12,0},{1,13},{5,9},{9,5},{13,1},{2,14},{6,10},... | collective-permute-start | bytes 786440 | tf_op jit(solution)/shard_map/ppermute | solution.py:22
  65.9 12.5 %copy-start.6 = (s32[4,128,128]{2,1,0:T(8,128)S(1)}, s32[4,128,128]{2,1,0:T(8,128)}, u32[]{:S(2)}) copy-start(s32[4,128,128]{2,1,0:T(8,128)} %broadcast_in_dim.96.refs_3_) | copy-start | bytes 786436
  65.9 12.5 %copy-start.10 = (bf16[256,512]{1,0:T(8,128)(2,1)S(1)}, bf16[256,512]{1,0:T(8,128)(2,1)}, u32[]{:S(2)}) copy-start(bf16[256,512]{1,0:T(8,128)(2,1)} %copy-done.9) | copy-start | bytes 786436
  66.0 4.7 %collective-permute-start.11 = (bf16[4,64,128]{2,1,0:T(8,128)(2,1)S(1)}, bf16[4,64,128]{2,1,0:T(8,128)(2,1)S(1)}, u32[]{:S(2)}, u32[]{:S(2)}) collective-permute-start(bf16[4,64,128]{2,1,0:T(8,128)(2,1)S(1)} %fusion.6), channel_id=1, source_target_pairs={{0,1},{1,0},{2,3},{3,2},{4,5},{5,4},{6,7},{7,6},{8,9},{9,8},{10,11... | collective-permute-start | bytes 196616 | tf_op jit(solution)/shard_map/ppermute | solution.py:22
  70.7 6.4 %collective-permute-start.13 = (bf16[4,64,128]{2,1,0:T(8,128)(2,1)S(1)}, bf16[4,64,128]{2,1,0:T(8,128)(2,1)S(1)}, u32[]{:S(2)}, u32[]{:S(2)}) collective-permute-start(bf16[4,64,128]{2,1,0:T(8,128)(2,1)S(1)} %get-tuple-element.161), channel_id=1, source_target_pairs={{0,2},{1,3},{2,0},{3,1},{4,6},{5,7},{6,4},{7,5},{8,10},{9,11},{10,... | collective-permute-start | bytes 196616 | tf_op jit(solution)/shard_map/ppermute | solution.py:22
  77.2 12.9 %collective-permute-start.17 = (bf16[256,512]{1,0:T(8,128)(2,1)}, bf16[256,512]{1,0:T(8,128)(2,1)}, u32[]{:S(2)}, u32[]{:S(2)}) collective-permute-start(bf16[256,512]{1,0:T(8,128)(2,1)} %get-tuple-element.129), channel_id=1, source_target_pairs={{0,8},{4,12},{8,0},{12,4},{1,9},{5,13},{9,1},{13,5},{2,10},{6,14},... | collective-permute-start | bytes 786440 | tf_op jit(solution)/shard_map/ppermute | solution.py:22
  83.6 10.1 %collective-permute-start.16 = (bf16[2,128,512]{2,1,0:T(8,128)(2,1)}, bf16[2,128,512]{2,1,0:T(8,128)(2,1)}, u32[]{:S(2)}, u32[]{:S(2)}) collective-permute-start(bf16[2,128,512]{2,1,0:T(8,128)(2,1)} %get-tuple-element.126), channel_id=1, source_target_pairs={{0,1},{1,0},{2,3},{3,2},{4,5},{5,4},{6,7},{7,6},{8,9},{9,8},{10,11... | collective-permute-start | bytes 786440 | tf_op jit(solution)/shard_map/ppermute | solution.py:22
  84.1 12.7 %collective-permute-start.21 = (bf16[256,512]{1,0:T(8,128)(2,1)}, bf16[256,512]{1,0:T(8,128)(2,1)S(1)}, u32[]{:S(2)}, u32[]{:S(2)}) collective-permute-start(bf16[256,512]{1,0:T(8,128)(2,1)} %get-tuple-element.143), channel_id=1, source_target_pairs={{0,12},{4,8},{8,4},{12,0},{1,13},{5,9},{9,5},{13,1},{2,14},{6,10},... | collective-permute-start | bytes 786440 | tf_op jit(solution)/shard_map/ppermute | solution.py:22
  84.2 21.2 %collective-permute-start.24 = (bf16[256,512]{1,0:T(8,128)(2,1)}, bf16[256,512]{1,0:T(8,128)(2,1)S(1)}, u32[]{:S(2)}, u32[]{:S(2)}) collective-permute-start(bf16[256,512]{1,0:T(8,128)(2,1)} %get-tuple-element.151), channel_id=1, source_target_pairs={{0,8},{4,12},{8,0},{12,4},{1,9},{5,13},{9,1},{13,5},{2,10},{6,14},... | collective-permute-start | bytes 786440 | tf_op jit(solution)/shard_map/ppermute | solution.py:22
  85.4 20.0 %collective-permute-start.25 = (bf16[256,512]{1,0:T(8,128)(2,1)}, bf16[256,512]{1,0:T(8,128)(2,1)S(1)}, u32[]{:S(2)}, u32[]{:S(2)}) collective-permute-start(bf16[256,512]{1,0:T(8,128)(2,1)} %get-tuple-element.154), channel_id=1, source_target_pairs={{0,12},{4,8},{8,4},{12,0},{1,13},{5,9},{9,5},{13,1},{2,14},{6,10},... | collective-permute-start | bytes 786440 | tf_op jit(solution)/shard_map/ppermute | solution.py:22
  92.6 12.1 %collective-permute-start.20 = (bf16[2,128,512]{2,1,0:T(8,128)(2,1)S(1)}, bf16[2,128,512]{2,1,0:T(8,128)(2,1)S(1)}, u32[]{:S(2)}, u32[]{:S(2)}) collective-permute-start(bf16[2,128,512]{2,1,0:T(8,128)(2,1)S(1)} %get-tuple-element.137), channel_id=1, source_target_pairs={{0,1},{1,0},{2,3},{3,2},{4,5},{5,4},{6,7},{7,6},{8,9},{9,8},{10,11... | collective-permute-start | bytes 786440 | tf_op jit(solution)/shard_map/ppermute | solution.py:22
  94.7 13.8 %collective-permute-start.19 = (bf16[128,512]{1,0:T(8,128)(2,1)S(1)}, bf16[128,512]{1,0:T(8,128)(2,1)S(1)}, u32[]{:S(2)}, u32[]{:S(2)}) collective-permute-start(bf16[128,512]{1,0:T(8,128)(2,1)S(1)} %fusion.2), channel_id=1, source_target_pairs={{0,2},{1,3},{2,0},{3,1},{4,6},{5,7},{6,4},{7,5},{8,10},{9,11},{10,... | collective-permute-start | bytes 393224 | tf_op jit(solution)/shard_map/ppermute | solution.py:22
  99.3 14.3 %collective-permute-start.23 = (bf16[2,128,512]{2,1,0:T(8,128)(2,1)S(1)}, bf16[2,128,512]{2,1,0:T(8,128)(2,1)S(1)}, u32[]{:S(2)}, u32[]{:S(2)}) collective-permute-start(bf16[2,128,512]{2,1,0:T(8,128)(2,1)S(1)} %get-tuple-element.145), channel_id=1, source_target_pairs={{0,1},{1,0},{2,3},{3,2},{4,5},{5,4},{6,7},{7,6},{8,9},{9,8},{10,11... | collective-permute-start | bytes 786440 | tf_op jit(solution)/shard_map/ppermute | solution.py:22
  104.8 8.7 %collective-permute-start.22 = (bf16[128,512]{1,0:T(8,128)(2,1)S(1)}, bf16[128,512]{1,0:T(8,128)(2,1)S(1)}, u32[]{:S(2)}, u32[]{:S(2)}) collective-permute-start(bf16[128,512]{1,0:T(8,128)(2,1)S(1)} %fusion.3), channel_id=1, source_target_pairs={{0,2},{1,3},{2,0},{3,1},{4,6},{5,7},{6,4},{7,5},{8,10},{9,11},{10,... | collective-permute-start | bytes 393224 | tf_op jit(solution)/shard_map/ppermute | solution.py:22
  110.9 8.9 %collective-permute-start.27 = (bf16[2,128,512]{2,1,0:T(8,128)(2,1)S(1)}, bf16[2,128,512]{2,1,0:T(8,128)(2,1)S(1)}, u32[]{:S(2)}, u32[]{:S(2)}) collective-permute-start(bf16[2,128,512]{2,1,0:T(8,128)(2,1)S(1)} %get-tuple-element.156), channel_id=1, source_target_pairs={{0,1},{1,0},{2,3},{3,2},{4,5},{5,4},{6,7},{7,6},{8,9},{9,8},{10,11... | collective-permute-start | bytes 786440 | tf_op jit(solution)/shard_map/ppermute | solution.py:22
  113.7 8.7 %collective-permute-start.26 = (bf16[128,512]{1,0:T(8,128)(2,1)S(1)}, bf16[128,512]{1,0:T(8,128)(2,1)S(1)}, u32[]{:S(2)}, u32[]{:S(2)}) collective-permute-start(bf16[128,512]{1,0:T(8,128)(2,1)S(1)} %fusion.4), channel_id=1, source_target_pairs={{0,2},{1,3},{2,0},{3,1},{4,6},{5,7},{6,4},{7,5},{8,10},{9,11},{10,... | collective-permute-start | bytes 393224 | tf_op jit(solution)/shard_map/ppermute | solution.py:22
  119.9 8.7 %collective-permute-start.28 = (bf16[128,512]{1,0:T(8,128)(2,1)S(1)}, bf16[128,512]{1,0:T(8,128)(2,1)S(1)}, u32[]{:S(2)}, u32[]{:S(2)}) collective-permute-start(bf16[128,512]{1,0:T(8,128)(2,1)S(1)} %fusion.5), channel_id=1, source_target_pairs={{0,2},{1,3},{2,0},{3,1},{4,6},{5,7},{6,4},{7,5},{8,10},{9,11},{10,... | collective-permute-start | bytes 393224 | tf_op jit(solution)/shard_map/ppermute | solution.py:22
  (12 other events, 37.0 us)
